TPU v7x, 256 devices: a whole 4x4x8 slice. The times are simulated.
256 devices in a mesh: ctx: 32 (over y, z_hi, core), section: 8 (over z_lo, x).
Axes of the slice: x: 4, y: 4, z: 8 (z_hi: 4, z_lo: 2; z = z_hi * 2 + z_lo), core: 2. Of those that a mesh axis runs over, the one named last changes fastest.
Arguments:
- hidden: bfloat16 [8192, 5120], P('ctx'), may hold values from -6 to 6
- k_cache: bfloat16 [8192, 1024], P('ctx', 'section'), may hold values from -200 to 200
- v_cache: bfloat16 [8192, 1024], P('ctx', 'section'), may hold values from -6 to 6
- segment: int32 [8192], P('ctx'), may hold values from 0 to 15, never falling along the last dimension, each value on 1 to 6144 neighbouring positions
- w_query: bfloat16 [5120, 4096], P(None, 'section'), may hold values from -0.078125 to 0.078125
- w_out: bfloat16 [4096, 5120], P('section'), may hold values from -0.25 to 0.25
Outputs:
- mixed: bfloat16 [8192, 5120], P('ctx', 'section')
Inputs may be any that keep to these rules, and one draw needn't show every extreme that they name: `segment`: document ids never fall along the tokens.
All inputs are finite; a program needn't handle non-finite values.
Results may differ from a plain program's by a relative error of at most 0.018.
The roundings to bfloat16 on the way count: a program that leaves them out, or rounds other values in their place, can miss the bound.
Values may be sent and summed in bfloat16 or wider, within the bound.
No kernel may reach another device: no remote copies, remote signals or barrier semaphores. Data moves between devices by JAX's collectives and lax.ppermute only.
A program may use at most 128 MiB of HBM per device.

v0:
```python
import jax
import jax.numpy as jnp
from jax import lax
from jax.sharding import PartitionSpec as P

HEAD_DIM = 128


NEG_BIG = -1e30


def per_device(hidden, k_cache, v_cache, segment, w_query, w_out):
    tokens = hidden.shape[0]
    kv_local = k_cache.shape[1] // HEAD_DIM
    heads_local = w_query.shape[1] // HEAD_DIM
    per_group = heads_local // kv_local
    widened = hidden.astype(jnp.float32)
    normed = (
        widened * lax.rsqrt(jnp.mean(widened * widened, axis=-1, keepdims=True) + 1e-06)
    ).astype(jnp.bfloat16)
    queries = (
        jnp.dot(normed, w_query, preferred_element_type=jnp.float32) * HEAD_DIM ** (-0.5)
    ).astype(jnp.bfloat16)
    queries = queries.reshape(tokens, kv_local, per_group, HEAD_DIM)
    first_pos = lax.axis_index("ctx") * tokens
    query_pos = first_pos + jnp.arange(tokens, dtype=jnp.int32)
    row_shape = (kv_local, per_group, tokens)
    initial = (
        jnp.full(row_shape, NEG_BIG, jnp.float32),
        jnp.zeros(row_shape, jnp.float32),
        jnp.zeros(row_shape + (HEAD_DIM,), jnp.float32),
    )
    key_rows = lax.all_gather(k_cache, "ctx", axis=0, tiled=True)
    value_rows = lax.all_gather(v_cache, "ctx", axis=0, tiled=True)
    key_seg = lax.all_gather(segment, "ctx", axis=0, tiled=True)
    length = key_rows.shape[0]
    key_pos = jnp.arange(length, dtype=jnp.int32)
    visible = (key_pos[None, :] <= query_pos[:, None]) & (key_seg[None, :] == segment[:, None])

    def update(state_old):
        run_max, run_sum, run_acc = state_old
        key_heads = key_rows.reshape(length, kv_local, HEAD_DIM)
        value_heads = value_rows.reshape(length, kv_local, HEAD_DIM)
        scores = jnp.einsum(
            "tgrd,ngd->grtn", queries, key_heads, preferred_element_type=jnp.float32
        )
        masked = jnp.where(visible, scores, NEG_BIG)
        new_max = jnp.maximum(run_max, jnp.max(masked, axis=-1))
        weights = jnp.where(visible, jnp.exp(masked - new_max[..., None]), 0.0)
        new_sum = jnp.sum(weights, axis=-1)
        gathered_vals = jnp.einsum(
            "grtn,ngd->grtd",
            weights.astype(jnp.bfloat16),
            value_heads,
            preferred_element_type=jnp.float32,
        )
        return (new_max, new_sum, gathered_vals)

    final = lax.cond(jnp.any(visible), update, lambda state_old: state_old, initial)
    run_max, run_sum, run_acc = final
    attended = (
        (run_acc / run_sum[..., None])
        .transpose(2, 0, 1, 3)
        .reshape(tokens, heads_local * HEAD_DIM)
        .astype(jnp.bfloat16)
    )
    partial_value = jnp.dot(attended, w_out, preferred_element_type=jnp.float32)
    return lax.psum_scatter(
        partial_value.astype(jnp.bfloat16), "section", scatter_dimension=1, tiled=True
    )


def solution(mesh):
    return jax.shard_map(
        per_device,
        mesh=mesh,
        in_specs=(
            P("ctx", None),
            P("ctx", "section"),
            P("ctx", "section"),
            P("ctx"),
            P(None, "section"),
            P("section", None),
        ),
        out_specs=P("ctx", "section"),
        check_vma=False,
    )
```

profile of v0, /device:TPU:24, one launch (start us, length us, event | category | flops | bytes accessed | tf_op | source)
XLA Modules:
  0.0 224.5 jit_solution(10010100486645421310)
XLA Ops:
  6.5 0.0 all-gather.4.cloned.1.call-start
  6.5 0.7 all-gather.4.cloned.1.call-update
  7.3 0.0 all-gather.6.cloned.1.call-start
  7.3 0.7 all-gather.6.cloned.1.call-update
  8.0 0.0 reduce-scatter.4.cloned.1.call-start
  8.1 40.8 %all-gather = s32[32,1,256]{2,1,0:T(1,128)S(1)} all-gather(s32[1,1,256]{2,1,0:T(1,128)} %bitcast.62), channel_id=1, replica_groups=mesh['ctx'=32,'section'=8] {'ctx'}, dimensions={0}, use_global_device_ids=true | all-gather | bytes 33792 | tf_op jit(solution)/shard_map/all_gather | solution.py:35
  48.9 5.2 %fusion.19 = (pred[256,8192]{0,1:T(8,128)(4,1)S(1)}, pred[]{:T(512)}) fusion(s32[256]{0:T(256)} %param.11, s32[256]{0:T(256)S(1)} %iota_add_fusion, s32[8192]{0:T(1024)S(1)} %bitcast.59), kind=kLoop, calls=%fused_computation.18 | loop fusion | flops 8388607 | bytes 2131969 | tf_op jit(solution)/shard_map/and | solution.py:38
  54.8 2.4 %fusion.20 = f32[256]{0:T(256)S(1)} fusion(bf16[256,5120]{1,0:T(8,128)(2,1)} %param.8), kind=kLoop, calls=%fused_computation.22 | loop fusion | flops 3931904 | bytes 2622464 | tf_op jit(solution)/shard_map/reduce_sum | solution.py:19
  57.2 4.9 %fusion.28 = bf16[256,512]{1,0:T(8,128)(2,1)S(1)} fusion(bf16[5120,512]{1,0:T(8,128)(2,1)} %param.12, bf16[256,5120]{1,0:T(8,128)(2,1)} %param.8, f32[256]{0:T(256)S(1)} %add_rsqrt_fusion), kind=kOutput, calls=%fused_computation.27 | convolution fusion | flops 1346371584 | bytes 8127488 | tf_op jit(solution)/shard_map/dot_general | solution.py:22
  62.1 3.4 %all-gather.4.cloned.1.call-done = bf16[8192,128]{1,0:T(8,128)(2,1)} async-done(((bf16[256,128]{1,0:T(8,128)(2,1)}), bf16[8192,128]{1,0:T(8,128)(2,1)}) %all-gather.4.cloned.1.call-update) | async-done | bytes 2097168 | tf_op jit(solution)/shard_map/all_gather | solution.py:33
  65.6 54.3 %all-gather.6.cloned.1.call-done = bf16[8192,128]{1,0:T(8,128)(2,1)} async-done(((bf16[256,128]{1,0:T(8,128)(2,1)}), bf16[8192,128]{1,0:T(8,128)(2,1)}) %all-gather.6.cloned.1.call-update) | async-done | bytes 2097168 | tf_op jit(solution)/shard_map/all_gather | solution.py:34
  119.9 43.7 %conditional.1 = (f32[1,4,256]{2,1,0:T(4,128)S(1)}, f32[1,4,256,128]{2,3,1,0:T(8,128)S(1)}) conditional(s32[]{:T(128)} %convert_element_type.27, () %tuple.13, (pred[256,8192]{0,1:T(8,128)(4,1)S(1)}, bf16[256,512]{1,0:T(8,128)(2,1)S(1)}, bf16[8192,128]{1,0:T(8,128)(2,1)}, bf16[8192,128]{1,0:T(8,128)(2,1)}) %tuple.14), branch_computations={%region_2.0_spmd, %region_3.6_spmd} | conditional | flops 4378852352 | bytes 111960080 | solution.py:59
  119.9 14.8 %fusion = (f32[4,256]{1,0:T(4,128)S(1)}, f32[8192,256,4]{1,0,2:T(8,128)}) fusion(pred[256,8192]{0,1:T(8,128)(4,1)S(1)} %get-tuple-element.14, bf16[8192,128]{1,0:T(8,128)(2,1)} %get-tuple-element.15, bf16[256,512]{1,0:T(8,128)(2,1)S(1)} %get-tuple-element.16), kind=kOutput, calls=%fused_computation.2 | convolution fusion | flops 2164259840 | bytes 38014976 | tf_op jit(solution)/shard_map/cond/branch_1_fun/tgrd,ngd->grtn/dot_general | solution.py:44
  134.7 14.4 %fusion.10 = f32[1,4,256,128]{2,3,1,0:T(8,128)S(1)} fusion(bf16[8192,128]{1,0:T(8,128)(2,1)} %get-tuple-element.17, f32[8192,256,4]{1,0,2:T(8,128)} %get-tuple-element.24, f32[4,256]{1,0:T(4,128)S(1)} %broadcast_maximum_fusion, pred[256,8192]{0,1:T(8,128)(4,1)S(1)} %get-tuple-element.14), kind=kOutput, calls=%fused_computation.11 | convolution fusion | flops 2181038080 | bytes 38277120 | tf_op jit(solution)/shard_map/cond/branch_1_fun/grtn,ngd->grtd/dot_general | solution.py:51
  149.1 14.5 %fusion.2 = f32[4,256]{1,0:T(4,128)S(1)} fusion(f32[8192,256,4]{1,0,2:T(8,128)} %get-tuple-element.24, f32[4,256]{1,0:T(4,128)S(1)} %broadcast_maximum_fusion, pred[256,8192]{0,1:T(8,128)(4,1)S(1)} %get-tuple-element.14), kind=kLoop, calls=%fused_computation.4 | loop fusion | flops 33553408 | bytes 35659776 | tf_op jit(solution)/shard_map/cond/branch_1_fun/reduce_sum | solution.py:50
  163.6 4.0 %convolution_convert_fusion = bf16[256,5120]{1,0:T(8,128)(2,1)S(1)} fusion(bf16[256,512]{0,1:T(8,128)(2,1)S(1)} %bitcast.57, bf16[512,5120]{1,0:T(8,128)(2,1)} %param.13), kind=kOutput, calls=%fused_computation.21 | convolution fusion | flops 1343488000 | bytes 8126464 | tf_op jit(solution)/shard_map/dot_general | solution.py:67
  167.6 2.6 %copy.16 = bf16[256,5120]{0,1:T(8,128)(2,1)} copy(bf16[256,5120]{1,0:T(8,128)(2,1)S(1)} %convolution_convert_fusion) | data formatting | bytes 5242880
  170.2 0.0 reduce-scatter.4.cloned.1.call-update
  170.3 45.9 %reduce-scatter.4.cloned.1.call-done = bf16[640,256]{1,0:T(8,128)(2,1)} async-done(((bf16[5120,256]{1,0:T(8,128)(2,1)}), bf16[640,256]{1,0:T(8,128)(2,1)}) %reduce-scatter.4.cloned.1.call-update) | async-done | bytes 327696
  216.1 1.9 copy.17
  (4 shorter events, 0.1 us)
Async XLA Ops:
  6.5 59.0 %all-gather.4.cloned.1.call-start = ((), (), s32[]{:S(2)}) async-start(), calls=%async_computation.1 | async-start | bytes 2162688 | tf_op jit(solution)/shard_map/all_gather | solution.py:33
  7.3 112.6 %all-gather.6.cloned.1.call-start = ((), (), s32[]{:S(2)}) async-start(), calls=%async_computation.2 | async-start | bytes 2162688 | tf_op jit(solution)/shard_map/all_gather | solution.py:34
  8.0 208.1 %reduce-scatter.4.cloned.1.call-start = ((), (), s32[]{:S(2)}) async-start(), calls=%async_computation.3 | async-start | bytes 2949120
Sparse Core Ops, SparseCore 0:
  9.9 55.5 all-gather.3
  68.1 51.7 all-gather.5
  170.4 45.7 reduce-scatter.3
where the time goes:
time: 225 us
  waiting for transfers between devices  105 us (47%)
  blocking collectives  40.8 us (18%)
  matrix products  38.2 us (17%)
  other arithmetic  22.1 us (10%)
  between operations  13.8 us (6%)
  local copies, waits for them, and re-layouts  4.45 us (2%)
    all_gather x1, waiting for transfers between devices, per_device(): value_rows = lax.all_gather(v_cache, 'ctx', axis=0, tiled=True)  54.3 us
    unnamed x4, waiting for transfers between devices  47.3 us
    all_gather x1, blocking collectives, per_device(): key_seg = lax.all_gather(segment, 'ctx', axis=0, tiled=True)  40.8 us
    dot_general x1, matrix products, update(): jnp.einsum('tgrd,ngd->grtn', queries, key_heads, preferred_element_type=j...  14.8 us
    reduce_sum x1, other arithmetic, update(): new_sum = jnp.sum(weights, axis=-1)  14.5 us
    dot_general x1, matrix products, update(): jnp.einsum('grtn,ngd->grtd', weights.astype(jnp.bfloat16), value_heads, p...  14.4 us
    and x1, other arithmetic, per_device(): (key_pos[None, :] <= query_pos[:, None]) & (key_seg[None, :] == segment[:...  5.19 us
    dot_general x1, matrix products, per_device(): jnp.dot(normed, w_query, preferred_element_type=jnp.float32)  4.94 us
  transfers between devices with their start and end apart: 3, of which 3 were waited for; matrix products, arithmetic and copies ran while one was open for 6% of the time, Pallas kernels for 0%

commit v1 on v0

v1 whole, which is shorter than its diff:
```python
import functools

import jax
import jax.numpy as jnp
from jax import lax
from jax.experimental import pallas as pl
from jax.experimental.pallas import tpu as pltpu
from jax.sharding import PartitionSpec as P

HEAD_DIM = 128
BLOCK = 256
PACK = 2 * BLOCK + 16
REACH = 24
COLS = 640
FLOOR = -1e30
HIDDEN = -2e30

F32 = jnp.float32
BF16 = jnp.bfloat16


def ctx_id(y, z, c):
    return ((y + 8) % 4) * 8 + ((z + 8) % 4) * 2 + c


def ctx_pairs(step, planes=None):
    pairs = []
    for y in range(4):
        for z in range(4):
            for c in range(2):
                to = step(y, z, c)
                if to is not None:
                    pairs.append((ctx_id(y, z, c), ctx_id(*to)))
    return pairs


def move(x, step):
    return lax.ppermute(x, "ctx", ctx_pairs(step))


def swap_cores(x):
    return move(x, lambda y, z, c: (y, z, 1 - c))


def along_z(x):
    return move(x, lambda y, z, c: (y, z + 1 if c == 0 else z - 1, c))


def along_y(x):
    def step(y, z, c):
        if c == 0:
            return (y + 1, z, c) if y < 3 else None
        return (3, z, c) if y == 0 else None

    return move(x, step)


def attend_block(kv_ref, at, diagonal, q_ref, hot_ref, m_ref, l_ref, acc_ref):
    k = kv_ref[at, 0:BLOCK, :]
    v_t = jnp.transpose(kv_ref[at, BLOCK : 2 * BLOCK, :])
    counts = kv_ref[at, 2 * BLOCK : PACK, :]
    first = jnp.dot(counts, hot_ref[...], preferred_element_type=F32)[0:1, :]
    row = lax.broadcasted_iota(jnp.int32, (BLOCK, BLOCK), 0)
    visible = row >= first.astype(jnp.int32)
    if diagonal:
        visible &= row <= lax.broadcasted_iota(jnp.int32, (BLOCK, BLOCK), 1)
    for h in range(4):
        rows = slice(h * HEAD_DIM, (h + 1) * HEAD_DIM)
        s = jnp.dot(k, q_ref[rows, :], preferred_element_type=F32)
        s = jnp.where(visible, s, HIDDEN)
        m_old = m_ref[h : h + 1, :]
        m_new = jnp.maximum(m_old, jnp.max(s, axis=0, keepdims=True))
        p = jnp.exp(s - m_new)
        fade = jnp.exp(m_old - m_new)
        m_ref[h : h + 1, :] = m_new
        l_ref[h : h + 1, :] = fade * l_ref[h : h + 1, :] + jnp.sum(p, axis=0, keepdims=True)
        acc_ref[rows, :] = fade * acc_ref[rows, :] + jnp.dot(v_t, p.astype(BF16), preferred_element_type=F32)


def attend_pieces(ids_ref, kv_refs, *refs):
    own = ids_ref[0]
    base = 1
    for kv_ref in kv_refs:
        n = kv_ref.shape[0]

        @pl.loop(0, n)
        def _(i, kv_ref=kv_ref, base=base):
            block = ids_ref[base + i]

            @pl.when((block < own) & (block >= own - REACH))
            def _():
                attend_block(kv_ref, i, False, *refs)

        base += n


def start_kernel(n, ids_ref, own_ref, *rest):
    kv_refs, (q_ref, hot_ref, m_ref, l_ref, acc_ref) = rest[:n], rest[n:]
    m_ref[...] = jnp.full_like(m_ref, FLOOR)
    l_ref[...] = jnp.zeros_like(l_ref)
    acc_ref[...] = jnp.zeros_like(acc_ref)
    refs = (q_ref, hot_ref, m_ref, l_ref, acc_ref)
    attend_block(own_ref, 0, True, *refs)
    attend_pieces(ids_ref, kv_refs, *refs)


def more_kernel(n, ids_ref, *rest):
    kv_refs, (q_ref, hot_ref, m_in, l_in, acc_in, m_ref, l_ref, acc_ref) = rest[:n], rest[n:]
    m_ref[...] = m_in[...]
    l_ref[...] = l_in[...]
    acc_ref[...] = acc_in[...]
    attend_pieces(ids_ref, kv_refs, q_ref, hot_ref, m_ref, l_ref, acc_ref)


def last_kernel(n, ids_ref, to_ref, *rest):
    kv_refs, rest = rest[:n], rest[n:]
    (q_ref, hot_ref, m_in, l_in, acc_in, w_hbm, b1, b0, a1, a3, a2, a0, m_ref, l_ref, acc_ref, att_ref, w_ref, sem) = rest
    copy = pltpu.make_async_copy(w_hbm, w_ref, sem)
    copy.start()
    m_ref[...] = m_in[...]
    l_ref[...] = l_in[...]
    acc_ref[...] = acc_in[...]
    attend_pieces(ids_ref, kv_refs, q_ref, hot_ref, m_ref, l_ref, acc_ref)
    for h in range(4):
        rows = slice(h * HEAD_DIM, (h + 1) * HEAD_DIM)
        att_ref[:, rows] = jnp.transpose(acc_ref[rows, :] / l_ref[h : h + 1, :]).astype(BF16)
    copy.wait()
    half = BLOCK // 2
    b_to, a_to = (b0, b1), (a0, a1, a2, a3)
    for dz in range(2):

        @pl.loop(0, 4)
        def _(dx, dz=dz):
            at = pl.multiple_of(to_ref[dz * 4 + dx] * COLS, 128)
            w = w_ref[:, pl.ds(at, COLS)]
            b_to[dz][dx] = jnp.dot(att_ref[half:, :], w, preferred_element_type=F32).astype(BF16)

    for dx in range(4):

        @pl.loop(0, 2)
        def _(dz, dx=dx):
            at = pl.multiple_of(to_ref[dz * 4 + dx] * COLS, 128)
            w = w_ref[:, pl.ds(at, COLS)]
            a_to[dx][dz] = jnp.dot(att_ref[:half, :], w, preferred_element_type=F32).astype(BF16)


VMEM = pl.BlockSpec(memory_space=pltpu.VMEM)
SMEM = pl.BlockSpec(memory_space=pltpu.SMEM)
CARRY = (
    jax.ShapeDtypeStruct((8, BLOCK), F32),
    jax.ShapeDtypeStruct((8, BLOCK), F32),
    jax.ShapeDtypeStruct((4 * HEAD_DIM, BLOCK), F32),
)
LIMIT = pltpu.CompilerParams(vmem_limit_bytes=32 * 1024 * 1024)


def cost(n):
    return pl.CostEstimate(
        flops=n * 4 * 4 * BLOCK * BLOCK * HEAD_DIM,
        bytes_accessed=n * PACK * HEAD_DIM * 2,
        transcendentals=n * 4 * BLOCK * BLOCK,
    )


def per_device(hidden, k_cache, v_cache, segment, w_query, w_out):
    ctx = lax.axis_index("ctx")
    y, z, c = ctx // 8, (ctx // 2) % 4, ctx % 2

    smaller = jnp.sum(
        (segment[:, None] < jnp.arange(HEAD_DIM, dtype=jnp.int32)[None, :]).astype(F32), axis=0
    ).astype(BF16)
    own = jnp.concatenate([k_cache, v_cache, jnp.broadcast_to(smaller[None, :], (16, HEAD_DIM))], axis=0)[None]

    other = swap_cores(own)
    z_far = move(own, lambda y, z, c: (y, z + 2, c))
    y_far = move(own, lambda y, z, c: (y + 2, z, c) if y < 2 else None)
    pair = jnp.concatenate([own, other], axis=0)
    z_near = along_z(pair)
    y_near = along_y(pair)

    widened = hidden.astype(F32)
    normed = (widened * lax.rsqrt(jnp.mean(widened * widened, axis=-1, keepdims=True) + 1e-06)).astype(BF16)
    q_t = (
        lax.dot_general(w_query, normed, (((0,), (1,)), ((), ())), preferred_element_type=F32) * HEAD_DIM ** (-0.5)
    ).astype(BF16)
    hot = (jnp.arange(HEAD_DIM, dtype=jnp.int32)[:, None] == segment[None, :]).astype(BF16)

    mine = jnp.concatenate([z_near, z_far, y_near, y_far], axis=0)
    theirs = swap_cores(mine)
    y_rest = along_y(jnp.concatenate([mine[:3], theirs[:3]], axis=0))
    across_far = move(y_far, lambda y, z, c: (y, z + 2, c) if y >= 2 else None)

    def ring_z(y, z, c):
        return (y, z + 1 if c == 0 else z - 1, c) if y >= 2 else None

    across_near = move(jnp.concatenate([y_far, theirs[5:]], axis=0), ring_z)

    def slots(c):
        d, e = 2 * c - 1, 1 - c
        mine = [
            (y, z + d, c), (y, z + d, e), (y, z + 2, c),
            (y + d, z, c), (y + d, z, e), (y + 2, z, c),
        ]
        y_rest = [
            (y + d, z + d, c), (y + d, z + d, e), (y + d, z + 2, c),
            (y + d, z - d, e), (y + d, z - d, c), (y + d, z + 2, e),
        ]
        across = [(y + 2, z + d, c), (y + 2, z + d, e), (y + 2, z + 2, c)]
        return mine, y_rest, across

    def ids_of(places):
        return jnp.stack([ctx] + [ctx_id(*p) for p in places]).astype(jnp.int32)

    mine_at, rest_at, across_at = slots(c)
    theirs_at, rest_at_2, across_at_2 = slots(1 - c)

    state = pl.pallas_call(
        functools.partial(start_kernel, 3),
        out_shape=CARRY,
        in_specs=[SMEM] + [VMEM] * 6,
        out_specs=(VMEM,) * 3,
        compiler_params=LIMIT,
        cost_estimate=cost(14),
        name="attend_row",
    )(ids_of([(y, z, 1 - c)] + mine_at + theirs_at), own, other, mine, theirs, q_t, hot)

    got = jnp.concatenate([y_rest, across_near, across_far], axis=0)
    got_2 = swap_cores(got)
    state = pl.pallas_call(
        functools.partial(more_kernel, 1),
        out_shape=CARRY,
        in_specs=[SMEM] + [VMEM] * 6,
        out_specs=(VMEM,) * 3,
        compiler_params=LIMIT,
        cost_estimate=cost(9),
        name="attend_received",
    )(ids_of(rest_at + across_at), got, q_t, hot, *state)

    section = lax.axis_index("section")
    to = jnp.stack([((section // 4 + dz) % 2) * 4 + (section % 4 + dx) % 4 for dz in range(2) for dx in range(4)])
    half = BLOCK // 2
    part = lambda n: jax.ShapeDtypeStruct((n, half, COLS), BF16)
    b1, b0, a1, a3, a2, a0 = pl.pallas_call(
        functools.partial(last_kernel, 1),
        out_shape=(part(4), part(4), part(2), part(2), part(2), part(2)),
        in_specs=[SMEM, SMEM] + [VMEM] * 6 + [pl.BlockSpec(memory_space=pl.ANY)],
        out_specs=(VMEM,) * 6,
        scratch_shapes=[
            pltpu.VMEM((8, BLOCK), F32),
            pltpu.VMEM((8, BLOCK), F32),
            pltpu.VMEM((4 * HEAD_DIM, BLOCK), F32),
            pltpu.VMEM((BLOCK, 4 * HEAD_DIM), BF16),
            pltpu.VMEM(w_out.shape, BF16),
            pltpu.SemaphoreType.DMA,
        ],
        compiler_params=LIMIT,
        cost_estimate=cost(12),
        name="attend_and_project",
    )(ids_of(rest_at_2 + across_at_2), to.astype(jnp.int32), got_2, q_t, hot, *state, w_out)

    def send_x(t, k):
        return lax.ppermute(t, "section", [(g * 4 + x, g * 4 + (x + k) % 4) for g in range(2) for x in range(4)])

    def send_z(t):
        return lax.ppermute(t, "section", [(g * 4 + x, (1 - g) * 4 + x) for g in range(2) for x in range(4)])

    b_in = send_z(b1)
    a_in = [send_x(a, k) for a, k in ((a1, 1), (a3, 3), (a2, 2))]
    b_sum = b0.astype(F32) + b_in.astype(F32)
    b_out = [send_x(b_sum[k].astype(BF16), k) for k in (1, 3, 2)]
    a_sum = a0.astype(F32) + a_in[0].astype(F32) + a_in[1].astype(F32) + a_in[2].astype(F32)
    a_out = send_z(a_sum[1].astype(BF16))
    a = a_sum[0] + a_out.astype(F32)
    b = b_sum[0] + b_out[0].astype(F32) + b_out[1].astype(F32) + b_out[2].astype(F32)
    return jnp.concatenate([a, b], axis=0).astype(BF16)


def solution(mesh):
    return jax.shard_map(
        per_device,
        mesh=mesh,
        in_specs=(
            P("ctx", None),
            P("ctx", "section"),
            P("ctx", "section"),
            P("ctx"),
            P(None, "section"),
            P("section", None),
        ),
        out_specs=P("ctx", "section"),
        check_vma=False,
    )
```

time: 225 us -> 126 us (0.56)
  waiting for transfers between devices: 105 us -> 35.5 us
  blocking collectives: 40.8 us -> 0 us
  Pallas kernels: 0 us -> 39.2 us
  starting transfers between devices: 0.08 us -> 37.9 us
  matrix products: 38.2 us -> 5.05 us
  other arithmetic: 22.1 us -> 6.31 us
  between operations: 13.8 us -> 0.64 us
  local copies, waits for them, and re-layouts: 4.45 us -> 1.23 us
    all_gather x2 -> x0, waiting for transfers between devices: 57.8 us -> none  [the longest x1 54.3 us: per_device(): value_rows = lax.all_gather(v_cache, 'ctx', axis=0, tiled=True)]
    unnamed x4 -> x0, waiting for transfers between devices: 47.3 us -> none
    all_gather x1 -> x0, blocking collectives: 40.8 us -> none  [per_device(): key_seg = lax.all_gather(segment, 'ctx', axis=0, tiled=True)]
    pallas_call x0 -> x3, Pallas kernels: none -> 39.2 us  [the longest x1 17.1 us: per_device(): pl.pallas_call(functools.partial(last_kernel, 1), out_shape=(part(4), par...]
    ppermute x0 -> x18, starting transfers between devices: none -> 37.9 us  [the longest x10 27.1 us: move(): return lax.ppermute(x, 'ctx', ctx_pairs(step))]
    ppermute x0 -> x18, waiting for transfers between devices: none -> 35.5 us  [the longest x6 18.3 us: send_x(): lax.ppermute(t, 'section', [(g * 4 + x, g * 4 + (x + k) % 4) for g in ran...]
    dot_general x4 -> x1, matrix products: 38.2 us -> 5.05 us  [per_device(): lax.dot_general(w_query, normed, (((0,), (1,)), ((), ())), preferred_elem...]
    reduce_sum x1, other arithmetic: 14.5 us -> 0.79 us  [per_device(): jnp.sum((segment[:, None] < jnp.arange(HEAD_DIM, dtype=jnp.int32)[None, :...]
  transfers between devices with their start and end apart: 3 -> 18, of which waited for: 3 -> 11; matrix products, arithmetic and copies ran while one was open for 6% -> 7% of each run, Pallas kernels for 0% -> 18%
where the time goes in v1:
time: 126 us
  Pallas kernels  39.2 us (31%)
  starting transfers between devices  37.9 us (30%)
  waiting for transfers between devices  35.5 us (28%)
  other arithmetic  6.31 us (5%)
  matrix products  5.05 us (4%)
    ppermute x10, starting transfers between devices, move(): return lax.ppermute(x, 'ctx', ctx_pairs(step))  27.1 us
    ppermute x6, waiting for transfers between devices, send_x(): lax.ppermute(t, 'section', [(g * 4 + x, g * 4 + (x + k) % 4) for g in ran...  18.3 us
    pallas_call x1, Pallas kernels, per_device(): pl.pallas_call(functools.partial(last_kernel, 1), out_shape=(part(4), par...  17.1 us
    ppermute x10, waiting for transfers between devices, move(): return lax.ppermute(x, 'ctx', ctx_pairs(step))  15.8 us
    pallas_call x1, Pallas kernels, per_device(): pl.pallas_call(functools.partial(more_kernel, 1), out_shape=CARRY, in_spe...  12.2 us
    ppermute x6, starting transfers between devices, send_x(): lax.ppermute(t, 'section', [(g * 4 + x, g * 4 + (x + k) % 4) for g in ran...  10.4 us
    pallas_call x1, Pallas kernels, per_device(): pl.pallas_call(functools.partial(start_kernel, 3), out_shape=CARRY, in_sp...  9.86 us
    dot_general x1, matrix products, per_device(): lax.dot_general(w_query, normed, (((0,), (1,)), ((), ())), preferred_elem...  5.05 us
  transfers between devices with their start and end apart: 18, of which 11 were waited for; matrix products, arithmetic and copies ran while one was open for 7% of the time, Pallas kernels for 18%

profile of v1, /device:TPU:24, one launch (start us, length us, event | category | flops | bytes accessed | tf_op | source)
XLA Modules:
  0.0 125.8 jit_solution(5547865128028530250)
XLA Ops:
  3.2 3.3 %collective-permute-start.1 = (bf16[2,528,128]{2,1,0:T(8,128)(2,1)S(1)}, bf16[2,528,128]{2,1,0:T(8,128)(2,1)S(1)}, u32[]{:S(2)}, u32[]{:S(2)}) collective-permute-start(bf16[2,528,128]{2,1,0:T(8,128)(2,1)S(1)} %pad_maximum_fusion.2), channel_id=1, source_target_pairs={{0,16},{8,56},{16,32},{24,8},{32,48},{40,24},{48,0},{56,40},{64,80... | collective-permute-start | bytes 811016 | tf_op jit(solution)/shard_map/ppermute | solution.py:38
  7.8 5.5 %collective-permute-start.2 = (bf16[1,528,128]{2,1,0:T(8,128)(2,1)S(1)}, bf16[1,528,128]{2,1,0:T(8,128)(2,1)S(1)}, u32[]{:S(2)}, u32[]{:S(2)}) collective-permute-start(bf16[1,528,128]{2,1,0:T(8,128)(2,1)S(1)} %maximum_bitcast_fusion.own_ref), channel_id=1, source_target_pairs={{0,32},{8,40},{16,48},{24,56},{32,0},{40,8},{48,16},{56,24},{64,96... | collective-permute-start | bytes 405512 | tf_op jit(solution)/shard_map/ppermute | solution.py:38
  14.6 1.8 %collective-permute-done.1 = bf16[2,528,128]{2,1,0:T(8,128)(2,1)S(1)} collective-permute-done((bf16[2,528,128]{2,1,0:T(8,128)(2,1)S(1)}, bf16[2,528,128]{2,1,0:T(8,128)(2,1)S(1)}, u32[]{:S(2)}, u32[]{:S(2)}) %collective-permute-start.1) | collective-permute-done | bytes 270368 | tf_op jit(solution)/shard_map/ppermute | solution.py:38
  16.4 7.0 %collective-permute-done.2 = bf16[1,528,128]{2,1,0:T(8,128)(2,1)S(1)} collective-permute-done((bf16[1,528,128]{2,1,0:T(8,128)(2,1)S(1)}, bf16[1,528,128]{2,1,0:T(8,128)(2,1)S(1)}, u32[]{:S(2)}, u32[]{:S(2)}) %collective-permute-start.2) | collective-permute-done | bytes 135200 | tf_op jit(solution)/shard_map/ppermute | solution.py:38
  24.2 1.8 %collective-permute-done.5.rest_2_ = bf16[6,528,128]{2,1,0:T(8,128)(2,1)S(1)} collective-permute-done((bf16[6,528,128]{2,1,0:T(8,128)(2,1)S(1)}, bf16[6,528,128]{2,1,0:T(8,128)(2,1)S(1)}, u32[]{:S(2)}, u32[]{:S(2)}) %collective-permute-start.5) | collective-permute-done | bytes 811040 | tf_op jit(solution)/shard_map/ppermute | solution.py:38
  29.1 2.8 %collective-permute-start.7 = (bf16[2,528,128]{2,1,0:T(8,128)(2,1)S(1)}, bf16[2,528,128]{2,1,0:T(8,128)(2,1)S(1)}, u32[]{:S(2)}, u32[]{:S(2)}) collective-permute-start(bf16[2,528,128]{2,1,0:T(8,128)(2,1)S(1)} %pad_maximum_fusion.3), channel_id=1, source_target_pairs={{128,144},{136,184},{144,160},{152,136},{160,176},{168,152},{176,1... | collective-permute-start | bytes 811016 | tf_op jit(solution)/shard_map/ppermute | solution.py:38
  31.8 2.3 %fusion = f32[256]{0:T(256)S(1)} fusion(bf16[256,5120]{1,0:T(8,128)(2,1)} %param.6), kind=kLoop, calls=%fused_computation.2 | loop fusion | flops 3931904 | bytes 2622464 | tf_op jit(solution)/shard_map/reduce_sum | solution.py:182
  34.2 7.9 %collective-permute-start.8 = (bf16[1,528,128]{2,1,0:T(8,128)(2,1)S(1)}, bf16[1,528,128]{2,1,0:T(8,128)(2,1)S(1)}, u32[]{:S(2)}, u32[]{:S(2)}) collective-permute-start(bf16[1,528,128]{2,1,0:T(8,128)(2,1)S(1)} %copy-done.2), channel_id=1, source_target_pairs={{128,160},{136,168},{144,176},{152,184},{160,128},{168,136},{176,1... | collective-permute-start | bytes 405512 | tf_op jit(solution)/shard_map/ppermute | solution.py:38
  42.2 3.8 %collective-permute-done.8 = bf16[1,528,128]{2,1,0:T(8,128)(2,1)S(1)} collective-permute-done((bf16[1,528,128]{2,1,0:T(8,128)(2,1)S(1)}, bf16[1,528,128]{2,1,0:T(8,128)(2,1)S(1)}, u32[]{:S(2)}, u32[]{:S(2)}) %collective-permute-start.8) | collective-permute-done | bytes 135200 | tf_op jit(solution)/shard_map/ppermute | solution.py:38
  46.0 3.6 %collective-permute-start.9 = (bf16[9,528,128]{2,1,0:T(8,128)(2,1)S(1)}, bf16[9,528,128]{2,1,0:T(8,128)(2,1)S(1)}, u32[]{:S(2)}, u32[]{:S(2)}) collective-permute-start(bf16[9,528,128]{2,1,0:T(8,128)(2,1)S(1)} %constant_dynamic-update-slice_fusion.4.rest_0_), channel_id=1, source_target_pairs={{0,8},{8,0},{16,24},{24,16},{32,40},{40,32},{48,56},{56,48},{64,72... | collective-permute-start | bytes 3649544 | tf_op jit(solution)/shard_map/ppermute | solution.py:38
  49.7 5.0 %fusion.11.rest_3_.rest_1_ = bf16[512,256]{1,0:T(8,128)(2,1)S(1)} fusion(bf16[5120,512]{1,0:T(8,128)(2,1)} %param.10, bf16[256,5120]{1,0:T(8,128)(2,1)S(1)} %copy-done, f32[256]{0:T(256)S(1)} %add_rsqrt_fusion), kind=kOutput, calls=%fused_computation.9 | convolution fusion | flops 1346371584 | bytes 8127488 | tf_op jit(solution)/shard_map/dot_general | solution.py:184
  54.8 9.9 %attend_row.1 = (f32[8,256]{1,0:T(8,128)S(1)}, f32[8,256]{1,0:T(8,128)S(1)}, f32[512,256]{1,0:T(8,128)S(1)}) custom-call(s32[14]{0:T(128)S(1)} %stack.177.ids_ref, bf16[1,528,128]{2,1,0:T(8,128)(2,1)S(1)} %maximum_bitcast_fusion.own_ref, bf16[1,528,128]{2,1,0:T(8,128)(2,1)S(1)} %collective-permute-done.rest_0_, ...), custom_call_target="tpu_custom_call" | custom-call | flops 1879048192 | bytes 1892352 | tf_op jit(solution)/shard_map/attend_row/pallas_call | solution.py:217
  64.6 12.2 %attend_received.1 = (f32[8,256]{1,0:T(8,128)S(1)}, f32[8,256]{1,0:T(8,128)S(1)}, f32[512,256]{1,0:T(8,128)S(1)}) custom-call(s32[10]{0:T(128)S(1)} %stack.163.ids_ref, bf16[9,528,128]{2,1,0:T(8,128)(2,1)S(1)} %constant_dynamic-update-slice_fusion.4.rest_0_, bf16[512,256]{1,0:T(8,128)(2,1)S(1)} %fusion.11.rest_3_.rest_1_, ...), custom_call_target="tpu_custom_call" | custom-call | flops 1207959552 | bytes 1216512 | tf_op jit(solution)/shard_map/attend_received/pallas_call | solution.py:229
  76.9 17.1 %attend_and_project.1 = (bf16[4,128,640]{2,1,0:T(8,128)(2,1)S(1)}, bf16[4,128,640]{2,1,0:T(8,128)(2,1)S(1)}, bf16[2,128,640]{2,1,0:T(8,128)(2,1)S(1)}, bf16[2,12...) custom-call(s32[10]{0:T(128)S(1)} %stack.144.ids_ref, ...), custom_call_target="tpu_custom_call" | custom-call | flops 1610612736 | bytes 1622016 | tf_op jit(solution)/shard_map/attend_and_project/pallas_call | solution.py:243
  94.0 1.6 %collective-permute-start.10 = (bf16[2,128,640]{2,1,0:T(8,128)(2,1)S(1)}, bf16[2,128,640]{2,1,0:T(8,128)(2,1)S(1)}, u32[]{:S(2)}, u32[]{:S(2)}) collective-permute-start(bf16[2,128,640]{2,1,0:T(8,128)(2,1)S(1)} %get-tuple-element.24), channel_id=1, source_target_pairs={{0,1},{1,2},{2,3},{3,0},{4,5},{5,6},{6,7},{7,4},{8,9},{9,10},{10,1... | collective-permute-start | bytes 983048 | tf_op jit(solution)/shard_map/ppermute | solution.py:262
  95.6 1.7 %collective-permute-start.11 = (bf16[2,128,640]{2,1,0:T(8,128)(2,1)S(1)}, bf16[2,128,640]{2,1,0:T(8,128)(2,1)S(1)}, u32[]{:S(2)}, u32[]{:S(2)}) collective-permute-start(bf16[2,128,640]{2,1,0:T(8,128)(2,1)S(1)} %get-tuple-element.25), channel_id=1, source_target_pairs={{0,3},{1,0},{2,1},{3,2},{4,7},{5,4},{6,5},{7,6},{8,11},{9,8},{10,9... | collective-permute-start | bytes 983048 | tf_op jit(solution)/shard_map/ppermute | solution.py:262
  97.3 1.8 %collective-permute-start.12 = (bf16[2,128,640]{2,1,0:T(8,128)(2,1)S(1)}, bf16[2,128,640]{2,1,0:T(8,128)(2,1)S(1)}, u32[]{:S(2)}, u32[]{:S(2)}) collective-permute-start(bf16[2,128,640]{2,1,0:T(8,128)(2,1)S(1)} %get-tuple-element.26), channel_id=1, source_target_pairs={{0,2},{1,3},{2,0},{3,1},{4,6},{5,7},{6,4},{7,5},{8,10},{9,11},{10,... | collective-permute-start | bytes 983048 | tf_op jit(solution)/shard_map/ppermute | solution.py:262
  99.1 5.8 %collective-permute-done.10 = bf16[2,128,640]{2,1,0:T(8,128)(2,1)S(1)} collective-permute-done((bf16[2,128,640]{2,1,0:T(8,128)(2,1)S(1)}, bf16[2,128,640]{2,1,0:T(8,128)(2,1)S(1)}, u32[]{:S(2)}, u32[]{:S(2)}) %collective-permute-start.10) | collective-permute-done | bytes 327712 | tf_op jit(solution)/shard_map/ppermute | solution.py:262
  104.9 6.3 %collective-permute-done.11 = bf16[2,128,640]{2,1,0:T(8,128)(2,1)S(1)} collective-permute-done((bf16[2,128,640]{2,1,0:T(8,128)(2,1)S(1)}, bf16[2,128,640]{2,1,0:T(8,128)(2,1)S(1)}, u32[]{:S(2)}, u32[]{:S(2)}) %collective-permute-start.11) | collective-permute-done | bytes 327712 | tf_op jit(solution)/shard_map/ppermute | solution.py:262
  111.3 1.7 %collective-permute-done.12 = bf16[2,128,640]{2,1,0:T(8,128)(2,1)S(1)} collective-permute-done((bf16[2,128,640]{2,1,0:T(8,128)(2,1)S(1)}, bf16[2,128,640]{2,1,0:T(8,128)(2,1)S(1)}, u32[]{:S(2)}, u32[]{:S(2)}) %collective-permute-start.12) | collective-permute-done | bytes 327712 | tf_op jit(solution)/shard_map/ppermute | solution.py:262
  113.5 1.4 %collective-permute-done.14 = bf16[4,128,640]{2,1,0:T(8,128)(2,1)S(1)} collective-permute-done((bf16[4,128,640]{2,1,0:T(8,128)(2,1)S(1)}, bf16[4,128,640]{2,1,0:T(8,128)(2,1)S(1)}, u32[]{:S(2)}, u32[]{:S(2)}) %collective-permute-start.14) | collective-permute-done | bytes 655392 | tf_op jit(solution)/shard_map/ppermute | solution.py:265
  115.9 2.0 %collective-permute-start.17 = (bf16[128,640]{1,0:T(8,128)(2,1)S(1)}, bf16[128,640]{1,0:T(8,128)(2,1)S(1)}, u32[]{:S(2)}, u32[]{:S(2)}) collective-permute-start(bf16[128,640]{1,0:T(8,128)(2,1)S(1)} %get-tuple-element.32), channel_id=1, source_target_pairs={{0,2},{1,3},{2,0},{3,1},{4,6},{5,7},{6,4},{7,5},{8,10},{9,11},{10,... | collective-permute-start | bytes 491528 | tf_op jit(solution)/shard_map/ppermute | solution.py:262
  117.9 2.5 %collective-permute-start.16 = (bf16[128,640]{1,0:T(8,128)(2,1)S(1)}, bf16[128,640]{1,0:T(8,128)(2,1)S(1)}, u32[]{:S(2)}, u32[]{:S(2)}) collective-permute-start(bf16[128,640]{1,0:T(8,128)(2,1)S(1)} %get-tuple-element.33), channel_id=1, source_target_pairs={{0,3},{1,0},{2,1},{3,2},{4,7},{5,4},{6,5},{7,6},{8,11},{9,8},{10,9... | collective-permute-start | bytes 491528 | tf_op jit(solution)/shard_map/ppermute | solution.py:262
  120.5 3.9 %collective-permute-done.15 = bf16[128,640]{1,0:T(8,128)(2,1)S(1)} collective-permute-done((bf16[128,640]{1,0:T(8,128)(2,1)S(1)}, bf16[128,640]{1,0:T(8,128)(2,1)S(1)}, u32[]{:S(2)}, u32[]{:S(2)}) %collective-permute-start.15) | collective-permute-done | bytes 163872 | tf_op jit(solution)/shard_map/ppermute | solution.py:262
  (58 shorter events, 12.2 us)
Async XLA Ops:
  1.7 1.4 %collective-permute-start = (bf16[1,528,128]{2,1,0:T(8,128)(2,1)S(1)}, bf16[1,528,128]{2,1,0:T(8,128)(2,1)S(1)}, u32[]{:S(2)}, u32[]{:S(2)}) collective-permute-start(bf16[1,528,128]{2,1,0:T(8,128)(2,1)S(1)} %maximum_bitcast_fusion.own_ref), channel_id=1, source_target_pairs={{0,8},{8,0},{16,24},{24,16},{32,40},{40,32},{48,56},{56,48},{64,72... | collective-permute-start | bytes 405512 | tf_op jit(solution)/shard_map/ppermute | solution.py:38
  3.2 13.3 %collective-permute-start.1 = (bf16[2,528,128]{2,1,0:T(8,128)(2,1)S(1)}, bf16[2,528,128]{2,1,0:T(8,128)(2,1)S(1)}, u32[]{:S(2)}, u32[]{:S(2)}) collective-permute-start(bf16[2,528,128]{2,1,0:T(8,128)(2,1)S(1)} %pad_maximum_fusion.2), channel_id=1, source_target_pairs={{0,16},{8,56},{16,32},{24,8},{32,48},{40,24},{48,0},{56,40},{64,80... | collective-permute-start | bytes 811016 | tf_op jit(solution)/shard_map/ppermute | solution.py:38
  6.5 16.9 %collective-permute-start.3 = (bf16[2,528,128]{2,1,0:T(8,128)(2,1)S(1)}, bf16[2,528,128]{2,1,0:T(8,128)(2,1)S(1)}, u32[]{:S(2)}, u32[]{:S(2)}) collective-permute-start(bf16[2,528,128]{2,1,0:T(8,128)(2,1)S(1)} %pad_maximum_fusion.2), channel_id=1, source_target_pairs={{0,64},{8,200},{16,80},{24,216},{32,96},{40,232},{48,112},{56,248}... | collective-permute-start | bytes 811016 | tf_op jit(solution)/shard_map/ppermute | solution.py:38
  7.8 15.6 %collective-permute-start.2 = (bf16[1,528,128]{2,1,0:T(8,128)(2,1)S(1)}, bf16[1,528,128]{2,1,0:T(8,128)(2,1)S(1)}, u32[]{:S(2)}, u32[]{:S(2)}) collective-permute-start(bf16[1,528,128]{2,1,0:T(8,128)(2,1)S(1)} %maximum_bitcast_fusion.own_ref), channel_id=1, source_target_pairs={{0,32},{8,40},{16,48},{24,56},{32,0},{40,8},{48,16},{56,24},{64,96... | collective-permute-start | bytes 405512 | tf_op jit(solution)/shard_map/ppermute | solution.py:38
  13.3 10.2 %collective-permute-start.4 = (bf16[1,528,128]{2,1,0:T(8,128)(2,1)S(1)}, bf16[1,528,128]{2,1,0:T(8,128)(2,1)S(1)}, u32[]{:S(2)}, u32[]{:S(2)}) collective-permute-start(bf16[1,528,128]{2,1,0:T(8,128)(2,1)S(1)} %maximum_bitcast_fusion.own_ref), channel_id=1, source_target_pairs={{0,128},{8,136},{16,144},{24,152},{32,160},{40,168},{48,176},{56,1... | collective-permute-start | bytes 405512 | tf_op jit(solution)/shard_map/ppermute | solution.py:38
  23.5 0.7 copy-start.1
  23.5 2.4 %collective-permute-start.5 = (bf16[6,528,128]{2,1,0:T(8,128)(2,1)S(1)}, bf16[6,528,128]{2,1,0:T(8,128)(2,1)S(1)}, u32[]{:S(2)}, u32[]{:S(2)}) collective-permute-start(bf16[6,528,128]{2,1,0:T(8,128)(2,1)S(1)} %constant_dynamic-update-slice_fusion.rest_1_), channel_id=1, source_target_pairs={{0,8},{8,0},{16,24},{24,16},{32,40},{40,32},{48,56},{56,48},{64,72... | collective-permute-start | bytes 2433032 | tf_op jit(solution)/shard_map/ppermute | solution.py:38
  26.1 16.0 %collective-permute-start.6 = (bf16[6,528,128]{2,1,0:T(8,128)(2,1)S(1)}, bf16[6,528,128]{2,1,0:T(8,128)(2,1)S(1)}, u32[]{:S(2)}, u32[]{:S(2)}) collective-permute-start(bf16[6,528,128]{2,1,0:T(8,128)(2,1)S(1)} %pad_maximum_fusion), channel_id=1, source_target_pairs={{0,64},{8,200},{16,80},{24,216},{32,96},{40,232},{48,112},{56,248}... | collective-permute-start | bytes 2433032 | tf_op jit(solution)/shard_map/ppermute | solution.py:38
  28.0 6.1 %copy-start.2 = (bf16[1,528,128]{2,1,0:T(8,128)(2,1)S(1)}, bf16[1,528,128]{2,1,0:T(8,128)(2,1)}, u32[]{:S(2)}) copy-start(bf16[1,528,128]{2,1,0:T(8,128)(2,1)} %copy-done.1) | copy-start | bytes 405508
  29.1 20.6 %copy-start.3 = (s32[256]{0:T(256)S(1)}, s32[256]{0:T(256)}, u32[]{:S(2)}) copy-start(s32[256]{0:T(256)} %param.9) | copy-start | bytes 3076
  29.1 20.6 %copy-start = (bf16[256,5120]{1,0:T(8,128)(2,1)S(1)}, bf16[256,5120]{1,0:T(8,128)(2,1)}, u32[]{:S(2)}) copy-start(bf16[256,5120]{1,0:T(8,128)(2,1)} %param.6) | copy-start | bytes 7864324
  29.1 13.0 %collective-permute-start.7 = (bf16[2,528,128]{2,1,0:T(8,128)(2,1)S(1)}, bf16[2,528,128]{2,1,0:T(8,128)(2,1)S(1)}, u32[]{:S(2)}, u32[]{:S(2)}) collective-permute-start(bf16[2,528,128]{2,1,0:T(8,128)(2,1)S(1)} %pad_maximum_fusion.3), channel_id=1, source_target_pairs={{128,144},{136,184},{144,160},{152,136},{160,176},{168,152},{176,1... | collective-permute-start | bytes 811016 | tf_op jit(solution)/shard_map/ppermute | solution.py:38
  34.2 11.8 %collective-permute-start.8 = (bf16[1,528,128]{2,1,0:T(8,128)(2,1)S(1)}, bf16[1,528,128]{2,1,0:T(8,128)(2,1)S(1)}, u32[]{:S(2)}, u32[]{:S(2)}) collective-permute-start(bf16[1,528,128]{2,1,0:T(8,128)(2,1)S(1)} %copy-done.2), channel_id=1, source_target_pairs={{128,160},{136,168},{144,176},{152,184},{160,128},{168,136},{176,1... | collective-permute-start | bytes 405512 | tf_op jit(solution)/shard_map/ppermute | solution.py:38
  46.0 30.8 %collective-permute-start.9 = (bf16[9,528,128]{2,1,0:T(8,128)(2,1)S(1)}, bf16[9,528,128]{2,1,0:T(8,128)(2,1)S(1)}, u32[]{:S(2)}, u32[]{:S(2)}) collective-permute-start(bf16[9,528,128]{2,1,0:T(8,128)(2,1)S(1)} %constant_dynamic-update-slice_fusion.4.rest_0_), channel_id=1, source_target_pairs={{0,8},{8,0},{16,24},{24,16},{32,40},{40,32},{48,56},{56,48},{64,72... | collective-permute-start | bytes 3649544 | tf_op jit(solution)/shard_map/ppermute | solution.py:38
  49.7 27.1 %slice-start = ((s8[5242880]{0:T(1024)(128)(4,1)}), s8[4194304]{0:T(1024)(128)(4,1)S(1)}, s32[]{:S(2)}) async-start(s8[5242880]{0:T(1024)(128)(4,1)} %bitcast.69), calls=%async_computation | async-start | bytes 8388608
  54.8 22.1 %slice-start.1 = ((s8[5242880]{0:T(1024)(128)(4,1)}), s8[1048576]{0:T(1024)(128)(4,1)S(1)}, s32[]{:S(2)}) async-start(s8[5242880]{0:T(1024)(128)(4,1)} %bitcast.69), calls=%async_computation.1 | async-start | bytes 2097152
  94.0 10.9 %collective-permute-start.10 = (bf16[2,128,640]{2,1,0:T(8,128)(2,1)S(1)}, bf16[2,128,640]{2,1,0:T(8,128)(2,1)S(1)}, u32[]{:S(2)}, u32[]{:S(2)}) collective-permute-start(bf16[2,128,640]{2,1,0:T(8,128)(2,1)S(1)} %get-tuple-element.24), channel_id=1, source_target_pairs={{0,1},{1,2},{2,3},{3,0},{4,5},{5,6},{6,7},{7,4},{8,9},{9,10},{10,1... | collective-permute-start | bytes 983048 | tf_op jit(solution)/shard_map/ppermute | solution.py:262
  95.6 15.7 %collective-permute-start.11 = (bf16[2,128,640]{2,1,0:T(8,128)(2,1)S(1)}, bf16[2,128,640]{2,1,0:T(8,128)(2,1)S(1)}, u32[]{:S(2)}, u32[]{:S(2)}) collective-permute-start(bf16[2,128,640]{2,1,0:T(8,128)(2,1)S(1)} %get-tuple-element.25), channel_id=1, source_target_pairs={{0,3},{1,0},{2,1},{3,2},{4,7},{5,4},{6,5},{7,6},{8,11},{9,8},{10,9... | collective-permute-start | bytes 983048 | tf_op jit(solution)/shard_map/ppermute | solution.py:262
  97.3 15.6 %collective-permute-start.12 = (bf16[2,128,640]{2,1,0:T(8,128)(2,1)S(1)}, bf16[2,128,640]{2,1,0:T(8,128)(2,1)S(1)}, u32[]{:S(2)}, u32[]{:S(2)}) collective-permute-start(bf16[2,128,640]{2,1,0:T(8,128)(2,1)S(1)} %get-tuple-element.26), channel_id=1, source_target_pairs={{0,2},{1,3},{2,0},{3,1},{4,6},{5,7},{6,4},{7,5},{8,10},{9,11},{10,... | collective-permute-start | bytes 983048 | tf_op jit(solution)/shard_map/ppermute | solution.py:262
  99.1 15.8 %collective-permute-start.14 = (bf16[4,128,640]{2,1,0:T(8,128)(2,1)S(1)}, bf16[4,128,640]{2,1,0:T(8,128)(2,1)S(1)}, u32[]{:S(2)}, u32[]{:S(2)}) collective-permute-start(bf16[4,128,640]{2,1,0:T(8,128)(2,1)S(1)} %get-tuple-element.28), channel_id=1, source_target_pairs={{0,4},{1,5},{2,6},{3,7},{4,0},{5,1},{6,2},{7,3},{8,12},{9,13},{10,... | collective-permute-start | bytes 1966088 | tf_op jit(solution)/shard_map/ppermute | solution.py:265
  113.1 7.3 %collective-permute-start.13 = (bf16[128,640]{1,0:T(8,128)(2,1)S(1)}, bf16[128,640]{1,0:T(8,128)(2,1)S(1)}, u32[]{:S(2)}, u32[]{:S(2)}) collective-permute-start(bf16[128,640]{1,0:T(8,128)(2,1)S(1)} %fusion.20), channel_id=1, source_target_pairs={{0,4},{1,5},{2,6},{3,7},{4,0},{5,1},{6,2},{7,3},{8,12},{9,13},{10,... | collective-permute-start | bytes 491528 | tf_op jit(solution)/shard_map/ppermute | solution.py:265
  115.2 9.2 %collective-permute-start.15 = (bf16[128,640]{1,0:T(8,128)(2,1)S(1)}, bf16[128,640]{1,0:T(8,128)(2,1)S(1)}, u32[]{:S(2)}, u32[]{:S(2)}) collective-permute-start(bf16[128,640]{1,0:T(8,128)(2,1)S(1)} %get-tuple-element.31), channel_id=1, source_target_pairs={{0,1},{1,2},{2,3},{3,0},{4,5},{5,6},{6,7},{7,4},{8,9},{9,10},{10,1... | collective-permute-start | bytes 491528 | tf_op jit(solution)/shard_map/ppermute | solution.py:262
  115.9 8.5 %collective-permute-start.17 = (bf16[128,640]{1,0:T(8,128)(2,1)S(1)}, bf16[128,640]{1,0:T(8,128)(2,1)S(1)}, u32[]{:S(2)}, u32[]{:S(2)}) collective-permute-start(bf16[128,640]{1,0:T(8,128)(2,1)S(1)} %get-tuple-element.32), channel_id=1, source_target_pairs={{0,2},{1,3},{2,0},{3,1},{4,6},{5,7},{6,4},{7,5},{8,10},{9,11},{10,... | collective-permute-start | bytes 491528 | tf_op jit(solution)/shard_map/ppermute | solution.py:262
  117.9 7.0 %collective-permute-start.16 = (bf16[128,640]{1,0:T(8,128)(2,1)S(1)}, bf16[128,640]{1,0:T(8,128)(2,1)S(1)}, u32[]{:S(2)}, u32[]{:S(2)}) collective-permute-start(bf16[128,640]{1,0:T(8,128)(2,1)S(1)} %get-tuple-element.33), channel_id=1, source_target_pairs={{0,3},{1,0},{2,1},{3,2},{4,7},{5,4},{6,5},{7,6},{8,11},{9,8},{10,9... | collective-permute-start | bytes 491528 | tf_op jit(solution)/shard_map/ppermute | solution.py:262

commit v2 on v1

v2 whole, which is shorter than its diff:
```python
import functools

import jax
import jax.numpy as jnp
from jax import lax
from jax.experimental import pallas as pl
from jax.experimental.pallas import tpu as pltpu
from jax.sharding import PartitionSpec as P
import numpy as np

HEAD_DIM = 128
BLOCK = 256
PACK = 2 * BLOCK + 16
REACH = 24
COLS = 640
FLOOR = -1e30
HIDDEN = -2e30

F32 = jnp.float32
BF16 = jnp.bfloat16


def ctx_id(y, z, c):
    return ((y + 8) % 4) * 8 + ((z + 8) % 4) * 2 + c


def ctx_pairs(step, planes=None):
    pairs = []
    for y in range(4):
        for z in range(4):
            for c in range(2):
                to = step(y, z, c)
                if to is not None:
                    pairs.append((ctx_id(y, z, c), ctx_id(*to)))
    return pairs


def move(x, step):
    return lax.ppermute(x, "ctx", ctx_pairs(step))


def swap_cores(x):
    return move(x, lambda y, z, c: (y, z, 1 - c))


def along_z(x):
    return move(x, lambda y, z, c: (y, z + 1 if c == 0 else z - 1, c))


def along_y(x):
    def step(y, z, c):
        if c == 0:
            return (y + 1, z, c) if y < 3 else None
        return (3, z, c) if y == 0 else None

    return move(x, step)


def attend_blocks(kv_ref, places, diagonal, q_ref, hot_ref, m_ref, l_ref, acc_ref):
    heads = [slice(h * HEAD_DIM, (h + 1) * HEAD_DIM) for h in range(4)]
    keys, values, visible = [], [], []
    for at, low in places:
        keys.append(kv_ref[at, 0:BLOCK, :])
        values.append(jnp.transpose(kv_ref[at, BLOCK : 2 * BLOCK, :]))
        counts = kv_ref[at, 2 * BLOCK : PACK, :]
        first = jnp.dot(counts, hot_ref[...], preferred_element_type=F32)[0:1, :].astype(jnp.int32)
        row = lax.broadcasted_iota(jnp.int32, (BLOCK, BLOCK), 0)
        seen = row >= jnp.maximum(first, low)
        if diagonal:
            seen &= row <= lax.broadcasted_iota(jnp.int32, (BLOCK, BLOCK), 1)
        visible.append(seen)
    scores = [[jnp.dot(k, q_ref[rows, :], preferred_element_type=F32) for k in keys] for rows in heads]
    old = [(m_ref[h : h + 1, :], l_ref[h : h + 1, :]) for h in range(4)]
    new = []
    for h in range(4):
        masked = [jnp.where(seen, s, HIDDEN) for seen, s in zip(visible, scores[h])]
        m_old, total = old[h]
        m_new = m_old
        for s in masked:
            m_new = jnp.maximum(m_new, jnp.max(s, axis=0, keepdims=True))
        weights = [jnp.exp(s - m_new) for s in masked]
        fade = jnp.exp(m_old - m_new)
        total = fade * total
        for p in weights:
            total = total + jnp.sum(p, axis=0, keepdims=True)
        added = sum(jnp.dot(v, p.astype(BF16), preferred_element_type=F32) for v, p in zip(values, weights))
        new.append((m_new, total, fade, added))
    for h, rows in enumerate(heads):
        m_new, total, fade, added = new[h]
        m_ref[h : h + 1, :] = m_new
        l_ref[h : h + 1, :] = total
        acc_ref[rows, :] = fade * acc_ref[rows, :] + added


def attend_pieces(ids_ref, base, kv_refs, order_ref, *refs):
    own = ids_ref[0]
    for kv_ref in kv_refs:
        n = kv_ref.shape[0]
        count = jnp.int32(0)
        for i in range(n):
            block = ids_ref[base + i]
            order_ref[count] = i
            count += ((block < own) & (block >= own - REACH)).astype(jnp.int32)

        @pl.loop(0, (count + 1) // 2)
        def _(g, kv_ref=kv_ref, count=count):
            one = order_ref[2 * g]
            both = 2 * g + 1 < count
            two = jnp.where(both, order_ref[2 * g + 1], one)
            places = [(one, 0), (two, jnp.where(both, 0, BLOCK))]
            attend_blocks(kv_ref, places, False, *refs)

        base += n


def start_kernel(n, base, ids_ref, own_ref, *rest):
    kv_refs, (q_ref, hot_ref, m_ref, l_ref, acc_ref, order_ref) = rest[:n], rest[n:]
    m_ref[...] = jnp.full_like(m_ref, FLOOR)
    l_ref[...] = jnp.zeros_like(l_ref)
    acc_ref[...] = jnp.zeros_like(acc_ref)
    refs = (q_ref, hot_ref, m_ref, l_ref, acc_ref)
    attend_blocks(own_ref, [(0, 0)], True, *refs)
    attend_pieces(ids_ref, base, kv_refs, order_ref, *refs)


def more_kernel(n, base, ids_ref, *rest):
    kv_refs, (q_ref, hot_ref, m_in, l_in, acc_in, m_ref, l_ref, acc_ref, order_ref) = rest[:n], rest[n:]
    m_ref[...] = m_in[...]
    l_ref[...] = l_in[...]
    acc_ref[...] = acc_in[...]
    attend_pieces(ids_ref, base, kv_refs, order_ref, q_ref, hot_ref, m_ref, l_ref, acc_ref)


def last_kernel(n, base, ids_ref, to_ref, *rest):
    kv_refs, rest = rest[:n], rest[n:]
    (q_ref, hot_ref, m_in, l_in, acc_in, w_hbm, b1, b0, a1, a3, a2, a0) = rest[:12]
    m_ref, l_ref, acc_ref, att_ref, w_ref, order_ref, sem = rest[12:]
    copy = pltpu.make_async_copy(w_hbm, w_ref, sem)
    copy.start()
    m_ref[...] = m_in[...]
    l_ref[...] = l_in[...]
    acc_ref[...] = acc_in[...]
    attend_pieces(ids_ref, base, kv_refs, order_ref, q_ref, hot_ref, m_ref, l_ref, acc_ref)
    for h in range(4):
        rows = slice(h * HEAD_DIM, (h + 1) * HEAD_DIM)
        att_ref[:, rows] = jnp.transpose(acc_ref[rows, :] / l_ref[h : h + 1, :]).astype(BF16)
    copy.wait()
    half = BLOCK // 2
    b_to, a_to = (b0, b1), (a0, a1, a2, a3)
    for dz in range(2):
        for dx in range(4):
            at = pl.multiple_of(to_ref[dz * 4 + dx] * COLS, 128)
            part = jnp.dot(att_ref[...], w_ref[:, pl.ds(at, COLS)], preferred_element_type=F32).astype(BF16)
            a_to[dx][dz] = part[:half]
            b_to[dz][dx] = part[half:]


VMEM = pl.BlockSpec(memory_space=pltpu.VMEM)
SMEM = pl.BlockSpec(memory_space=pltpu.SMEM)
CARRY = (
    jax.ShapeDtypeStruct((8, BLOCK), F32),
    jax.ShapeDtypeStruct((8, BLOCK), F32),
    jax.ShapeDtypeStruct((4 * HEAD_DIM, BLOCK), F32),
)
LIMIT = pltpu.CompilerParams(vmem_limit_bytes=32 * 1024 * 1024)


def cost(n):
    return pl.CostEstimate(
        flops=n * 4 * 4 * BLOCK * BLOCK * HEAD_DIM,
        bytes_accessed=n * PACK * HEAD_DIM * 2,
        transcendentals=n * 4 * BLOCK * BLOCK,
    )


def per_device(hidden, k_cache, v_cache, segment, w_query, w_out):
    ctx = lax.axis_index("ctx")
    y, z, c = ctx // 8, (ctx // 2) % 4, ctx % 2

    smaller = jnp.sum(
        (segment[:, None] < jnp.arange(HEAD_DIM, dtype=jnp.int32)[None, :]).astype(F32), axis=0
    ).astype(BF16)
    own = jnp.concatenate([k_cache, v_cache, jnp.broadcast_to(smaller[None, :], (16, HEAD_DIM))], axis=0)[None]

    other = swap_cores(own)
    z_far = move(own, lambda y, z, c: (y, z + 2, c))
    y_far = move(own, lambda y, z, c: (y + 2, z, c) if y < 2 else None)
    pair = jnp.concatenate([own, other], axis=0)
    z_near = along_z(pair)
    y_near = along_y(pair)

    widened = hidden.astype(F32)
    normed = (widened * lax.rsqrt(jnp.mean(widened * widened, axis=-1, keepdims=True) + 1e-06)).astype(BF16)
    q_t = (
        lax.dot_general(w_query, normed, (((0,), (1,)), ((), ())), preferred_element_type=F32) * HEAD_DIM ** (-0.5)
    ).astype(BF16)
    hot = (jnp.arange(HEAD_DIM, dtype=jnp.int32)[:, None] == segment[None, :]).astype(BF16)

    def slots(y, z, c):
        d, e = 2 * c - 1, 1 - c
        mine = [
            (y, z + d, c), (y, z + d, e), (y, z + 2, c),
            (y + d, z, c), (y + d, z, e), (y + 2, z, c),
        ]
        y_rest = [
            (y + d, z + d, c), (y + d, z + d, e), (y + d, z + 2, c),
            (y + d, z - d, e), (y + d, z - d, c), (y + d, z + 2, e),
        ]
        across = [(y + 2, z + d, c), (y + 2, z + d, e), (y + 2, z + 2, c)]
        return mine, y_rest + across

    def row_of(y, z, c):
        mine, later = slots(y, z, c)
        theirs, later_2 = slots(y, z, 1 - c)
        return [ctx_id(*p) for p in [(y, z, c), (y, z, 1 - c)] + mine + theirs + later + later_2]

    table = np.array([row_of(i // 8, i // 2 % 4, i % 2) for i in range(32)], np.int32)
    ids = lax.dynamic_index_in_dim(jnp.asarray(table), ctx, 0, keepdims=False)

    mine = jnp.concatenate([z_near, z_far, y_near, y_far], axis=0)
    mine, q_t = lax.optimization_barrier((mine, q_t))
    theirs = swap_cores(mine)
    y_rest = along_y(jnp.concatenate([mine[:3], theirs[:3]], axis=0))
    across_far = move(y_far, lambda y, z, c: (y, z + 2, c) if y >= 2 else None)

    def ring_z(y, z, c):
        return (y, z + 1 if c == 0 else z - 1, c) if y >= 2 else None

    across_near = move(jnp.concatenate([y_far, theirs[5:]], axis=0), ring_z)

    state = pl.pallas_call(
        functools.partial(start_kernel, 3, 1),
        out_shape=CARRY,
        in_specs=[SMEM] + [VMEM] * 6,
        out_specs=(VMEM,) * 3,
        scratch_shapes=[pltpu.SMEM((16,), jnp.int32)],
        compiler_params=LIMIT,
        cost_estimate=cost(14),
        name="attend_row",
    )(ids, own, other, mine, theirs, q_t, hot)

    got = jnp.concatenate([y_rest, across_near, across_far], axis=0)
    got, state = lax.optimization_barrier((got, state))
    got_2 = swap_cores(got)
    state = pl.pallas_call(
        functools.partial(more_kernel, 1, 14),
        out_shape=CARRY,
        in_specs=[SMEM] + [VMEM] * 6,
        out_specs=(VMEM,) * 3,
        scratch_shapes=[pltpu.SMEM((16,), jnp.int32)],
        compiler_params=LIMIT,
        cost_estimate=cost(9),
        name="attend_received",
    )(ids, got, q_t, hot, *state)

    section = lax.axis_index("section")
    place = np.array(
        [[(s // 4 + dz) % 2 * 4 + (s % 4 + dx) % 4 for dz in range(2) for dx in range(4)] for s in range(8)], np.int32
    )
    to = lax.dynamic_index_in_dim(jnp.asarray(place), section, 0, keepdims=False)
    half = BLOCK // 2
    part = lambda n: jax.ShapeDtypeStruct((n, half, COLS), BF16)
    b1, b0, a1, a3, a2, a0 = pl.pallas_call(
        functools.partial(last_kernel, 1, 23),
        out_shape=(part(4), part(4), part(2), part(2), part(2), part(2)),
        in_specs=[SMEM, SMEM] + [VMEM] * 6 + [pl.BlockSpec(memory_space=pl.ANY)],
        out_specs=(VMEM,) * 6,
        scratch_shapes=[
            pltpu.VMEM((8, BLOCK), F32),
            pltpu.VMEM((8, BLOCK), F32),
            pltpu.VMEM((4 * HEAD_DIM, BLOCK), F32),
            pltpu.VMEM((BLOCK, 4 * HEAD_DIM), BF16),
            pltpu.VMEM(w_out.shape, BF16),
            pltpu.SMEM((16,), jnp.int32),
            pltpu.SemaphoreType.DMA,
        ],
        compiler_params=LIMIT,
        cost_estimate=cost(12),
        name="attend_and_project",
    )(ids, to, got_2, q_t, hot, *state, w_out)

    def send_x(t, k):
        return lax.ppermute(t, "section", [(g * 4 + x, g * 4 + (x + k) % 4) for g in range(2) for x in range(4)])

    def send_z(t):
        return lax.ppermute(t, "section", [(g * 4 + x, (1 - g) * 4 + x) for g in range(2) for x in range(4)])

    b_in = send_z(b1)
    a_in = [send_x(a, k) for a, k in ((a1, 1), (a3, 3), (a2, 2))]
    b_sum = b0.astype(F32) + b_in.astype(F32)
    b_out = [send_x(b_sum[k].astype(BF16), k) for k in (1, 3, 2)]
    a_in, b_out = list(a_in), list(b_out)
    a_in[0], b_out[0] = lax.optimization_barrier((a_in[0], b_out[0]))
    a_sum = a0.astype(F32) + a_in[0].astype(F32) + a_in[1].astype(F32) + a_in[2].astype(F32)
    a_out = send_z(a_sum[1].astype(BF16))
    a = a_sum[0] + a_out.astype(F32)
    b = b_sum[0] + b_out[0].astype(F32) + b_out[1].astype(F32) + b_out[2].astype(F32)
    return jnp.concatenate([a, b], axis=0).astype(BF16)


def solution(mesh):
    return jax.shard_map(
        per_device,
        mesh=mesh,
        in_specs=(
            P("ctx", None),
            P("ctx", "section"),
            P("ctx", "section"),
            P("ctx"),
            P(None, "section"),
            P("section", None),
        ),
        out_specs=P("ctx", "section"),
        check_vma=False,
    )
```

time: 126 us -> 101 us (0.80)
  the two profiles are of different devices: /device:TPU:24 before, /device:TPU:28 now
where the time goes in v2:
time: 101 us
  waiting for transfers between devices  35.6 us (35%)
  starting transfers between devices  27.2 us (27%)
  Pallas kernels  21.1 us (21%)
  other arithmetic  7.83 us (8%)
  matrix products  4.88 us (5%)
  local copies, waits for them, and re-layouts  4.02 us (4%)
    ppermute x10, starting transfers between devices, move(): return lax.ppermute(x, 'ctx', ctx_pairs(step))  20 us
    ppermute x2, waiting for transfers between devices, send_z(): lax.ppermute(t, 'section', [(g * 4 + x, (1 - g) * 4 + x) for g in range(2...  16.9 us
    ppermute x10, waiting for transfers between devices, move(): return lax.ppermute(x, 'ctx', ctx_pairs(step))  11.1 us
    pallas_call x1, Pallas kernels, per_device(): pl.pallas_call(functools.partial(last_kernel, 1, 23), out_shape=(part(4),...  8.91 us
    ppermute x6, waiting for transfers between devices, send_x(): lax.ppermute(t, 'section', [(g * 4 + x, g * 4 + (x + k) % 4) for g in ran...  7.63 us
    ppermute x6, starting transfers between devices, send_x(): lax.ppermute(t, 'section', [(g * 4 + x, g * 4 + (x + k) % 4) for g in ran...  7.04 us
    pallas_call x1, Pallas kernels, per_device(): pl.pallas_call(functools.partial(more_kernel, 1, 14), out_shape=CARRY, in...  6.35 us
    pallas_call x1, Pallas kernels, per_device(): pl.pallas_call(functools.partial(start_kernel, 3, 1), out_shape=CARRY, in...  5.82 us
  transfers between devices with their start and end apart: 18, of which 8 were waited for; matrix products, arithmetic and copies ran while one was open for 9% of the time, Pallas kernels for 12%

profile of v2, /device:TPU:28, one launch (start us, length us, event | category | flops | bytes accessed | tf_op | source)
XLA Modules:
  0.0 100.9 jit_solution(15017400473925545545)
XLA Ops:
  1.8 1.3 %collective-permute-start.4 = (bf16[1,528,128]{2,1,0:T(8,128)(2,1)S(1)}, bf16[1,528,128]{2,1,0:T(8,128)(2,1)S(1)}, u32[]{:S(2)}, u32[]{:S(2)}) collective-permute-start(bf16[1,528,128]{2,1,0:T(8,128)(2,1)S(1)} %maximum_bitcast_fusion.own_ref), channel_id=1, source_target_pairs={{0,128},{8,136},{16,144},{24,152},{32,160},{40,168},{48,176},{56,1... | collective-permute-start | bytes 405512 | tf_op jit(solution)/shard_map/ppermute | solution.py:39
  3.1 7.3 %collective-permute-start.2 = (bf16[1,528,128]{2,1,0:T(8,128)(2,1)S(1)}, bf16[1,528,128]{2,1,0:T(8,128)(2,1)S(1)}, u32[]{:S(2)}, u32[]{:S(2)}) collective-permute-start(bf16[1,528,128]{2,1,0:T(8,128)(2,1)S(1)} %maximum_bitcast_fusion.own_ref), channel_id=1, source_target_pairs={{0,32},{8,40},{16,48},{24,56},{32,0},{40,8},{48,16},{56,24},{64,96... | collective-permute-start | bytes 405512 | tf_op jit(solution)/shard_map/ppermute | solution.py:39
  10.4 2.3 %fusion = f32[256]{0:T(256)S(1)} fusion(bf16[256,5120]{1,0:T(8,128)(2,1)} %param.8), kind=kLoop, calls=%fused_computation.2 | loop fusion | flops 3931904 | bytes 2622464 | tf_op jit(solution)/shard_map/reduce_sum | solution.py:193
  12.8 1.3 %collective-permute-start.3 = (bf16[2,528,128]{2,1,0:T(8,128)(2,1)S(1)}, bf16[2,528,128]{2,1,0:T(8,128)(2,1)S(1)}, u32[]{:S(2)}, u32[]{:S(2)}) collective-permute-start(bf16[2,528,128]{2,1,0:T(8,128)(2,1)S(1)} %pad_maximum_fusion.4), channel_id=1, source_target_pairs={{0,64},{8,200},{16,80},{24,216},{32,96},{40,232},{48,112},{56,248}... | collective-permute-start | bytes 811016 | tf_op jit(solution)/shard_map/ppermute | solution.py:39
  14.1 1.6 %collective-permute-start.1 = (bf16[2,528,128]{2,1,0:T(8,128)(2,1)S(1)}, bf16[2,528,128]{2,1,0:T(8,128)(2,1)S(1)}, u32[]{:S(2)}, u32[]{:S(2)}) collective-permute-start(bf16[2,528,128]{2,1,0:T(8,128)(2,1)S(1)} %pad_maximum_fusion.4), channel_id=1, source_target_pairs={{0,16},{8,56},{16,32},{24,8},{32,48},{40,24},{48,0},{56,40},{64,80... | collective-permute-start | bytes 811016 | tf_op jit(solution)/shard_map/ppermute | solution.py:39
  15.7 4.9 %fusion.11.rest_3_.rest_1_ = bf16[512,256]{1,0:T(8,128)(2,1)S(1)} fusion(bf16[5120,512]{1,0:T(8,128)(2,1)} %param.12, bf16[256,5120]{1,0:T(8,128)(2,1)S(1)} %copy-done.1, f32[256]{0:T(256)S(1)} %add_rsqrt_fusion), kind=kOutput, calls=%fused_computation.10 | convolution fusion | flops 1346371584 | bytes 8127488 | tf_op jit(solution)/shard_map/dot_general | solution.py:195
  21.2 4.4 %collective-permute-done.1 = bf16[2,528,128]{2,1,0:T(8,128)(2,1)S(1)} collective-permute-done((bf16[2,528,128]{2,1,0:T(8,128)(2,1)S(1)}, bf16[2,528,128]{2,1,0:T(8,128)(2,1)S(1)}, u32[]{:S(2)}, u32[]{:S(2)}) %collective-permute-start.1) | collective-permute-done | bytes 270368 | tf_op jit(solution)/shard_map/ppermute | solution.py:39
  25.9 2.3 %collective-permute-done.5.rest_2_ = bf16[6,528,128]{2,1,0:T(8,128)(2,1)S(1)} collective-permute-done((bf16[6,528,128]{2,1,0:T(8,128)(2,1)S(1)}, bf16[6,528,128]{2,1,0:T(8,128)(2,1)S(1)}, u32[]{:S(2)}, u32[]{:S(2)}) %collective-permute-start.5) | collective-permute-done | bytes 811040 | tf_op jit(solution)/shard_map/ppermute | solution.py:39
  29.1 1.3 %collective-permute-start.6 = (bf16[6,528,128]{2,1,0:T(8,128)(2,1)}, bf16[6,528,128]{2,1,0:T(8,128)(2,1)}, u32[]{:S(2)}, u32[]{:S(2)}) collective-permute-start(bf16[6,528,128]{2,1,0:T(8,128)(2,1)} %pad_maximum_fusion.2), channel_id=1, source_target_pairs={{0,64},{8,200},{16,80},{24,216},{32,96},{40,232},{48,112},{56,248}... | collective-permute-start | bytes 2433032 | tf_op jit(solution)/shard_map/ppermute | solution.py:39
  30.5 1.9 %collective-permute-start.7 = (bf16[2,528,128]{2,1,0:T(8,128)(2,1)S(1)}, bf16[2,528,128]{2,1,0:T(8,128)(2,1)S(1)}, u32[]{:S(2)}, u32[]{:S(2)}) collective-permute-start(bf16[2,528,128]{2,1,0:T(8,128)(2,1)S(1)} %pad_maximum_fusion.5), channel_id=1, source_target_pairs={{128,144},{136,184},{144,160},{152,136},{160,176},{168,152},{176,1... | collective-permute-start | bytes 811016 | tf_op jit(solution)/shard_map/ppermute | solution.py:39
  33.1 5.1 %collective-permute-start.8 = (bf16[1,528,128]{2,1,0:T(8,128)(2,1)S(1)}, bf16[1,528,128]{2,1,0:T(8,128)(2,1)S(1)}, u32[]{:S(2)}, u32[]{:S(2)}) collective-permute-start(bf16[1,528,128]{2,1,0:T(8,128)(2,1)S(1)} %collective-permute-done.4), channel_id=1, source_target_pairs={{128,160},{136,168},{144,176},{152,184},{160,128},{168,136},{176,1... | collective-permute-start | bytes 405512 | tf_op jit(solution)/shard_map/ppermute | solution.py:39
  38.2 5.8 %attend_row.1 = (f32[8,256]{1,0:T(8,128)S(1)}, f32[8,256]{1,0:T(8,128)S(1)}, f32[512,256]{1,0:T(8,128)S(1)}) custom-call(s32[32]{0:T(128)S(1)} %dynamic-slice_bitcast_fusion.1.ids_ref, bf16[1,528,128]{2,1,0:T(8,128)(2,1)S(1)} %maximum_bitcast_fusion.own_ref, bf16[1,528,128]{2,1,0:T(8,128)(2,1)S(1)} %collective-permute-done.rest_0_, ...), custom_call_target="tpu_custom_call" | custom-call | flops 1879048192 | bytes 1892352 | tf_op jit(solution)/shard_map/attend_row/pallas_call | solution.py:231
  44.1 3.8 %collective-permute-done.8 = bf16[1,528,128]{2,1,0:T(8,128)(2,1)S(1)} collective-permute-done((bf16[1,528,128]{2,1,0:T(8,128)(2,1)S(1)}, bf16[1,528,128]{2,1,0:T(8,128)(2,1)S(1)}, u32[]{:S(2)}, u32[]{:S(2)}) %collective-permute-start.8) | collective-permute-done | bytes 135200 | tf_op jit(solution)/shard_map/ppermute | solution.py:39
  47.9 1.3 %pad_maximum_fusion.rest_0_ = bf16[9,528,128]{2,1,0:T(8,128)(2,1)S(1)} fusion(bf16[1,528,128]{2,1,0:T(8,128)(2,1)S(1)} %collective-permute-done.8, bf16[2,528,128]{2,1,0:T(8,128)(2,1)S(1)} %collective-permute-done.7, bf16[6,528,128]{2,1,0:T(8,128)(2,1)} %collective-permute-done.6), kind=kLoop, calls=%fused_computation.8 | loop fusion | flops 1216512 | bytes 2433024 | tf_op jit(solution)/shard_map/concatenate | solution.py:242
  50.0 6.4 %attend_received.1 = (f32[8,256]{1,0:T(8,128)S(1)}, f32[8,256]{1,0:T(8,128)S(1)}, f32[512,256]{1,0:T(8,128)S(1)}) custom-call(s32[32]{0:T(128)S(1)} %dynamic-slice_bitcast_fusion.1.ids_ref, bf16[9,528,128]{2,1,0:T(8,128)(2,1)S(1)} %pad_maximum_fusion.rest_0_, bf16[512,256]{1,0:T(8,128)(2,1)S(1)} %fusion.11.rest_3_.rest_1_, ...), custom_call_target="tpu_custom_call" | custom-call | flops 1207959552 | bytes 1216512 | tf_op jit(solution)/shard_map/attend_received/pallas_call | solution.py:245
  56.4 2.5 %copy-done = bf16[512,5120]{1,0:T(8,128)(2,1)S(1)} copy-done((bf16[512,5120]{1,0:T(8,128)(2,1)S(1)}, bf16[512,5120]{1,0:T(8,128)(2,1)}, u32[]{:S(2)}) %copy-start) | copy-done | bytes 5242904
  58.9 8.9 %attend_and_project.1 = (bf16[4,128,640]{2,1,0:T(8,128)(2,1)S(1)}, bf16[4,128,640]{2,1,0:T(8,128)(2,1)S(1)}, bf16[2,128,640]{2,1,0:T(8,128)(2,1)S(1)}, bf16[2,12...) custom-call(s32[32]{0:T(128)S(1)} %dynamic-slice_bitcast_fusion.1.ids_ref, ...), custom_call_target="tpu_custom_call" | custom-call | flops 1610612736 | bytes 1622016 | tf_op jit(solution)/shard_map/attend_and_project/pallas_call | solution.py:263
  67.9 1.3 %collective-permute-start.10 = (bf16[2,128,640]{2,1,0:T(8,128)(2,1)S(1)}, bf16[2,128,640]{2,1,0:T(8,128)(2,1)S(1)}, u32[]{:S(2)}, u32[]{:S(2)}) collective-permute-start(bf16[2,128,640]{2,1,0:T(8,128)(2,1)S(1)} %get-tuple-element.38), channel_id=1, source_target_pairs={{0,1},{1,2},{2,3},{3,0},{4,5},{5,6},{6,7},{7,4},{8,9},{9,10},{10,1... | collective-permute-start | bytes 983048 | tf_op jit(solution)/shard_map/ppermute | solution.py:283
  70.0 1.7 %collective-permute-start.14 = (bf16[2,128,640]{2,1,0:T(8,128)(2,1)S(1)}, bf16[2,128,640]{2,1,0:T(8,128)(2,1)S(1)}, u32[]{:S(2)}, u32[]{:S(2)}) collective-permute-start(bf16[2,128,640]{2,1,0:T(8,128)(2,1)S(1)} %get-tuple-element.43), channel_id=1, source_target_pairs={{0,2},{1,3},{2,0},{3,1},{4,6},{5,7},{6,4},{7,5},{8,10},{9,11},{10,... | collective-permute-start | bytes 983048 | tf_op jit(solution)/shard_map/ppermute | solution.py:283
  71.8 13.2 %collective-permute-done.11 = bf16[4,128,640]{2,1,0:T(8,128)(2,1)S(1)} collective-permute-done((bf16[4,128,640]{2,1,0:T(8,128)(2,1)S(1)}, bf16[4,128,640]{2,1,0:T(8,128)(2,1)S(1)}, u32[]{:S(2)}, u32[]{:S(2)}) %collective-permute-start.11) | collective-permute-done | bytes 655392 | tf_op jit(solution)/shard_map/ppermute | solution.py:286
  85.2 1.3 %collective-permute-start.12 = (bf16[128,640]{1,0:T(8,128)(2,1)S(1)}, bf16[128,640]{1,0:T(8,128)(2,1)S(1)}, u32[]{:S(2)}, u32[]{:S(2)}) collective-permute-start(bf16[128,640]{1,0:T(8,128)(2,1)S(1)} %get-tuple-element.47), channel_id=1, source_target_pairs={{0,1},{1,2},{2,3},{3,0},{4,5},{5,6},{6,7},{7,4},{8,9},{9,10},{10,1... | collective-permute-start | bytes 491528 | tf_op jit(solution)/shard_map/ppermute | solution.py:283
  88.4 6.1 %collective-permute-done.12 = bf16[128,640]{1,0:T(8,128)(2,1)S(1)} collective-permute-done((bf16[128,640]{1,0:T(8,128)(2,1)S(1)}, bf16[128,640]{1,0:T(8,128)(2,1)S(1)}, u32[]{:S(2)}, u32[]{:S(2)}) %collective-permute-start.12) | collective-permute-done | bytes 163872 | tf_op jit(solution)/shard_map/ppermute | solution.py:283
  94.9 1.5 %collective-permute-done.16 = bf16[128,640]{1,0:T(8,128)(2,1)S(1)} collective-permute-done((bf16[128,640]{1,0:T(8,128)(2,1)S(1)}, bf16[128,640]{1,0:T(8,128)(2,1)S(1)}, u32[]{:S(2)}, u32[]{:S(2)}) %collective-permute-start.16) | collective-permute-done | bytes 163872 | tf_op jit(solution)/shard_map/ppermute | solution.py:283
  96.5 3.7 %collective-permute-done.15 = bf16[128,640]{1,0:T(8,128)(2,1)S(1)} collective-permute-done((bf16[128,640]{1,0:T(8,128)(2,1)S(1)}, bf16[128,640]{1,0:T(8,128)(2,1)S(1)}, u32[]{:S(2)}, u32[]{:S(2)}) %collective-permute-start.15) | collective-permute-done | bytes 163872 | tf_op jit(solution)/shard_map/ppermute | solution.py:286
  (45 shorter events, 9.6 us)
Async XLA Ops:
  0.0 15.7 %copy-start.1 = (bf16[256,5120]{1,0:T(8,128)(2,1)S(1)}, bf16[256,5120]{1,0:T(8,128)(2,1)}, u32[]{:S(2)}) copy-start(bf16[256,5120]{1,0:T(8,128)(2,1)} %param.8) | copy-start | bytes 7864324
  1.8 18.7 %collective-permute-start.4 = (bf16[1,528,128]{2,1,0:T(8,128)(2,1)S(1)}, bf16[1,528,128]{2,1,0:T(8,128)(2,1)S(1)}, u32[]{:S(2)}, u32[]{:S(2)}) collective-permute-start(bf16[1,528,128]{2,1,0:T(8,128)(2,1)S(1)} %maximum_bitcast_fusion.own_ref), channel_id=1, source_target_pairs={{0,128},{8,136},{16,144},{24,152},{32,160},{40,168},{48,176},{56,1... | collective-permute-start | bytes 405512 | tf_op jit(solution)/shard_map/ppermute | solution.py:39
  3.1 17.4 %collective-permute-start.2 = (bf16[1,528,128]{2,1,0:T(8,128)(2,1)S(1)}, bf16[1,528,128]{2,1,0:T(8,128)(2,1)S(1)}, u32[]{:S(2)}, u32[]{:S(2)}) collective-permute-start(bf16[1,528,128]{2,1,0:T(8,128)(2,1)S(1)} %maximum_bitcast_fusion.own_ref), channel_id=1, source_target_pairs={{0,32},{8,40},{16,48},{24,56},{32,0},{40,8},{48,16},{56,24},{64,96... | collective-permute-start | bytes 405512 | tf_op jit(solution)/shard_map/ppermute | solution.py:39
  10.4 2.4 %collective-permute-start = (bf16[1,528,128]{2,1,0:T(8,128)(2,1)S(1)}, bf16[1,528,128]{2,1,0:T(8,128)(2,1)S(1)}, u32[]{:S(2)}, u32[]{:S(2)}) collective-permute-start(bf16[1,528,128]{2,1,0:T(8,128)(2,1)S(1)} %maximum_bitcast_fusion.own_ref), channel_id=1, source_target_pairs={{0,8},{8,0},{16,24},{24,16},{32,40},{40,32},{48,56},{56,48},{64,72... | collective-permute-start | bytes 405512 | tf_op jit(solution)/shard_map/ppermute | solution.py:39
  12.8 8.4 %collective-permute-start.3 = (bf16[2,528,128]{2,1,0:T(8,128)(2,1)S(1)}, bf16[2,528,128]{2,1,0:T(8,128)(2,1)S(1)}, u32[]{:S(2)}, u32[]{:S(2)}) collective-permute-start(bf16[2,528,128]{2,1,0:T(8,128)(2,1)S(1)} %pad_maximum_fusion.4), channel_id=1, source_target_pairs={{0,64},{8,200},{16,80},{24,216},{32,96},{40,232},{48,112},{56,248}... | collective-permute-start | bytes 811016 | tf_op jit(solution)/shard_map/ppermute | solution.py:39
  14.1 11.5 %collective-permute-start.1 = (bf16[2,528,128]{2,1,0:T(8,128)(2,1)S(1)}, bf16[2,528,128]{2,1,0:T(8,128)(2,1)S(1)}, u32[]{:S(2)}, u32[]{:S(2)}) collective-permute-start(bf16[2,528,128]{2,1,0:T(8,128)(2,1)S(1)} %pad_maximum_fusion.4), channel_id=1, source_target_pairs={{0,16},{8,56},{16,32},{24,8},{32,48},{40,24},{48,0},{56,40},{64,80... | collective-permute-start | bytes 811016 | tf_op jit(solution)/shard_map/ppermute | solution.py:39
  20.6 9.9 %copy-start.2 = (s32[256]{0:T(256)S(1)}, s32[256]{0:T(256)}, u32[]{:S(2)}) copy-start(s32[256]{0:T(256)} %param.11) | copy-start | bytes 3076
  25.7 2.4 %collective-permute-start.5 = (bf16[6,528,128]{2,1,0:T(8,128)(2,1)S(1)}, bf16[6,528,128]{2,1,0:T(8,128)(2,1)S(1)}, u32[]{:S(2)}, u32[]{:S(2)}) collective-permute-start(bf16[6,528,128]{2,1,0:T(8,128)(2,1)S(1)} %pad_maximum_fusion.1.rest_1_), channel_id=1, source_target_pairs={{0,8},{8,0},{16,24},{24,16},{32,40},{40,32},{48,56},{56,48},{64,72... | collective-permute-start | bytes 2433032 | tf_op jit(solution)/shard_map/ppermute | solution.py:39
  29.1 18.7 %collective-permute-start.6 = (bf16[6,528,128]{2,1,0:T(8,128)(2,1)}, bf16[6,528,128]{2,1,0:T(8,128)(2,1)}, u32[]{:S(2)}, u32[]{:S(2)}) collective-permute-start(bf16[6,528,128]{2,1,0:T(8,128)(2,1)} %pad_maximum_fusion.2), channel_id=1, source_target_pairs={{0,64},{8,200},{16,80},{24,216},{32,96},{40,232},{48,112},{56,248}... | collective-permute-start | bytes 2433032 | tf_op jit(solution)/shard_map/ppermute | solution.py:39
  30.5 17.3 %collective-permute-start.7 = (bf16[2,528,128]{2,1,0:T(8,128)(2,1)S(1)}, bf16[2,528,128]{2,1,0:T(8,128)(2,1)S(1)}, u32[]{:S(2)}, u32[]{:S(2)}) collective-permute-start(bf16[2,528,128]{2,1,0:T(8,128)(2,1)S(1)} %pad_maximum_fusion.5), channel_id=1, source_target_pairs={{128,144},{136,184},{144,160},{152,136},{160,176},{168,152},{176,1... | collective-permute-start | bytes 811016 | tf_op jit(solution)/shard_map/ppermute | solution.py:39
  33.1 14.7 %collective-permute-start.8 = (bf16[1,528,128]{2,1,0:T(8,128)(2,1)S(1)}, bf16[1,528,128]{2,1,0:T(8,128)(2,1)S(1)}, u32[]{:S(2)}, u32[]{:S(2)}) collective-permute-start(bf16[1,528,128]{2,1,0:T(8,128)(2,1)S(1)} %collective-permute-done.4), channel_id=1, source_target_pairs={{128,160},{136,168},{144,176},{152,184},{160,128},{168,136},{176,1... | collective-permute-start | bytes 405512 | tf_op jit(solution)/shard_map/ppermute | solution.py:39
  49.2 7.3 %collective-permute-start.9 = (bf16[9,528,128]{2,1,0:T(8,128)(2,1)S(1)}, bf16[9,528,128]{2,1,0:T(8,128)(2,1)S(1)}, u32[]{:S(2)}, u32[]{:S(2)}) collective-permute-start(bf16[9,528,128]{2,1,0:T(8,128)(2,1)S(1)} %pad_maximum_fusion.rest_0_), channel_id=1, source_target_pairs={{0,8},{8,0},{16,24},{24,16},{32,40},{40,32},{48,56},{56,48},{64,72... | collective-permute-start | bytes 3649544 | tf_op jit(solution)/shard_map/ppermute | solution.py:39
  56.4 2.5 %copy-start = (bf16[512,5120]{1,0:T(8,128)(2,1)S(1)}, bf16[512,5120]{1,0:T(8,128)(2,1)}, u32[]{:S(2)}) copy-start(bf16[512,5120]{1,0:T(8,128)(2,1)} %rest_6_.1) | copy-start | bytes 15728644
  67.8 17.2 %collective-permute-start.11 = (bf16[4,128,640]{2,1,0:T(8,128)(2,1)S(1)}, bf16[4,128,640]{2,1,0:T(8,128)(2,1)S(1)}, u32[]{:S(2)}, u32[]{:S(2)}) collective-permute-start(bf16[4,128,640]{2,1,0:T(8,128)(2,1)S(1)} %get-tuple-element.40), channel_id=1, source_target_pairs={{0,4},{1,5},{2,6},{3,7},{4,0},{5,1},{6,2},{7,3},{8,12},{9,13},{10,... | collective-permute-start | bytes 1966088 | tf_op jit(solution)/shard_map/ppermute | solution.py:286
  67.9 19.3 %collective-permute-start.10 = (bf16[2,128,640]{2,1,0:T(8,128)(2,1)S(1)}, bf16[2,128,640]{2,1,0:T(8,128)(2,1)S(1)}, u32[]{:S(2)}, u32[]{:S(2)}) collective-permute-start(bf16[2,128,640]{2,1,0:T(8,128)(2,1)S(1)} %get-tuple-element.38), channel_id=1, source_target_pairs={{0,1},{1,2},{2,3},{3,0},{4,5},{5,6},{6,7},{7,4},{8,9},{9,10},{10,1... | collective-permute-start | bytes 983048 | tf_op jit(solution)/shard_map/ppermute | solution.py:283
  69.2 25.3 %collective-permute-start.13 = (bf16[2,128,640]{2,1,0:T(8,128)(2,1)S(1)}, bf16[2,128,640]{2,1,0:T(8,128)(2,1)S(1)}, u32[]{:S(2)}, u32[]{:S(2)}) collective-permute-start(bf16[2,128,640]{2,1,0:T(8,128)(2,1)S(1)} %get-tuple-element.42), channel_id=1, source_target_pairs={{0,3},{1,0},{2,1},{3,2},{4,7},{5,4},{6,5},{7,6},{8,11},{9,8},{10,9... | collective-permute-start | bytes 983048 | tf_op jit(solution)/shard_map/ppermute | solution.py:283
  70.0 24.5 %collective-permute-start.14 = (bf16[2,128,640]{2,1,0:T(8,128)(2,1)S(1)}, bf16[2,128,640]{2,1,0:T(8,128)(2,1)S(1)}, u32[]{:S(2)}, u32[]{:S(2)}) collective-permute-start(bf16[2,128,640]{2,1,0:T(8,128)(2,1)S(1)} %get-tuple-element.43), channel_id=1, source_target_pairs={{0,2},{1,3},{2,0},{3,1},{4,6},{5,7},{6,4},{7,5},{8,10},{9,11},{10,... | collective-permute-start | bytes 983048 | tf_op jit(solution)/shard_map/ppermute | solution.py:283
  85.2 9.3 %collective-permute-start.12 = (bf16[128,640]{1,0:T(8,128)(2,1)S(1)}, bf16[128,640]{1,0:T(8,128)(2,1)S(1)}, u32[]{:S(2)}, u32[]{:S(2)}) collective-permute-start(bf16[128,640]{1,0:T(8,128)(2,1)S(1)} %get-tuple-element.47), channel_id=1, source_target_pairs={{0,1},{1,2},{2,3},{3,0},{4,5},{5,6},{6,7},{7,4},{8,9},{9,10},{10,1... | collective-permute-start | bytes 491528 | tf_op jit(solution)/shard_map/ppermute | solution.py:283
  86.5 8.4 %collective-permute-start.17 = (bf16[128,640]{1,0:T(8,128)(2,1)S(1)}, bf16[128,640]{1,0:T(8,128)(2,1)S(1)}, u32[]{:S(2)}, u32[]{:S(2)}) collective-permute-start(bf16[128,640]{1,0:T(8,128)(2,1)S(1)} %get-tuple-element.48), channel_id=1, source_target_pairs={{0,2},{1,3},{2,0},{3,1},{4,6},{5,7},{6,4},{7,5},{8,10},{9,11},{10,... | collective-permute-start | bytes 491528 | tf_op jit(solution)/shard_map/ppermute | solution.py:283
  87.2 9.1 %collective-permute-start.16 = (bf16[128,640]{1,0:T(8,128)(2,1)S(1)}, bf16[128,640]{1,0:T(8,128)(2,1)S(1)}, u32[]{:S(2)}, u32[]{:S(2)}) collective-permute-start(bf16[128,640]{1,0:T(8,128)(2,1)S(1)} %get-tuple-element.49), channel_id=1, source_target_pairs={{0,3},{1,0},{2,1},{3,2},{4,7},{5,4},{6,5},{7,6},{8,11},{9,8},{10,9... | collective-permute-start | bytes 491528 | tf_op jit(solution)/shard_map/ppermute | solution.py:283
  94.7 5.4 %collective-permute-start.15 = (bf16[128,640]{1,0:T(8,128)(2,1)S(1)}, bf16[128,640]{1,0:T(8,128)(2,1)S(1)}, u32[]{:S(2)}, u32[]{:S(2)}) collective-permute-start(bf16[128,640]{1,0:T(8,128)(2,1)S(1)} %fusion.20), channel_id=1, source_target_pairs={{0,4},{1,5},{2,6},{3,7},{4,0},{5,1},{6,2},{7,3},{8,12},{9,13},{10,... | collective-permute-start | bytes 491528 | tf_op jit(solution)/shard_map/ppermute | solution.py:286

commit v3 on v2

v3 whole, which is shorter than its diff:
```python
import functools

import jax
import jax.numpy as jnp
from jax import lax
from jax.experimental import pallas as pl
from jax.experimental.pallas import tpu as pltpu
from jax.sharding import PartitionSpec as P
import numpy as np

HEAD_DIM = 128
BLOCK = 256
PACK = 2 * BLOCK + 16
REACH = 24
HALF = BLOCK // 2
COLS = 640
FLOOR = -1e30
HIDDEN = -2e30

F32 = jnp.float32
BF16 = jnp.bfloat16


def ctx_id(y, z, c):
    return ((y + 8) % 4) * 8 + ((z + 8) % 4) * 2 + c


def ctx_pairs(step, planes=None):
    pairs = []
    for y in range(4):
        for z in range(4):
            for c in range(2):
                to = step(y, z, c)
                if to is not None:
                    pairs.append((ctx_id(y, z, c), ctx_id(*to)))
    return pairs


def move(x, step):
    return lax.ppermute(x, "ctx", ctx_pairs(step))


def swap_cores(x):
    return move(x, lambda y, z, c: (y, z, 1 - c))


def up_y(x):
    return move(x, lambda y, z, c: (y + 1, z, c) if y < 3 else None)


def round_y(x):
    return move(x, lambda y, z, c: (3, z, c) if y == 0 else None)


def first_slots(y, z, c):
    row = [(y, z - 1, c), (y, z + 1, c), (y, z + 2, c)]
    return row + [(y - 1, z, c), (y + 1, z, c), (y + 2, z, c)]


def later_slots(y, z, c):
    around = [(y - 1, z - 1, c), (y - 1, z + 1, c), (y - 1, z + 2, c)]
    around += [(y + 1, z - 1, c), (y + 1, z + 1, c), (y + 1, z + 2, c)]
    return around + [(y + 2, z - 1, c), (y + 2, z + 1, c), (y + 2, z + 2, c)]


def pair_rows(group):
    half, pair = group // 2, group % 2
    cols = slice(half * HALF, (half + 1) * HALF)
    return [(h, slice(h * HEAD_DIM, (h + 1) * HEAD_DIM), cols) for h in (2 * pair, 2 * pair + 1)]


def attend_blocks(kv_ref, places, diagonal, groups, q_ref, hot_ref, m_ref, l_ref, acc_ref):
    halves = sorted({g // 2 for g in groups})
    keys, values, visible = [], [], []
    row = lax.broadcasted_iota(jnp.int32, (BLOCK, BLOCK), 0)
    for at, low in places:
        keys.append(kv_ref[at, 0:BLOCK, :])
        values.append(jnp.transpose(kv_ref[at, BLOCK : 2 * BLOCK, :]))
        counts = kv_ref[at, 2 * BLOCK : PACK, :]
        first = jnp.dot(counts, hot_ref[...], preferred_element_type=F32)[0:1, :].astype(jnp.int32)
        first = jnp.maximum(first, low)
        seen = {}
        for half in halves:
            mine = first[:, half * HALF : (half + 1) * HALF]
            seen[half] = row >= jnp.concatenate([mine, mine], axis=1)
            if diagonal:
                token = lax.broadcasted_iota(jnp.int32, (BLOCK, BLOCK), 1) % HALF + half * HALF
                seen[half] &= row <= token
        visible.append(seen)

    def side(ref_of):
        return jnp.concatenate(ref_of, axis=1)

    scores, old = [], []
    for group in groups:
        rows = pair_rows(group)
        q = side([q_ref[r, c] for _, r, c in rows])
        scores.append([jnp.dot(k, q, preferred_element_type=F32) for k in keys])
        old.append((side([m_ref[h : h + 1, c] for h, _, c in rows]), side([l_ref[h : h + 1, c] for h, _, c in rows])))
    new = []
    for n, group in enumerate(groups):
        masked = [jnp.where(seen[group // 2], s, HIDDEN) for seen, s in zip(visible, scores[n])]
        m_old, total = old[n]
        m_new = m_old
        for s in masked:
            m_new = jnp.maximum(m_new, jnp.max(s, axis=0, keepdims=True))
        weights = [jnp.exp(s - m_new) for s in masked]
        fade = jnp.exp(m_old - m_new)
        total = fade * total
        for p in weights:
            total = total + jnp.sum(p, axis=0, keepdims=True)
        added = sum(jnp.dot(v, p.astype(BF16), preferred_element_type=F32) for v, p in zip(values, weights))
        new.append((m_new, total, fade, added))
    for n, group in enumerate(groups):
        m_new, total, fade, added = new[n]
        for i, (h, r, c) in enumerate(pair_rows(group)):
            part = slice(i * HALF, (i + 1) * HALF)
            m_ref[h : h + 1, c] = m_new[:, part]
            l_ref[h : h + 1, c] = total[:, part]
            acc_ref[r, c] = fade[:, part] * acc_ref[r, c] + added[:, part]


def attend_pieces(own, pieces, order_ref, groups, *refs):
    for kv_ref, places in pieces:
        count = jnp.int32(0)
        for i, place in enumerate(places):
            block = ctx_id(*place)
            order_ref[count] = i
            count += ((block < own) & (block >= own - REACH)).astype(jnp.int32)

        @pl.loop(0, (count + 1) // 2)
        def _(g, kv_ref=kv_ref, count=count):
            one = order_ref[2 * g]
            both = 2 * g + 1 < count
            two = jnp.where(both, order_ref[2 * g + 1], one)
            attend_blocks(kv_ref, [(one, 0), (two, jnp.where(both, 0, BLOCK))], False, groups, *refs)


def where_am_i(at_ref):
    own = at_ref[0]
    return own, own // 8, (own // 2) % 4, own % 2


def start_kernel(at_ref, own_ref, mine_ref, theirs_ref, q_ref, hot_ref, m_ref, l_ref, acc_ref, order_ref):
    own, y, z, c = where_am_i(at_ref)
    m_ref[...] = jnp.full_like(m_ref, FLOOR)
    l_ref[...] = jnp.zeros_like(l_ref)
    acc_ref[...] = jnp.zeros_like(acc_ref)
    refs = (q_ref, hot_ref, m_ref, l_ref, acc_ref)
    attend_blocks(own_ref, [(0, 0)], True, range(4), *refs)
    pieces = [
        (mine_ref, first_slots(y, z, c)),
        (theirs_ref, [(y, z, 1 - c)] + first_slots(y, z, 1 - c)),
    ]
    attend_pieces(own, pieces, order_ref, range(4), *refs)


def more_kernel(at_ref, got_ref, q_ref, hot_ref, m_in, l_in, acc_in, m_ref, l_ref, acc_ref, order_ref):
    own, y, z, c = where_am_i(at_ref)
    m_ref[...] = m_in[...]
    l_ref[...] = l_in[...]
    acc_ref[...] = acc_in[...]
    pieces = [(got_ref, later_slots(y, z, c))]
    attend_pieces(own, pieces, order_ref, range(4), q_ref, hot_ref, m_ref, l_ref, acc_ref)


def target(at_ref, dz, dx):
    section = at_ref[1]
    to = (section // 4 + dz) % 2 * 4 + (section + dx) % 4
    return pl.ds(pl.multiple_of(to * COLS, 128), COLS)


def project(at_ref, att, w_ref, dz, dx):
    return jnp.dot(att, w_ref[:, target(at_ref, dz, dx)], preferred_element_type=F32).astype(BF16)


def finish_kernel(half, places, at_ref, got_ref, q_ref, hot_ref, m_in, l_in, acc_in, w_hbm, *rest):
    att_ref, parts, (m_ref, l_ref, acc_ref, w_ref, order_ref, sem) = rest[0], rest[1:-6], rest[-6:]
    copy = pltpu.make_async_copy(w_hbm, w_ref, sem)
    copy.start()
    own, y, z, c = where_am_i(at_ref)
    m_ref[...] = m_in[...]
    l_ref[...] = l_in[...]
    acc_ref[...] = acc_in[...]
    pieces = [(got_ref, later_slots(y, z, 1 - c))]
    attend_pieces(own, pieces, order_ref, range(2 * half, 2 * half + 2), q_ref, hot_ref, m_ref, l_ref, acc_ref)
    cols = slice(half * HALF, (half + 1) * HALF)
    for h in range(4):
        rows = slice(h * HEAD_DIM, (h + 1) * HEAD_DIM)
        att_ref[:, rows] = jnp.transpose(acc_ref[rows, cols] / l_ref[h : h + 1, cols]).astype(BF16)
    copy.wait()
    for part, targets in zip(parts, places):
        for i, (dz, dx) in enumerate(targets):
            part[i] = project(at_ref, att_ref[...], w_ref, dz, dx)


def own_kernel(at_ref, att_a, att_b, w_hbm, a_ref, b_ref, w_ref, sem):
    copy = pltpu.make_async_copy(w_hbm, w_ref, sem)
    copy.start()
    copy.wait()
    for dz in range(2):
        a_ref[dz] = project(at_ref, att_a[...], w_ref, dz, 0)
    for dx in range(4):
        b_ref[dx] = project(at_ref, att_b[...], w_ref, 0, dx)


VMEM = pl.BlockSpec(memory_space=pltpu.VMEM)
SMEM = pl.BlockSpec(memory_space=pltpu.SMEM)
CARRY = (
    jax.ShapeDtypeStruct((8, BLOCK), F32),
    jax.ShapeDtypeStruct((8, BLOCK), F32),
    jax.ShapeDtypeStruct((4 * HEAD_DIM, BLOCK), F32),
)
LIMIT = pltpu.CompilerParams(vmem_limit_bytes=32 * 1024 * 1024)
WHOLE = pltpu.CompilerParams(vmem_limit_bytes=59 * 1024 * 1024)


def cost(n):
    return pl.CostEstimate(
        flops=n * 4 * 4 * BLOCK * BLOCK * HEAD_DIM,
        bytes_accessed=n * PACK * HEAD_DIM * 2,
        transcendentals=n * 4 * BLOCK * BLOCK,
    )


def per_device(hidden, k_cache, v_cache, segment, w_query, w_out):
    ctx = lax.axis_index("ctx")

    smaller = jnp.sum(
        (segment[:, None] < jnp.arange(HEAD_DIM, dtype=jnp.int32)[None, :]).astype(F32), axis=0
    ).astype(BF16)
    own = jnp.concatenate([k_cache, v_cache, jnp.broadcast_to(smaller[None, :], (16, HEAD_DIM))], axis=0)[None]

    z_1 = move(own, lambda y, z, c: (y, z + 1, c))
    z_3 = move(own, lambda y, z, c: (y, z - 1, c))
    z_2 = move(own, lambda y, z, c: (y, z + 2, c))
    y_1 = up_y(own)
    y_3 = round_y(own)
    y_2 = move(own, lambda y, z, c: (y + 2, z, c) if y < 2 else None)

    widened = hidden.astype(F32)
    normed = (widened * lax.rsqrt(jnp.mean(widened * widened, axis=-1, keepdims=True) + 1e-06)).astype(BF16)
    q_t = (
        lax.dot_general(w_query, normed, (((0,), (1,)), ((), ())), preferred_element_type=F32) * HEAD_DIM ** (-0.5)
    ).astype(BF16)
    hot = (jnp.arange(HEAD_DIM, dtype=jnp.int32)[:, None] == segment[None, :]).astype(BF16)

    far_1 = move(y_2, lambda y, z, c: (y, z + 1, c) if y >= 2 else None)
    far_3 = move(y_2, lambda y, z, c: (y, z - 1, c) if y >= 2 else None)
    far_2 = move(y_2, lambda y, z, c: (y, z + 2, c) if y >= 2 else None)
    row = jnp.concatenate([z_1, z_3, z_2], axis=0)
    up = up_y(row)
    around = round_y(row)
    mine = jnp.concatenate([row, y_1, y_3, y_2], axis=0)
    theirs = swap_cores(jnp.concatenate([own, mine], axis=0))

    at = jnp.stack([ctx, lax.axis_index("section")]).astype(jnp.int32)
    state = pl.pallas_call(
        start_kernel,
        out_shape=CARRY,
        in_specs=[SMEM] + [VMEM] * 5,
        out_specs=(VMEM,) * 3,
        scratch_shapes=[pltpu.SMEM((16,), jnp.int32)],
        compiler_params=LIMIT,
        cost_estimate=cost(1),
        name="attend_first",
    )(at, own, mine, theirs, q_t, hot)

    pieces, state = lax.optimization_barrier(((up, around, far_1, far_3, far_2), state))
    got = jnp.concatenate(pieces, axis=0)
    got_2 = swap_cores(got)
    state = pl.pallas_call(
        more_kernel,
        out_shape=CARRY,
        in_specs=[SMEM] + [VMEM] * 6,
        out_specs=(VMEM,) * 3,
        scratch_shapes=[pltpu.SMEM((16,), jnp.int32)],
        compiler_params=LIMIT,
        cost_estimate=cost(9),
        name="attend_later",
    )(at, got, q_t, hot, *state)

    part = lambda n: jax.ShapeDtypeStruct((n, HALF, COLS), BF16)
    attended = jax.ShapeDtypeStruct((HALF, 4 * HEAD_DIM), BF16)
    w_at = pl.BlockSpec(memory_space=pltpu.HBM)

    def finish(half, places):
        return pl.pallas_call(
            functools.partial(finish_kernel, half, places),
            out_shape=(attended,) + tuple(part(len(p)) for p in places),
            in_specs=[SMEM] + [VMEM] * 6 + [w_at],
            out_specs=(VMEM,) * (1 + len(places)),
            scratch_shapes=[
                pltpu.VMEM((8, BLOCK), F32),
                pltpu.VMEM((8, BLOCK), F32),
                pltpu.VMEM((4 * HEAD_DIM, BLOCK), F32),
                pltpu.VMEM(w_out.shape, BF16),
                pltpu.SMEM((16,), jnp.int32),
                pltpu.SemaphoreType.DMA,
            ],
            compiler_params=WHOLE,
            cost_estimate=cost(6),
            name=f"attend_and_project_{half}",
        )(at, got_2, q_t, hot, *state, w_out)

    att_b, b1 = finish(1, [[(1, dx) for dx in range(4)]])
    att_a, a1, a3, a2 = finish(0, [[(0, dx), (1, dx)] for dx in (1, 3, 2)])
    a0, b0 = pl.pallas_call(
        own_kernel,
        out_shape=(part(2), part(4)),
        in_specs=[SMEM, VMEM, VMEM, w_at],
        out_specs=(VMEM,) * 2,
        scratch_shapes=[pltpu.VMEM(w_out.shape, BF16), pltpu.SemaphoreType.DMA],
        compiler_params=WHOLE,
        cost_estimate=cost(4),
        name="project_own",
    )(at, att_a, att_b, w_out)

    def send_x(t, k):
        return lax.ppermute(t, "section", [(g * 4 + x, g * 4 + (x + k) % 4) for g in range(2) for x in range(4)])

    def send_z(t):
        return lax.ppermute(t, "section", [(g * 4 + x, (1 - g) * 4 + x) for g in range(2) for x in range(4)])

    b_in = send_z(b1)
    a_in = [send_x(a, k) for a, k in ((a1, 1), (a3, 3), (a2, 2))]
    b_sum = b0.astype(F32) + b_in.astype(F32)
    a_in = list(a_in)
    b_sum, a_in[0] = lax.optimization_barrier((b_sum, a_in[0]))
    b_out = [send_x(b_sum[k].astype(BF16), k) for k in (1, 3, 2)]
    a_sum = a0.astype(F32) + a_in[0].astype(F32) + a_in[1].astype(F32) + a_in[2].astype(F32)
    a_out = send_z(a_sum[1].astype(BF16))
    a = a_sum[0] + a_out.astype(F32)
    b = b_sum[0] + b_out[0].astype(F32) + b_out[1].astype(F32) + b_out[2].astype(F32)
    return jnp.concatenate([a, b], axis=0).astype(BF16)


def solution(mesh):
    return jax.shard_map(
        per_device,
        mesh=mesh,
        in_specs=(
            P("ctx", None),
            P("ctx", "section"),
            P("ctx", "section"),
            P("ctx"),
            P(None, "section"),
            P("section", None),
        ),
        out_specs=P("ctx", "section"),
        check_vma=False,
    )
```

time: 101 us -> 113 us (1.12)
  the two profiles are of different devices: /device:TPU:28 before, /device:TPU:24 now
where the time goes in v3:
time: 113 us
  starting transfers between devices  42 us (37%)
  Pallas kernels  30.1 us (27%)
  waiting for transfers between devices  23.4 us (21%)
  local copies, waits for them, and re-layouts  6.38 us (6%)
  other arithmetic  5.61 us (5%)
  matrix products  4.88 us (4%)
    ppermute x13, starting transfers between devices, move(): return lax.ppermute(x, 'ctx', ctx_pairs(step))  31 us
    ppermute x6, waiting for transfers between devices, send_x(): lax.ppermute(t, 'section', [(g * 4 + x, g * 4 + (x + k) % 4) for g in ran...  13.6 us
    pallas_call x2, Pallas kernels, finish(): pl.pallas_call(functools.partial(finish_kernel, half, places), out_shape=...  13.5 us
    ppermute x13, waiting for transfers between devices, move(): return lax.ppermute(x, 'ctx', ctx_pairs(step))  8.9 us
    ppermute x6, starting transfers between devices, send_x(): lax.ppermute(t, 'section', [(g * 4 + x, g * 4 + (x + k) % 4) for g in ran...  8.63 us
    pallas_call x1, Pallas kernels, per_device(): pl.pallas_call(more_kernel, out_shape=CARRY, in_specs=[SMEM] + [VMEM] * 6...  6.02 us
    pallas_call x1, Pallas kernels, per_device(): pl.pallas_call(start_kernel, out_shape=CARRY, in_specs=[SMEM] + [VMEM] *...  5.46 us
    unnamed x29, local copies, waits for them, and re-layouts  5.34 us
  transfers between devices with their start and end apart: 21, of which 10 were waited for; matrix products, arithmetic and copies ran while one was open for 9% of the time, Pallas kernels for 21%

profile of v3, /device:TPU:24, one launch (start us, length us, event | category | flops | bytes accessed | tf_op | source)
XLA Modules:
  0.0 112.7 jit_solution(16515734278109140069)
XLA Ops:
  1.7 3.3 %collective-permute-start = (bf16[1,528,128]{2,1,0:T(8,128)(2,1)S(1)}, bf16[1,528,128]{2,1,0:T(8,128)(2,1)S(1)}, u32[]{:S(2)}, u32[]{:S(2)}) collective-permute-start(bf16[1,528,128]{2,1,0:T(8,128)(2,1)S(1)} %maximum_bitcast_fusion.own_ref), channel_id=1, source_target_pairs={{0,16},{8,24},{16,32},{24,40},{32,48},{40,56},{48,0},{56,8},{64,80... | collective-permute-start | bytes 405512 | tf_op jit(solution)/shard_map/ppermute | solution.py:40
  5.0 3.1 %collective-permute-start.1 = (bf16[1,528,128]{2,1,0:T(8,128)(2,1)S(1)}, bf16[1,528,128]{2,1,0:T(8,128)(2,1)S(1)}, u32[]{:S(2)}, u32[]{:S(2)}) collective-permute-start(bf16[1,528,128]{2,1,0:T(8,128)(2,1)S(1)} %maximum_bitcast_fusion.own_ref), channel_id=1, source_target_pairs={{0,48},{8,56},{16,0},{24,8},{32,16},{40,24},{48,32},{56,40},{64,11... | collective-permute-start | bytes 405512 | tf_op jit(solution)/shard_map/ppermute | solution.py:40
  8.2 4.9 %collective-permute-start.2 = (bf16[1,528,128]{2,1,0:T(8,128)(2,1)S(1)}, bf16[1,528,128]{2,1,0:T(8,128)(2,1)S(1)}, u32[]{:S(2)}, u32[]{:S(2)}) collective-permute-start(bf16[1,528,128]{2,1,0:T(8,128)(2,1)S(1)} %maximum_bitcast_fusion.own_ref), channel_id=1, source_target_pairs={{0,32},{8,40},{16,48},{24,56},{32,0},{40,8},{48,16},{56,24},{64,96... | collective-permute-start | bytes 405512 | tf_op jit(solution)/shard_map/ppermute | solution.py:40
  21.5 3.9 %collective-permute-done.10 = bf16[1,528,128]{2,1,0:T(8,128)(2,1)S(1)} collective-permute-done((bf16[1,528,128]{2,1,0:T(8,128)(2,1)S(1)}, bf16[1,528,128]{2,1,0:T(8,128)(2,1)S(1)}, u32[]{:S(2)}, u32[]{:S(2)}) %collective-permute-start.10) | collective-permute-done | bytes 135200 | tf_op jit(solution)/shard_map/ppermute | solution.py:40
  26.2 1.4 %collective-permute-start.3 = (bf16[3,528,128]{2,1,0:T(8,128)(2,1)}, bf16[3,528,128]{2,1,0:T(8,128)(2,1)S(1)}, u32[]{:S(2)}, u32[]{:S(2)}) collective-permute-start(bf16[3,528,128]{2,1,0:T(8,128)(2,1)} %get-tuple-element.64), channel_id=1, source_target_pairs={{0,64},{8,72},{16,80},{24,88},{32,96},{40,104},{48,112},{56,120},{... | collective-permute-start | bytes 1216520 | tf_op jit(solution)/shard_map/ppermute | solution.py:40
  29.0 4.9 %fusion.11.q_ref = bf16[512,256]{1,0:T(8,128)(2,1)S(1)} fusion(bf16[5120,512]{1,0:T(8,128)(2,1)} %param.10, bf16[256,5120]{1,0:T(8,128)(2,1)S(1)} %copy-done.7, f32[256]{0:T(256)S(1)} %add_rsqrt_fusion), kind=kOutput, calls=%fused_computation.9 | convolution fusion | flops 1346371584 | bytes 8127488 | tf_op jit(solution)/shard_map/dot_general | solution.py:244
  33.9 3.3 %collective-permute-start.6 = (bf16[1,528,128]{2,1,0:T(8,128)(2,1)S(1)}, bf16[1,528,128]{2,1,0:T(8,128)(2,1)S(1)}, u32[]{:S(2)}, u32[]{:S(2)}) collective-permute-start(bf16[1,528,128]{2,1,0:T(8,128)(2,1)S(1)} %collective-permute-done.5), channel_id=1, source_target_pairs={{128,144},{136,152},{144,160},{152,168},{160,176},{168,184},{176,1... | collective-permute-start | bytes 405512 | tf_op jit(solution)/shard_map/ppermute | solution.py:40
  37.2 4.6 %collective-permute-start.7 = (bf16[1,528,128]{2,1,0:T(8,128)(2,1)S(1)}, bf16[1,528,128]{2,1,0:T(8,128)(2,1)S(1)}, u32[]{:S(2)}, u32[]{:S(2)}) collective-permute-start(bf16[1,528,128]{2,1,0:T(8,128)(2,1)S(1)} %collective-permute-done.5), channel_id=1, source_target_pairs={{128,176},{136,184},{144,128},{152,136},{160,144},{168,152},{176,1... | collective-permute-start | bytes 405512 | tf_op jit(solution)/shard_map/ppermute | solution.py:40
  41.8 4.7 %collective-permute-start.8 = (bf16[1,528,128]{2,1,0:T(8,128)(2,1)S(1)}, bf16[1,528,128]{2,1,0:T(8,128)(2,1)}, u32[]{:S(2)}, u32[]{:S(2)}) collective-permute-start(bf16[1,528,128]{2,1,0:T(8,128)(2,1)S(1)} %collective-permute-done.5), channel_id=1, source_target_pairs={{128,160},{136,168},{144,176},{152,184},{160,128},{168,136},{176,1... | collective-permute-start | bytes 405512 | tf_op jit(solution)/shard_map/ppermute | solution.py:40
  46.7 5.5 %attend_first.1 = (f32[8,256]{1,0:T(8,128)S(1)}, f32[8,256]{1,0:T(8,128)S(1)}, f32[512,256]{1,0:T(8,128)S(1)}) custom-call(s32[2]{0:T(128)S(1)} %pad_add_fusion.at_ref, bf16[1,528,128]{2,1,0:T(8,128)(2,1)S(1)} %maximum_bitcast_fusion.own_ref, bf16[6,528,128]{2,1,0:T(8,128)(2,1)S(1)} %get-tuple-element.57.mine_ref, ...), custom_call_target="tpu_custom_call" | custom-call | flops 134217728 | bytes 135168 | tf_op jit(solution)/shard_map/attend_first/pallas_call | solution.py:258
  52.2 3.6 %collective-permute-done.8 = bf16[1,528,128]{2,1,0:T(8,128)(2,1)} collective-permute-done((bf16[1,528,128]{2,1,0:T(8,128)(2,1)S(1)}, bf16[1,528,128]{2,1,0:T(8,128)(2,1)}, u32[]{:S(2)}, u32[]{:S(2)}) %collective-permute-start.8) | collective-permute-done | bytes 135200 | tf_op jit(solution)/shard_map/ppermute | solution.py:40
  57.0 6.0 %attend_later.1 = (f32[8,256]{1,0:T(8,128)S(1)}, f32[8,256]{1,0:T(8,128)S(1)}, f32[512,256]{1,0:T(8,128)S(1)}) custom-call(s32[2]{0:T(128)S(1)} %pad_add_fusion.at_ref, bf16[9,528,128]{2,1,0:T(8,128)(2,1)S(1)} %constant_dynamic-update-slice_fusion.16.got_ref, bf16[512,256]{1,0:T(8,128)(2,1)S(1)} %fusion.11.q_ref, bf16[128,256]{1,0:T(8,128)(2,1)S(1)} %fusion.20.hot_ref, ...), custom_call_target="tpu_custom_call" | custom-call | flops 1207959552 | bytes 1216512 | tf_op jit(solution)/shard_map/attend_later/pallas_call | solution.py:272
  66.1 6.7 %attend_and_project_1.1 = (bf16[128,512]{1,0:T(8,128)(2,1)}, bf16[4,128,640]{2,1,0:T(8,128)(2,1)}) custom-call(s32[2]{0:T(128)} %copy-done.5, bf16[9,528,128]{2,1,0:T(8,128)(2,1)} %copy-done.6, bf16[512,256]{1,0:T(8,128)(2,1)} %copy-done, bf16[128,256]{1,0:T(8,128)(2,1)} %copy-done.2, f32[8,256]{1,0:T(8,128)} %copy-done.3, f32[8,256]{1,0:T(8,128)} %copy-done.4, ...), custom_call_target="tpu_custom_call" | custom-call | flops 805306368 | bytes 811008 | tf_op jit(solution)/shard_map/attend_and_project_1/pallas_call | solution.py:288
  72.8 1.4 %collective-permute-start.13 = (bf16[4,128,640]{2,1,0:T(8,128)(2,1)}, bf16[4,128,640]{2,1,0:T(8,128)(2,1)S(1)}, u32[]{:S(2)}, u32[]{:S(2)}) collective-permute-start(bf16[4,128,640]{2,1,0:T(8,128)(2,1)} %get-tuple-element.47), channel_id=1, source_target_pairs={{0,4},{1,5},{2,6},{3,7},{4,0},{5,1},{6,2},{7,3},{8,12},{9,13},{10,... | collective-permute-start | bytes 1966088 | tf_op jit(solution)/shard_map/ppermute | solution.py:323
  74.2 6.8 %attend_and_project_0.1 = (bf16[128,512]{1,0:T(8,128)(2,1)}, bf16[2,128,640]{2,1,0:T(8,128)(2,1)}, bf16[2,128,640]{2,1,0:T(8,128)(2,1)}, bf16[2,128,640]{2,1,0:T(8,128)(2,1)}) custom-call(s32[2]{0:T(128)} %copy-done.5, bf16[9,528,128]{2,1,0:T(8,128)(2,1)} %copy-done.6, bf16[512,256]{1,0:T(8,128)(2,1)} %copy-done, bf16[128,256]{1,0:T(8,128)(2,1)} %copy-done.2, ...), custom_call_target="tpu_custom_call" | custom-call | flops 805306368 | bytes 811008 | tf_op jit(solution)/shard_map/attend_and_project_0/pallas_call | solution.py:288
  81.0 1.5 %collective-permute-start.14 = (bf16[2,128,640]{2,1,0:T(8,128)(2,1)}, bf16[2,128,640]{2,1,0:T(8,128)(2,1)S(1)}, u32[]{:S(2)}, u32[]{:S(2)}) collective-permute-start(bf16[2,128,640]{2,1,0:T(8,128)(2,1)} %get-tuple-element.48), channel_id=1, source_target_pairs={{0,1},{1,2},{2,3},{3,0},{4,5},{5,6},{6,7},{7,4},{8,9},{9,10},{10,1... | collective-permute-start | bytes 983048 | tf_op jit(solution)/shard_map/ppermute | solution.py:320
  82.6 1.8 %collective-permute-start.15 = (bf16[2,128,640]{2,1,0:T(8,128)(2,1)}, bf16[2,128,640]{2,1,0:T(8,128)(2,1)S(1)}, u32[]{:S(2)}, u32[]{:S(2)}) collective-permute-start(bf16[2,128,640]{2,1,0:T(8,128)(2,1)} %get-tuple-element.50), channel_id=1, source_target_pairs={{0,3},{1,0},{2,1},{3,2},{4,7},{5,4},{6,5},{7,6},{8,11},{9,8},{10,9... | collective-permute-start | bytes 983048 | tf_op jit(solution)/shard_map/ppermute | solution.py:320
  84.3 1.8 %collective-permute-start.16 = (bf16[2,128,640]{2,1,0:T(8,128)(2,1)}, bf16[2,128,640]{2,1,0:T(8,128)(2,1)S(1)}, u32[]{:S(2)}, u32[]{:S(2)}) collective-permute-start(bf16[2,128,640]{2,1,0:T(8,128)(2,1)} %get-tuple-element.51), channel_id=1, source_target_pairs={{0,2},{1,3},{2,0},{3,1},{4,6},{5,7},{6,4},{7,5},{8,10},{9,11},{10,... | collective-permute-start | bytes 983048 | tf_op jit(solution)/shard_map/ppermute | solution.py:320
  86.1 5.1 %project_own.1 = (bf16[2,128,640]{2,1,0:T(8,128)(2,1)}, bf16[4,128,640]{2,1,0:T(8,128)(2,1)}) custom-call(s32[2]{0:T(128)} %copy-done.5, bf16[128,512]{1,0:T(8,128)(2,1)} %get-tuple-element.43.att_a, bf16[128,512]{1,0:T(8,128)(2,1)} %get-tuple-element.44.att_b, bf16[512,5120]{1,0:T(8,128)(2,1)} %w_hbm.5), custom_call_target="tpu_custom_call" | custom-call | flops 536870912 | bytes 540672 | tf_op jit(solution)/shard_map/project_own/pallas_call | solution.py:308
  92.5 6.2 %collective-permute-done.15 = bf16[2,128,640]{2,1,0:T(8,128)(2,1)S(1)} collective-permute-done((bf16[2,128,640]{2,1,0:T(8,128)(2,1)}, bf16[2,128,640]{2,1,0:T(8,128)(2,1)S(1)}, u32[]{:S(2)}, u32[]{:S(2)}) %collective-permute-start.15) | collective-permute-done | bytes 327712 | tf_op jit(solution)/shard_map/ppermute | solution.py:320
  98.8 1.6 %collective-permute-done.16 = bf16[2,128,640]{2,1,0:T(8,128)(2,1)S(1)} collective-permute-done((bf16[2,128,640]{2,1,0:T(8,128)(2,1)}, bf16[2,128,640]{2,1,0:T(8,128)(2,1)S(1)}, u32[]{:S(2)}, u32[]{:S(2)}) %collective-permute-start.16) | collective-permute-done | bytes 327712 | tf_op jit(solution)/shard_map/ppermute | solution.py:320
  102.8 2.1 %collective-permute-start.19 = (bf16[128,640]{1,0:T(8,128)(2,1)S(1)}, bf16[128,640]{1,0:T(8,128)(2,1)S(1)}, u32[]{:S(2)}, u32[]{:S(2)}) collective-permute-start(bf16[128,640]{1,0:T(8,128)(2,1)S(1)} %get-tuple-element.55), channel_id=1, source_target_pairs={{0,3},{1,0},{2,1},{3,2},{4,7},{5,4},{6,5},{7,6},{8,11},{9,8},{10,9... | collective-permute-start | bytes 491528 | tf_op jit(solution)/shard_map/ppermute | solution.py:320
  106.1 2.8 %collective-permute-done.18 = bf16[128,640]{1,0:T(8,128)(2,1)S(1)} collective-permute-done((bf16[128,640]{1,0:T(8,128)(2,1)S(1)}, bf16[128,640]{1,0:T(8,128)(2,1)S(1)}, u32[]{:S(2)}, u32[]{:S(2)}) %collective-permute-start.18) | collective-permute-done | bytes 163872 | tf_op jit(solution)/shard_map/ppermute | solution.py:320
  108.9 2.0 %collective-permute-done.19 = bf16[128,640]{1,0:T(8,128)(2,1)S(1)} collective-permute-done((bf16[128,640]{1,0:T(8,128)(2,1)S(1)}, bf16[128,640]{1,0:T(8,128)(2,1)S(1)}, u32[]{:S(2)}, u32[]{:S(2)}) %collective-permute-start.19) | collective-permute-done | bytes 163872 | tf_op jit(solution)/shard_map/ppermute | solution.py:320
  (71 shorter events, 23.2 us)
Async XLA Ops:
  1.7 14.9 %collective-permute-start = (bf16[1,528,128]{2,1,0:T(8,128)(2,1)S(1)}, bf16[1,528,128]{2,1,0:T(8,128)(2,1)S(1)}, u32[]{:S(2)}, u32[]{:S(2)}) collective-permute-start(bf16[1,528,128]{2,1,0:T(8,128)(2,1)S(1)} %maximum_bitcast_fusion.own_ref), channel_id=1, source_target_pairs={{0,16},{8,24},{16,32},{24,40},{32,48},{40,56},{48,0},{56,8},{64,80... | collective-permute-start | bytes 405512 | tf_op jit(solution)/shard_map/ppermute | solution.py:40
  5.0 13.9 %collective-permute-start.1 = (bf16[1,528,128]{2,1,0:T(8,128)(2,1)S(1)}, bf16[1,528,128]{2,1,0:T(8,128)(2,1)S(1)}, u32[]{:S(2)}, u32[]{:S(2)}) collective-permute-start(bf16[1,528,128]{2,1,0:T(8,128)(2,1)S(1)} %maximum_bitcast_fusion.own_ref), channel_id=1, source_target_pairs={{0,48},{8,56},{16,0},{24,8},{32,16},{40,24},{48,32},{56,40},{64,11... | collective-permute-start | bytes 405512 | tf_op jit(solution)/shard_map/ppermute | solution.py:40
  8.2 12.6 %collective-permute-start.2 = (bf16[1,528,128]{2,1,0:T(8,128)(2,1)S(1)}, bf16[1,528,128]{2,1,0:T(8,128)(2,1)S(1)}, u32[]{:S(2)}, u32[]{:S(2)}) collective-permute-start(bf16[1,528,128]{2,1,0:T(8,128)(2,1)S(1)} %maximum_bitcast_fusion.own_ref), channel_id=1, source_target_pairs={{0,32},{8,40},{16,48},{24,56},{32,0},{40,8},{48,16},{56,24},{64,96... | collective-permute-start | bytes 405512 | tf_op jit(solution)/shard_map/ppermute | solution.py:40
  13.1 8.4 %collective-permute-start.9 = (bf16[1,528,128]{2,1,0:T(8,128)(2,1)S(1)}, bf16[1,528,128]{2,1,0:T(8,128)(2,1)S(1)}, u32[]{:S(2)}, u32[]{:S(2)}) collective-permute-start(bf16[1,528,128]{2,1,0:T(8,128)(2,1)S(1)} %maximum_bitcast_fusion.own_ref), channel_id=1, source_target_pairs={{0,64},{8,72},{16,80},{24,88},{32,96},{40,104},{48,112},{56,120},{... | collective-permute-start | bytes 405512 | tf_op jit(solution)/shard_map/ppermute | solution.py:40
  14.4 11.0 %collective-permute-start.10 = (bf16[1,528,128]{2,1,0:T(8,128)(2,1)S(1)}, bf16[1,528,128]{2,1,0:T(8,128)(2,1)S(1)}, u32[]{:S(2)}, u32[]{:S(2)}) collective-permute-start(bf16[1,528,128]{2,1,0:T(8,128)(2,1)S(1)} %maximum_bitcast_fusion.own_ref), channel_id=1, source_target_pairs={{0,192},{8,200},{16,208},{24,216},{32,224},{40,232},{48,240},{56,2... | collective-permute-start | bytes 405512 | tf_op jit(solution)/shard_map/ppermute | solution.py:40
  16.6 8.9 %collective-permute-start.5 = (bf16[1,528,128]{2,1,0:T(8,128)(2,1)S(1)}, bf16[1,528,128]{2,1,0:T(8,128)(2,1)S(1)}, u32[]{:S(2)}, u32[]{:S(2)}) collective-permute-start(bf16[1,528,128]{2,1,0:T(8,128)(2,1)S(1)} %maximum_bitcast_fusion.own_ref), channel_id=1, source_target_pairs={{0,128},{8,136},{16,144},{24,152},{32,160},{40,168},{48,176},{56,1... | collective-permute-start | bytes 405512 | tf_op jit(solution)/shard_map/ppermute | solution.py:40
  25.5 16.3 %collective-permute-start.11 = (bf16[7,528,128]{2,1,0:T(8,128)(2,1)S(1)}, bf16[7,528,128]{2,1,0:T(8,128)(2,1)S(1)}, u32[]{:S(2)}, u32[]{:S(2)}) collective-permute-start(bf16[7,528,128]{2,1,0:T(8,128)(2,1)S(1)} %get-tuple-element.56), channel_id=1, source_target_pairs={{0,8},{8,0},{16,24},{24,16},{32,40},{40,32},{48,56},{56,48},{64,72... | collective-permute-start | bytes 2838536 | tf_op jit(solution)/shard_map/ppermute | solution.py:40
  26.2 20.3 %copy-start.9 = (s32[256]{0:T(256)S(1)}, s32[256]{0:T(256)}, u32[]{:S(2)}) copy-start(s32[256]{0:T(256)} %param.9) | copy-start | bytes 3076
  26.2 29.6 %collective-permute-start.3 = (bf16[3,528,128]{2,1,0:T(8,128)(2,1)}, bf16[3,528,128]{2,1,0:T(8,128)(2,1)S(1)}, u32[]{:S(2)}, u32[]{:S(2)}) collective-permute-start(bf16[3,528,128]{2,1,0:T(8,128)(2,1)} %get-tuple-element.64), channel_id=1, source_target_pairs={{0,64},{8,72},{16,80},{24,88},{32,96},{40,104},{48,112},{56,120},{... | collective-permute-start | bytes 1216520 | tf_op jit(solution)/shard_map/ppermute | solution.py:40
  27.7 28.1 %collective-permute-start.4 = (bf16[3,528,128]{2,1,0:T(8,128)(2,1)}, bf16[3,528,128]{2,1,0:T(8,128)(2,1)S(1)}, u32[]{:S(2)}, u32[]{:S(2)}) collective-permute-start(bf16[3,528,128]{2,1,0:T(8,128)(2,1)} %get-tuple-element.64), channel_id=1, source_target_pairs={{0,192},{8,200},{16,208},{24,216},{32,224},{40,232},{48,240},{56,2... | collective-permute-start | bytes 1216520 | tf_op jit(solution)/shard_map/ppermute | solution.py:40
  33.9 23.1 %copy-start = (bf16[512,256]{1,0:T(8,128)(2,1)}, bf16[512,256]{1,0:T(8,128)(2,1)S(1)}, u32[]{:S(2)}) copy-start(bf16[512,256]{1,0:T(8,128)(2,1)S(1)} %fusion.11.q_ref) | copy-start | bytes 786436
  33.9 18.3 %collective-permute-start.6 = (bf16[1,528,128]{2,1,0:T(8,128)(2,1)S(1)}, bf16[1,528,128]{2,1,0:T(8,128)(2,1)S(1)}, u32[]{:S(2)}, u32[]{:S(2)}) collective-permute-start(bf16[1,528,128]{2,1,0:T(8,128)(2,1)S(1)} %collective-permute-done.5), channel_id=1, source_target_pairs={{128,144},{136,152},{144,160},{152,168},{160,176},{168,184},{176,1... | collective-permute-start | bytes 405512 | tf_op jit(solution)/shard_map/ppermute | solution.py:40
  37.2 15.0 %collective-permute-start.7 = (bf16[1,528,128]{2,1,0:T(8,128)(2,1)S(1)}, bf16[1,528,128]{2,1,0:T(8,128)(2,1)S(1)}, u32[]{:S(2)}, u32[]{:S(2)}) collective-permute-start(bf16[1,528,128]{2,1,0:T(8,128)(2,1)S(1)} %collective-permute-done.5), channel_id=1, source_target_pairs={{128,176},{136,184},{144,128},{152,136},{160,144},{168,152},{176,1... | collective-permute-start | bytes 405512 | tf_op jit(solution)/shard_map/ppermute | solution.py:40
  41.8 14.0 %collective-permute-start.8 = (bf16[1,528,128]{2,1,0:T(8,128)(2,1)S(1)}, bf16[1,528,128]{2,1,0:T(8,128)(2,1)}, u32[]{:S(2)}, u32[]{:S(2)}) collective-permute-start(bf16[1,528,128]{2,1,0:T(8,128)(2,1)S(1)} %collective-permute-done.5), channel_id=1, source_target_pairs={{128,160},{136,168},{144,176},{152,184},{160,128},{168,136},{176,1... | collective-permute-start | bytes 405512 | tf_op jit(solution)/shard_map/ppermute | solution.py:40
  46.6 10.4 %copy-start.2 = (bf16[128,256]{1,0:T(8,128)(2,1)}, bf16[128,256]{1,0:T(8,128)(2,1)S(1)}, u32[]{:S(2)}) copy-start(bf16[128,256]{1,0:T(8,128)(2,1)S(1)} %fusion.20.hot_ref) | copy-start | bytes 196612
  56.9 8.2 %collective-permute-start.12 = (bf16[9,528,128]{2,1,0:T(8,128)(2,1)S(1)}, bf16[9,528,128]{2,1,0:T(8,128)(2,1)S(1)}, u32[]{:S(2)}, u32[]{:S(2)}) collective-permute-start(bf16[9,528,128]{2,1,0:T(8,128)(2,1)S(1)} %constant_dynamic-update-slice_fusion.16.got_ref), channel_id=1, source_target_pairs={{0,8},{8,0},{16,24},{24,16},{32,40},{40,32},{48,56},{56,48},{64,72... | collective-permute-start | bytes 3649544 | tf_op jit(solution)/shard_map/ppermute | solution.py:40
  72.8 18.5 %collective-permute-start.13 = (bf16[4,128,640]{2,1,0:T(8,128)(2,1)}, bf16[4,128,640]{2,1,0:T(8,128)(2,1)S(1)}, u32[]{:S(2)}, u32[]{:S(2)}) collective-permute-start(bf16[4,128,640]{2,1,0:T(8,128)(2,1)} %get-tuple-element.47), channel_id=1, source_target_pairs={{0,4},{1,5},{2,6},{3,7},{4,0},{5,1},{6,2},{7,3},{8,12},{9,13},{10,... | collective-permute-start | bytes 1966088 | tf_op jit(solution)/shard_map/ppermute | solution.py:323
  81.0 11.5 %collective-permute-start.14 = (bf16[2,128,640]{2,1,0:T(8,128)(2,1)}, bf16[2,128,640]{2,1,0:T(8,128)(2,1)S(1)}, u32[]{:S(2)}, u32[]{:S(2)}) collective-permute-start(bf16[2,128,640]{2,1,0:T(8,128)(2,1)} %get-tuple-element.48), channel_id=1, source_target_pairs={{0,1},{1,2},{2,3},{3,0},{4,5},{5,6},{6,7},{7,4},{8,9},{9,10},{10,1... | collective-permute-start | bytes 983048 | tf_op jit(solution)/shard_map/ppermute | solution.py:320
  82.6 16.2 %collective-permute-start.15 = (bf16[2,128,640]{2,1,0:T(8,128)(2,1)}, bf16[2,128,640]{2,1,0:T(8,128)(2,1)S(1)}, u32[]{:S(2)}, u32[]{:S(2)}) collective-permute-start(bf16[2,128,640]{2,1,0:T(8,128)(2,1)} %get-tuple-element.50), channel_id=1, source_target_pairs={{0,3},{1,0},{2,1},{3,2},{4,7},{5,4},{6,5},{7,6},{8,11},{9,8},{10,9... | collective-permute-start | bytes 983048 | tf_op jit(solution)/shard_map/ppermute | solution.py:320
  84.3 16.0 %collective-permute-start.16 = (bf16[2,128,640]{2,1,0:T(8,128)(2,1)}, bf16[2,128,640]{2,1,0:T(8,128)(2,1)S(1)}, u32[]{:S(2)}, u32[]{:S(2)}) collective-permute-start(bf16[2,128,640]{2,1,0:T(8,128)(2,1)} %get-tuple-element.51), channel_id=1, source_target_pairs={{0,2},{1,3},{2,0},{3,1},{4,6},{5,7},{6,4},{7,5},{8,10},{9,11},{10,... | collective-permute-start | bytes 983048 | tf_op jit(solution)/shard_map/ppermute | solution.py:320
  100.5 5.6 %collective-permute-start.17 = (bf16[128,640]{1,0:T(8,128)(2,1)S(1)}, bf16[128,640]{1,0:T(8,128)(2,1)S(1)}, u32[]{:S(2)}, u32[]{:S(2)}) collective-permute-start(bf16[128,640]{1,0:T(8,128)(2,1)S(1)} %fusion.19), channel_id=1, source_target_pairs={{0,4},{1,5},{2,6},{3,7},{4,0},{5,1},{6,2},{7,3},{8,12},{9,13},{10,... | collective-permute-start | bytes 491528 | tf_op jit(solution)/shard_map/ppermute | solution.py:323
  101.6 7.3 %collective-permute-start.18 = (bf16[128,640]{1,0:T(8,128)(2,1)S(1)}, bf16[128,640]{1,0:T(8,128)(2,1)S(1)}, u32[]{:S(2)}, u32[]{:S(2)}) collective-permute-start(bf16[128,640]{1,0:T(8,128)(2,1)S(1)} %get-tuple-element.53), channel_id=1, source_target_pairs={{0,1},{1,2},{2,3},{3,0},{4,5},{5,6},{6,7},{7,4},{8,9},{9,10},{10,1... | collective-permute-start | bytes 491528 | tf_op jit(solution)/shard_map/ppermute | solution.py:320
  102.8 8.1 %collective-permute-start.19 = (bf16[128,640]{1,0:T(8,128)(2,1)S(1)}, bf16[128,640]{1,0:T(8,128)(2,1)S(1)}, u32[]{:S(2)}, u32[]{:S(2)}) collective-permute-start(bf16[128,640]{1,0:T(8,128)(2,1)S(1)} %get-tuple-element.55), channel_id=1, source_target_pairs={{0,3},{1,0},{2,1},{3,2},{4,7},{5,4},{6,5},{7,6},{8,11},{9,8},{10,9... | collective-permute-start | bytes 491528 | tf_op jit(solution)/shard_map/ppermute | solution.py:320
  104.9 7.0 %collective-permute-start.20 = (bf16[128,640]{1,0:T(8,128)(2,1)S(1)}, bf16[128,640]{1,0:T(8,128)(2,1)S(1)}, u32[]{:S(2)}, u32[]{:S(2)}) collective-permute-start(bf16[128,640]{1,0:T(8,128)(2,1)S(1)} %get-tuple-element.54), channel_id=1, source_target_pairs={{0,2},{1,3},{2,0},{3,1},{4,6},{5,7},{6,4},{7,5},{8,10},{9,11},{10,... | collective-permute-start | bytes 491528 | tf_op jit(solution)/shard_map/ppermute | solution.py:320
  (7 other events, 31.5 us)

commit v4 on v2

v4 whole, which is shorter than its diff:
```python
import functools

import jax
import jax.numpy as jnp
from jax import lax
from jax.experimental import pallas as pl
from jax.experimental.pallas import tpu as pltpu
from jax.sharding import PartitionSpec as P
import numpy as np

HEAD_DIM = 128
BLOCK = 256
PACK = 2 * BLOCK + 16
REACH = 24
HALF = BLOCK // 2
COLS = 640
FLOOR = -1e30
HIDDEN = -2e30

F32 = jnp.float32
BF16 = jnp.bfloat16


def ctx_id(y, z, c):
    return ((y + 8) % 4) * 8 + ((z + 8) % 4) * 2 + c


def ctx_pairs(step, planes=None):
    pairs = []
    for y in range(4):
        for z in range(4):
            for c in range(2):
                to = step(y, z, c)
                if to is not None:
                    pairs.append((ctx_id(y, z, c), ctx_id(*to)))
    return pairs


def move(x, step):
    return lax.ppermute(x, "ctx", ctx_pairs(step))


def swap_cores(x):
    return move(x, lambda y, z, c: (y, z, 1 - c))


def along_z(x, first_plane=0):
    def step(y, z, c):
        return (y, z + 1 if c == 0 else z - 1, c) if y >= first_plane else None

    return move(x, step)


def along_y(x):
    def step(y, z, c):
        if c == 0:
            return (y + 1, z, c) if y < 3 else None
        return (3, z, c) if y == 0 else None

    return move(x, step)


def up_y(x):
    return move(x, lambda y, z, c: (y + 1, z, c) if y < 3 else None)


def round_y(x):
    return move(x, lambda y, z, c: (3, z, c) if y == 0 else None)


def first_slots(y, z, c):
    d = 2 * c - 1
    return [[(y, z + d, c), (y, z + d, 1 - c)], [(y, z + 2, c)], [(y + d, z, c), (y + d, z, 1 - c)]]


def far_slots(y, z, c):
    d = 2 * c - 1
    return [[(y + 2, z, c)], [(y + 2, z + d, c), (y + 2, z + d, 1 - c)], [(y + 2, z + 2, c)]]


def later_slots(y, z, c):
    d = 2 * c - 1
    return [[(y + e, z + d, c), (y + e, z + d, 1 - c), (y + e, z + 2, c)] for e in (-1, 1)]


def attend_blocks(kv_ref, places, diagonal, q_ref, hot_ref, m_ref, l_ref, acc_ref):
    heads = [slice(h * HEAD_DIM, (h + 1) * HEAD_DIM) for h in range(4)]
    keys, values, visible = [], [], []
    for at, low in places:
        keys.append(kv_ref[at, 0:BLOCK, :])
        values.append(jnp.transpose(kv_ref[at, BLOCK : 2 * BLOCK, :]))
        counts = kv_ref[at, 2 * BLOCK : PACK, :]
        first = jnp.dot(counts, hot_ref[...], preferred_element_type=F32)[0:1, :].astype(jnp.int32)
        row = lax.broadcasted_iota(jnp.int32, (BLOCK, BLOCK), 0)
        seen = row >= jnp.maximum(first, low)
        if diagonal:
            seen &= row <= lax.broadcasted_iota(jnp.int32, (BLOCK, BLOCK), 1)
        visible.append(seen)
    scores = [[jnp.dot(k, q_ref[rows, :], preferred_element_type=F32) for k in keys] for rows in heads]
    old = [(m_ref[h : h + 1, :], l_ref[h : h + 1, :]) for h in range(4)]
    new = []
    for h in range(4):
        masked = [jnp.where(seen, s, HIDDEN) for seen, s in zip(visible, scores[h])]
        m_old, total = old[h]
        m_new = m_old
        for s in masked:
            m_new = jnp.maximum(m_new, jnp.max(s, axis=0, keepdims=True))
        weights = [jnp.exp(s - m_new) for s in masked]
        fade = jnp.exp(m_old - m_new)
        total = fade * total
        for p in weights:
            total = total + jnp.sum(p, axis=0, keepdims=True)
        added = sum(jnp.dot(v, p.astype(BF16), preferred_element_type=F32) for v, p in zip(values, weights))
        new.append((m_new, total, fade, added))
    for h, rows in enumerate(heads):
        m_new, total, fade, added = new[h]
        m_ref[h : h + 1, :] = m_new
        l_ref[h : h + 1, :] = total
        acc_ref[rows, :] = fade * acc_ref[rows, :] + added


def attend_pieces(at_ref, slots, piece_refs, all_ref, order_ref, *refs):
    own, y, z, c = where_am_i(at_ref)
    places = slots(y, z, c)
    count = jnp.int32(0)
    n = 0
    for piece_ref, places_of in zip(piece_refs, places):
        for i, place in enumerate(places_of):
            block = ctx_id(*place)
            all_ref[n] = piece_ref[i]
            order_ref[count] = n
            count += ((block < own) & (block >= own - REACH)).astype(jnp.int32)
            n += 1

    @pl.loop(0, (count + 1) // 2)
    def _(g):
        one = order_ref[2 * g]
        both = 2 * g + 1 < count
        two = jnp.where(both, order_ref[2 * g + 1], one)
        attend_blocks(all_ref, [(one, 0), (two, jnp.where(both, 0, BLOCK))], False, *refs)


def where_am_i(at_ref):
    own = at_ref[0]
    return own, own // 8, (own // 2) % 4, own % 2


def start_kernel(slots, n, at_ref, own_ref, *rest):
    pieces, (q_ref, hot_ref, m_ref, l_ref, acc_ref, all_ref, order_ref) = rest[:n], rest[n:]
    m_ref[...] = jnp.full_like(m_ref, FLOOR)
    l_ref[...] = jnp.zeros_like(l_ref)
    acc_ref[...] = jnp.zeros_like(acc_ref)
    refs = (q_ref, hot_ref, m_ref, l_ref, acc_ref)
    attend_blocks(own_ref, [(0, 0)], True, *refs)
    attend_pieces(at_ref, slots, pieces, all_ref, order_ref, *refs)


def more_kernel(slots, n, at_ref, *rest):
    pieces, (q_ref, hot_ref, m_in, l_in, acc_in, m_ref, l_ref, acc_ref, all_ref, order_ref) = rest[:n], rest[n:]
    m_ref[...] = m_in[...]
    l_ref[...] = l_in[...]
    acc_ref[...] = acc_in[...]
    attend_pieces(at_ref, slots, pieces, all_ref, order_ref, q_ref, hot_ref, m_ref, l_ref, acc_ref)


def last_kernel(slots, n, at_ref, *rest):
    pieces, (q_ref, hot_ref, m_in, l_in, acc_in, w_ref, b1, b0, a1, a3, a2, a0) = rest[:n], rest[n : n + 12]
    m_ref, l_ref, acc_ref, all_ref, order_ref, att_ref = rest[n + 12 :]
    m_ref[...] = m_in[...]
    l_ref[...] = l_in[...]
    acc_ref[...] = acc_in[...]
    attend_pieces(at_ref, slots, pieces, all_ref, order_ref, q_ref, hot_ref, m_ref, l_ref, acc_ref)
    for h in range(4):
        rows = slice(h * HEAD_DIM, (h + 1) * HEAD_DIM)
        att_ref[:, rows] = jnp.transpose(acc_ref[rows, :] / l_ref[h : h + 1, :]).astype(BF16)
    b_to, a_to = (b0, b1), (a0, a1, a2, a3)
    section = at_ref[1]
    for dz in range(2):
        for dx in range(4):
            to = (section // 4 + dz) % 2 * 4 + (section + dx) % 4
            cols = pl.ds(pl.multiple_of(to * COLS, 128), COLS)
            part = jnp.dot(att_ref[...], w_ref[:, cols], preferred_element_type=F32).astype(BF16)
            a_to[dx][dz] = part[:HALF]
            b_to[dz][dx] = part[HALF:]


def fetch_kernel(from_ref, to_ref, sem):
    copy = pltpu.make_async_copy(from_ref, to_ref, sem)
    copy.start()
    copy.wait()


VMEM = pl.BlockSpec(memory_space=pltpu.VMEM)
SMEM = pl.BlockSpec(memory_space=pltpu.SMEM)
CARRY = (
    jax.ShapeDtypeStruct((8, BLOCK), F32),
    jax.ShapeDtypeStruct((8, BLOCK), F32),
    jax.ShapeDtypeStruct((4 * HEAD_DIM, BLOCK), F32),
)
LIMIT = pltpu.CompilerParams(vmem_limit_bytes=24 * 1024 * 1024)


def cost(n):
    return pl.CostEstimate(
        flops=n * 4 * 4 * BLOCK * BLOCK * HEAD_DIM,
        bytes_accessed=n * PACK * HEAD_DIM * 2,
        transcendentals=n * 4 * BLOCK * BLOCK,
    )


def per_device(hidden, k_cache, v_cache, segment, w_query, w_out):
    ctx = lax.axis_index("ctx")

    smaller = jnp.sum(
        (segment[:, None] < jnp.arange(HEAD_DIM, dtype=jnp.int32)[None, :]).astype(F32), axis=0
    ).astype(BF16)
    own = jnp.concatenate([k_cache, v_cache, jnp.broadcast_to(smaller[None, :], (16, HEAD_DIM))], axis=0)[None]

    y_far = move(own, lambda y, z, c: (y + 2, z, c) if y < 2 else None)
    other = swap_cores(own)
    pair = jnp.concatenate([own, other], axis=0)
    z_near = along_z(pair)
    y_near = along_y(pair)
    z_far = along_z(z_near[:1])

    widened = hidden.astype(F32)
    normed = (widened * lax.rsqrt(jnp.mean(widened * widened, axis=-1, keepdims=True) + 1e-06)).astype(BF16)
    q_t = (
        lax.dot_general(w_query, normed, (((0,), (1,)), ((), ())), preferred_element_type=F32) * HEAD_DIM ** (-0.5)
    ).astype(BF16)
    hot = (jnp.arange(HEAD_DIM, dtype=jnp.int32)[:, None] == segment[None, :]).astype(BF16)
    w_held = pl.pallas_call(
        fetch_kernel,
        out_shape=jax.ShapeDtypeStruct(w_out.shape, w_out.dtype),
        in_specs=[pl.BlockSpec(memory_space=pltpu.HBM)],
        out_specs=VMEM,
        scratch_shapes=[pltpu.SemaphoreType.DMA],
        compiler_params=LIMIT,
        name="fetch_w_out",
    )(w_out)
    q_t, w_held = lax.optimization_barrier((q_t, w_held))

    row = jnp.concatenate([z_near, z_far], axis=0)
    up = up_y(row)
    around = round_y(row)
    far_other = swap_cores(y_far)
    far_pair, _ = lax.optimization_barrier((jnp.concatenate([y_far, far_other], axis=0), z_far))
    far_near = along_z(far_pair, 2)

    at = jnp.stack([ctx, lax.axis_index("section")]).astype(jnp.int32)

    def scratch(n):
        return [pltpu.VMEM((n, PACK, HEAD_DIM), BF16), pltpu.SMEM((16,), jnp.int32)]

    def attend(kernel, slots, n, pieces, state, name):
        return pl.pallas_call(
            functools.partial(kernel, slots, len(pieces) - (not state)),
            out_shape=CARRY,
            in_specs=[SMEM] + [VMEM] * (len(pieces) + 2 + len(state)),
            out_specs=(VMEM,) * 3,
            scratch_shapes=scratch(n),
            compiler_params=LIMIT,
            cost_estimate=cost(1),
            name=name,
        )(at, *pieces, q_t, hot, *state)

    def slots_1(y, z, c):
        mine, theirs = first_slots(y, z, c), first_slots(y, z, 1 - c)
        return [[(y, z, 1 - c)]] + mine + theirs + far_slots(y, z, c)[:1] + far_slots(y, z, 1 - c)[:1]

    def slots_2(y, z, c):
        return later_slots(y, z, c) + far_slots(y, z, c)[1:2] + far_slots(y, z, 1 - c)[1:2]

    def slots_3(y, z, c):
        return later_slots(y, z, 1 - c)

    def slots_4(y, z, c):
        return far_slots(y, z, c)[2:] + far_slots(y, z, 1 - c)[2:]

    firsts = [z_near, z_far, y_near]
    pieces = [own, other] + firsts + [swap_cores(t) for t in firsts] + [y_far, far_other]
    state = attend(start_kernel, slots_1, 13, pieces, (), "attend_first")

    far_near, state = lax.optimization_barrier((far_near, state))
    far_far = along_z(far_near[:1], 2)
    far_near_other = swap_cores(far_near)
    (up, around), state = lax.optimization_barrier(((up, around), state))
    up_other, around_other = swap_cores(up), swap_cores(around)
    state = attend(more_kernel, slots_2, 10, [up, around, far_near, far_near_other], state, "attend_next")
    far_far, state = lax.optimization_barrier((far_far, state))
    far_far_other = swap_cores(far_far)
    state = attend(more_kernel, slots_3, 6, [up_other, around_other], state, "attend_third")

    part = lambda n: jax.ShapeDtypeStruct((n, HALF, COLS), BF16)
    b1, b0, a1, a3, a2, a0 = pl.pallas_call(
        functools.partial(last_kernel, slots_4, 2),
        out_shape=(part(4), part(4), part(2), part(2), part(2), part(2)),
        in_specs=[SMEM] + [VMEM] * 8,
        out_specs=(VMEM,) * 6,
        scratch_shapes=[
            pltpu.VMEM((8, BLOCK), F32),
            pltpu.VMEM((8, BLOCK), F32),
            pltpu.VMEM((4 * HEAD_DIM, BLOCK), F32),
            *scratch(2),
            pltpu.VMEM((BLOCK, 4 * HEAD_DIM), BF16),
        ],
        compiler_params=LIMIT,
        cost_estimate=cost(12),
        name="attend_and_project",
    )(at, far_far, far_far_other, q_t, hot, *state, w_held)

    def send_x(t, k):
        return lax.ppermute(t, "section", [(g * 4 + x, g * 4 + (x + k) % 4) for g in range(2) for x in range(4)])

    def send_z(t):
        return lax.ppermute(t, "section", [(g * 4 + x, (1 - g) * 4 + x) for g in range(2) for x in range(4)])

    b_in = send_z(b1)
    a_in = [send_x(a, k) for a, k in ((a1, 1), (a3, 3), (a2, 2))]
    b_sum = b0.astype(F32) + b_in.astype(F32)
    b_out = [send_x(b_sum[k].astype(BF16), k) for k in (1, 3, 2)]
    a_in[0], b_out[0] = lax.optimization_barrier((a_in[0], b_out[0]))
    a_sum = a0.astype(F32) + a_in[0].astype(F32) + a_in[1].astype(F32) + a_in[2].astype(F32)
    a_out = send_z(a_sum[1].astype(BF16))
    a = a_sum[0] + a_out.astype(F32)
    b = b_sum[0] + b_out[0].astype(F32) + b_out[1].astype(F32) + b_out[2].astype(F32)
    return jnp.concatenate([a, b], axis=0).astype(BF16)


def solution(mesh):
    return jax.shard_map(
        per_device,
        mesh=mesh,
        in_specs=(
            P("ctx", None),
            P("ctx", "section"),
            P("ctx", "section"),
            P("ctx"),
            P(None, "section"),
            P("section", None),
        ),
        out_specs=P("ctx", "section"),
        check_vma=False,
    )
```

time: 101 us -> 99.9 us (0.989)
  the two profiles are of different devices: /device:TPU:28 before, /device:TPU:24 now
where the time goes in v4:
time: 99.9 us; the launch traced here: 99.5 us
  starting transfers between devices  38.2 us (38%)
  waiting for transfers between devices  26 us (26%)
  Pallas kernels  19.4 us (19%)
  other arithmetic  6.07 us (6%)
  matrix products  5.57 us (6%)
  local copies, waits for them, and re-layouts  3.95 us (4%)
    ppermute x17, starting transfers between devices, move(): return lax.ppermute(x, 'ctx', ctx_pairs(step))  27.2 us
    pallas_call x3, Pallas kernels, attend(): pl.pallas_call(functools.partial(kernel, slots, len(pieces) - (not state)...  15.4 us
    ppermute x2, waiting for transfers between devices, send_z(): lax.ppermute(t, 'section', [(g * 4 + x, (1 - g) * 4 + x) for g in range(2...  13.1 us
    ppermute x6, starting transfers between devices, send_x(): lax.ppermute(t, 'section', [(g * 4 + x, g * 4 + (x + k) % 4) for g in ran...  10.2 us
    ppermute x17, waiting for transfers between devices, move(): return lax.ppermute(x, 'ctx', ctx_pairs(step))  7.78 us
    dot_general x1, matrix products, per_device(): lax.dot_general(w_query, normed, (((0,), (1,)), ((), ())), preferred_elem...  5.57 us
    ppermute x6, waiting for transfers between devices, send_x(): lax.ppermute(t, 'section', [(g * 4 + x, g * 4 + (x + k) % 4) for g in ran...  5.1 us
    pallas_call x1, Pallas kernels, per_device(): pl.pallas_call(functools.partial(last_kernel, slots_4, 2), out_shape=(par...  3.68 us
  transfers between devices with their start and end apart: 25, of which 8 were waited for; matrix products, arithmetic and copies ran while one was open for 11% of the time, Pallas kernels for 16%

profile of v4, /device:TPU:24, one launch (start us, length us, event | category | flops | bytes accessed | tf_op | source)
XLA Modules:
  0.0 99.5 jit_solution(4524211444750008432)
XLA Ops:
  3.2 3.3 %collective-permute-start.3 = (bf16[2,528,128]{2,1,0:T(8,128)(2,1)S(1)}, bf16[2,528,128]{2,1,0:T(8,128)(2,1)S(1)}, u32[]{:S(2)}, u32[]{:S(2)}) collective-permute-start(bf16[2,528,128]{2,1,0:T(8,128)(2,1)S(1)} %pad_maximum_fusion.2), channel_id=1, source_target_pairs={{0,16},{8,56},{16,32},{24,8},{32,48},{40,24},{48,0},{56,40},{64,80... | collective-permute-start | bytes 811016 | tf_op jit(solution)/shard_map/ppermute | solution.py:40
  6.5 2.3 %fusion = f32[256]{0:T(256)S(1)} fusion(bf16[256,5120]{1,0:T(8,128)(2,1)} %param.6), kind=kLoop, calls=%fused_computation.2 | loop fusion | flops 3931904 | bytes 2622464 | tf_op jit(solution)/shard_map/reduce_sum | solution.py:227
  8.9 5.7 %collective-permute-done.3.rest_1_ = bf16[2,528,128]{2,1,0:T(8,128)(2,1)S(1)} collective-permute-done((bf16[2,528,128]{2,1,0:T(8,128)(2,1)S(1)}, bf16[2,528,128]{2,1,0:T(8,128)(2,1)S(1)}, u32[]{:S(2)}, u32[]{:S(2)}) %collective-permute-start.3) | collective-permute-done | bytes 270368 | tf_op jit(solution)/shard_map/ppermute | solution.py:40
  14.6 3.3 %collective-permute-start.4 = (bf16[1,528,128]{2,1,0:T(8,128)(2,1)S(1)}, bf16[1,528,128]{2,1,0:T(8,128)(2,1)S(1)}, u32[]{:S(2)}, u32[]{:S(2)}) collective-permute-start(bf16[1,528,128]{2,1,0:T(8,128)(2,1)S(1)} %slice.36), channel_id=1, source_target_pairs={{0,16},{8,56},{16,32},{24,8},{32,48},{40,24},{48,0},{56,40},{64,80... | collective-permute-start | bytes 405512 | tf_op jit(solution)/shard_map/ppermute | solution.py:40
  17.9 5.6 %fusion.11.rest_9_.rest_4_.rest_2_ = bf16[512,256]{1,0:T(8,128)(2,1)S(1)} fusion(bf16[5120,512]{1,0:T(8,128)(2,1)} %param.10, bf16[256,5120]{1,0:T(8,128)(2,1)} %param.6, f32[256]{0:T(256)S(1)} %add_rsqrt_fusion), kind=kOutput, calls=%fused_computation.9 | convolution fusion | flops 1346371584 | bytes 8127488 | tf_op jit(solution)/shard_map/dot_general | solution.py:229
  24.8 2.4 %collective-permute-start.1 = (bf16[1,528,128]{2,1,0:T(8,128)(2,1)S(1)}, bf16[1,528,128]{2,1,0:T(8,128)(2,1)S(1)}, u32[]{:S(2)}, u32[]{:S(2)}) collective-permute-start(bf16[1,528,128]{2,1,0:T(8,128)(2,1)S(1)} %collective-permute-done.rest_7_), channel_id=1, source_target_pairs={{0,8},{8,0},{16,24},{24,16},{32,40},{40,32},{48,56},{56,48},{64,72... | collective-permute-start | bytes 405512 | tf_op jit(solution)/shard_map/ppermute | solution.py:40
  31.9 2.4 %collective-permute-start.9 = (bf16[2,528,128]{2,1,0:T(8,128)(2,1)S(1)}, bf16[2,528,128]{2,1,0:T(8,128)(2,1)S(1)}, u32[]{:S(2)}, u32[]{:S(2)}) collective-permute-start(bf16[2,528,128]{2,1,0:T(8,128)(2,1)S(1)} %collective-permute-done.6.rest_3_), channel_id=1, source_target_pairs={{0,8},{8,0},{16,24},{24,16},{32,40},{40,32},{48,56},{56,48},{64,72... | collective-permute-start | bytes 811016 | tf_op jit(solution)/shard_map/ppermute | solution.py:40
  34.3 4.0 %collective-permute-start.5 = (bf16[2,528,128]{2,1,0:T(8,128)(2,1)}, bf16[2,528,128]{2,1,0:T(8,128)(2,1)S(1)}, u32[]{:S(2)}, u32[]{:S(2)}) collective-permute-start(bf16[2,528,128]{2,1,0:T(8,128)(2,1)} %pad_maximum_fusion.1), channel_id=1, source_target_pairs={{128,144},{136,184},{144,160},{152,136},{160,176},{168,152},{176,1... | collective-permute-start | bytes 811016 | tf_op jit(solution)/shard_map/ppermute | solution.py:40
  38.5 2.5 %copy-done = bf16[512,5120]{1,0:T(8,128)(2,1)S(1)} copy-done((bf16[512,5120]{1,0:T(8,128)(2,1)S(1)}, bf16[512,5120]{1,0:T(8,128)(2,1)}, u32[]{:S(2)}) %copy-start) | copy-done | bytes 5242904
  41.4 4.6 %attend_first.1 = (f32[8,256]{1,0:T(8,128)S(1)}, f32[8,256]{1,0:T(8,128)S(1)}, f32[512,256]{1,0:T(8,128)S(1)}) custom-call(s32[2]{0:T(128)S(1)} %pad_add_fusion.at_ref, bf16[1,528,128]{2,1,0:T(8,128)(2,1)S(1)} %maximum_bitcast_fusion.own_ref, bf16[1,528,128]{2,1,0:T(8,128)(2,1)S(1)} %collective-permute-done.2.rest_0_, ...), custom_call_target="tpu_custom_call" | custom-call | flops 134217728 | bytes 135168 | tf_op jit(solution)/shard_map/attend_first/pallas_call | solution.py:256
  48.2 3.7 %collective-permute-start.10 = (bf16[1,528,128]{2,1,0:T(8,128)(2,1)S(1)}, bf16[1,528,128]{2,1,0:T(8,128)(2,1)S(1)}, u32[]{:S(2)}, u32[]{:S(2)}) collective-permute-start(bf16[1,528,128]{2,1,0:T(8,128)(2,1)S(1)} %slice.29), channel_id=1, source_target_pairs={{128,144},{136,184},{144,160},{152,136},{160,176},{168,152},{176,1... | collective-permute-start | bytes 405512 | tf_op jit(solution)/shard_map/ppermute | solution.py:40
  51.9 6.6 %attend_next.1 = (f32[8,256]{1,0:T(8,128)S(1)}, f32[8,256]{1,0:T(8,128)S(1)}, f32[512,256]{1,0:T(8,128)S(1)}) custom-call(s32[2]{0:T(128)S(1)} %pad_add_fusion.at_ref, bf16[3,528,128]{2,1,0:T(8,128)(2,1)S(1)} %collective-permute-done.11.rest_0_, bf16[3,528,128]{2,1,0:T(8,128)(2,1)S(1)} %collective-permute-done.12.rest_1_, ...), custom_call_target="tpu_custom_call" | custom-call | flops 134217728 | bytes 135168 | tf_op jit(solution)/shard_map/attend_next/pallas_call | solution.py:256
  59.0 2.2 %collective-permute-start.14 = (bf16[1,528,128]{2,1,0:T(8,128)(2,1)S(1)}, bf16[1,528,128]{2,1,0:T(8,128)(2,1)S(1)}, u32[]{:S(2)}, u32[]{:S(2)}) collective-permute-start(bf16[1,528,128]{2,1,0:T(8,128)(2,1)S(1)} %collective-permute-done.10.rest_0_), channel_id=1, source_target_pairs={{0,8},{8,0},{16,24},{24,16},{32,40},{40,32},{48,56},{56,48},{64,72... | collective-permute-start | bytes 405512 | tf_op jit(solution)/shard_map/ppermute | solution.py:40
  61.2 4.1 %attend_third.1 = (f32[8,256]{1,0:T(8,128)S(1)}, f32[8,256]{1,0:T(8,128)S(1)}, f32[512,256]{1,0:T(8,128)S(1)}) custom-call(s32[2]{0:T(128)S(1)} %pad_add_fusion.at_ref, bf16[3,528,128]{2,1,0:T(8,128)(2,1)S(1)} %collective-permute-done.15.rest_0_, bf16[3,528,128]{2,1,0:T(8,128)(2,1)S(1)} %collective-permute-done.16.rest_1_, ...), custom_call_target="tpu_custom_call" | custom-call | flops 134217728 | bytes 135168 | tf_op jit(solution)/shard_map/attend_third/pallas_call | solution.py:256
  65.3 3.7 %attend_and_project.1 = (bf16[4,128,640]{2,1,0:T(8,128)(2,1)S(1)}, bf16[4,128,640]{2,1,0:T(8,128)(2,1)S(1)}, bf16[2,128,640]{2,1,0:T(8,128)(2,1)S(1)}, bf16[2,12...) custom-call(s32[2]{0:T(128)S(1)} %pad_add_fusion.at_ref, ...), custom_call_target="tpu_custom_call" | custom-call | flops 1610612736 | bytes 1622016 | tf_op jit(solution)/shard_map/attend_and_project/pallas_call | solution.py:295
  69.1 1.6 %collective-permute-start.17 = (bf16[2,128,640]{2,1,0:T(8,128)(2,1)S(1)}, bf16[2,128,640]{2,1,0:T(8,128)(2,1)S(1)}, u32[]{:S(2)}, u32[]{:S(2)}) collective-permute-start(bf16[2,128,640]{2,1,0:T(8,128)(2,1)S(1)} %get-tuple-element.64), channel_id=1, source_target_pairs={{0,1},{1,2},{2,3},{3,0},{4,5},{5,6},{6,7},{7,4},{8,9},{9,10},{10,1... | collective-permute-start | bytes 983048 | tf_op jit(solution)/shard_map/ppermute | solution.py:313
  70.7 1.7 %collective-permute-start.20 = (bf16[2,128,640]{2,1,0:T(8,128)(2,1)S(1)}, bf16[2,128,640]{2,1,0:T(8,128)(2,1)S(1)}, u32[]{:S(2)}, u32[]{:S(2)}) collective-permute-start(bf16[2,128,640]{2,1,0:T(8,128)(2,1)S(1)} %get-tuple-element.68), channel_id=1, source_target_pairs={{0,3},{1,0},{2,1},{3,2},{4,7},{5,4},{6,5},{7,6},{8,11},{9,8},{10,9... | collective-permute-start | bytes 983048 | tf_op jit(solution)/shard_map/ppermute | solution.py:313
  72.4 1.8 %collective-permute-start.21 = (bf16[2,128,640]{2,1,0:T(8,128)(2,1)S(1)}, bf16[2,128,640]{2,1,0:T(8,128)(2,1)S(1)}, u32[]{:S(2)}, u32[]{:S(2)}) collective-permute-start(bf16[2,128,640]{2,1,0:T(8,128)(2,1)S(1)} %get-tuple-element.69), channel_id=1, source_target_pairs={{0,2},{1,3},{2,0},{3,1},{4,6},{5,7},{6,4},{7,5},{8,10},{9,11},{10,... | collective-permute-start | bytes 983048 | tf_op jit(solution)/shard_map/ppermute | solution.py:313
  74.2 11.5 %collective-permute-done.18 = bf16[4,128,640]{2,1,0:T(8,128)(2,1)S(1)} collective-permute-done((bf16[4,128,640]{2,1,0:T(8,128)(2,1)S(1)}, bf16[4,128,640]{2,1,0:T(8,128)(2,1)S(1)}, u32[]{:S(2)}, u32[]{:S(2)}) %collective-permute-start.18) | collective-permute-done | bytes 655392 | tf_op jit(solution)/shard_map/ppermute | solution.py:316
  86.0 1.6 %collective-permute-start.19 = (bf16[128,640]{1,0:T(8,128)(2,1)S(1)}, bf16[128,640]{1,0:T(8,128)(2,1)S(1)}, u32[]{:S(2)}, u32[]{:S(2)}) collective-permute-start(bf16[128,640]{1,0:T(8,128)(2,1)S(1)} %get-tuple-element.73), channel_id=1, source_target_pairs={{0,1},{1,2},{2,3},{3,0},{4,5},{5,6},{6,7},{7,4},{8,9},{9,10},{10,1... | collective-permute-start | bytes 491528 | tf_op jit(solution)/shard_map/ppermute | solution.py:313
  87.5 1.7 %collective-permute-start.23 = (bf16[128,640]{1,0:T(8,128)(2,1)S(1)}, bf16[128,640]{1,0:T(8,128)(2,1)S(1)}, u32[]{:S(2)}, u32[]{:S(2)}) collective-permute-start(bf16[128,640]{1,0:T(8,128)(2,1)S(1)} %get-tuple-element.75), channel_id=1, source_target_pairs={{0,3},{1,0},{2,1},{3,2},{4,7},{5,4},{6,5},{7,6},{8,11},{9,8},{10,9... | collective-permute-start | bytes 491528 | tf_op jit(solution)/shard_map/ppermute | solution.py:313
  89.3 1.8 %collective-permute-start.24 = (bf16[128,640]{1,0:T(8,128)(2,1)S(1)}, bf16[128,640]{1,0:T(8,128)(2,1)S(1)}, u32[]{:S(2)}, u32[]{:S(2)}) collective-permute-start(bf16[128,640]{1,0:T(8,128)(2,1)S(1)} %get-tuple-element.74), channel_id=1, source_target_pairs={{0,2},{1,3},{2,0},{3,1},{4,6},{5,7},{6,4},{7,5},{8,10},{9,11},{10,... | collective-permute-start | bytes 491528 | tf_op jit(solution)/shard_map/ppermute | solution.py:313
  91.1 2.1 %collective-permute-done.19 = bf16[128,640]{1,0:T(8,128)(2,1)S(1)} collective-permute-done((bf16[128,640]{1,0:T(8,128)(2,1)S(1)}, bf16[128,640]{1,0:T(8,128)(2,1)S(1)}, u32[]{:S(2)}, u32[]{:S(2)}) %collective-permute-start.19) | collective-permute-done | bytes 163872 | tf_op jit(solution)/shard_map/ppermute | solution.py:313
  94.4 2.7 %collective-permute-done.24 = bf16[128,640]{1,0:T(8,128)(2,1)S(1)} collective-permute-done((bf16[128,640]{1,0:T(8,128)(2,1)S(1)}, bf16[128,640]{1,0:T(8,128)(2,1)S(1)}, u32[]{:S(2)}, u32[]{:S(2)}) %collective-permute-start.24) | collective-permute-done | bytes 163872 | tf_op jit(solution)/shard_map/ppermute | solution.py:313
  (56 shorter events, 16.4 us)
Async XLA Ops:
  1.8 23.0 %collective-permute-start = (bf16[1,528,128]{2,1,0:T(8,128)(2,1)S(1)}, bf16[1,528,128]{2,1,0:T(8,128)(2,1)S(1)}, u32[]{:S(2)}, u32[]{:S(2)}) collective-permute-start(bf16[1,528,128]{2,1,0:T(8,128)(2,1)S(1)} %maximum_bitcast_fusion.own_ref), channel_id=1, source_target_pairs={{0,128},{8,136},{16,144},{24,152},{32,160},{40,168},{48,176},{56,1... | collective-permute-start | bytes 405512 | tf_op jit(solution)/shard_map/ppermute | solution.py:40
  3.2 11.4 %collective-permute-start.3 = (bf16[2,528,128]{2,1,0:T(8,128)(2,1)S(1)}, bf16[2,528,128]{2,1,0:T(8,128)(2,1)S(1)}, u32[]{:S(2)}, u32[]{:S(2)}) collective-permute-start(bf16[2,528,128]{2,1,0:T(8,128)(2,1)S(1)} %pad_maximum_fusion.2), channel_id=1, source_target_pairs={{0,16},{8,56},{16,32},{24,8},{32,48},{40,24},{48,0},{56,40},{64,80... | collective-permute-start | bytes 811016 | tf_op jit(solution)/shard_map/ppermute | solution.py:40
  14.6 13.3 %collective-permute-start.4 = (bf16[1,528,128]{2,1,0:T(8,128)(2,1)S(1)}, bf16[1,528,128]{2,1,0:T(8,128)(2,1)S(1)}, u32[]{:S(2)}, u32[]{:S(2)}) collective-permute-start(bf16[1,528,128]{2,1,0:T(8,128)(2,1)S(1)} %slice.36), channel_id=1, source_target_pairs={{0,16},{8,56},{16,32},{24,8},{32,48},{40,24},{48,0},{56,40},{64,80... | collective-permute-start | bytes 405512 | tf_op jit(solution)/shard_map/ppermute | solution.py:40
  23.5 8.5 %collective-permute-start.6 = (bf16[2,528,128]{2,1,0:T(8,128)(2,1)S(1)}, bf16[2,528,128]{2,1,0:T(8,128)(2,1)S(1)}, u32[]{:S(2)}, u32[]{:S(2)}) collective-permute-start(bf16[2,528,128]{2,1,0:T(8,128)(2,1)S(1)} %pad_maximum_fusion.2), channel_id=1, source_target_pairs={{0,64},{8,200},{16,80},{24,216},{32,96},{40,232},{48,112},{56,248}... | collective-permute-start | bytes 811016 | tf_op jit(solution)/shard_map/ppermute | solution.py:40
  24.8 6.4 %collective-permute-start.1 = (bf16[1,528,128]{2,1,0:T(8,128)(2,1)S(1)}, bf16[1,528,128]{2,1,0:T(8,128)(2,1)S(1)}, u32[]{:S(2)}, u32[]{:S(2)}) collective-permute-start(bf16[1,528,128]{2,1,0:T(8,128)(2,1)S(1)} %collective-permute-done.rest_7_), channel_id=1, source_target_pairs={{0,8},{8,0},{16,24},{24,16},{32,40},{40,32},{48,56},{56,48},{64,72... | collective-permute-start | bytes 405512 | tf_op jit(solution)/shard_map/ppermute | solution.py:40
  27.1 11.2 %collective-permute-start.7 = (bf16[2,528,128]{2,1,0:T(8,128)(2,1)S(1)}, bf16[2,528,128]{2,1,0:T(8,128)(2,1)S(1)}, u32[]{:S(2)}, u32[]{:S(2)}) collective-permute-start(bf16[2,528,128]{2,1,0:T(8,128)(2,1)S(1)} %collective-permute-done.3.rest_1_), channel_id=1, source_target_pairs={{0,8},{8,0},{16,24},{24,16},{32,40},{40,32},{48,56},{56,48},{64,72... | collective-permute-start | bytes 811016 | tf_op jit(solution)/shard_map/ppermute | solution.py:40
  28.6 18.9 %collective-permute-start.11 = (bf16[3,528,128]{2,1,0:T(8,128)(2,1)}, bf16[3,528,128]{2,1,0:T(8,128)(2,1)S(1)}, u32[]{:S(2)}, u32[]{:S(2)}) collective-permute-start(bf16[3,528,128]{2,1,0:T(8,128)(2,1)} %constant_dynamic-update-slice_fusion), channel_id=1, source_target_pairs={{0,64},{8,72},{16,80},{24,88},{32,96},{40,104},{48,112},{56,120},{... | collective-permute-start | bytes 1216520 | tf_op jit(solution)/shard_map/ppermute | solution.py:40
  29.9 17.7 %collective-permute-start.12 = (bf16[3,528,128]{2,1,0:T(8,128)(2,1)}, bf16[3,528,128]{2,1,0:T(8,128)(2,1)S(1)}, u32[]{:S(2)}, u32[]{:S(2)}) collective-permute-start(bf16[3,528,128]{2,1,0:T(8,128)(2,1)} %constant_dynamic-update-slice_fusion), channel_id=1, source_target_pairs={{0,192},{8,200},{16,208},{24,216},{32,224},{40,232},{48,240},{56,2... | collective-permute-start | bytes 1216520 | tf_op jit(solution)/shard_map/ppermute | solution.py:40
  31.9 9.5 %collective-permute-start.9 = (bf16[2,528,128]{2,1,0:T(8,128)(2,1)S(1)}, bf16[2,528,128]{2,1,0:T(8,128)(2,1)S(1)}, u32[]{:S(2)}, u32[]{:S(2)}) collective-permute-start(bf16[2,528,128]{2,1,0:T(8,128)(2,1)S(1)} %collective-permute-done.6.rest_3_), channel_id=1, source_target_pairs={{0,8},{8,0},{16,24},{24,16},{32,40},{40,32},{48,56},{56,48},{64,72... | collective-permute-start | bytes 811016 | tf_op jit(solution)/shard_map/ppermute | solution.py:40
  34.3 13.2 %collective-permute-start.5 = (bf16[2,528,128]{2,1,0:T(8,128)(2,1)}, bf16[2,528,128]{2,1,0:T(8,128)(2,1)S(1)}, u32[]{:S(2)}, u32[]{:S(2)}) collective-permute-start(bf16[2,528,128]{2,1,0:T(8,128)(2,1)} %pad_maximum_fusion.1), channel_id=1, source_target_pairs={{128,144},{136,184},{144,160},{152,136},{160,176},{168,152},{176,1... | collective-permute-start | bytes 811016 | tf_op jit(solution)/shard_map/ppermute | solution.py:40
  38.3 3.1 %collective-permute-start.8 = (bf16[1,528,128]{2,1,0:T(8,128)(2,1)S(1)}, bf16[1,528,128]{2,1,0:T(8,128)(2,1)S(1)}, u32[]{:S(2)}, u32[]{:S(2)}) collective-permute-start(bf16[1,528,128]{2,1,0:T(8,128)(2,1)S(1)} %collective-permute-done.4.rest_2_), channel_id=1, source_target_pairs={{0,8},{8,0},{16,24},{24,16},{32,40},{40,32},{48,56},{56,48},{64,72... | collective-permute-start | bytes 405512 | tf_op jit(solution)/shard_map/ppermute | solution.py:40
  47.5 4.3 %collective-permute-start.13 = (bf16[2,528,128]{2,1,0:T(8,128)(2,1)S(1)}, bf16[2,528,128]{2,1,0:T(8,128)(2,1)S(1)}, u32[]{:S(2)}, u32[]{:S(2)}) collective-permute-start(bf16[2,528,128]{2,1,0:T(8,128)(2,1)S(1)} %collective-permute-done.5.rest_2_), channel_id=1, source_target_pairs={{0,8},{8,0},{16,24},{24,16},{32,40},{40,32},{48,56},{56,48},{64,72... | collective-permute-start | bytes 811016 | tf_op jit(solution)/shard_map/ppermute | solution.py:40
  47.5 13.6 %collective-permute-start.15 = (bf16[3,528,128]{2,1,0:T(8,128)(2,1)S(1)}, bf16[3,528,128]{2,1,0:T(8,128)(2,1)S(1)}, u32[]{:S(2)}, u32[]{:S(2)}) collective-permute-start(bf16[3,528,128]{2,1,0:T(8,128)(2,1)S(1)} %collective-permute-done.11.rest_0_), channel_id=1, source_target_pairs={{0,8},{8,0},{16,24},{24,16},{32,40},{40,32},{48,56},{56,48},{64,72... | collective-permute-start | bytes 1216520 | tf_op jit(solution)/shard_map/ppermute | solution.py:40
  48.0 13.1 %collective-permute-start.16 = (bf16[3,528,128]{2,1,0:T(8,128)(2,1)S(1)}, bf16[3,528,128]{2,1,0:T(8,128)(2,1)S(1)}, u32[]{:S(2)}, u32[]{:S(2)}) collective-permute-start(bf16[3,528,128]{2,1,0:T(8,128)(2,1)S(1)} %collective-permute-done.12.rest_1_), channel_id=1, source_target_pairs={{0,8},{8,0},{16,24},{24,16},{32,40},{40,32},{48,56},{56,48},{64,72... | collective-permute-start | bytes 1216520 | tf_op jit(solution)/shard_map/ppermute | solution.py:40
  48.2 10.9 %collective-permute-start.10 = (bf16[1,528,128]{2,1,0:T(8,128)(2,1)S(1)}, bf16[1,528,128]{2,1,0:T(8,128)(2,1)S(1)}, u32[]{:S(2)}, u32[]{:S(2)}) collective-permute-start(bf16[1,528,128]{2,1,0:T(8,128)(2,1)S(1)} %slice.29), channel_id=1, source_target_pairs={{128,144},{136,184},{144,160},{152,136},{160,176},{168,152},{176,1... | collective-permute-start | bytes 405512 | tf_op jit(solution)/shard_map/ppermute | solution.py:40
  59.0 6.3 %collective-permute-start.14 = (bf16[1,528,128]{2,1,0:T(8,128)(2,1)S(1)}, bf16[1,528,128]{2,1,0:T(8,128)(2,1)S(1)}, u32[]{:S(2)}, u32[]{:S(2)}) collective-permute-start(bf16[1,528,128]{2,1,0:T(8,128)(2,1)S(1)} %collective-permute-done.10.rest_0_), channel_id=1, source_target_pairs={{0,8},{8,0},{16,24},{24,16},{32,40},{40,32},{48,56},{56,48},{64,72... | collective-permute-start | bytes 405512 | tf_op jit(solution)/shard_map/ppermute | solution.py:40
  69.0 16.8 %collective-permute-start.18 = (bf16[4,128,640]{2,1,0:T(8,128)(2,1)S(1)}, bf16[4,128,640]{2,1,0:T(8,128)(2,1)S(1)}, u32[]{:S(2)}, u32[]{:S(2)}) collective-permute-start(bf16[4,128,640]{2,1,0:T(8,128)(2,1)S(1)} %get-tuple-element.66), channel_id=1, source_target_pairs={{0,4},{1,5},{2,6},{3,7},{4,0},{5,1},{6,2},{7,3},{8,12},{9,13},{10,... | collective-permute-start | bytes 1966088 | tf_op jit(solution)/shard_map/ppermute | solution.py:316
  69.1 20.2 %collective-permute-start.17 = (bf16[2,128,640]{2,1,0:T(8,128)(2,1)S(1)}, bf16[2,128,640]{2,1,0:T(8,128)(2,1)S(1)}, u32[]{:S(2)}, u32[]{:S(2)}) collective-permute-start(bf16[2,128,640]{2,1,0:T(8,128)(2,1)S(1)} %get-tuple-element.64), channel_id=1, source_target_pairs={{0,1},{1,2},{2,3},{3,0},{4,5},{5,6},{6,7},{7,4},{8,9},{9,10},{10,1... | collective-permute-start | bytes 983048 | tf_op jit(solution)/shard_map/ppermute | solution.py:313
  70.7 22.5 %collective-permute-start.20 = (bf16[2,128,640]{2,1,0:T(8,128)(2,1)S(1)}, bf16[2,128,640]{2,1,0:T(8,128)(2,1)S(1)}, u32[]{:S(2)}, u32[]{:S(2)}) collective-permute-start(bf16[2,128,640]{2,1,0:T(8,128)(2,1)S(1)} %get-tuple-element.68), channel_id=1, source_target_pairs={{0,3},{1,0},{2,1},{3,2},{4,7},{5,4},{6,5},{7,6},{8,11},{9,8},{10,9... | collective-permute-start | bytes 983048 | tf_op jit(solution)/shard_map/ppermute | solution.py:313
  72.4 20.7 %collective-permute-start.21 = (bf16[2,128,640]{2,1,0:T(8,128)(2,1)S(1)}, bf16[2,128,640]{2,1,0:T(8,128)(2,1)S(1)}, u32[]{:S(2)}, u32[]{:S(2)}) collective-permute-start(bf16[2,128,640]{2,1,0:T(8,128)(2,1)S(1)} %get-tuple-element.69), channel_id=1, source_target_pairs={{0,2},{1,3},{2,0},{3,1},{4,6},{5,7},{6,4},{7,5},{8,10},{9,11},{10,... | collective-permute-start | bytes 983048 | tf_op jit(solution)/shard_map/ppermute | solution.py:313
  86.0 7.2 %collective-permute-start.19 = (bf16[128,640]{1,0:T(8,128)(2,1)S(1)}, bf16[128,640]{1,0:T(8,128)(2,1)S(1)}, u32[]{:S(2)}, u32[]{:S(2)}) collective-permute-start(bf16[128,640]{1,0:T(8,128)(2,1)S(1)} %get-tuple-element.73), channel_id=1, source_target_pairs={{0,1},{1,2},{2,3},{3,0},{4,5},{5,6},{6,7},{7,4},{8,9},{9,10},{10,1... | collective-permute-start | bytes 491528 | tf_op jit(solution)/shard_map/ppermute | solution.py:313
  87.5 6.8 %collective-permute-start.23 = (bf16[128,640]{1,0:T(8,128)(2,1)S(1)}, bf16[128,640]{1,0:T(8,128)(2,1)S(1)}, u32[]{:S(2)}, u32[]{:S(2)}) collective-permute-start(bf16[128,640]{1,0:T(8,128)(2,1)S(1)} %get-tuple-element.75), channel_id=1, source_target_pairs={{0,3},{1,0},{2,1},{3,2},{4,7},{5,4},{6,5},{7,6},{8,11},{9,8},{10,9... | collective-permute-start | bytes 491528 | tf_op jit(solution)/shard_map/ppermute | solution.py:313
  89.3 7.8 %collective-permute-start.24 = (bf16[128,640]{1,0:T(8,128)(2,1)S(1)}, bf16[128,640]{1,0:T(8,128)(2,1)S(1)}, u32[]{:S(2)}, u32[]{:S(2)}) collective-permute-start(bf16[128,640]{1,0:T(8,128)(2,1)S(1)} %get-tuple-element.74), channel_id=1, source_target_pairs={{0,2},{1,3},{2,0},{3,1},{4,6},{5,7},{6,4},{7,5},{8,10},{9,11},{10,... | collective-permute-start | bytes 491528 | tf_op jit(solution)/shard_map/ppermute | solution.py:313
  93.3 5.4 %collective-permute-start.22 = (bf16[128,640]{1,0:T(8,128)(2,1)S(1)}, bf16[128,640]{1,0:T(8,128)(2,1)S(1)}, u32[]{:S(2)}, u32[]{:S(2)}) collective-permute-start(bf16[128,640]{1,0:T(8,128)(2,1)S(1)} %fusion.20), channel_id=1, source_target_pairs={{0,4},{1,5},{2,6},{3,7},{4,0},{5,1},{6,2},{7,3},{8,12},{9,13},{10,... | collective-permute-start | bytes 491528 | tf_op jit(solution)/shard_map/ppermute | solution.py:316
  (3 other events, 27.8 us)

commit v5 on v4

--- a/solution.py
+++ b/solution.py
@@ -1,4 +1,5 @@
 import functools
+import itertools
 
 import jax
 import jax.numpy as jnp
@@ -11,8 +12,8 @@
 HEAD_DIM = 128
 BLOCK = 256
 PACK = 2 * BLOCK + 16
+CHAINS = ((slice(0, 96), (1, 3, 4)), (slice(96, 176), (3, 4, 1)), (slice(176, 256), (4, 1, 3)))
 REACH = 24
-HALF = BLOCK // 2
 COLS = 640
 FLOOR = -1e30
 HIDDEN = -2e30
@@ -78,9 +79,10 @@
     return [[(y + 2, z, c)], [(y + 2, z + d, c), (y + 2, z + d, 1 - c)], [(y + 2, z + 2, c)]]
 
 
-def later_slots(y, z, c):
+def next_slots(y, z, c):
     d = 2 * c - 1
-    return [[(y + e, z + d, c), (y + e, z + d, 1 - c), (y + e, z + 2, c)] for e in (-1, 1)]
+    near = [[(y + e, z + d, c), (y + e, z + d, 1 - c)] for e in (-1, 1)]
+    return near + [[(y + e, z + 2, c)] for e in (-1, 1)]
 
 
 def attend_blocks(kv_ref, places, diagonal, q_ref, hot_ref, m_ref, l_ref, acc_ref):
@@ -164,7 +166,7 @@
 
 
 def last_kernel(slots, n, at_ref, *rest):
-    pieces, (q_ref, hot_ref, m_in, l_in, acc_in, w_ref, b1, b0, a1, a3, a2, a0) = rest[:n], rest[n : n + 12]
+    pieces, (q_ref, hot_ref, m_in, l_in, acc_in, w_ref), outs = rest[:n], rest[n : n + 6], rest[n + 6 : n + 12]
     m_ref, l_ref, acc_ref, all_ref, order_ref, att_ref = rest[n + 12 :]
     m_ref[...] = m_in[...]
     l_ref[...] = l_in[...]
@@ -173,21 +175,17 @@
     for h in range(4):
         rows = slice(h * HEAD_DIM, (h + 1) * HEAD_DIM)
         att_ref[:, rows] = jnp.transpose(acc_ref[rows, :] / l_ref[h : h + 1, :]).astype(BF16)
-    b_to, a_to = (b0, b1), (a0, a1, a2, a3)
     section = at_ref[1]
-    for dz in range(2):
-        for dx in range(4):
-            to = (section // 4 + dz) % 2 * 4 + (section + dx) % 4
-            cols = pl.ds(pl.multiple_of(to * COLS, 128), COLS)
-            part = jnp.dot(att_ref[...], w_ref[:, cols], preferred_element_type=F32).astype(BF16)
-            a_to[dx][dz] = part[:HALF]
-            b_to[dz][dx] = part[HALF:]
-
-
-def fetch_kernel(from_ref, to_ref, sem):
-    copy = pltpu.make_async_copy(from_ref, to_ref, sem)
-    copy.start()
-    copy.wait()
+    for sides in itertools.product((0, 1), repeat=3):
+        away = 0
+        for step, side in zip(CHAINS[0][1], sides):
+            away ^= step * side
+        cols = pl.ds(pl.multiple_of((section ^ away) * COLS, 128), COLS)
+        part = jnp.dot(att_ref[...], w_ref[:, cols], preferred_element_type=F32).astype(BF16)
+        crossed = dict(zip(CHAINS[0][1], sides))
+        for i, (rows, order) in enumerate(CHAINS):
+            first, second, third = (crossed[step] for step in order)
+            outs[2 * i + 1 - first][2 * second + third] = part[rows]
 
 
 VMEM = pl.BlockSpec(memory_space=pltpu.VMEM)
@@ -221,7 +219,7 @@
     pair = jnp.concatenate([own, other], axis=0)
     z_near = along_z(pair)
     y_near = along_y(pair)
-    z_far = along_z(z_near[:1])
+    far_other = swap_cores(y_far)
 
     widened = hidden.astype(F32)
     normed = (widened * lax.rsqrt(jnp.mean(widened * widened, axis=-1, keepdims=True) + 1e-06)).astype(BF16)
@@ -229,21 +227,14 @@
         lax.dot_general(w_query, normed, (((0,), (1,)), ((), ())), preferred_element_type=F32) * HEAD_DIM ** (-0.5)
     ).astype(BF16)
     hot = (jnp.arange(HEAD_DIM, dtype=jnp.int32)[:, None] == segment[None, :]).astype(BF16)
-    w_held = pl.pallas_call(
-        fetch_kernel,
-        out_shape=jax.ShapeDtypeStruct(w_out.shape, w_out.dtype),
-        in_specs=[pl.BlockSpec(memory_space=pltpu.HBM)],
-        out_specs=VMEM,
-        scratch_shapes=[pltpu.SemaphoreType.DMA],
-        compiler_params=LIMIT,
-        name="fetch_w_out",
-    )(w_out)
-    q_t, w_held = lax.optimization_barrier((q_t, w_held))
-
-    row = jnp.concatenate([z_near, z_far], axis=0)
-    up = up_y(row)
-    around = round_y(row)
-    far_other = swap_cores(y_far)
+
+    (z_near, y_near, far_other), q_t = lax.optimization_barrier(((z_near, y_near, far_other), q_t))
+    z_far = along_z(z_near[:1])
+    up_near = up_y(z_near)
+    around_near = round_y(z_near)
+
+    up_far = up_y(z_far)
+    around_far = round_y(z_far)
     far_pair, _ = lax.optimization_barrier((jnp.concatenate([y_far, far_other], axis=0), z_far))
     far_near = along_z(far_pair, 2)
 
@@ -269,10 +260,10 @@
         return [[(y, z, 1 - c)]] + mine + theirs + far_slots(y, z, c)[:1] + far_slots(y, z, 1 - c)[:1]
 
     def slots_2(y, z, c):
-        return later_slots(y, z, c) + far_slots(y, z, c)[1:2] + far_slots(y, z, 1 - c)[1:2]
+        return next_slots(y, z, c) + far_slots(y, z, c)[1:2] + far_slots(y, z, 1 - c)[1:2]
 
     def slots_3(y, z, c):
-        return later_slots(y, z, 1 - c)
+        return next_slots(y, z, 1 - c)
 
     def slots_4(y, z, c):
         return far_slots(y, z, c)[2:] + far_slots(y, z, 1 - c)[2:]
@@ -284,17 +275,20 @@
     far_near, state = lax.optimization_barrier((far_near, state))
     far_far = along_z(far_near[:1], 2)
     far_near_other = swap_cores(far_near)
-    (up, around), state = lax.optimization_barrier(((up, around), state))
-    up_other, around_other = swap_cores(up), swap_cores(around)
-    state = attend(more_kernel, slots_2, 10, [up, around, far_near, far_near_other], state, "attend_next")
+    nexts = (up_near, around_near, up_far, around_far)
+    nexts, state = lax.optimization_barrier((nexts, state))
+    others = [swap_cores(t) for t in nexts]
+    state = attend(more_kernel, slots_2, 10, [*nexts, far_near, far_near_other], state, "attend_next")
     far_far, state = lax.optimization_barrier((far_far, state))
     far_far_other = swap_cores(far_far)
-    state = attend(more_kernel, slots_3, 6, [up_other, around_other], state, "attend_third")
-
-    part = lambda n: jax.ShapeDtypeStruct((n, HALF, COLS), BF16)
-    b1, b0, a1, a3, a2, a0 = pl.pallas_call(
+    state = attend(more_kernel, slots_3, 6, others, state, "attend_third")
+
+    out_shape = []
+    for rows, _ in CHAINS:
+        out_shape += [jax.ShapeDtypeStruct((4, rows.stop - rows.start, COLS), BF16)] * 2
+    outs = pl.pallas_call(
         functools.partial(last_kernel, slots_4, 2),
-        out_shape=(part(4), part(4), part(2), part(2), part(2), part(2)),
+        out_shape=tuple(out_shape),
         in_specs=[SMEM] + [VMEM] * 8,
         out_specs=(VMEM,) * 6,
         scratch_shapes=[
@@ -307,24 +301,18 @@
         compiler_params=LIMIT,
         cost_estimate=cost(12),
         name="attend_and_project",
-    )(at, far_far, far_far_other, q_t, hot, *state, w_held)
-
-    def send_x(t, k):
-        return lax.ppermute(t, "section", [(g * 4 + x, g * 4 + (x + k) % 4) for g in range(2) for x in range(4)])
-
-    def send_z(t):
-        return lax.ppermute(t, "section", [(g * 4 + x, (1 - g) * 4 + x) for g in range(2) for x in range(4)])
-
-    b_in = send_z(b1)
-    a_in = [send_x(a, k) for a, k in ((a1, 1), (a3, 3), (a2, 2))]
-    b_sum = b0.astype(F32) + b_in.astype(F32)
-    b_out = [send_x(b_sum[k].astype(BF16), k) for k in (1, 3, 2)]
-    a_in[0], b_out[0] = lax.optimization_barrier((a_in[0], b_out[0]))
-    a_sum = a0.astype(F32) + a_in[0].astype(F32) + a_in[1].astype(F32) + a_in[2].astype(F32)
-    a_out = send_z(a_sum[1].astype(BF16))
-    a = a_sum[0] + a_out.astype(F32)
-    b = b_sum[0] + b_out[0].astype(F32) + b_out[1].astype(F32) + b_out[2].astype(F32)
-    return jnp.concatenate([a, b], axis=0).astype(BF16)
+    )(at, far_far, far_far_other, q_t, hot, *state, w_out)
+
+    def exchange(x, step):
+        return lax.ppermute(x, "section", [(i, i ^ step) for i in range(8)])
+
+    mixed = []
+    for i, (_, (first, second, third)) in enumerate(CHAINS):
+        sent, kept = outs[2 * i], outs[2 * i + 1]
+        four = kept.astype(F32) + exchange(sent, first).astype(F32)
+        two = four[:2] + exchange(four[2:].astype(BF16), second).astype(F32)
+        mixed.append(two[0] + exchange(two[1].astype(BF16), third).astype(F32))
+    return jnp.concatenate(mixed, axis=0).astype(BF16)
 
 
 def solution(mesh):

time: 99.9 us -> 98.7 us (0.988)
  local copies, waits for them, and re-layouts: 3.95 us -> 2.64 us
    ppermute x8 -> x9, waiting for transfers between devices: 18.2 us -> 20.8 us  [exchange(): return lax.ppermute(x, 'section', [(i, i ^ step) for i in range(8)])]
    ppermute x17 -> x21, waiting for transfers between devices: 7.78 us -> 5.84 us  [move(): return lax.ppermute(x, 'ctx', ctx_pairs(step))]
    ppermute x17 -> x21, starting transfers between devices: 27.2 us -> 28.7 us  [move(): return lax.ppermute(x, 'ctx', ctx_pairs(step))]
    ppermute x8 -> x9, starting transfers between devices: 11 us -> 10.2 us  [exchange(): return lax.ppermute(x, 'section', [(i, i ^ step) for i in range(8)])]
    unnamed x5 -> x4, local copies, waits for them, and re-layouts: 3.2 us -> 2.49 us
    pallas_call x2 -> x1, Pallas kernels: 4.03 us -> 3.67 us  [per_device(): pl.pallas_call(functools.partial(last_kernel, slots_4, 2), out_shape=tupl...]
  transfers between devices with their start and end apart: 25 -> 30, of which waited for: 8 -> 10; matrix products, arithmetic and copies ran while one was open for 11% -> 9% of each run, Pallas kernels for 16% -> 15%
where the time goes in v5:
time: 98.7 us; the launch traced here: 98.4 us
  starting transfers between devices  38.9 us (39%)
  waiting for transfers between devices  26.6 us (27%)
  Pallas kernels  18.8 us (19%)
  matrix products  5.57 us (6%)
  other arithmetic  5.44 us (6%)
  local copies, waits for them, and re-layouts  2.64 us (3%)
    ppermute x21, starting transfers between devices, move(): return lax.ppermute(x, 'ctx', ctx_pairs(step))  28.7 us
    ppermute x9, waiting for transfers between devices, exchange(): return lax.ppermute(x, 'section', [(i, i ^ step) for i in range(8)])  20.8 us
    pallas_call x3, Pallas kernels, attend(): pl.pallas_call(functools.partial(kernel, slots, len(pieces) - (not state)...  15.2 us
    ppermute x9, starting transfers between devices, exchange(): return lax.ppermute(x, 'section', [(i, i ^ step) for i in range(8)])  10.2 us
    ppermute x21, waiting for transfers between devices, move(): return lax.ppermute(x, 'ctx', ctx_pairs(step))  5.84 us
    dot_general x1, matrix products, per_device(): lax.dot_general(w_query, normed, (((0,), (1,)), ((), ())), preferred_elem...  5.57 us
    pallas_call x1, Pallas kernels, per_device(): pl.pallas_call(functools.partial(last_kernel, slots_4, 2), out_shape=tupl...  3.67 us
    unnamed x4, local copies, waits for them, and re-layouts  2.49 us
  transfers between devices with their start and end apart: 30, of which 10 were waited for; matrix products, arithmetic and copies ran while one was open for 9% of the time, Pallas kernels for 15%

profile of v5, /device:TPU:24, one launch (start us, length us, event | category | flops | bytes accessed | tf_op | source)
XLA Modules:
  0.0 98.4 jit_solution(1584149208210929558)
XLA Ops:
  3.1 2.3 %fusion = f32[256]{0:T(256)S(1)} fusion(bf16[256,5120]{1,0:T(8,128)(2,1)} %param.6), kind=kLoop, calls=%fused_computation.2 | loop fusion | flops 3931904 | bytes 2622464 | tf_op jit(solution)/shard_map/reduce_sum | solution.py:225
  5.5 3.3 %collective-permute-start.2 = (bf16[2,528,128]{2,1,0:T(8,128)(2,1)S(1)}, bf16[2,528,128]{2,1,0:T(8,128)(2,1)S(1)}, u32[]{:S(2)}, u32[]{:S(2)}) collective-permute-start(bf16[2,528,128]{2,1,0:T(8,128)(2,1)S(1)} %pad_maximum_fusion.1), channel_id=1, source_target_pairs={{0,16},{8,56},{16,32},{24,8},{32,48},{40,24},{48,0},{56,40},{64,80... | collective-permute-start | bytes 811016 | tf_op jit(solution)/shard_map/ppermute | solution.py:41
  11.2 2.3 %collective-permute-start.4 = (bf16[1,528,128]{2,1,0:T(8,128)(2,1)S(1)}, bf16[1,528,128]{2,1,0:T(8,128)(2,1)S(1)}, u32[]{:S(2)}, u32[]{:S(2)}) collective-permute-start(bf16[1,528,128]{2,1,0:T(8,128)(2,1)S(1)} %collective-permute-done.rest_7_), channel_id=1, source_target_pairs={{0,8},{8,0},{16,24},{24,16},{32,40},{40,32},{48,56},{56,48},{64,72... | collective-permute-start | bytes 405512 | tf_op jit(solution)/shard_map/ppermute | solution.py:41
  13.5 5.6 %fusion.11.rest_9_.rest_6_.rest_4_.rest_2_ = bf16[512,256]{1,0:T(8,128)(2,1)S(1)} fusion(bf16[5120,512]{1,0:T(8,128)(2,1)} %param.10, bf16[256,5120]{1,0:T(8,128)(2,1)} %param.6, f32[256]{0:T(256)S(1)} %add_rsqrt_fusion), kind=kOutput, calls=%fused_computation.8 | convolution fusion | flops 1346371584 | bytes 8127488 | tf_op jit(solution)/shard_map/dot_general | solution.py:227
  24.4 1.8 %collective-permute-start.9 = (bf16[2,528,128]{2,1,0:T(8,128)(2,1)S(1)}, bf16[2,528,128]{2,1,0:T(8,128)(2,1)S(1)}, u32[]{:S(2)}, u32[]{:S(2)}) collective-permute-start(bf16[2,528,128]{2,1,0:T(8,128)(2,1)S(1)} %collective-permute-done.3.rest_3_), channel_id=1, source_target_pairs={{0,8},{8,0},{16,24},{24,16},{32,40},{40,32},{48,56},{56,48},{64,72... | collective-permute-start | bytes 811016 | tf_op jit(solution)/shard_map/ppermute | solution.py:41
  26.2 2.2 %collective-permute-done.5.rest_2_ = bf16[1,528,128]{2,1,0:T(8,128)(2,1)S(1)} collective-permute-done((bf16[1,528,128]{2,1,0:T(8,128)(2,1)S(1)}, bf16[1,528,128]{2,1,0:T(8,128)(2,1)S(1)}, u32[]{:S(2)}, u32[]{:S(2)}) %collective-permute-start.5) | collective-permute-done | bytes 135200 | tf_op jit(solution)/shard_map/ppermute | solution.py:41
  28.4 2.1 %collective-permute-start.6 = (bf16[2,528,128]{2,1,0:T(8,128)(2,1)S(1)}, bf16[2,528,128]{2,1,0:T(8,128)(2,1)S(1)}, u32[]{:S(2)}, u32[]{:S(2)}) collective-permute-start(bf16[2,528,128]{2,1,0:T(8,128)(2,1)S(1)} %pad_maximum_fusion.2), channel_id=1, source_target_pairs={{128,144},{136,184},{144,160},{152,136},{160,176},{168,152},{176,1... | collective-permute-start | bytes 811016 | tf_op jit(solution)/shard_map/ppermute | solution.py:41
  30.6 2.4 %collective-permute-start.8 = (bf16[1,528,128]{2,1,0:T(8,128)(2,1)S(1)}, bf16[1,528,128]{2,1,0:T(8,128)(2,1)S(1)}, u32[]{:S(2)}, u32[]{:S(2)}) collective-permute-start(bf16[1,528,128]{2,1,0:T(8,128)(2,1)S(1)} %collective-permute-done.5.rest_2_), channel_id=1, source_target_pairs={{0,8},{8,0},{16,24},{24,16},{32,40},{40,32},{48,56},{56,48},{64,72... | collective-permute-start | bytes 405512 | tf_op jit(solution)/shard_map/ppermute | solution.py:41
  35.6 4.6 %attend_first.1 = (f32[8,256]{1,0:T(8,128)S(1)}, f32[8,256]{1,0:T(8,128)S(1)}, f32[512,256]{1,0:T(8,128)S(1)}) custom-call(s32[2]{0:T(128)S(1)} %pad_add_fusion.at_ref, bf16[1,528,128]{2,1,0:T(8,128)(2,1)S(1)} %maximum_bitcast_fusion.own_ref, bf16[1,528,128]{2,1,0:T(8,128)(2,1)S(1)} %collective-permute-done.1.rest_0_, ...), custom_call_target="tpu_custom_call" | custom-call | flops 134217728 | bytes 135168 | tf_op jit(solution)/shard_map/attend_first/pallas_call | solution.py:247
  40.4 2.5 %collective-permute-done.14.rest_3_ = bf16[1,528,128]{2,1,0:T(8,128)(2,1)S(1)} collective-permute-done((bf16[1,528,128]{2,1,0:T(8,128)(2,1)S(1)}, bf16[1,528,128]{2,1,0:T(8,128)(2,1)S(1)}, u32[]{:S(2)}, u32[]{:S(2)}) %collective-permute-start.14) | collective-permute-done | bytes 135200 | tf_op jit(solution)/shard_map/ppermute | solution.py:41
  43.5 4.7 %collective-permute-start.10 = (bf16[1,528,128]{2,1,0:T(8,128)(2,1)S(1)}, bf16[1,528,128]{2,1,0:T(8,128)(2,1)S(1)}, u32[]{:S(2)}, u32[]{:S(2)}) collective-permute-start(bf16[1,528,128]{2,1,0:T(8,128)(2,1)S(1)} %slice.49), channel_id=1, source_target_pairs={{128,144},{136,184},{144,160},{152,136},{160,176},{168,152},{176,1... | collective-permute-start | bytes 405512 | tf_op jit(solution)/shard_map/ppermute | solution.py:41
  48.8 6.4 %attend_next.1 = (f32[8,256]{1,0:T(8,128)S(1)}, f32[8,256]{1,0:T(8,128)S(1)}, f32[512,256]{1,0:T(8,128)S(1)}) custom-call(s32[2]{0:T(128)S(1)} %pad_add_fusion.at_ref, bf16[2,528,128]{2,1,0:T(8,128)(2,1)S(1)} %collective-permute-done.11.rest_0_, bf16[2,528,128]{2,1,0:T(8,128)(2,1)S(1)} %collective-permute-done.12.rest_1_, ...), custom_call_target="tpu_custom_call" | custom-call | flops 134217728 | bytes 135168 | tf_op jit(solution)/shard_map/attend_next/pallas_call | solution.py:247
  55.7 4.1 %attend_third.1 = (f32[8,256]{1,0:T(8,128)S(1)}, f32[8,256]{1,0:T(8,128)S(1)}, f32[512,256]{1,0:T(8,128)S(1)}) custom-call(s32[2]{0:T(128)S(1)} %pad_add_fusion.at_ref, bf16[2,528,128]{2,1,0:T(8,128)(2,1)S(1)} %collective-permute-done.17.rest_0_, bf16[2,528,128]{2,1,0:T(8,128)(2,1)S(1)} %collective-permute-done.18.rest_1_, ...), custom_call_target="tpu_custom_call" | custom-call | flops 134217728 | bytes 135168 | tf_op jit(solution)/shard_map/attend_third/pallas_call | solution.py:247
  59.8 2.5 %copy-done = bf16[512,5120]{1,0:T(8,128)(2,1)S(1)} copy-done((bf16[512,5120]{1,0:T(8,128)(2,1)S(1)}, bf16[512,5120]{1,0:T(8,128)(2,1)}, u32[]{:S(2)}) %copy-start) | copy-done | bytes 5242904
  62.2 3.7 %attend_and_project.1 = (bf16[4,96,640]{2,1,0:T(8,128)(2,1)S(1)}, bf16[4,96,640]{2,1,0:T(8,128)(2,1)S(1)}, bf16[4,80,640]{2,1,0:T(8,128)(2,1)S(1)}, bf16[4,80,64...) custom-call(s32[2]{0:T(128)S(1)} %pad_add_fusion.at_ref, ...), custom_call_target="tpu_custom_call" | custom-call | flops 1610612736 | bytes 1622016 | tf_op jit(solution)/shard_map/attend_and_project/pallas_call | solution.py:289
  65.9 2.9 %collective-permute-start.24 = (bf16[4,80,640]{2,1,0:T(8,128)(2,1)S(1)}, bf16[4,80,640]{2,1,0:T(8,128)(2,1)S(1)}, u32[]{:S(2)}, u32[]{:S(2)}) collective-permute-start(bf16[4,80,640]{2,1,0:T(8,128)(2,1)S(1)} %get-tuple-element.72), channel_id=1, source_target_pairs={{0,3},{1,2},{2,1},{3,0},{4,7},{5,6},{6,5},{7,4},{8,11},{9,10},{10,... | collective-permute-start | bytes 1228808 | tf_op jit(solution)/shard_map/ppermute | solution.py:307
  68.8 1.8 %collective-permute-start.27 = (bf16[4,80,640]{2,1,0:T(8,128)(2,1)S(1)}, bf16[4,80,640]{2,1,0:T(8,128)(2,1)S(1)}, u32[]{:S(2)}, u32[]{:S(2)}) collective-permute-start(bf16[4,80,640]{2,1,0:T(8,128)(2,1)S(1)} %get-tuple-element.74), channel_id=1, source_target_pairs={{0,4},{1,5},{2,6},{3,7},{4,0},{5,1},{6,2},{7,3},{8,12},{9,13},{10,... | collective-permute-start | bytes 1228808 | tf_op jit(solution)/shard_map/ppermute | solution.py:307
  70.8 8.0 %collective-permute-done.24 = bf16[4,80,640]{2,1,0:T(8,128)(2,1)S(1)} collective-permute-done((bf16[4,80,640]{2,1,0:T(8,128)(2,1)S(1)}, bf16[4,80,640]{2,1,0:T(8,128)(2,1)S(1)}, u32[]{:S(2)}, u32[]{:S(2)}) %collective-permute-start.24) | collective-permute-done | bytes 409632 | tf_op jit(solution)/shard_map/ppermute | solution.py:307
  79.0 2.0 %collective-permute-start.25 = (bf16[2,80,640]{2,1,0:T(8,128)(2,1)S(1)}, bf16[2,80,640]{2,1,0:T(8,128)(2,1)S(1)}, u32[]{:S(2)}, u32[]{:S(2)}) collective-permute-start(bf16[2,80,640]{2,1,0:T(8,128)(2,1)S(1)} %slice.106), channel_id=1, source_target_pairs={{0,4},{1,5},{2,6},{3,7},{4,0},{5,1},{6,2},{7,3},{8,12},{9,13},{10,... | collective-permute-start | bytes 614408 | tf_op jit(solution)/shard_map/ppermute | solution.py:307
  81.4 2.5 %collective-permute-done.21 = bf16[4,96,640]{2,1,0:T(8,128)(2,1)S(1)} collective-permute-done((bf16[4,96,640]{2,1,0:T(8,128)(2,1)S(1)}, bf16[4,96,640]{2,1,0:T(8,128)(2,1)S(1)}, u32[]{:S(2)}, u32[]{:S(2)}) %collective-permute-start.21) | collective-permute-done | bytes 491552 | tf_op jit(solution)/shard_map/ppermute | solution.py:307
  86.1 2.4 %collective-permute-done.28 = bf16[2,80,640]{2,1,0:T(8,128)(2,1)S(1)} collective-permute-done((bf16[2,80,640]{2,1,0:T(8,128)(2,1)S(1)}, bf16[2,80,640]{2,1,0:T(8,128)(2,1)S(1)}, u32[]{:S(2)}, u32[]{:S(2)}) %collective-permute-start.28) | collective-permute-done | bytes 204832 | tf_op jit(solution)/shard_map/ppermute | solution.py:307
  88.6 1.8 %collective-permute-start.29 = (bf16[80,640]{1,0:T(8,128)(2,1)S(1)}, bf16[80,640]{1,0:T(8,128)(2,1)S(1)}, u32[]{:S(2)}, u32[]{:S(2)}) collective-permute-start(bf16[80,640]{1,0:T(8,128)(2,1)S(1)} %fusion.23), channel_id=1, source_target_pairs={{0,3},{1,2},{2,1},{3,0},{4,7},{5,6},{6,5},{7,4},{8,11},{9,10},{10,... | collective-permute-start | bytes 307208 | tf_op jit(solution)/shard_map/ppermute | solution.py:307
  90.5 2.0 %collective-permute-done.22 = bf16[2,96,640]{2,1,0:T(8,128)(2,1)S(1)} collective-permute-done((bf16[2,96,640]{2,1,0:T(8,128)(2,1)S(1)}, bf16[2,96,640]{2,1,0:T(8,128)(2,1)S(1)}, u32[]{:S(2)}, u32[]{:S(2)}) %collective-permute-start.22) | collective-permute-done | bytes 245792 | tf_op jit(solution)/shard_map/ppermute | solution.py:307
  94.6 3.0 %collective-permute-done.23 = bf16[96,640]{1,0:T(8,128)(2,1)S(1)} collective-permute-done((bf16[96,640]{1,0:T(8,128)(2,1)S(1)}, bf16[96,640]{1,0:T(8,128)(2,1)S(1)}, u32[]{:S(2)}, u32[]{:S(2)}) %collective-permute-start.23) | collective-permute-done | bytes 122912 | tf_op jit(solution)/shard_map/ppermute | solution.py:307
  (72 shorter events, 21.0 us)
Async XLA Ops:
  1.8 9.4 %collective-permute-start = (bf16[1,528,128]{2,1,0:T(8,128)(2,1)S(1)}, bf16[1,528,128]{2,1,0:T(8,128)(2,1)S(1)}, u32[]{:S(2)}, u32[]{:S(2)}) collective-permute-start(bf16[1,528,128]{2,1,0:T(8,128)(2,1)S(1)} %maximum_bitcast_fusion.own_ref), channel_id=1, source_target_pairs={{0,128},{8,136},{16,144},{24,152},{32,160},{40,168},{48,176},{56,1... | collective-permute-start | bytes 405512 | tf_op jit(solution)/shard_map/ppermute | solution.py:41
  5.5 13.6 %collective-permute-start.2 = (bf16[2,528,128]{2,1,0:T(8,128)(2,1)S(1)}, bf16[2,528,128]{2,1,0:T(8,128)(2,1)S(1)}, u32[]{:S(2)}, u32[]{:S(2)}) collective-permute-start(bf16[2,528,128]{2,1,0:T(8,128)(2,1)S(1)} %pad_maximum_fusion.1), channel_id=1, source_target_pairs={{0,16},{8,56},{16,32},{24,8},{32,48},{40,24},{48,0},{56,40},{64,80... | collective-permute-start | bytes 811016 | tf_op jit(solution)/shard_map/ppermute | solution.py:41
  8.8 10.2 %collective-permute-start.3 = (bf16[2,528,128]{2,1,0:T(8,128)(2,1)S(1)}, bf16[2,528,128]{2,1,0:T(8,128)(2,1)S(1)}, u32[]{:S(2)}, u32[]{:S(2)}) collective-permute-start(bf16[2,528,128]{2,1,0:T(8,128)(2,1)S(1)} %pad_maximum_fusion.1), channel_id=1, source_target_pairs={{0,64},{8,200},{16,80},{24,216},{32,96},{40,232},{48,112},{56,248}... | collective-permute-start | bytes 811016 | tf_op jit(solution)/shard_map/ppermute | solution.py:41
  11.2 7.9 %collective-permute-start.4 = (bf16[1,528,128]{2,1,0:T(8,128)(2,1)S(1)}, bf16[1,528,128]{2,1,0:T(8,128)(2,1)S(1)}, u32[]{:S(2)}, u32[]{:S(2)}) collective-permute-start(bf16[1,528,128]{2,1,0:T(8,128)(2,1)S(1)} %collective-permute-done.rest_7_), channel_id=1, source_target_pairs={{0,8},{8,0},{16,24},{24,16},{32,40},{40,32},{48,56},{56,48},{64,72... | collective-permute-start | bytes 405512 | tf_op jit(solution)/shard_map/ppermute | solution.py:41
  19.1 11.5 %collective-permute-start.7 = (bf16[2,528,128]{2,1,0:T(8,128)(2,1)S(1)}, bf16[2,528,128]{2,1,0:T(8,128)(2,1)S(1)}, u32[]{:S(2)}, u32[]{:S(2)}) collective-permute-start(bf16[2,528,128]{2,1,0:T(8,128)(2,1)S(1)} %collective-permute-done.2.rest_1_), channel_id=1, source_target_pairs={{0,8},{8,0},{16,24},{24,16},{32,40},{40,32},{48,56},{56,48},{64,72... | collective-permute-start | bytes 811016 | tf_op jit(solution)/shard_map/ppermute | solution.py:41
  20.7 7.8 %collective-permute-start.5 = (bf16[1,528,128]{2,1,0:T(8,128)(2,1)S(1)}, bf16[1,528,128]{2,1,0:T(8,128)(2,1)S(1)}, u32[]{:S(2)}, u32[]{:S(2)}) collective-permute-start(bf16[1,528,128]{2,1,0:T(8,128)(2,1)S(1)} %slice.48), channel_id=1, source_target_pairs={{0,16},{8,56},{16,32},{24,8},{32,48},{40,24},{48,0},{56,40},{64,80... | collective-permute-start | bytes 405512 | tf_op jit(solution)/shard_map/ppermute | solution.py:41
  21.8 18.6 %collective-permute-start.11 = (bf16[2,528,128]{2,1,0:T(8,128)(2,1)S(1)}, bf16[2,528,128]{2,1,0:T(8,128)(2,1)S(1)}, u32[]{:S(2)}, u32[]{:S(2)}) collective-permute-start(bf16[2,528,128]{2,1,0:T(8,128)(2,1)S(1)} %collective-permute-done.2.rest_1_), channel_id=1, source_target_pairs={{0,64},{8,72},{16,80},{24,88},{32,96},{40,104},{48,112},{56,120},{... | collective-permute-start | bytes 811016 | tf_op jit(solution)/shard_map/ppermute | solution.py:41
  23.1 17.4 %collective-permute-start.12 = (bf16[2,528,128]{2,1,0:T(8,128)(2,1)S(1)}, bf16[2,528,128]{2,1,0:T(8,128)(2,1)S(1)}, u32[]{:S(2)}, u32[]{:S(2)}) collective-permute-start(bf16[2,528,128]{2,1,0:T(8,128)(2,1)S(1)} %collective-permute-done.2.rest_1_), channel_id=1, source_target_pairs={{0,192},{8,200},{16,208},{24,216},{32,224},{40,232},{48,240},{56,2... | collective-permute-start | bytes 811016 | tf_op jit(solution)/shard_map/ppermute | solution.py:41
  24.4 8.7 %collective-permute-start.9 = (bf16[2,528,128]{2,1,0:T(8,128)(2,1)S(1)}, bf16[2,528,128]{2,1,0:T(8,128)(2,1)S(1)}, u32[]{:S(2)}, u32[]{:S(2)}) collective-permute-start(bf16[2,528,128]{2,1,0:T(8,128)(2,1)S(1)} %collective-permute-done.3.rest_3_), channel_id=1, source_target_pairs={{0,8},{8,0},{16,24},{24,16},{32,40},{40,32},{48,56},{56,48},{64,72... | collective-permute-start | bytes 811016 | tf_op jit(solution)/shard_map/ppermute | solution.py:41
  28.4 11.8 %collective-permute-start.6 = (bf16[2,528,128]{2,1,0:T(8,128)(2,1)S(1)}, bf16[2,528,128]{2,1,0:T(8,128)(2,1)S(1)}, u32[]{:S(2)}, u32[]{:S(2)}) collective-permute-start(bf16[2,528,128]{2,1,0:T(8,128)(2,1)S(1)} %pad_maximum_fusion.2), channel_id=1, source_target_pairs={{128,144},{136,184},{144,160},{152,136},{160,176},{168,152},{176,1... | collective-permute-start | bytes 811016 | tf_op jit(solution)/shard_map/ppermute | solution.py:41
  33.0 7.4 %collective-permute-start.13 = (bf16[1,528,128]{2,1,0:T(8,128)(2,1)S(1)}, bf16[1,528,128]{2,1,0:T(8,128)(2,1)S(1)}, u32[]{:S(2)}, u32[]{:S(2)}) collective-permute-start(bf16[1,528,128]{2,1,0:T(8,128)(2,1)S(1)} %collective-permute-done.5.rest_2_), channel_id=1, source_target_pairs={{0,64},{8,72},{16,80},{24,88},{32,96},{40,104},{48,112},{56,120},{... | collective-permute-start | bytes 405512 | tf_op jit(solution)/shard_map/ppermute | solution.py:41
  34.3 8.6 %collective-permute-start.14 = (bf16[1,528,128]{2,1,0:T(8,128)(2,1)S(1)}, bf16[1,528,128]{2,1,0:T(8,128)(2,1)S(1)}, u32[]{:S(2)}, u32[]{:S(2)}) collective-permute-start(bf16[1,528,128]{2,1,0:T(8,128)(2,1)S(1)} %collective-permute-done.5.rest_2_), channel_id=1, source_target_pairs={{0,192},{8,200},{16,208},{24,216},{32,224},{40,232},{48,240},{56,2... | collective-permute-start | bytes 405512 | tf_op jit(solution)/shard_map/ppermute | solution.py:41
  40.3 8.2 %collective-permute-start.15 = (bf16[2,528,128]{2,1,0:T(8,128)(2,1)S(1)}, bf16[2,528,128]{2,1,0:T(8,128)(2,1)S(1)}, u32[]{:S(2)}, u32[]{:S(2)}) collective-permute-start(bf16[2,528,128]{2,1,0:T(8,128)(2,1)S(1)} %collective-permute-done.6.rest_4_), channel_id=1, source_target_pairs={{0,8},{8,0},{16,24},{24,16},{32,40},{40,32},{48,56},{56,48},{64,72... | collective-permute-start | bytes 811016 | tf_op jit(solution)/shard_map/ppermute | solution.py:41
  43.0 12.7 %collective-permute-start.17 = (bf16[2,528,128]{2,1,0:T(8,128)(2,1)S(1)}, bf16[2,528,128]{2,1,0:T(8,128)(2,1)S(1)}, u32[]{:S(2)}, u32[]{:S(2)}) collective-permute-start(bf16[2,528,128]{2,1,0:T(8,128)(2,1)S(1)} %collective-permute-done.11.rest_0_), channel_id=1, source_target_pairs={{0,8},{8,0},{16,24},{24,16},{32,40},{40,32},{48,56},{56,48},{64,72... | collective-permute-start | bytes 811016 | tf_op jit(solution)/shard_map/ppermute | solution.py:41
  43.0 12.7 %collective-permute-start.18 = (bf16[2,528,128]{2,1,0:T(8,128)(2,1)S(1)}, bf16[2,528,128]{2,1,0:T(8,128)(2,1)S(1)}, u32[]{:S(2)}, u32[]{:S(2)}) collective-permute-start(bf16[2,528,128]{2,1,0:T(8,128)(2,1)S(1)} %collective-permute-done.12.rest_1_), channel_id=1, source_target_pairs={{0,8},{8,0},{16,24},{24,16},{32,40},{40,32},{48,56},{56,48},{64,72... | collective-permute-start | bytes 811016 | tf_op jit(solution)/shard_map/ppermute | solution.py:41
  43.5 11.8 %collective-permute-start.10 = (bf16[1,528,128]{2,1,0:T(8,128)(2,1)S(1)}, bf16[1,528,128]{2,1,0:T(8,128)(2,1)S(1)}, u32[]{:S(2)}, u32[]{:S(2)}) collective-permute-start(bf16[1,528,128]{2,1,0:T(8,128)(2,1)S(1)} %slice.49), channel_id=1, source_target_pairs={{128,144},{136,184},{144,160},{152,136},{160,176},{168,152},{176,1... | collective-permute-start | bytes 405512 | tf_op jit(solution)/shard_map/ppermute | solution.py:41
  48.2 7.4 %collective-permute-start.19 = (bf16[1,528,128]{2,1,0:T(8,128)(2,1)S(1)}, bf16[1,528,128]{2,1,0:T(8,128)(2,1)S(1)}, u32[]{:S(2)}, u32[]{:S(2)}) collective-permute-start(bf16[1,528,128]{2,1,0:T(8,128)(2,1)S(1)} %collective-permute-done.13.rest_2_), channel_id=1, source_target_pairs={{0,8},{8,0},{16,24},{24,16},{32,40},{40,32},{48,56},{56,48},{64,72... | collective-permute-start | bytes 405512 | tf_op jit(solution)/shard_map/ppermute | solution.py:41
  48.5 7.2 %collective-permute-start.20 = (bf16[1,528,128]{2,1,0:T(8,128)(2,1)S(1)}, bf16[1,528,128]{2,1,0:T(8,128)(2,1)S(1)}, u32[]{:S(2)}, u32[]{:S(2)}) collective-permute-start(bf16[1,528,128]{2,1,0:T(8,128)(2,1)S(1)} %collective-permute-done.14.rest_3_), channel_id=1, source_target_pairs={{0,8},{8,0},{16,24},{24,16},{32,40},{40,32},{48,56},{56,48},{64,72... | collective-permute-start | bytes 405512 | tf_op jit(solution)/shard_map/ppermute | solution.py:41
  65.9 12.9 %collective-permute-start.24 = (bf16[4,80,640]{2,1,0:T(8,128)(2,1)S(1)}, bf16[4,80,640]{2,1,0:T(8,128)(2,1)S(1)}, u32[]{:S(2)}, u32[]{:S(2)}) collective-permute-start(bf16[4,80,640]{2,1,0:T(8,128)(2,1)S(1)} %get-tuple-element.72), channel_id=1, source_target_pairs={{0,3},{1,2},{2,1},{3,0},{4,7},{5,6},{6,5},{7,4},{8,11},{9,10},{10,... | collective-permute-start | bytes 1228808 | tf_op jit(solution)/shard_map/ppermute | solution.py:307
  68.8 12.1 %collective-permute-start.27 = (bf16[4,80,640]{2,1,0:T(8,128)(2,1)S(1)}, bf16[4,80,640]{2,1,0:T(8,128)(2,1)S(1)}, u32[]{:S(2)}, u32[]{:S(2)}) collective-permute-start(bf16[4,80,640]{2,1,0:T(8,128)(2,1)S(1)} %get-tuple-element.74), channel_id=1, source_target_pairs={{0,4},{1,5},{2,6},{3,7},{4,0},{5,1},{6,2},{7,3},{8,12},{9,13},{10,... | collective-permute-start | bytes 1228808 | tf_op jit(solution)/shard_map/ppermute | solution.py:307
  70.6 13.3 %collective-permute-start.21 = (bf16[4,96,640]{2,1,0:T(8,128)(2,1)S(1)}, bf16[4,96,640]{2,1,0:T(8,128)(2,1)S(1)}, u32[]{:S(2)}, u32[]{:S(2)}) collective-permute-start(bf16[4,96,640]{2,1,0:T(8,128)(2,1)S(1)} %get-tuple-element.70), channel_id=1, source_target_pairs={{0,1},{1,0},{2,3},{3,2},{4,5},{5,4},{6,7},{7,6},{8,9},{9,8},{10,11... | collective-permute-start | bytes 1474568 | tf_op jit(solution)/shard_map/ppermute | solution.py:307
  79.0 6.7 %collective-permute-start.25 = (bf16[2,80,640]{2,1,0:T(8,128)(2,1)S(1)}, bf16[2,80,640]{2,1,0:T(8,128)(2,1)S(1)}, u32[]{:S(2)}, u32[]{:S(2)}) collective-permute-start(bf16[2,80,640]{2,1,0:T(8,128)(2,1)S(1)} %slice.106), channel_id=1, source_target_pairs={{0,4},{1,5},{2,6},{3,7},{4,0},{5,1},{6,2},{7,3},{8,12},{9,13},{10,... | collective-permute-start | bytes 614408 | tf_op jit(solution)/shard_map/ppermute | solution.py:307
  81.1 7.4 %collective-permute-start.28 = (bf16[2,80,640]{2,1,0:T(8,128)(2,1)S(1)}, bf16[2,80,640]{2,1,0:T(8,128)(2,1)S(1)}, u32[]{:S(2)}, u32[]{:S(2)}) collective-permute-start(bf16[2,80,640]{2,1,0:T(8,128)(2,1)S(1)} %slice.105), channel_id=1, source_target_pairs={{0,1},{1,0},{2,3},{3,2},{4,5},{5,4},{6,7},{7,6},{8,9},{9,8},{10,11... | collective-permute-start | bytes 614408 | tf_op jit(solution)/shard_map/ppermute | solution.py:307
  84.0 8.5 %collective-permute-start.22 = (bf16[2,96,640]{2,1,0:T(8,128)(2,1)S(1)}, bf16[2,96,640]{2,1,0:T(8,128)(2,1)S(1)}, u32[]{:S(2)}, u32[]{:S(2)}) collective-permute-start(bf16[2,96,640]{2,1,0:T(8,128)(2,1)S(1)} %slice.104), channel_id=1, source_target_pairs={{0,3},{1,2},{2,1},{3,0},{4,7},{5,6},{6,5},{7,4},{8,11},{9,10},{10,... | collective-permute-start | bytes 737288 | tf_op jit(solution)/shard_map/ppermute | solution.py:307
  (8 other events, 57.6 us)

commit v6 on v5

v6 whole, which is shorter than its diff:
```python
import functools
import itertools

import jax
import jax.numpy as jnp
from jax import lax
from jax.experimental import pallas as pl
from jax.experimental.pallas import tpu as pltpu
from jax.sharding import PartitionSpec as P
import numpy as np

HEAD_DIM = 128
BLOCK = 256
PACK = 2 * BLOCK + 16
CHAINS = ((slice(0, 96), (1, 3, 4)), (slice(96, 176), (3, 4, 1)), (slice(176, 256), (4, 1, 3)))
REACH = 24
COLS = 640
TOP, SUM = 4 * HEAD_DIM, 4 * HEAD_DIM + 8
HOT = slice(4 * HEAD_DIM, 5 * HEAD_DIM)
FLOOR = -1e30
HIDDEN = -2e30

F32 = jnp.float32
BF16 = jnp.bfloat16


def ctx_id(y, z, c):
    return ((y + 8) % 4) * 8 + ((z + 8) % 4) * 2 + c


def ctx_pairs(step, planes=None):
    pairs = []
    for y in range(4):
        for z in range(4):
            for c in range(2):
                to = step(y, z, c)
                if to is not None:
                    pairs.append((ctx_id(y, z, c), ctx_id(*to)))
    return pairs


def move(x, step):
    return lax.ppermute(x, "ctx", ctx_pairs(step))


def swap_cores(x):
    return move(x, lambda y, z, c: (y, z, 1 - c))


def along_z(x, first_plane=0):
    def step(y, z, c):
        return (y, z + 1 if c == 0 else z - 1, c) if y >= first_plane else None

    return move(x, step)


def along_y(x):
    def step(y, z, c):
        if c == 0:
            return (y + 1, z, c) if y < 3 else None
        return (3, z, c) if y == 0 else None

    return move(x, step)


def up_y(x):
    return move(x, lambda y, z, c: (y + 1, z, c) if y < 3 else None)


def round_y(x):
    return move(x, lambda y, z, c: (3, z, c) if y == 0 else None)


def first_slots(y, z, c):
    d = 2 * c - 1
    row = [[(y, z, c)], [(y, z + d, c), (y, z + d, 1 - c)], [(y, z + 2, c)]]
    return row + [[(y + d, z, c), (y + d, z, 1 - c)], [(y + 2, z, c)]]


def next_slots(y, z, c):
    d = 2 * c - 1
    near = [[(y + e, z + d, c), (y + e, z + d, 1 - c)] for e in (-1, 1)]
    return near + [[(y + e, z + 2, c)] for e in (-1, 1)]


def far_slots(y, z, c):
    d = 2 * c - 1
    return [[(y + 2, z + d, c), (y + 2, z + d, 1 - c)], [(y + 2, z + 2, c)]]


def attend_blocks(kv_ref, places, diagonal, q_ref, state_ref):
    heads = [slice(h * HEAD_DIM, (h + 1) * HEAD_DIM) for h in range(4)]
    keys, values, visible = [], [], []
    for at, low in places:
        keys.append(kv_ref[at, 0:BLOCK, :])
        values.append(jnp.transpose(kv_ref[at, BLOCK : 2 * BLOCK, :]))
        counts = kv_ref[at, 2 * BLOCK : PACK, :]
        first = jnp.dot(counts, q_ref[HOT, :], preferred_element_type=F32)[0:1, :].astype(jnp.int32)
        row = lax.broadcasted_iota(jnp.int32, (BLOCK, BLOCK), 0)
        seen = row >= jnp.maximum(first, low)
        if diagonal:
            seen &= row <= lax.broadcasted_iota(jnp.int32, (BLOCK, BLOCK), 1)
        visible.append(seen)
    scores = [[jnp.dot(k, q_ref[rows, :], preferred_element_type=F32) for k in keys] for rows in heads]
    old = [(state_ref[TOP + h : TOP + h + 1, :], state_ref[SUM + h : SUM + h + 1, :]) for h in range(4)]
    new = []
    for h in range(4):
        masked = [jnp.where(seen, s, HIDDEN) for seen, s in zip(visible, scores[h])]
        m_old, total = old[h]
        m_new = m_old
        for s in masked:
            m_new = jnp.maximum(m_new, jnp.max(s, axis=0, keepdims=True))
        weights = [jnp.exp(s - m_new) for s in masked]
        fade = jnp.exp(m_old - m_new)
        total = fade * total
        for p in weights:
            total = total + jnp.sum(p, axis=0, keepdims=True)
        added = sum(jnp.dot(v, p.astype(BF16), preferred_element_type=F32) for v, p in zip(values, weights))
        new.append((m_new, total, fade, added))
    for h, rows in enumerate(heads):
        m_new, total, fade, added = new[h]
        state_ref[TOP + h : TOP + h + 1, :] = m_new
        state_ref[SUM + h : SUM + h + 1, :] = total
        state_ref[rows, :] = fade * state_ref[rows, :] + added


def where_am_i(at_ref):
    own = at_ref[0]
    return own // 8, (own // 2) % 4, own % 2


def attend_pieces(at_ref, slots, piece_refs, all_ref, order_ref, sets):
    y, z, c = where_am_i(at_ref)
    blocks = []
    for piece_ref, places_of in zip(piece_refs, slots(y, z, c)):
        for i, place in enumerate(places_of):
            all_ref[len(blocks)] = piece_ref[i]
            blocks.append(ctx_id(*place))
    for core, q_ref, state_ref in zip((c, 1 - c), sets[::2], sets[1::2]):
        own = ctx_id(y, z, core)
        count = jnp.int32(0)
        for n, block in enumerate(blocks):
            order_ref[count] = n
            count += ((block < own) & (block >= own - REACH)).astype(jnp.int32)

        @pl.loop(0, (count + 1) // 2)
        def _(g, count=count, q_ref=q_ref, state_ref=state_ref):
            one = order_ref[2 * g]
            both = 2 * g + 1 < count
            two = jnp.where(both, order_ref[2 * g + 1], one)
            attend_blocks(all_ref, [(one, 0), (two, jnp.where(both, 0, BLOCK))], False, q_ref, state_ref)


def start_kernel(slots, n, at_ref, *rest):
    pieces, (q_ref, q_2_ref, s_ref, s_2_ref, all_ref, order_ref) = rest[:n], rest[n:]
    for state_ref in (s_ref, s_2_ref):
        state_ref[...] = jnp.zeros_like(state_ref)
        state_ref[TOP : TOP + 8, :] = jnp.full((8, BLOCK), FLOOR, F32)
    attend_blocks(pieces[0], [(0, 0)], True, q_ref, s_ref)
    attend_pieces(at_ref, slots, pieces, all_ref, order_ref, (q_ref, s_ref, q_2_ref, s_2_ref))


def more_kernel(slots, n, at_ref, *rest):
    pieces, (q_ref, q_2_ref, s_in, s_2_in, s_ref, s_2_ref, all_ref, order_ref) = rest[:n], rest[n:]
    s_ref[...] = s_in[...]
    s_2_ref[...] = s_2_in[...]
    attend_pieces(at_ref, slots, pieces, all_ref, order_ref, (q_ref, s_ref, q_2_ref, s_2_ref))


def query_kernel(hidden_ref, w_ref, segment_ref, out_ref, normed_ref):
    @pl.loop(0, BLOCK // 16)
    def _(i):
        rows = pl.ds(pl.multiple_of(i * 16, 16), 16)
        x = hidden_ref[rows, :].astype(F32)
        normed_ref[rows, :] = (x * lax.rsqrt(jnp.mean(x * x, axis=-1, keepdims=True) + 1e-06)).astype(BF16)

    q = jnp.zeros((BLOCK, w_ref.shape[1]), F32)
    for k in range(0, w_ref.shape[0], 1024):
        q += jnp.dot(normed_ref[:, k : k + 1024], w_ref[k : k + 1024, :], preferred_element_type=F32)
    out_ref[0 : 4 * HEAD_DIM, :] = jnp.transpose(q * HEAD_DIM ** (-0.5)).astype(BF16)
    ids = lax.broadcasted_iota(jnp.int32, (HEAD_DIM, BLOCK), 0)
    out_ref[HOT, :] = (ids == segment_ref[...]).astype(BF16)


def last_kernel(at_ref, s_ref, s_2_ref, w_ref, *rest):
    outs, att_ref = rest[:6], rest[6]
    for h in range(4):
        rows = slice(h * HEAD_DIM, (h + 1) * HEAD_DIM)
        tops = [r[TOP + h : TOP + h + 1, :] for r in (s_ref, s_2_ref)]
        top = jnp.maximum(*tops)
        fades = [jnp.exp(t - top) for t in tops]
        total = sum(f * r[SUM + h : SUM + h + 1, :] for f, r in zip(fades, (s_ref, s_2_ref)))
        value = sum(f * r[rows, :] for f, r in zip(fades, (s_ref, s_2_ref)))
        att_ref[:, rows] = jnp.transpose(value / total).astype(BF16)
    section = at_ref[1]
    for sides in itertools.product((0, 1), repeat=3):
        away = 0
        for step, side in zip(CHAINS[0][1], sides):
            away ^= step * side
        cols = pl.ds(pl.multiple_of((section ^ away) * COLS, 128), COLS)
        part = jnp.dot(att_ref[...], w_ref[:, cols], preferred_element_type=F32).astype(BF16)
        crossed = dict(zip(CHAINS[0][1], sides))
        for i, (rows, order) in enumerate(CHAINS):
            first, second, third = (crossed[step] for step in order)
            outs[2 * i + 1 - first][2 * second + third] = part[rows]


VMEM = pl.BlockSpec(memory_space=pltpu.VMEM)
SMEM = pl.BlockSpec(memory_space=pltpu.SMEM)
STATE = jax.ShapeDtypeStruct((4 * HEAD_DIM + 16, BLOCK), F32)
LIMIT = pltpu.CompilerParams(vmem_limit_bytes=24 * 1024 * 1024)


def cost(n):
    return pl.CostEstimate(
        flops=n * 4 * 4 * BLOCK * BLOCK * HEAD_DIM,
        bytes_accessed=n * PACK * HEAD_DIM * 2,
        transcendentals=n * 4 * BLOCK * BLOCK,
    )


def per_device(hidden, k_cache, v_cache, segment, w_query, w_out):
    ctx = lax.axis_index("ctx")

    smaller = jnp.sum(
        (segment[:, None] < jnp.arange(HEAD_DIM, dtype=jnp.int32)[None, :]).astype(F32), axis=0
    ).astype(BF16)
    own = jnp.concatenate([k_cache, v_cache, jnp.broadcast_to(smaller[None, :], (16, HEAD_DIM))], axis=0)[None]

    other = swap_cores(own)
    pair = jnp.concatenate([own, other], axis=0)
    z_near = along_z(pair)
    y_near = along_y(pair)
    y_far = move(pair, lambda y, z, c: (y + 2, z, c) if y < 2 else None)

    q = pl.pallas_call(
        query_kernel,
        out_shape=jax.ShapeDtypeStruct((5 * HEAD_DIM, BLOCK), BF16),
        in_specs=[VMEM] * 3,
        out_specs=VMEM,
        scratch_shapes=[pltpu.VMEM(hidden.shape, BF16)],
        compiler_params=LIMIT,
        cost_estimate=pl.CostEstimate(flops=2 * hidden.size * w_query.shape[1], bytes_accessed=8 * 10**6, transcendentals=0),
        name="project_queries",
    )(hidden, w_query, segment[None, :])

    (z_near, y_near), q = lax.optimization_barrier(((z_near, y_near), q))
    q_2 = swap_cores(q)
    z_far = along_z(z_near[:1])
    up_near = up_y(z_near)
    around_near = round_y(z_near)
    y_far, z_far = lax.optimization_barrier((y_far, z_far))
    up_far = up_y(z_far)
    around_far = round_y(z_far)
    far_near = along_z(y_far, 2)

    at = jnp.stack([ctx, lax.axis_index("section")]).astype(jnp.int32)

    def attend(kernel, slots, n, pieces, state, name):
        return pl.pallas_call(
            functools.partial(kernel, slots, len(pieces)),
            out_shape=(STATE, STATE),
            in_specs=[SMEM] + [VMEM] * (len(pieces) + 2 + len(state)),
            out_specs=(VMEM,) * 2,
            scratch_shapes=[pltpu.VMEM((n, PACK, HEAD_DIM), BF16), pltpu.SMEM((16,), jnp.int32)],
            compiler_params=LIMIT,
            cost_estimate=cost(1),
            name=name,
        )(at, *pieces, q, q_2, *state)

    state = attend(start_kernel, first_slots, 7, [own, z_near, z_far, y_near, y_far], (), "attend_first")
    far_near, state = lax.optimization_barrier((far_near, state))
    far_far = along_z(far_near[:1], 2)
    nexts = (up_near, around_near, up_far, around_far)
    nexts, state = lax.optimization_barrier((nexts, state))
    state = attend(more_kernel, next_slots, 6, nexts, state, "attend_next")
    far_far, state = lax.optimization_barrier((far_far, state))
    state, state_2 = attend(more_kernel, far_slots, 3, [far_near, far_far], state, "attend_far")
    state_2 = swap_cores(state_2)

    out_shape = []
    for rows, _ in CHAINS:
        out_shape += [jax.ShapeDtypeStruct((4, rows.stop - rows.start, COLS), BF16)] * 2
    outs = pl.pallas_call(
        last_kernel,
        out_shape=tuple(out_shape),
        in_specs=[SMEM] + [VMEM] * 3,
        out_specs=(VMEM,) * 6,
        scratch_shapes=[pltpu.VMEM((BLOCK, 4 * HEAD_DIM), BF16)],
        compiler_params=LIMIT,
        cost_estimate=cost(12),
        name="project_attended",
    )(at, state, state_2, w_out)

    def exchange(x, step):
        return lax.ppermute(x, "section", [(i, i ^ step) for i in range(8)])

    mixed = []
    for i, (_, (first, second, third)) in enumerate(CHAINS):
        sent, kept = outs[2 * i], outs[2 * i + 1]
        four = kept.astype(F32) + exchange(sent, first).astype(F32)
        two = four[:2] + exchange(four[2:].astype(BF16), second).astype(F32)
        mixed.append(two[0] + exchange(two[1].astype(BF16), third).astype(F32))
    return jnp.concatenate(mixed, axis=0).astype(BF16)


def solution(mesh):
    return jax.shard_map(
        per_device,
        mesh=mesh,
        in_specs=(
            P("ctx", None),
            P("ctx", "section"),
            P("ctx", "section"),
            P("ctx"),
            P(None, "section"),
            P("section", None),
        ),
        out_specs=P("ctx", "section"),
        check_vma=False,
    )
```

time: 98.7 us -> 101 us (1.023)
  Pallas kernels: 18.8 us -> 25.1 us
  matrix products: 5.57 us -> 0 us
  waiting for transfers between devices: 26.6 us -> 31.2 us
  starting transfers between devices: 38.9 us -> 36 us
  local copies, waits for them, and re-layouts: 2.64 us -> 5.06 us
  other arithmetic: 5.44 us -> 3.05 us
    pallas_call x4 -> x5, Pallas kernels: 18.8 us -> 25.1 us  [the longest x3 18.6 us: attend(): pl.pallas_call(functools.partial(kernel, slots, len(pieces)), out_shape=(...]
    dot_general x1 -> x0, matrix products: 5.57 us -> none  [per_device(): lax.dot_general(w_query, normed, (((0,), (1,)), ((), ())), preferred_elem...]
    ppermute x21 -> x13, waiting for transfers between devices: 5.84 us -> 9.35 us  [move(): return lax.ppermute(x, 'ctx', ctx_pairs(step))]
    unnamed x4 -> x8, local copies, waits for them, and re-layouts: 2.49 us -> 4.91 us
    reduce_sum x1 -> x0, other arithmetic: 2.34 us -> none  [per_device(): jnp.mean(widened * widened, axis=-1, keepdims=True) + 1e-06]
    ppermute x21 -> x13, starting transfers between devices: 28.7 us -> 27.2 us  [move(): return lax.ppermute(x, 'ctx', ctx_pairs(step))]
    ppermute x9, starting transfers between devices: 10.2 us -> 8.86 us  [exchange(): return lax.ppermute(x, 'section', [(i, i ^ step) for i in range(8)])]
    ppermute x9, waiting for transfers between devices: 20.8 us -> 21.9 us  [exchange(): return lax.ppermute(x, 'section', [(i, i ^ step) for i in range(8)])]
  transfers between devices with their start and end apart: 30 -> 22, of which waited for: 10 -> 11; matrix products, arithmetic and copies ran while one was open for 9% -> 1% of each run, Pallas kernels for 15% -> 17%
where the time goes in v6:
time: 101 us
  starting transfers between devices  36 us (36%)
  waiting for transfers between devices  31.2 us (31%)
  Pallas kernels  25.1 us (25%)
  local copies, waits for them, and re-layouts  5.06 us (5%)
  other arithmetic  3.05 us (3%)
    ppermute x13, starting transfers between devices, move(): return lax.ppermute(x, 'ctx', ctx_pairs(step))  27.2 us
    ppermute x9, waiting for transfers between devices, exchange(): return lax.ppermute(x, 'section', [(i, i ^ step) for i in range(8)])  21.9 us
    pallas_call x3, Pallas kernels, attend(): pl.pallas_call(functools.partial(kernel, slots, len(pieces)), out_shape=(...  18.6 us
    ppermute x13, waiting for transfers between devices, move(): return lax.ppermute(x, 'ctx', ctx_pairs(step))  9.35 us
    ppermute x9, starting transfers between devices, exchange(): return lax.ppermute(x, 'section', [(i, i ^ step) for i in range(8)])  8.86 us
    unnamed x8, local copies, waits for them, and re-layouts  4.91 us
    pallas_call x1, Pallas kernels, per_device(): pl.pallas_call(query_kernel, out_shape=jax.ShapeDtypeStruct((5 * HEAD_DIM...  3.99 us
    pallas_call x1, Pallas kernels, per_device(): pl.pallas_call(last_kernel, out_shape=tuple(out_shape), in_specs=[SMEM] +...  2.48 us
  transfers between devices with their start and end apart: 22, of which 11 were waited for; matrix products, arithmetic and copies ran while one was open for 1% of the time, Pallas kernels for 17%

profile of v6, /device:TPU:24, one launch (start us, length us, event | category | flops | bytes accessed | tf_op | source)
XLA Modules:
  0.0 100.8 jit_solution(6188748417613677621)
XLA Ops:
  4.5 3.3 %collective-permute-start.2 = (bf16[2,528,128]{2,1,0:T(8,128)(2,1)S(1)}, bf16[2,528,128]{2,1,0:T(8,128)(2,1)S(1)}, u32[]{:S(2)}, u32[]{:S(2)}) collective-permute-start(bf16[2,528,128]{2,1,0:T(8,128)(2,1)S(1)} %pad_maximum_fusion.1), channel_id=1, source_target_pairs={{0,16},{8,56},{16,32},{24,8},{32,48},{40,24},{48,0},{56,40},{64,80... | collective-permute-start | bytes 811016 | tf_op jit(solution)/shard_map/ppermute | solution.py:43
  9.1 2.5 %copy-done = bf16[5120,512]{1,0:T(8,128)(2,1)S(1)} copy-done((bf16[5120,512]{1,0:T(8,128)(2,1)S(1)}, bf16[5120,512]{1,0:T(8,128)(2,1)}, u32[]{:S(2)}) %copy-start) | copy-done | bytes 5242904
  11.6 1.7 %copy-done.2 = bf16[256,5120]{1,0:T(8,128)(2,1)S(1)} copy-done((bf16[256,5120]{1,0:T(8,128)(2,1)S(1)}, bf16[256,5120]{1,0:T(8,128)(2,1)}, u32[]{:S(2)}) %copy-start.2) | copy-done | bytes 2621464
  14.0 4.0 %project_queries.1.rest_5_.rest_4_.rest_2_ = bf16[640,256]{1,0:T(8,128)(2,1)S(1)} custom-call(bf16[256,5120]{1,0:T(8,128)(2,1)S(1)} %copy-done.2, bf16[5120,512]{1,0:T(8,128)(2,1)S(1)} %copy-done, s32[1,256]{1,0:T(1,128)S(1)} %bitcast.29), custom_call_target="tpu_custom_call" | custom-call | flops 1342177280 | bytes 8000000 | tf_op jit(solution)/shard_map/project_queries/pallas_call | solution.py:236
  18.0 3.0 %collective-permute-start.6 = (bf16[640,256]{1,0:T(8,128)(2,1)S(1)}, bf16[640,256]{1,0:T(8,128)(2,1)S(1)}, u32[]{:S(2)}, u32[]{:S(2)}) collective-permute-start(bf16[640,256]{1,0:T(8,128)(2,1)S(1)} %project_queries.1.rest_5_.rest_4_.rest_2_), channel_id=1, source_target_pairs={{0,8},{8,0},{16,24},{24,16},{32,40},{40,32},{48,56},{56,48},{64,72... | collective-permute-start | bytes 983048 | tf_op jit(solution)/shard_map/ppermute | solution.py:43
  21.0 1.7 %collective-permute-start.4 = (bf16[1,528,128]{2,1,0:T(8,128)(2,1)S(1)}, bf16[1,528,128]{2,1,0:T(8,128)(2,1)S(1)}, u32[]{:S(2)}, u32[]{:S(2)}) collective-permute-start(bf16[1,528,128]{2,1,0:T(8,128)(2,1)S(1)} %slice.48), channel_id=1, source_target_pairs={{0,16},{8,56},{16,32},{24,8},{32,48},{40,24},{48,0},{56,40},{64,80... | collective-permute-start | bytes 405512 | tf_op jit(solution)/shard_map/ppermute | solution.py:43
  22.7 6.1 %collective-permute-done.4.rest_2_ = bf16[1,528,128]{2,1,0:T(8,128)(2,1)S(1)} collective-permute-done((bf16[1,528,128]{2,1,0:T(8,128)(2,1)S(1)}, bf16[1,528,128]{2,1,0:T(8,128)(2,1)S(1)}, u32[]{:S(2)}, u32[]{:S(2)}) %collective-permute-start.4) | collective-permute-done | bytes 135200 | tf_op jit(solution)/shard_map/ppermute | solution.py:43
  28.8 1.9 %collective-permute-start.5 = (bf16[2,528,128]{2,1,0:T(8,128)(2,1)S(1)}, bf16[2,528,128]{2,1,0:T(8,128)(2,1)S(1)}, u32[]{:S(2)}, u32[]{:S(2)}) collective-permute-start(bf16[2,528,128]{2,1,0:T(8,128)(2,1)S(1)} %collective-permute-done.1.rest_4_), channel_id=1, source_target_pairs={{128,144},{136,184},{144,160},{152,136},{160,176},{168,152},{176,1... | collective-permute-start | bytes 811016 | tf_op jit(solution)/shard_map/ppermute | solution.py:43
  33.3 1.6 %collective-permute-start.11 = (bf16[1,528,128]{2,1,0:T(8,128)(2,1)S(1)}, bf16[1,528,128]{2,1,0:T(8,128)(2,1)S(1)}, u32[]{:S(2)}, u32[]{:S(2)}) collective-permute-start(bf16[1,528,128]{2,1,0:T(8,128)(2,1)S(1)} %collective-permute-done.4.rest_2_), channel_id=1, source_target_pairs={{0,192},{8,200},{16,208},{24,216},{32,224},{40,232},{48,240},{56,2... | collective-permute-start | bytes 405512 | tf_op jit(solution)/shard_map/ppermute | solution.py:43
  36.3 5.8 %attend_first.1 = (f32[528,256]{1,0:T(8,128)S(1)}, f32[528,256]{1,0:T(8,128)S(1)}) custom-call(s32[2]{0:T(128)S(1)} %pad_add_fusion.at_ref, bf16[1,528,128]{2,1,0:T(8,128)(2,1)S(1)} %maximum_bitcast_fusion.rest_0_, bf16[2,528,128]{2,1,0:T(8,128)(2,1)S(1)} %collective-permute-done.2.rest_1_, bf16[1,528,128]{2,1,0:T(8,128)(2,1)S(1)} %collective-permute-done.4.rest_2_, ...), custom_call_target="tpu_custom_call" | custom-call | flops 134217728 | bytes 135168 | tf_op jit(solution)/shard_map/attend_first/pallas_call | solution.py:260
  42.1 8.9 %collective-permute-start.7 = (bf16[1,528,128]{2,1,0:T(8,128)(2,1)S(1)}, bf16[1,528,128]{2,1,0:T(8,128)(2,1)S(1)}, u32[]{:S(2)}, u32[]{:S(2)}) collective-permute-start(bf16[1,528,128]{2,1,0:T(8,128)(2,1)S(1)} %slice.49), channel_id=1, source_target_pairs={{128,144},{136,184},{144,160},{152,136},{160,176},{168,152},{176,1... | collective-permute-start | bytes 405512 | tf_op jit(solution)/shard_map/ppermute | solution.py:43
  51.0 7.6 %attend_next.1 = (f32[528,256]{1,0:T(8,128)S(1)}, f32[528,256]{1,0:T(8,128)S(1)}) custom-call(s32[2]{0:T(128)S(1)} %pad_add_fusion.at_ref, bf16[2,528,128]{2,1,0:T(8,128)(2,1)S(1)} %collective-permute-done.8.rest_0_, bf16[2,528,128]{2,1,0:T(8,128)(2,1)S(1)} %collective-permute-done.9.rest_1_, bf16[1,528,128]{2,1,0:T(8,128)(2,1)S(1)} %collective-permute-done.10.rest_2_, ...), custom_call_target="tpu_custom_call" | custom-call | flops 134217728 | bytes 135168 | tf_op jit(solution)/shard_map/attend_next/pallas_call | solution.py:260
  58.6 5.2 %attend_far.1 = (f32[528,256]{1,0:T(8,128)S(1)}, f32[528,256]{1,0:T(8,128)S(1)}) custom-call(s32[2]{0:T(128)S(1)} %pad_add_fusion.at_ref, bf16[2,528,128]{2,1,0:T(8,128)(2,1)S(1)} %collective-permute-done.5.rest_0_, bf16[1,528,128]{2,1,0:T(8,128)(2,1)S(1)} %collective-permute-done.7.rest_1_, bf16[640,256]{1,0:T(8,128)(2,1)S(1)} %project_queries.1.rest_5_.rest_4_.rest_2_, ...), custom_call_target="tpu_custom_call" | custom-call | flops 134217728 | bytes 135168 | tf_op jit(solution)/shard_map/attend_far/pallas_call | solution.py:260
  64.1 1.9 %collective-permute-done.12.s_2_ref = f32[528,256]{1,0:T(8,128)S(1)} collective-permute-done((f32[528,256]{1,0:T(8,128)S(1)}, f32[528,256]{1,0:T(8,128)S(1)}, u32[]{:S(2)}, u32[]{:S(2)}) %collective-permute-start.12) | collective-permute-done | bytes 540704 | tf_op jit(solution)/shard_map/ppermute | solution.py:43
  66.1 2.5 %project_attended.1 = (bf16[4,96,640]{2,1,0:T(8,128)(2,1)S(1)}, bf16[4,96,640]{2,1,0:T(8,128)(2,1)S(1)}, bf16[4,80,640]{2,1,0:T(8,128)(2,1)S(1)}, bf16[4,80,640]...) custom-call(s32[2]{0:T(128)S(1)} %pad_add_fusion.at_ref, ...), custom_call_target="tpu_custom_call" | custom-call | flops 1610612736 | bytes 1622016 | tf_op jit(solution)/shard_map/project_attended/pallas_call | solution.py:284
  68.5 2.9 %collective-permute-start.16 = (bf16[4,80,640]{2,1,0:T(8,128)(2,1)S(1)}, bf16[4,80,640]{2,1,0:T(8,128)(2,1)S(1)}, u32[]{:S(2)}, u32[]{:S(2)}) collective-permute-start(bf16[4,80,640]{2,1,0:T(8,128)(2,1)S(1)} %get-tuple-element.60), channel_id=1, source_target_pairs={{0,3},{1,2},{2,1},{3,0},{4,7},{5,6},{6,5},{7,4},{8,11},{9,10},{10,... | collective-permute-start | bytes 1228808 | tf_op jit(solution)/shard_map/ppermute | solution.py:296
  71.4 1.5 %collective-permute-start.19 = (bf16[4,80,640]{2,1,0:T(8,128)(2,1)S(1)}, bf16[4,80,640]{2,1,0:T(8,128)(2,1)S(1)}, u32[]{:S(2)}, u32[]{:S(2)}) collective-permute-start(bf16[4,80,640]{2,1,0:T(8,128)(2,1)S(1)} %get-tuple-element.62), channel_id=1, source_target_pairs={{0,4},{1,5},{2,6},{3,7},{4,0},{5,1},{6,2},{7,3},{8,12},{9,13},{10,... | collective-permute-start | bytes 1228808 | tf_op jit(solution)/shard_map/ppermute | solution.py:296
  73.1 8.2 %collective-permute-done.16 = bf16[4,80,640]{2,1,0:T(8,128)(2,1)S(1)} collective-permute-done((bf16[4,80,640]{2,1,0:T(8,128)(2,1)S(1)}, bf16[4,80,640]{2,1,0:T(8,128)(2,1)S(1)}, u32[]{:S(2)}, u32[]{:S(2)}) %collective-permute-start.16) | collective-permute-done | bytes 409632 | tf_op jit(solution)/shard_map/ppermute | solution.py:296
  81.5 1.6 %collective-permute-start.17 = (bf16[2,80,640]{2,1,0:T(8,128)(2,1)S(1)}, bf16[2,80,640]{2,1,0:T(8,128)(2,1)S(1)}, u32[]{:S(2)}, u32[]{:S(2)}) collective-permute-start(bf16[2,80,640]{2,1,0:T(8,128)(2,1)S(1)} %slice.106), channel_id=1, source_target_pairs={{0,4},{1,5},{2,6},{3,7},{4,0},{5,1},{6,2},{7,3},{8,12},{9,13},{10,... | collective-permute-start | bytes 614408 | tf_op jit(solution)/shard_map/ppermute | solution.py:296
  83.6 2.7 %collective-permute-done.13 = bf16[4,96,640]{2,1,0:T(8,128)(2,1)S(1)} collective-permute-done((bf16[4,96,640]{2,1,0:T(8,128)(2,1)S(1)}, bf16[4,96,640]{2,1,0:T(8,128)(2,1)S(1)}, u32[]{:S(2)}, u32[]{:S(2)}) %collective-permute-start.13) | collective-permute-done | bytes 491552 | tf_op jit(solution)/shard_map/ppermute | solution.py:296
  88.3 2.7 %collective-permute-done.20 = bf16[2,80,640]{2,1,0:T(8,128)(2,1)S(1)} collective-permute-done((bf16[2,80,640]{2,1,0:T(8,128)(2,1)S(1)}, bf16[2,80,640]{2,1,0:T(8,128)(2,1)S(1)}, u32[]{:S(2)}, u32[]{:S(2)}) %collective-permute-start.20) | collective-permute-done | bytes 204832 | tf_op jit(solution)/shard_map/ppermute | solution.py:296
  92.7 2.2 %collective-permute-done.14 = bf16[2,96,640]{2,1,0:T(8,128)(2,1)S(1)} collective-permute-done((bf16[2,96,640]{2,1,0:T(8,128)(2,1)S(1)}, bf16[2,96,640]{2,1,0:T(8,128)(2,1)S(1)}, u32[]{:S(2)}, u32[]{:S(2)}) %collective-permute-start.14) | collective-permute-done | bytes 245792 | tf_op jit(solution)/shard_map/ppermute | solution.py:296
  95.4 1.7 %collective-permute-done.21 = bf16[80,640]{1,0:T(8,128)(2,1)S(1)} collective-permute-done((bf16[80,640]{1,0:T(8,128)(2,1)S(1)}, bf16[80,640]{1,0:T(8,128)(2,1)S(1)}, u32[]{:S(2)}, u32[]{:S(2)}) %collective-permute-start.21) | collective-permute-done | bytes 102432 | tf_op jit(solution)/shard_map/ppermute | solution.py:296
  97.0 2.9 %collective-permute-done.15 = bf16[96,640]{1,0:T(8,128)(2,1)S(1)} collective-permute-done((bf16[96,640]{1,0:T(8,128)(2,1)S(1)}, bf16[96,640]{1,0:T(8,128)(2,1)S(1)}, u32[]{:S(2)}, u32[]{:S(2)}) %collective-permute-start.15) | collective-permute-done | bytes 122912 | tf_op jit(solution)/shard_map/ppermute | solution.py:296
  (56 shorter events, 16.5 us)
Async XLA Ops:
  1.7 1.4 %collective-permute-start = (bf16[1,528,128]{2,1,0:T(8,128)(2,1)S(1)}, bf16[1,528,128]{2,1,0:T(8,128)(2,1)S(1)}, u32[]{:S(2)}, u32[]{:S(2)}) collective-permute-start(bf16[1,528,128]{2,1,0:T(8,128)(2,1)S(1)} %maximum_bitcast_fusion.rest_0_), channel_id=1, source_target_pairs={{0,8},{8,0},{16,24},{24,16},{32,40},{40,32},{48,56},{56,48},{64,72... | collective-permute-start | bytes 405512 | tf_op jit(solution)/shard_map/ppermute | solution.py:43
  3.2 14.8 %collective-permute-start.3 = (bf16[2,528,128]{2,1,0:T(8,128)(2,1)S(1)}, bf16[2,528,128]{2,1,0:T(8,128)(2,1)S(1)}, u32[]{:S(2)}, u32[]{:S(2)}) collective-permute-start(bf16[2,528,128]{2,1,0:T(8,128)(2,1)S(1)} %pad_maximum_fusion.1), channel_id=1, source_target_pairs={{0,64},{8,200},{16,80},{24,216},{32,96},{40,232},{48,112},{56,248}... | collective-permute-start | bytes 811016 | tf_op jit(solution)/shard_map/ppermute | solution.py:43
  4.5 13.6 %collective-permute-start.2 = (bf16[2,528,128]{2,1,0:T(8,128)(2,1)S(1)}, bf16[2,528,128]{2,1,0:T(8,128)(2,1)S(1)}, u32[]{:S(2)}, u32[]{:S(2)}) collective-permute-start(bf16[2,528,128]{2,1,0:T(8,128)(2,1)S(1)} %pad_maximum_fusion.1), channel_id=1, source_target_pairs={{0,16},{8,56},{16,32},{24,8},{32,48},{40,24},{48,0},{56,40},{64,80... | collective-permute-start | bytes 811016 | tf_op jit(solution)/shard_map/ppermute | solution.py:43
  7.8 14.9 %collective-permute-start.1 = (bf16[2,528,128]{2,1,0:T(8,128)(2,1)S(1)}, bf16[2,528,128]{2,1,0:T(8,128)(2,1)S(1)}, u32[]{:S(2)}, u32[]{:S(2)}) collective-permute-start(bf16[2,528,128]{2,1,0:T(8,128)(2,1)S(1)} %pad_maximum_fusion.1), channel_id=1, source_target_pairs={{0,128},{8,136},{16,144},{24,152},{32,160},{40,168},{48,176},{56,1... | collective-permute-start | bytes 811016 | tf_op jit(solution)/shard_map/ppermute | solution.py:43
  9.1 2.5 %copy-start = (bf16[5120,512]{1,0:T(8,128)(2,1)S(1)}, bf16[5120,512]{1,0:T(8,128)(2,1)}, u32[]{:S(2)}) copy-start(bf16[5120,512]{1,0:T(8,128)(2,1)} %w_ref.2) | copy-start | bytes 15728644
  18.0 16.8 %collective-permute-start.6 = (bf16[640,256]{1,0:T(8,128)(2,1)S(1)}, bf16[640,256]{1,0:T(8,128)(2,1)S(1)}, u32[]{:S(2)}, u32[]{:S(2)}) collective-permute-start(bf16[640,256]{1,0:T(8,128)(2,1)S(1)} %project_queries.1.rest_5_.rest_4_.rest_2_), channel_id=1, source_target_pairs={{0,8},{8,0},{16,24},{24,16},{32,40},{40,32},{48,56},{56,48},{64,72... | collective-permute-start | bytes 983048 | tf_op jit(solution)/shard_map/ppermute | solution.py:43
  21.0 7.8 %collective-permute-start.4 = (bf16[1,528,128]{2,1,0:T(8,128)(2,1)S(1)}, bf16[1,528,128]{2,1,0:T(8,128)(2,1)S(1)}, u32[]{:S(2)}, u32[]{:S(2)}) collective-permute-start(bf16[1,528,128]{2,1,0:T(8,128)(2,1)S(1)} %slice.48), channel_id=1, source_target_pairs={{0,16},{8,56},{16,32},{24,8},{32,48},{40,24},{48,0},{56,40},{64,80... | collective-permute-start | bytes 405512 | tf_op jit(solution)/shard_map/ppermute | solution.py:43
  28.8 13.3 %collective-permute-start.5 = (bf16[2,528,128]{2,1,0:T(8,128)(2,1)S(1)}, bf16[2,528,128]{2,1,0:T(8,128)(2,1)S(1)}, u32[]{:S(2)}, u32[]{:S(2)}) collective-permute-start(bf16[2,528,128]{2,1,0:T(8,128)(2,1)S(1)} %collective-permute-done.1.rest_4_), channel_id=1, source_target_pairs={{128,144},{136,184},{144,160},{152,136},{160,176},{168,152},{176,1... | collective-permute-start | bytes 811016 | tf_op jit(solution)/shard_map/ppermute | solution.py:43
  30.7 20.3 %collective-permute-start.9 = (bf16[2,528,128]{2,1,0:T(8,128)(2,1)S(1)}, bf16[2,528,128]{2,1,0:T(8,128)(2,1)S(1)}, u32[]{:S(2)}, u32[]{:S(2)}) collective-permute-start(bf16[2,528,128]{2,1,0:T(8,128)(2,1)S(1)} %collective-permute-done.2.rest_1_), channel_id=1, source_target_pairs={{0,192},{8,200},{16,208},{24,216},{32,224},{40,232},{48,240},{56,2... | collective-permute-start | bytes 811016 | tf_op jit(solution)/shard_map/ppermute | solution.py:43
  32.0 19.0 %collective-permute-start.8 = (bf16[2,528,128]{2,1,0:T(8,128)(2,1)S(1)}, bf16[2,528,128]{2,1,0:T(8,128)(2,1)S(1)}, u32[]{:S(2)}, u32[]{:S(2)}) collective-permute-start(bf16[2,528,128]{2,1,0:T(8,128)(2,1)S(1)} %collective-permute-done.2.rest_1_), channel_id=1, source_target_pairs={{0,64},{8,72},{16,80},{24,88},{32,96},{40,104},{48,112},{56,120},{... | collective-permute-start | bytes 811016 | tf_op jit(solution)/shard_map/ppermute | solution.py:43
  33.3 32.8 %copy-start.1 = (bf16[512,5120]{1,0:T(8,128)(2,1)S(1)}, bf16[512,5120]{1,0:T(8,128)(2,1)}, u32[]{:S(2)}) copy-start(bf16[512,5120]{1,0:T(8,128)(2,1)} %w_ref.3) | copy-start | bytes 15728644
  33.3 17.7 %collective-permute-start.11 = (bf16[1,528,128]{2,1,0:T(8,128)(2,1)S(1)}, bf16[1,528,128]{2,1,0:T(8,128)(2,1)S(1)}, u32[]{:S(2)}, u32[]{:S(2)}) collective-permute-start(bf16[1,528,128]{2,1,0:T(8,128)(2,1)S(1)} %collective-permute-done.4.rest_2_), channel_id=1, source_target_pairs={{0,192},{8,200},{16,208},{24,216},{32,224},{40,232},{48,240},{56,2... | collective-permute-start | bytes 405512 | tf_op jit(solution)/shard_map/ppermute | solution.py:43
  34.9 16.1 %collective-permute-start.10 = (bf16[1,528,128]{2,1,0:T(8,128)(2,1)S(1)}, bf16[1,528,128]{2,1,0:T(8,128)(2,1)S(1)}, u32[]{:S(2)}, u32[]{:S(2)}) collective-permute-start(bf16[1,528,128]{2,1,0:T(8,128)(2,1)S(1)} %collective-permute-done.4.rest_2_), channel_id=1, source_target_pairs={{0,64},{8,72},{16,80},{24,88},{32,96},{40,104},{48,112},{56,120},{... | collective-permute-start | bytes 405512 | tf_op jit(solution)/shard_map/ppermute | solution.py:43
  42.1 16.6 %collective-permute-start.7 = (bf16[1,528,128]{2,1,0:T(8,128)(2,1)S(1)}, bf16[1,528,128]{2,1,0:T(8,128)(2,1)S(1)}, u32[]{:S(2)}, u32[]{:S(2)}) collective-permute-start(bf16[1,528,128]{2,1,0:T(8,128)(2,1)S(1)} %slice.49), channel_id=1, source_target_pairs={{128,144},{136,184},{144,160},{152,136},{160,176},{168,152},{176,1... | collective-permute-start | bytes 405512 | tf_op jit(solution)/shard_map/ppermute | solution.py:43
  63.9 2.2 %collective-permute-start.12 = (f32[528,256]{1,0:T(8,128)S(1)}, f32[528,256]{1,0:T(8,128)S(1)}, u32[]{:S(2)}, u32[]{:S(2)}) collective-permute-start(f32[528,256]{1,0:T(8,128)S(1)} %get-tuple-element.56), channel_id=1, source_target_pairs={{0,8},{8,0},{16,24},{24,16},{32,40},{40,32},{48,56},{56,48},{64,72... | collective-permute-start | bytes 1622024 | tf_op jit(solution)/shard_map/ppermute | solution.py:43
  68.5 12.8 %collective-permute-start.16 = (bf16[4,80,640]{2,1,0:T(8,128)(2,1)S(1)}, bf16[4,80,640]{2,1,0:T(8,128)(2,1)S(1)}, u32[]{:S(2)}, u32[]{:S(2)}) collective-permute-start(bf16[4,80,640]{2,1,0:T(8,128)(2,1)S(1)} %get-tuple-element.60), channel_id=1, source_target_pairs={{0,3},{1,2},{2,1},{3,0},{4,7},{5,6},{6,5},{7,4},{8,11},{9,10},{10,... | collective-permute-start | bytes 1228808 | tf_op jit(solution)/shard_map/ppermute | solution.py:296
  71.4 11.7 %collective-permute-start.19 = (bf16[4,80,640]{2,1,0:T(8,128)(2,1)S(1)}, bf16[4,80,640]{2,1,0:T(8,128)(2,1)S(1)}, u32[]{:S(2)}, u32[]{:S(2)}) collective-permute-start(bf16[4,80,640]{2,1,0:T(8,128)(2,1)S(1)} %get-tuple-element.62), channel_id=1, source_target_pairs={{0,4},{1,5},{2,6},{3,7},{4,0},{5,1},{6,2},{7,3},{8,12},{9,13},{10,... | collective-permute-start | bytes 1228808 | tf_op jit(solution)/shard_map/ppermute | solution.py:296
  72.9 13.3 %collective-permute-start.13 = (bf16[4,96,640]{2,1,0:T(8,128)(2,1)S(1)}, bf16[4,96,640]{2,1,0:T(8,128)(2,1)S(1)}, u32[]{:S(2)}, u32[]{:S(2)}) collective-permute-start(bf16[4,96,640]{2,1,0:T(8,128)(2,1)S(1)} %get-tuple-element.58), channel_id=1, source_target_pairs={{0,1},{1,0},{2,3},{3,2},{4,5},{5,4},{6,7},{7,6},{8,9},{9,8},{10,11... | collective-permute-start | bytes 1474568 | tf_op jit(solution)/shard_map/ppermute | solution.py:296
  81.5 6.4 %collective-permute-start.17 = (bf16[2,80,640]{2,1,0:T(8,128)(2,1)S(1)}, bf16[2,80,640]{2,1,0:T(8,128)(2,1)S(1)}, u32[]{:S(2)}, u32[]{:S(2)}) collective-permute-start(bf16[2,80,640]{2,1,0:T(8,128)(2,1)S(1)} %slice.106), channel_id=1, source_target_pairs={{0,4},{1,5},{2,6},{3,7},{4,0},{5,1},{6,2},{7,3},{8,12},{9,13},{10,... | collective-permute-start | bytes 614408 | tf_op jit(solution)/shard_map/ppermute | solution.py:296
  83.2 7.8 %collective-permute-start.20 = (bf16[2,80,640]{2,1,0:T(8,128)(2,1)S(1)}, bf16[2,80,640]{2,1,0:T(8,128)(2,1)S(1)}, u32[]{:S(2)}, u32[]{:S(2)}) collective-permute-start(bf16[2,80,640]{2,1,0:T(8,128)(2,1)S(1)} %slice.105), channel_id=1, source_target_pairs={{0,1},{1,0},{2,3},{3,2},{4,5},{5,4},{6,7},{7,6},{8,9},{9,8},{10,11... | collective-permute-start | bytes 614408 | tf_op jit(solution)/shard_map/ppermute | solution.py:296
  86.4 8.5 %collective-permute-start.14 = (bf16[2,96,640]{2,1,0:T(8,128)(2,1)S(1)}, bf16[2,96,640]{2,1,0:T(8,128)(2,1)S(1)}, u32[]{:S(2)}, u32[]{:S(2)}) collective-permute-start(bf16[2,96,640]{2,1,0:T(8,128)(2,1)S(1)} %slice.104), channel_id=1, source_target_pairs={{0,3},{1,2},{2,1},{3,0},{4,7},{5,6},{6,5},{7,4},{8,11},{9,10},{10,... | collective-permute-start | bytes 737288 | tf_op jit(solution)/shard_map/ppermute | solution.py:296
  87.9 4.7 %collective-permute-start.18 = (bf16[80,640]{1,0:T(8,128)(2,1)S(1)}, bf16[80,640]{1,0:T(8,128)(2,1)S(1)}, u32[]{:S(2)}, u32[]{:S(2)}) collective-permute-start(bf16[80,640]{1,0:T(8,128)(2,1)S(1)} %fusion.7), channel_id=1, source_target_pairs={{0,1},{1,0},{2,3},{3,2},{4,5},{5,4},{6,7},{7,6},{8,9},{9,8},{10,11... | collective-permute-start | bytes 307208 | tf_op jit(solution)/shard_map/ppermute | solution.py:296
  91.1 6.0 %collective-permute-start.21 = (bf16[80,640]{1,0:T(8,128)(2,1)S(1)}, bf16[80,640]{1,0:T(8,128)(2,1)S(1)}, u32[]{:S(2)}, u32[]{:S(2)}) collective-permute-start(bf16[80,640]{1,0:T(8,128)(2,1)S(1)} %fusion.8), channel_id=1, source_target_pairs={{0,3},{1,2},{2,1},{3,0},{4,7},{5,6},{6,5},{7,4},{8,11},{9,10},{10,... | collective-permute-start | bytes 307208 | tf_op jit(solution)/shard_map/ppermute | solution.py:296
  95.0 5.0 %collective-permute-start.15 = (bf16[96,640]{1,0:T(8,128)(2,1)S(1)}, bf16[96,640]{1,0:T(8,128)(2,1)S(1)}, u32[]{:S(2)}, u32[]{:S(2)}) collective-permute-start(bf16[96,640]{1,0:T(8,128)(2,1)S(1)} %fusion.6), channel_id=1, source_target_pairs={{0,4},{1,5},{2,6},{3,7},{4,0},{5,1},{6,2},{7,3},{8,12},{9,13},{10,... | collective-permute-start | bytes 368648 | tf_op jit(solution)/shard_map/ppermute | solution.py:296
  (2 other events, 2.4 us)

commit v7 on v6

--- a/solution.py
+++ b/solution.py
@@ -79,8 +79,7 @@
 
 def next_slots(y, z, c):
     d = 2 * c - 1
-    near = [[(y + e, z + d, c), (y + e, z + d, 1 - c)] for e in (-1, 1)]
-    return near + [[(y + e, z + 2, c)] for e in (-1, 1)]
+    return [[(y + e, z + d, c), (y + e, z + d, 1 - c), (y + e, z + 2, c)] for e in (-1, 1)]
 
 
 def far_slots(y, z, c):
@@ -161,25 +160,11 @@
 
 
 def more_kernel(slots, n, at_ref, *rest):
-    pieces, (q_ref, q_2_ref, s_in, s_2_in, s_ref, s_2_ref, all_ref, order_ref) = rest[:n], rest[n:]
+    pieces, (q_ref, q_2_ref, s_in, s_2_in) = rest[:n], rest[n : n + 4]
+    s_ref, s_2_ref, all_ref, order_ref = rest[-4:]
     s_ref[...] = s_in[...]
     s_2_ref[...] = s_2_in[...]
     attend_pieces(at_ref, slots, pieces, all_ref, order_ref, (q_ref, s_ref, q_2_ref, s_2_ref))
-
-
-def query_kernel(hidden_ref, w_ref, segment_ref, out_ref, normed_ref):
-    @pl.loop(0, BLOCK // 16)
-    def _(i):
-        rows = pl.ds(pl.multiple_of(i * 16, 16), 16)
-        x = hidden_ref[rows, :].astype(F32)
-        normed_ref[rows, :] = (x * lax.rsqrt(jnp.mean(x * x, axis=-1, keepdims=True) + 1e-06)).astype(BF16)
-
-    q = jnp.zeros((BLOCK, w_ref.shape[1]), F32)
-    for k in range(0, w_ref.shape[0], 1024):
-        q += jnp.dot(normed_ref[:, k : k + 1024], w_ref[k : k + 1024, :], preferred_element_type=F32)
-    out_ref[0 : 4 * HEAD_DIM, :] = jnp.transpose(q * HEAD_DIM ** (-0.5)).astype(BF16)
-    ids = lax.broadcasted_iota(jnp.int32, (HEAD_DIM, BLOCK), 0)
-    out_ref[HOT, :] = (ids == segment_ref[...]).astype(BF16)
 
 
 def last_kernel(at_ref, s_ref, s_2_ref, w_ref, *rest):
@@ -227,32 +212,28 @@
     ).astype(BF16)
     own = jnp.concatenate([k_cache, v_cache, jnp.broadcast_to(smaller[None, :], (16, HEAD_DIM))], axis=0)[None]
 
-    other = swap_cores(own)
+    own, other, hidden = lax.optimization_barrier((own, swap_cores(own), hidden))
     pair = jnp.concatenate([own, other], axis=0)
     z_near = along_z(pair)
     y_near = along_y(pair)
     y_far = move(pair, lambda y, z, c: (y + 2, z, c) if y < 2 else None)
-
-    q = pl.pallas_call(
-        query_kernel,
-        out_shape=jax.ShapeDtypeStruct((5 * HEAD_DIM, BLOCK), BF16),
-        in_specs=[VMEM] * 3,
-        out_specs=VMEM,
-        scratch_shapes=[pltpu.VMEM(hidden.shape, BF16)],
-        compiler_params=LIMIT,
-        cost_estimate=pl.CostEstimate(flops=2 * hidden.size * w_query.shape[1], bytes_accessed=8 * 10**6, transcendentals=0),
-        name="project_queries",
-    )(hidden, w_query, segment[None, :])
-
-    (z_near, y_near), q = lax.optimization_barrier(((z_near, y_near), q))
+    z_far = move(own, lambda y, z, c: (y, z + 2, c))
+
+    widened = hidden.astype(F32)
+    normed = (widened * lax.rsqrt(jnp.mean(widened * widened, axis=-1, keepdims=True) + 1e-06)).astype(BF16)
+    q_t = (
+        lax.dot_general(w_query, normed, (((0,), (1,)), ((), ())), preferred_element_type=F32) * HEAD_DIM ** (-0.5)
+    ).astype(BF16)
+    hot = (jnp.arange(HEAD_DIM, dtype=jnp.int32)[:, None] == segment[None, :]).astype(BF16)
+    q = jnp.concatenate([q_t, hot], axis=0)
+
+    (z_near, z_far, y_near, y_far), q = lax.optimization_barrier(((z_near, z_far, y_near, y_far), q))
+    row = jnp.concatenate([z_near, z_far], axis=0)
+    up = up_y(row)
+    around = round_y(row)
+    far_near = along_z(y_far, 2)
+    far_far = move(y_far[:1], lambda y, z, c: (y, z + 2, c) if y >= 2 else None)
     q_2 = swap_cores(q)
-    z_far = along_z(z_near[:1])
-    up_near = up_y(z_near)
-    around_near = round_y(z_near)
-    y_far, z_far = lax.optimization_barrier((y_far, z_far))
-    up_far = up_y(z_far)
-    around_far = round_y(z_far)
-    far_near = along_z(y_far, 2)
 
     at = jnp.stack([ctx, lax.axis_index("section")]).astype(jnp.int32)
 
@@ -269,12 +250,9 @@
         )(at, *pieces, q, q_2, *state)
 
     state = attend(start_kernel, first_slots, 7, [own, z_near, z_far, y_near, y_far], (), "attend_first")
-    far_near, state = lax.optimization_barrier((far_near, state))
-    far_far = along_z(far_near[:1], 2)
-    nexts = (up_near, around_near, up_far, around_far)
-    nexts, state = lax.optimization_barrier((nexts, state))
-    state = attend(more_kernel, next_slots, 6, nexts, state, "attend_next")
-    far_far, state = lax.optimization_barrier((far_far, state))
+    (up, around), state = lax.optimization_barrier(((up, around), state))
+    state = attend(more_kernel, next_slots, 6, [up, around], (*state, w_out), "attend_next")
+    (far_near, far_far), state = lax.optimization_barrier(((far_near, far_far), state))
     state, state_2 = attend(more_kernel, far_slots, 3, [far_near, far_far], state, "attend_far")
     state_2 = swap_cores(state_2)
 

time: 101 us -> 96.8 us (0.958)
  waiting for transfers between devices: 31.2 us -> 25 us
  matrix products: 0 us -> 5.58 us
  Pallas kernels: 25.1 us -> 21.7 us
  starting transfers between devices: 36 us -> 32.6 us
  other arithmetic: 3.05 us -> 6.07 us
    ppermute x13 -> x11, waiting for transfers between devices: 9.35 us -> 3.66 us  [move(): return lax.ppermute(x, 'ctx', ctx_pairs(step))]
    dot_general x0 -> x1, matrix products: none -> 5.58 us  [per_device(): lax.dot_general(w_query, normed, (((0,), (1,)), ((), ())), preferred_elem...]
    pallas_call x1 -> x0, Pallas kernels: 3.99 us -> none  [per_device(): pl.pallas_call(query_kernel, out_shape=jax.ShapeDtypeStruct((5 * HEAD_DIM...]
    ppermute x13 -> x11, starting transfers between devices: 27.2 us -> 24.4 us  [move(): return lax.ppermute(x, 'ctx', ctx_pairs(step))]
    reduce_sum x0 -> x1, other arithmetic: none -> 2.34 us  [per_device(): jnp.mean(widened * widened, axis=-1, keepdims=True) + 1e-06]
    unnamed x8 -> x12, local copies, waits for them, and re-layouts: 4.91 us -> 4.25 us
  transfers between devices with their start and end apart: 22 -> 20, of which waited for: 11 -> 11; matrix products, arithmetic and copies ran while one was open for 1% -> 10% of each run, Pallas kernels for 17% -> 14%
where the time goes in v7:
time: 96.8 us; the launch traced here: 96.4 us
  starting transfers between devices  32.6 us (34%)
  waiting for transfers between devices  25 us (26%)
  Pallas kernels  21.7 us (22%)
  other arithmetic  6.07 us (6%)
  matrix products  5.58 us (6%)
  local copies, waits for them, and re-layouts  5.07 us (5%)
    ppermute x11, starting transfers between devices, move(): return lax.ppermute(x, 'ctx', ctx_pairs(step))  24.4 us
    ppermute x9, waiting for transfers between devices, exchange(): return lax.ppermute(x, 'section', [(i, i ^ step) for i in range(8)])  21.3 us
    pallas_call x3, Pallas kernels, attend(): pl.pallas_call(functools.partial(kernel, slots, len(pieces)), out_shape=(...  19.2 us
    ppermute x9, starting transfers between devices, exchange(): return lax.ppermute(x, 'section', [(i, i ^ step) for i in range(8)])  8.26 us
    dot_general x1, matrix products, per_device(): lax.dot_general(w_query, normed, (((0,), (1,)), ((), ())), preferred_elem...  5.58 us
    unnamed x12, local copies, waits for them, and re-layouts  4.25 us
    ppermute x11, waiting for transfers between devices, move(): return lax.ppermute(x, 'ctx', ctx_pairs(step))  3.66 us
    pallas_call x1, Pallas kernels, per_device(): pl.pallas_call(last_kernel, out_shape=tuple(out_shape), in_specs=[SMEM] +...  2.5 us
  transfers between devices with their start and end apart: 20, of which 11 were waited for; matrix products, arithmetic and copies ran while one was open for 10% of the time, Pallas kernels for 14%

profile of v7, /device:TPU:24, one launch (start us, length us, event | category | flops | bytes accessed | tf_op | source)
XLA Modules:
  0.0 96.4 jit_solution(4805422582851774184)
XLA Ops:
  3.2 3.3 %collective-permute-start.1 = (bf16[2,528,128]{2,1,0:T(8,128)(2,1)S(1)}, bf16[2,528,128]{2,1,0:T(8,128)(2,1)S(1)}, u32[]{:S(2)}, u32[]{:S(2)}) collective-permute-start(bf16[2,528,128]{2,1,0:T(8,128)(2,1)S(1)} %constant_dynamic-update-slice_fusion), channel_id=1, source_target_pairs={{0,16},{8,56},{16,32},{24,8},{32,48},{40,24},{48,0},{56,40},{64,80... | collective-permute-start | bytes 811016 | tf_op jit(solution)/shard_map/ppermute | solution.py:43
  6.5 1.3 %collective-permute-start.3 = (bf16[2,528,128]{2,1,0:T(8,128)(2,1)S(1)}, bf16[2,528,128]{2,1,0:T(8,128)(2,1)S(1)}, u32[]{:S(2)}, u32[]{:S(2)}) collective-permute-start(bf16[2,528,128]{2,1,0:T(8,128)(2,1)S(1)} %constant_dynamic-update-slice_fusion), channel_id=1, source_target_pairs={{0,64},{8,200},{16,80},{24,216},{32,96},{40,232},{48,112},{56,248}... | collective-permute-start | bytes 811016 | tf_op jit(solution)/shard_map/ppermute | solution.py:43
  7.8 1.3 %collective-permute-start.4 = (bf16[2,528,128]{2,1,0:T(8,128)(2,1)S(1)}, bf16[2,528,128]{2,1,0:T(8,128)(2,1)S(1)}, u32[]{:S(2)}, u32[]{:S(2)}) collective-permute-start(bf16[2,528,128]{2,1,0:T(8,128)(2,1)S(1)} %constant_dynamic-update-slice_fusion), channel_id=1, source_target_pairs={{0,128},{8,136},{16,144},{24,152},{32,160},{40,168},{48,176},{56,1... | collective-permute-start | bytes 811016 | tf_op jit(solution)/shard_map/ppermute | solution.py:43
  9.1 5.5 %collective-permute-start.2 = (bf16[1,528,128]{2,1,0:T(8,128)(2,1)S(1)}, bf16[1,528,128]{2,1,0:T(8,128)(2,1)S(1)}, u32[]{:S(2)}, u32[]{:S(2)}) collective-permute-start(bf16[1,528,128]{2,1,0:T(8,128)(2,1)S(1)} %maximum_bitcast_fusion.rest_0_), channel_id=1, source_target_pairs={{0,32},{8,40},{16,48},{24,56},{32,0},{40,8},{48,16},{56,24},{64,96... | collective-permute-start | bytes 405512 | tf_op jit(solution)/shard_map/ppermute | solution.py:43
  14.6 2.3 %fusion = f32[256]{0:T(256)S(1)} fusion(bf16[256,5120]{1,0:T(8,128)(2,1)} %param.6), kind=kLoop, calls=%fused_computation.2 | loop fusion | flops 3931904 | bytes 2622464 | tf_op jit(solution)/shard_map/reduce_sum | solution.py:223
  16.9 5.6 %fusion.11 = bf16[512,256]{1,0:T(8,128)(2,1)S(1)} fusion(bf16[5120,512]{1,0:T(8,128)(2,1)} %param.10, bf16[256,5120]{1,0:T(8,128)(2,1)} %param.6, f32[256]{0:T(256)S(1)} %add_rsqrt_fusion), kind=kOutput, calls=%fused_computation.8 | convolution fusion | flops 1346371584 | bytes 8127488 | tf_op jit(solution)/shard_map/dot_general | solution.py:225
  25.1 1.3 %collective-permute-start.7 = (bf16[3,528,128]{2,1,0:T(8,128)(2,1)}, bf16[3,528,128]{2,1,0:T(8,128)(2,1)S(1)}, u32[]{:S(2)}, u32[]{:S(2)}) collective-permute-start(bf16[3,528,128]{2,1,0:T(8,128)(2,1)} %constant_dynamic-update-slice_fusion.2), channel_id=1, source_target_pairs={{0,64},{8,72},{16,80},{24,88},{32,96},{40,104},{48,112},{56,120},{... | collective-permute-start | bytes 1216520 | tf_op jit(solution)/shard_map/ppermute | solution.py:43
  26.4 1.3 %collective-permute-start.8 = (bf16[3,528,128]{2,1,0:T(8,128)(2,1)}, bf16[3,528,128]{2,1,0:T(8,128)(2,1)S(1)}, u32[]{:S(2)}, u32[]{:S(2)}) collective-permute-start(bf16[3,528,128]{2,1,0:T(8,128)(2,1)} %constant_dynamic-update-slice_fusion.2), channel_id=1, source_target_pairs={{0,192},{8,200},{16,208},{24,216},{32,224},{40,232},{48,240},{56,2... | collective-permute-start | bytes 1216520 | tf_op jit(solution)/shard_map/ppermute | solution.py:43
  27.8 2.2 %collective-permute-start.5 = (bf16[2,528,128]{2,1,0:T(8,128)(2,1)S(1)}, bf16[2,528,128]{2,1,0:T(8,128)(2,1)}, u32[]{:S(2)}, u32[]{:S(2)}) collective-permute-start(bf16[2,528,128]{2,1,0:T(8,128)(2,1)S(1)} %collective-permute-done.4.rest_4_), channel_id=1, source_target_pairs={{128,144},{136,184},{144,160},{152,136},{160,176},{168,152},{176,1... | collective-permute-start | bytes 811016 | tf_op jit(solution)/shard_map/ppermute | solution.py:43
  30.1 7.9 %collective-permute-start.6 = (bf16[1,528,128]{2,1,0:T(8,128)(2,1)S(1)}, bf16[1,528,128]{2,1,0:T(8,128)(2,1)S(1)}, u32[]{:S(2)}, u32[]{:S(2)}) collective-permute-start(bf16[1,528,128]{2,1,0:T(8,128)(2,1)S(1)} %slice.45), channel_id=1, source_target_pairs={{128,160},{136,168},{144,176},{152,184},{160,128},{168,136},{176,1... | collective-permute-start | bytes 405512 | tf_op jit(solution)/shard_map/ppermute | solution.py:43
  39.0 5.8 %attend_first.1 = (f32[528,256]{1,0:T(8,128)S(1)}, f32[528,256]{1,0:T(8,128)S(1)}) custom-call(s32[2]{0:T(128)S(1)} %pad_add_fusion.at_ref, bf16[1,528,128]{2,1,0:T(8,128)(2,1)S(1)} %maximum_bitcast_fusion.rest_0_, bf16[2,528,128]{2,1,0:T(8,128)(2,1)S(1)} %collective-permute-done.1.rest_1_, bf16[1,528,128]{2,1,0:T(8,128)(2,1)S(1)} %collective-permute-done.2.rest_2_, ...), custom_call_target="tpu_custom_call" | custom-call | flops 134217728 | bytes 135168 | tf_op jit(solution)/shard_map/attend_first/pallas_call | solution.py:241
  44.8 2.5 %copy-done = bf16[512,5120]{1,0:T(8,128)(2,1)S(1)} copy-done((bf16[512,5120]{1,0:T(8,128)(2,1)S(1)}, bf16[512,5120]{1,0:T(8,128)(2,1)}, u32[]{:S(2)}) %copy-start) | copy-done | bytes 5242904
  47.3 7.6 %attend_next.1 = (f32[528,256]{1,0:T(8,128)S(1)}, f32[528,256]{1,0:T(8,128)S(1)}) custom-call(s32[2]{0:T(128)S(1)} %pad_add_fusion.at_ref, bf16[3,528,128]{2,1,0:T(8,128)(2,1)S(1)} %collective-permute-done.7.rest_0_, bf16[3,528,128]{2,1,0:T(8,128)(2,1)S(1)} %collective-permute-done.8.rest_1_, bf16[640,256]{1,0:T(8,128)(2,1)S(1)} %pad_maximum_fusion.rest_5_.rest_2_, ...), custom_call_target="tpu_custom_call" | custom-call | flops 134217728 | bytes 135168 | tf_op jit(solution)/shard_map/attend_next/pallas_call | solution.py:241
  55.0 5.9 %attend_far.1 = (f32[528,256]{1,0:T(8,128)S(1)}, f32[528,256]{1,0:T(8,128)S(1)}) custom-call(s32[2]{0:T(128)S(1)} %pad_add_fusion.at_ref, bf16[2,528,128]{2,1,0:T(8,128)(2,1)} %collective-permute-done.5.rest_0_, bf16[1,528,128]{2,1,0:T(8,128)(2,1)S(1)} %collective-permute-done.6.rest_1_, bf16[640,256]{1,0:T(8,128)(2,1)S(1)} %pad_maximum_fusion.rest_5_.rest_2_, ...), custom_call_target="tpu_custom_call" | custom-call | flops 134217728 | bytes 135168 | tf_op jit(solution)/shard_map/attend_far/pallas_call | solution.py:241
  60.9 1.9 %collective-permute-done.10.s_2_ref = f32[528,256]{1,0:T(8,128)S(1)} collective-permute-done((f32[528,256]{1,0:T(8,128)S(1)}, f32[528,256]{1,0:T(8,128)S(1)}, u32[]{:S(2)}, u32[]{:S(2)}) %collective-permute-start.10) | collective-permute-done | bytes 540704 | tf_op jit(solution)/shard_map/ppermute | solution.py:43
  62.8 2.5 %project_attended.1 = (bf16[4,96,640]{2,1,0:T(8,128)(2,1)S(1)}, bf16[4,96,640]{2,1,0:T(8,128)(2,1)S(1)}, bf16[4,80,640]{2,1,0:T(8,128)(2,1)S(1)}, bf16[4,80,640]...) custom-call(s32[2]{0:T(128)S(1)} %pad_add_fusion.at_ref, ...), custom_call_target="tpu_custom_call" | custom-call | flops 1610612736 | bytes 1622016 | tf_op jit(solution)/shard_map/project_attended/pallas_call | solution.py:262
  65.3 2.8 %collective-permute-start.14 = (bf16[4,80,640]{2,1,0:T(8,128)(2,1)S(1)}, bf16[4,80,640]{2,1,0:T(8,128)(2,1)S(1)}, u32[]{:S(2)}, u32[]{:S(2)}) collective-permute-start(bf16[4,80,640]{2,1,0:T(8,128)(2,1)S(1)} %get-tuple-element.58), channel_id=1, source_target_pairs={{0,3},{1,2},{2,1},{3,0},{4,7},{5,6},{6,5},{7,4},{8,11},{9,10},{10,... | collective-permute-start | bytes 1228808 | tf_op jit(solution)/shard_map/ppermute | solution.py:274
  68.4 9.7 %collective-permute-done.14 = bf16[4,80,640]{2,1,0:T(8,128)(2,1)S(1)} collective-permute-done((bf16[4,80,640]{2,1,0:T(8,128)(2,1)S(1)}, bf16[4,80,640]{2,1,0:T(8,128)(2,1)S(1)}, u32[]{:S(2)}, u32[]{:S(2)}) %collective-permute-start.14) | collective-permute-done | bytes 409632 | tf_op jit(solution)/shard_map/ppermute | solution.py:274
  79.8 1.3 %collective-permute-done.11 = bf16[4,96,640]{2,1,0:T(8,128)(2,1)S(1)} collective-permute-done((bf16[4,96,640]{2,1,0:T(8,128)(2,1)S(1)}, bf16[4,96,640]{2,1,0:T(8,128)(2,1)S(1)}, u32[]{:S(2)}, u32[]{:S(2)}) %collective-permute-start.11) | collective-permute-done | bytes 491552 | tf_op jit(solution)/shard_map/ppermute | solution.py:274
  81.9 2.8 %collective-permute-done.15 = bf16[2,80,640]{2,1,0:T(8,128)(2,1)S(1)} collective-permute-done((bf16[2,80,640]{2,1,0:T(8,128)(2,1)S(1)}, bf16[2,80,640]{2,1,0:T(8,128)(2,1)S(1)}, u32[]{:S(2)}, u32[]{:S(2)}) %collective-permute-start.15) | collective-permute-done | bytes 204832 | tf_op jit(solution)/shard_map/ppermute | solution.py:274
  85.7 2.1 %collective-permute-start.19 = (bf16[80,640]{1,0:T(8,128)(2,1)S(1)}, bf16[80,640]{1,0:T(8,128)(2,1)S(1)}, u32[]{:S(2)}, u32[]{:S(2)}) collective-permute-start(bf16[80,640]{1,0:T(8,128)(2,1)S(1)} %fusion.23), channel_id=1, source_target_pairs={{0,3},{1,2},{2,1},{3,0},{4,7},{5,6},{6,5},{7,4},{8,11},{9,10},{10,... | collective-permute-start | bytes 307208 | tf_op jit(solution)/shard_map/ppermute | solution.py:274
  87.8 1.7 %collective-permute-done.16 = bf16[80,640]{1,0:T(8,128)(2,1)S(1)} collective-permute-done((bf16[80,640]{1,0:T(8,128)(2,1)S(1)}, bf16[80,640]{1,0:T(8,128)(2,1)S(1)}, u32[]{:S(2)}, u32[]{:S(2)}) %collective-permute-start.16) | collective-permute-done | bytes 102432 | tf_op jit(solution)/shard_map/ppermute | solution.py:274
  90.7 1.8 %collective-permute-start.13 = (bf16[96,640]{1,0:T(8,128)(2,1)S(1)}, bf16[96,640]{1,0:T(8,128)(2,1)S(1)}, u32[]{:S(2)}, u32[]{:S(2)}) collective-permute-start(bf16[96,640]{1,0:T(8,128)(2,1)S(1)} %fusion.21), channel_id=1, source_target_pairs={{0,4},{1,5},{2,6},{3,7},{4,0},{5,1},{6,2},{7,3},{8,12},{9,13},{10,... | collective-permute-start | bytes 368648 | tf_op jit(solution)/shard_map/ppermute | solution.py:274
  92.4 3.2 %collective-permute-done.13 = bf16[96,640]{1,0:T(8,128)(2,1)S(1)} collective-permute-done((bf16[96,640]{1,0:T(8,128)(2,1)S(1)}, bf16[96,640]{1,0:T(8,128)(2,1)S(1)}, u32[]{:S(2)}, u32[]{:S(2)}) %collective-permute-start.13) | collective-permute-done | bytes 122912 | tf_op jit(solution)/shard_map/ppermute | solution.py:274
  (61 shorter events, 12.5 us)
Async XLA Ops:
  1.7 1.4 %collective-permute-start = (bf16[1,528,128]{2,1,0:T(8,128)(2,1)S(1)}, bf16[1,528,128]{2,1,0:T(8,128)(2,1)S(1)}, u32[]{:S(2)}, u32[]{:S(2)}) collective-permute-start(bf16[1,528,128]{2,1,0:T(8,128)(2,1)S(1)} %maximum_bitcast_fusion.rest_0_), channel_id=1, source_target_pairs={{0,8},{8,0},{16,24},{24,16},{32,40},{40,32},{48,56},{56,48},{64,72... | collective-permute-start | bytes 405512 | tf_op jit(solution)/shard_map/ppermute | solution.py:43
  3.2 20.5 %collective-permute-start.1 = (bf16[2,528,128]{2,1,0:T(8,128)(2,1)S(1)}, bf16[2,528,128]{2,1,0:T(8,128)(2,1)S(1)}, u32[]{:S(2)}, u32[]{:S(2)}) collective-permute-start(bf16[2,528,128]{2,1,0:T(8,128)(2,1)S(1)} %constant_dynamic-update-slice_fusion), channel_id=1, source_target_pairs={{0,16},{8,56},{16,32},{24,8},{32,48},{40,24},{48,0},{56,40},{64,80... | collective-permute-start | bytes 811016 | tf_op jit(solution)/shard_map/ppermute | solution.py:43
  6.5 17.1 %collective-permute-start.3 = (bf16[2,528,128]{2,1,0:T(8,128)(2,1)S(1)}, bf16[2,528,128]{2,1,0:T(8,128)(2,1)S(1)}, u32[]{:S(2)}, u32[]{:S(2)}) collective-permute-start(bf16[2,528,128]{2,1,0:T(8,128)(2,1)S(1)} %constant_dynamic-update-slice_fusion), channel_id=1, source_target_pairs={{0,64},{8,200},{16,80},{24,216},{32,96},{40,232},{48,112},{56,248}... | collective-permute-start | bytes 811016 | tf_op jit(solution)/shard_map/ppermute | solution.py:43
  7.8 15.8 %collective-permute-start.4 = (bf16[2,528,128]{2,1,0:T(8,128)(2,1)S(1)}, bf16[2,528,128]{2,1,0:T(8,128)(2,1)S(1)}, u32[]{:S(2)}, u32[]{:S(2)}) collective-permute-start(bf16[2,528,128]{2,1,0:T(8,128)(2,1)S(1)} %constant_dynamic-update-slice_fusion), channel_id=1, source_target_pairs={{0,128},{8,136},{16,144},{24,152},{32,160},{40,168},{48,176},{56,1... | collective-permute-start | bytes 811016 | tf_op jit(solution)/shard_map/ppermute | solution.py:43
  9.1 14.5 %collective-permute-start.2 = (bf16[1,528,128]{2,1,0:T(8,128)(2,1)S(1)}, bf16[1,528,128]{2,1,0:T(8,128)(2,1)S(1)}, u32[]{:S(2)}, u32[]{:S(2)}) collective-permute-start(bf16[1,528,128]{2,1,0:T(8,128)(2,1)S(1)} %maximum_bitcast_fusion.rest_0_), channel_id=1, source_target_pairs={{0,32},{8,40},{16,48},{24,56},{32,0},{40,8},{48,16},{56,24},{64,96... | collective-permute-start | bytes 405512 | tf_op jit(solution)/shard_map/ppermute | solution.py:43
  23.6 2.8 %copy-start.1 = (bf16[2,528,128]{2,1,0:T(8,128)(2,1)}, bf16[2,528,128]{2,1,0:T(8,128)(2,1)S(1)}, u32[]{:S(2)}) copy-start(bf16[2,528,128]{2,1,0:T(8,128)(2,1)S(1)} %collective-permute-done.3.rest_3_) | copy-start | bytes 811012
  24.5 38.4 %slice-start = ((s8[5242880]{0:T(1024)(128)(4,1)}), s8[1048576]{0:T(1024)(128)(4,1)S(1)}, s32[]{:S(2)}) async-start(s8[5242880]{0:T(1024)(128)(4,1)} %bitcast.31), calls=%async_computation | async-start | bytes 2097152
  25.1 19.7 %collective-permute-start.7 = (bf16[3,528,128]{2,1,0:T(8,128)(2,1)}, bf16[3,528,128]{2,1,0:T(8,128)(2,1)S(1)}, u32[]{:S(2)}, u32[]{:S(2)}) collective-permute-start(bf16[3,528,128]{2,1,0:T(8,128)(2,1)} %constant_dynamic-update-slice_fusion.2), channel_id=1, source_target_pairs={{0,64},{8,72},{16,80},{24,88},{32,96},{40,104},{48,112},{56,120},{... | collective-permute-start | bytes 1216520 | tf_op jit(solution)/shard_map/ppermute | solution.py:43
  26.4 18.4 %collective-permute-start.8 = (bf16[3,528,128]{2,1,0:T(8,128)(2,1)}, bf16[3,528,128]{2,1,0:T(8,128)(2,1)S(1)}, u32[]{:S(2)}, u32[]{:S(2)}) collective-permute-start(bf16[3,528,128]{2,1,0:T(8,128)(2,1)} %constant_dynamic-update-slice_fusion.2), channel_id=1, source_target_pairs={{0,192},{8,200},{16,208},{24,216},{32,224},{40,232},{48,240},{56,2... | collective-permute-start | bytes 1216520 | tf_op jit(solution)/shard_map/ppermute | solution.py:43
  27.7 10.4 %collective-permute-start.9 = (bf16[640,256]{1,0:T(8,128)(2,1)S(1)}, bf16[640,256]{1,0:T(8,128)(2,1)S(1)}, u32[]{:S(2)}, u32[]{:S(2)}) collective-permute-start(bf16[640,256]{1,0:T(8,128)(2,1)S(1)} %pad_maximum_fusion.rest_5_.rest_2_), channel_id=1, source_target_pairs={{0,8},{8,0},{16,24},{24,16},{32,40},{40,32},{48,56},{56,48},{64,72... | collective-permute-start | bytes 983048 | tf_op jit(solution)/shard_map/ppermute | solution.py:43
  27.8 27.1 %collective-permute-start.5 = (bf16[2,528,128]{2,1,0:T(8,128)(2,1)S(1)}, bf16[2,528,128]{2,1,0:T(8,128)(2,1)}, u32[]{:S(2)}, u32[]{:S(2)}) collective-permute-start(bf16[2,528,128]{2,1,0:T(8,128)(2,1)S(1)} %collective-permute-done.4.rest_4_), channel_id=1, source_target_pairs={{128,144},{136,184},{144,160},{152,136},{160,176},{168,152},{176,1... | collective-permute-start | bytes 811016 | tf_op jit(solution)/shard_map/ppermute | solution.py:43
  30.1 24.9 %collective-permute-start.6 = (bf16[1,528,128]{2,1,0:T(8,128)(2,1)S(1)}, bf16[1,528,128]{2,1,0:T(8,128)(2,1)S(1)}, u32[]{:S(2)}, u32[]{:S(2)}) collective-permute-start(bf16[1,528,128]{2,1,0:T(8,128)(2,1)S(1)} %slice.45), channel_id=1, source_target_pairs={{128,160},{136,168},{144,176},{152,184},{160,128},{168,136},{176,1... | collective-permute-start | bytes 405512 | tf_op jit(solution)/shard_map/ppermute | solution.py:43
  44.8 2.5 %copy-start = (bf16[512,5120]{1,0:T(8,128)(2,1)S(1)}, bf16[512,5120]{1,0:T(8,128)(2,1)}, u32[]{:S(2)}) copy-start(bf16[512,5120]{1,0:T(8,128)(2,1)} %w_ref.1) | copy-start | bytes 15728644
  47.3 15.5 %slice-start.1 = ((s8[5242880]{0:T(1024)(128)(4,1)}), s8[4194304]{0:T(1024)(128)(4,1)S(1)}, s32[]{:S(2)}) async-start(s8[5242880]{0:T(1024)(128)(4,1)} %bitcast.31), calls=%async_computation.1 | async-start | bytes 8388608
  60.8 2.0 %collective-permute-start.10 = (f32[528,256]{1,0:T(8,128)S(1)}, f32[528,256]{1,0:T(8,128)S(1)}, u32[]{:S(2)}, u32[]{:S(2)}) collective-permute-start(f32[528,256]{1,0:T(8,128)S(1)} %get-tuple-element.54), channel_id=1, source_target_pairs={{0,8},{8,0},{16,24},{24,16},{32,40},{40,32},{48,56},{56,48},{64,72... | collective-permute-start | bytes 1622024 | tf_op jit(solution)/shard_map/ppermute | solution.py:43
  65.3 12.8 %collective-permute-start.14 = (bf16[4,80,640]{2,1,0:T(8,128)(2,1)S(1)}, bf16[4,80,640]{2,1,0:T(8,128)(2,1)S(1)}, u32[]{:S(2)}, u32[]{:S(2)}) collective-permute-start(bf16[4,80,640]{2,1,0:T(8,128)(2,1)S(1)} %get-tuple-element.58), channel_id=1, source_target_pairs={{0,3},{1,2},{2,1},{3,0},{4,7},{5,6},{6,5},{7,4},{8,11},{9,10},{10,... | collective-permute-start | bytes 1228808 | tf_op jit(solution)/shard_map/ppermute | solution.py:274
  68.2 11.2 %collective-permute-start.17 = (bf16[4,80,640]{2,1,0:T(8,128)(2,1)S(1)}, bf16[4,80,640]{2,1,0:T(8,128)(2,1)S(1)}, u32[]{:S(2)}, u32[]{:S(2)}) collective-permute-start(bf16[4,80,640]{2,1,0:T(8,128)(2,1)S(1)} %get-tuple-element.60), channel_id=1, source_target_pairs={{0,4},{1,5},{2,6},{3,7},{4,0},{5,1},{6,2},{7,3},{8,12},{9,13},{10,... | collective-permute-start | bytes 1228808 | tf_op jit(solution)/shard_map/ppermute | solution.py:274
  68.2 13.0 %collective-permute-start.11 = (bf16[4,96,640]{2,1,0:T(8,128)(2,1)S(1)}, bf16[4,96,640]{2,1,0:T(8,128)(2,1)S(1)}, u32[]{:S(2)}, u32[]{:S(2)}) collective-permute-start(bf16[4,96,640]{2,1,0:T(8,128)(2,1)S(1)} %get-tuple-element.56), channel_id=1, source_target_pairs={{0,1},{1,0},{2,3},{3,2},{4,5},{5,4},{6,7},{7,6},{8,9},{9,8},{10,11... | collective-permute-start | bytes 1474568 | tf_op jit(solution)/shard_map/ppermute | solution.py:274
  78.3 6.4 %collective-permute-start.15 = (bf16[2,80,640]{2,1,0:T(8,128)(2,1)S(1)}, bf16[2,80,640]{2,1,0:T(8,128)(2,1)S(1)}, u32[]{:S(2)}, u32[]{:S(2)}) collective-permute-start(bf16[2,80,640]{2,1,0:T(8,128)(2,1)S(1)} %slice.102), channel_id=1, source_target_pairs={{0,4},{1,5},{2,6},{3,7},{4,0},{5,1},{6,2},{7,3},{8,12},{9,13},{10,... | collective-permute-start | bytes 614408 | tf_op jit(solution)/shard_map/ppermute | solution.py:274
  79.5 6.1 %collective-permute-start.18 = (bf16[2,80,640]{2,1,0:T(8,128)(2,1)S(1)}, bf16[2,80,640]{2,1,0:T(8,128)(2,1)S(1)}, u32[]{:S(2)}, u32[]{:S(2)}) collective-permute-start(bf16[2,80,640]{2,1,0:T(8,128)(2,1)S(1)} %slice.101), channel_id=1, source_target_pairs={{0,1},{1,0},{2,3},{3,2},{4,5},{5,4},{6,7},{7,6},{8,9},{9,8},{10,11... | collective-permute-start | bytes 614408 | tf_op jit(solution)/shard_map/ppermute | solution.py:274
  81.3 9.2 %collective-permute-start.12 = (bf16[2,96,640]{2,1,0:T(8,128)(2,1)S(1)}, bf16[2,96,640]{2,1,0:T(8,128)(2,1)S(1)}, u32[]{:S(2)}, u32[]{:S(2)}) collective-permute-start(bf16[2,96,640]{2,1,0:T(8,128)(2,1)S(1)} %slice.100), channel_id=1, source_target_pairs={{0,3},{1,2},{2,1},{3,0},{4,7},{5,6},{6,5},{7,4},{8,11},{9,10},{10,... | collective-permute-start | bytes 737288 | tf_op jit(solution)/shard_map/ppermute | solution.py:274
  84.7 4.7 %collective-permute-start.16 = (bf16[80,640]{1,0:T(8,128)(2,1)S(1)}, bf16[80,640]{1,0:T(8,128)(2,1)S(1)}, u32[]{:S(2)}, u32[]{:S(2)}) collective-permute-start(bf16[80,640]{1,0:T(8,128)(2,1)S(1)} %fusion.22), channel_id=1, source_target_pairs={{0,1},{1,0},{2,3},{3,2},{4,5},{5,4},{6,7},{7,6},{8,9},{9,8},{10,11... | collective-permute-start | bytes 307208 | tf_op jit(solution)/shard_map/ppermute | solution.py:274
  85.7 6.7 %collective-permute-start.19 = (bf16[80,640]{1,0:T(8,128)(2,1)S(1)}, bf16[80,640]{1,0:T(8,128)(2,1)S(1)}, u32[]{:S(2)}, u32[]{:S(2)}) collective-permute-start(bf16[80,640]{1,0:T(8,128)(2,1)S(1)} %fusion.23), channel_id=1, source_target_pairs={{0,3},{1,2},{2,1},{3,0},{4,7},{5,6},{6,5},{7,4},{8,11},{9,10},{10,... | collective-permute-start | bytes 307208 | tf_op jit(solution)/shard_map/ppermute | solution.py:274
  90.7 5.0 %collective-permute-start.13 = (bf16[96,640]{1,0:T(8,128)(2,1)S(1)}, bf16[96,640]{1,0:T(8,128)(2,1)S(1)}, u32[]{:S(2)}, u32[]{:S(2)}) collective-permute-start(bf16[96,640]{1,0:T(8,128)(2,1)S(1)} %fusion.21), channel_id=1, source_target_pairs={{0,4},{1,5},{2,6},{3,7},{4,0},{5,1},{6,2},{7,3},{8,12},{9,13},{10,... | collective-permute-start | bytes 368648 | tf_op jit(solution)/shard_map/ppermute | solution.py:274
  (1 other events, 1.0 us)

commit v8 on v7

--- a/solution.py
+++ b/solution.py
@@ -12,7 +12,8 @@
 HEAD_DIM = 128
 BLOCK = 256
 PACK = 2 * BLOCK + 16
-CHAINS = ((slice(0, 96), (1, 3, 4)), (slice(96, 176), (3, 4, 1)), (slice(176, 256), (4, 1, 3)))
+CHAINS = ((slice(0, 80), (1, 3, 4)), (slice(80, 176), (3, 4, 1)), (slice(176, 256), (4, 1, 3)))
+SIDES = tuple(itertools.product((0, 1), repeat=3))
 REACH = 24
 COLS = 640
 TOP, SUM = 4 * HEAD_DIM, 4 * HEAD_DIM + 8
@@ -22,6 +23,10 @@
 
 F32 = jnp.float32
 BF16 = jnp.bfloat16
+
+
+def away(sides):
+    return sum(step * side for step, side in zip((1, 3, 4), sides)) if sides[:2] != (1, 1) else 2 + 4 * sides[2]
 
 
 def ctx_id(y, z, c):
@@ -77,26 +82,22 @@
     return row + [[(y + d, z, c), (y + d, z, 1 - c)], [(y + 2, z, c)]]
 
 
-def next_slots(y, z, c):
+def rest_slots(y, z, c):
     d = 2 * c - 1
-    return [[(y + e, z + d, c), (y + e, z + d, 1 - c), (y + e, z + 2, c)] for e in (-1, 1)]
-
-
-def far_slots(y, z, c):
-    d = 2 * c - 1
-    return [[(y + 2, z + d, c), (y + 2, z + d, 1 - c)], [(y + 2, z + 2, c)]]
+    near = [[(y + e, z + d, c), (y + e, z + d, 1 - c), (y + e, z + 2, c)] for e in (-1, 1)]
+    return near + [[(y + 2, z + d, c), (y + 2, z + d, 1 - c)], [(y + 2, z + 2, c)]]
 
 
 def attend_blocks(kv_ref, places, diagonal, q_ref, state_ref):
     heads = [slice(h * HEAD_DIM, (h + 1) * HEAD_DIM) for h in range(4)]
     keys, values, visible = [], [], []
-    for at, low in places:
+    for at in places:
         keys.append(kv_ref[at, 0:BLOCK, :])
         values.append(jnp.transpose(kv_ref[at, BLOCK : 2 * BLOCK, :]))
         counts = kv_ref[at, 2 * BLOCK : PACK, :]
         first = jnp.dot(counts, q_ref[HOT, :], preferred_element_type=F32)[0:1, :].astype(jnp.int32)
         row = lax.broadcasted_iota(jnp.int32, (BLOCK, BLOCK), 0)
-        seen = row >= jnp.maximum(first, low)
+        seen = row >= first
         if diagonal:
             seen &= row <= lax.broadcasted_iota(jnp.int32, (BLOCK, BLOCK), 1)
         visible.append(seen)
@@ -128,26 +129,27 @@
     return own // 8, (own // 2) % 4, own % 2
 
 
-def attend_pieces(at_ref, slots, piece_refs, all_ref, order_ref, sets):
+def attend_pieces(at_ref, slots, piece_refs, all_ref, order_ref, sets, others=(0, 1)):
     y, z, c = where_am_i(at_ref)
     blocks = []
     for piece_ref, places_of in zip(piece_refs, slots(y, z, c)):
         for i, place in enumerate(places_of):
             all_ref[len(blocks)] = piece_ref[i]
             blocks.append(ctx_id(*place))
-    for core, q_ref, state_ref in zip((c, 1 - c), sets[::2], sets[1::2]):
-        own = ctx_id(y, z, core)
+    for other, q_ref, state_ref in zip(others, sets[::2], sets[1::2]):
+        own = ctx_id(y, z, c + other - 2 * other * c)
         count = jnp.int32(0)
         for n, block in enumerate(blocks):
             order_ref[count] = n
             count += ((block < own) & (block >= own - REACH)).astype(jnp.int32)
 
-        @pl.loop(0, (count + 1) // 2)
-        def _(g, count=count, q_ref=q_ref, state_ref=state_ref):
-            one = order_ref[2 * g]
-            both = 2 * g + 1 < count
-            two = jnp.where(both, order_ref[2 * g + 1], one)
-            attend_blocks(all_ref, [(one, 0), (two, jnp.where(both, 0, BLOCK))], False, q_ref, state_ref)
+        @pl.loop(0, count // 2)
+        def _(g, q_ref=q_ref, state_ref=state_ref):
+            attend_blocks(all_ref, [order_ref[2 * g], order_ref[2 * g + 1]], False, q_ref, state_ref)
+
+        @pl.when(count % 2 == 1)
+        def _(count=count, q_ref=q_ref, state_ref=state_ref):
+            attend_blocks(all_ref, [order_ref[count - 1]], False, q_ref, state_ref)
 
 
 def start_kernel(slots, n, at_ref, *rest):
@@ -155,20 +157,24 @@
     for state_ref in (s_ref, s_2_ref):
         state_ref[...] = jnp.zeros_like(state_ref)
         state_ref[TOP : TOP + 8, :] = jnp.full((8, BLOCK), FLOOR, F32)
-    attend_blocks(pieces[0], [(0, 0)], True, q_ref, s_ref)
+    attend_blocks(pieces[0], [0], True, q_ref, s_ref)
     attend_pieces(at_ref, slots, pieces, all_ref, order_ref, (q_ref, s_ref, q_2_ref, s_2_ref))
 
 
-def more_kernel(slots, n, at_ref, *rest):
-    pieces, (q_ref, q_2_ref, s_in, s_2_in) = rest[:n], rest[n : n + 4]
-    s_ref, s_2_ref, all_ref, order_ref = rest[-4:]
+def more_kernel(slots, n, other, at_ref, *rest):
+    pieces, (q_ref, s_in, s_ref, all_ref, order_ref) = rest[:n], rest[n:]
     s_ref[...] = s_in[...]
-    s_2_ref[...] = s_2_in[...]
-    attend_pieces(at_ref, slots, pieces, all_ref, order_ref, (q_ref, s_ref, q_2_ref, s_2_ref))
-
-
-def last_kernel(at_ref, s_ref, s_2_ref, w_ref, *rest):
-    outs, att_ref = rest[:6], rest[6]
+    attend_pieces(at_ref, slots, pieces, all_ref, order_ref, (q_ref, s_ref), (other,))
+
+
+def last_kernel(at_ref, s_ref, s_2_ref, w_hbm, *rest):
+    outs, (att_ref, w_ref, sems) = rest[:6], rest[6:]
+    section = at_ref[1]
+    fetched = []
+    for n, sides in enumerate(SIDES):
+        cols = pl.ds(pl.multiple_of((section ^ away(sides)) * COLS, 128), COLS)
+        fetched.append(pltpu.make_async_copy(w_hbm.at[:, cols], w_ref.at[n], sems.at[n]))
+        fetched[-1].start()
     for h in range(4):
         rows = slice(h * HEAD_DIM, (h + 1) * HEAD_DIM)
         tops = [r[TOP + h : TOP + h + 1, :] for r in (s_ref, s_2_ref)]
@@ -177,13 +183,9 @@
         total = sum(f * r[SUM + h : SUM + h + 1, :] for f, r in zip(fades, (s_ref, s_2_ref)))
         value = sum(f * r[rows, :] for f, r in zip(fades, (s_ref, s_2_ref)))
         att_ref[:, rows] = jnp.transpose(value / total).astype(BF16)
-    section = at_ref[1]
-    for sides in itertools.product((0, 1), repeat=3):
-        away = 0
-        for step, side in zip(CHAINS[0][1], sides):
-            away ^= step * side
-        cols = pl.ds(pl.multiple_of((section ^ away) * COLS, 128), COLS)
-        part = jnp.dot(att_ref[...], w_ref[:, cols], preferred_element_type=F32).astype(BF16)
+    for n, sides in enumerate(SIDES):
+        fetched[n].wait()
+        part = jnp.dot(att_ref[...], w_ref[n], preferred_element_type=F32).astype(BF16)
         crossed = dict(zip(CHAINS[0][1], sides))
         for i, (rows, order) in enumerate(CHAINS):
             first, second, third = (crossed[step] for step in order)
@@ -193,6 +195,7 @@
 VMEM = pl.BlockSpec(memory_space=pltpu.VMEM)
 SMEM = pl.BlockSpec(memory_space=pltpu.SMEM)
 STATE = jax.ShapeDtypeStruct((4 * HEAD_DIM + 16, BLOCK), F32)
+LAST_LIMIT = 48
 LIMIT = pltpu.CompilerParams(vmem_limit_bytes=24 * 1024 * 1024)
 
 
@@ -232,28 +235,32 @@
     up = up_y(row)
     around = round_y(row)
     far_near = along_z(y_far, 2)
-    far_far = move(y_far[:1], lambda y, z, c: (y, z + 2, c) if y >= 2 else None)
+    far_far = move(z_far, lambda y, z, c: (y + 2, z, c) if y < 2 else None)
     q_2 = swap_cores(q)
 
     at = jnp.stack([ctx, lax.axis_index("section")]).astype(jnp.int32)
 
-    def attend(kernel, slots, n, pieces, state, name):
+    def attend(kernel, n, pieces, queries, states, name):
+        out_shape = (STATE,) * len(queries)
         return pl.pallas_call(
-            functools.partial(kernel, slots, len(pieces)),
-            out_shape=(STATE, STATE),
-            in_specs=[SMEM] + [VMEM] * (len(pieces) + 2 + len(state)),
-            out_specs=(VMEM,) * 2,
+            kernel,
+            out_shape=out_shape,
+            in_specs=[SMEM] + [VMEM] * (len(pieces) + len(queries) + len(states)),
+            out_specs=(VMEM,) * len(out_shape),
             scratch_shapes=[pltpu.VMEM((n, PACK, HEAD_DIM), BF16), pltpu.SMEM((16,), jnp.int32)],
             compiler_params=LIMIT,
             cost_estimate=cost(1),
             name=name,
-        )(at, *pieces, q, q_2, *state)
-
-    state = attend(start_kernel, first_slots, 7, [own, z_near, z_far, y_near, y_far], (), "attend_first")
-    (up, around), state = lax.optimization_barrier(((up, around), state))
-    state = attend(more_kernel, next_slots, 6, [up, around], (*state, w_out), "attend_next")
-    (far_near, far_far), state = lax.optimization_barrier(((far_near, far_far), state))
-    state, state_2 = attend(more_kernel, far_slots, 3, [far_near, far_far], state, "attend_far")
+        )(at, *pieces, *queries, *states)
+
+    pieces = [own, z_near, z_far, y_near, y_far]
+    first = functools.partial(start_kernel, first_slots, len(pieces))
+    state, state_2 = attend(first, 7, pieces, (q, q_2), (), "attend_first")
+    pieces, state, state_2 = lax.optimization_barrier(((up, around, far_near, far_far), state, state_2))
+    rest = [functools.partial(more_kernel, rest_slots, len(pieces), other) for other in (0, 1)]
+    (state_2,) = attend(rest[1], 9, pieces, (q_2,), (state_2,), "attend_rest_other")
+    state_2, state = lax.optimization_barrier((state_2, state))
+    (state,) = attend(rest[0], 9, pieces, (q,), (state,), "attend_rest_own")
     state_2 = swap_cores(state_2)
 
     out_shape = []
@@ -262,10 +269,14 @@
     outs = pl.pallas_call(
         last_kernel,
         out_shape=tuple(out_shape),
-        in_specs=[SMEM] + [VMEM] * 3,
+        in_specs=[SMEM, VMEM, VMEM, pl.BlockSpec(memory_space=pltpu.HBM)],
         out_specs=(VMEM,) * 6,
-        scratch_shapes=[pltpu.VMEM((BLOCK, 4 * HEAD_DIM), BF16)],
-        compiler_params=LIMIT,
+        scratch_shapes=[
+            pltpu.VMEM((BLOCK, 4 * HEAD_DIM), BF16),
+            pltpu.VMEM((8, w_out.shape[0], COLS), BF16),
+            pltpu.SemaphoreType.DMA((8,)),
+        ],
+        compiler_params=pltpu.CompilerParams(vmem_limit_bytes=LAST_LIMIT * 1024 * 1024),
         cost_estimate=cost(12),
         name="project_attended",
     )(at, state, state_2, w_out)

time: 96.8 us -> 91.9 us (0.949)
  local copies, waits for them, and re-layouts: 5.07 us -> 0.2 us
    ppermute x11, starting transfers between devices: 24.4 us -> 19.3 us  [move(): return lax.ppermute(x, 'ctx', ctx_pairs(step))]
    unnamed x12 -> x2, local copies, waits for them, and re-layouts: 4.25 us -> 0.03 us
    ppermute x9, starting transfers between devices: 8.26 us -> 12.4 us  [exchange(): return lax.ppermute(x, 'section', [(i, i ^ step) for i in range(8)])]
    ppermute x11, waiting for transfers between devices: 3.66 us -> 7.1 us  [move(): return lax.ppermute(x, 'ctx', ctx_pairs(step))]
    ppermute x9, waiting for transfers between devices: 21.3 us -> 18.5 us  [exchange(): return lax.ppermute(x, 'section', [(i, i ^ step) for i in range(8)])]
  transfers between devices with their start and end apart: 20 -> 20, of which waited for: 11 -> 10; matrix products, arithmetic and copies ran while one was open for 10% -> 10% of each run, Pallas kernels for 14% -> 12%
where the time goes in v8:
time: 91.9 us; the launch traced here: 91.6 us
  starting transfers between devices  31.7 us (34%)
  waiting for transfers between devices  25.6 us (28%)
  Pallas kernels  22.1 us (24%)
  other arithmetic  6.08 us (7%)
  matrix products  5.58 us (6%)
    ppermute x11, starting transfers between devices, move(): return lax.ppermute(x, 'ctx', ctx_pairs(step))  19.3 us
    ppermute x9, waiting for transfers between devices, exchange(): return lax.ppermute(x, 'section', [(i, i ^ step) for i in range(8)])  18.5 us
    pallas_call x3, Pallas kernels, attend(): pl.pallas_call(kernel, out_shape=out_shape, in_specs=[SMEM] + [VMEM] * (l...  17.3 us
    ppermute x9, starting transfers between devices, exchange(): return lax.ppermute(x, 'section', [(i, i ^ step) for i in range(8)])  12.4 us
    ppermute x11, waiting for transfers between devices, move(): return lax.ppermute(x, 'ctx', ctx_pairs(step))  7.1 us
    dot_general x1, matrix products, per_device(): lax.dot_general(w_query, normed, (((0,), (1,)), ((), ())), preferred_elem...  5.58 us
    pallas_call x1, Pallas kernels, per_device(): pl.pallas_call(last_kernel, out_shape=tuple(out_shape), in_specs=[SMEM, V...  4.81 us
    reduce_sum x1, other arithmetic, per_device(): jnp.mean(widened * widened, axis=-1, keepdims=True) + 1e-06  2.34 us
  transfers between devices with their start and end apart: 20, of which 10 were waited for; matrix products, arithmetic and copies ran while one was open for 10% of the time, Pallas kernels for 12%

profile of v8, /device:TPU:24, one launch (start us, length us, event | category | flops | bytes accessed | tf_op | source)
XLA Modules:
  0.0 91.6 jit_solution(15465615474736222685)
XLA Ops:
  3.1 7.2 %collective-permute-start.2 = (bf16[1,528,128]{2,1,0:T(8,128)(2,1)S(1)}, bf16[1,528,128]{2,1,0:T(8,128)(2,1)S(1)}, u32[]{:S(2)}, u32[]{:S(2)}) collective-permute-start(bf16[1,528,128]{2,1,0:T(8,128)(2,1)S(1)} %maximum_bitcast_fusion.rest_0_), channel_id=1, source_target_pairs={{0,32},{8,40},{16,48},{24,56},{32,0},{40,8},{48,16},{56,24},{64,96... | collective-permute-start | bytes 405512 | tf_op jit(solution)/shard_map/ppermute | solution.py:48
  10.4 1.3 %collective-permute-start.4 = (bf16[2,528,128]{2,1,0:T(8,128)(2,1)S(1)}, bf16[2,528,128]{2,1,0:T(8,128)(2,1)S(1)}, u32[]{:S(2)}, u32[]{:S(2)}) collective-permute-start(bf16[2,528,128]{2,1,0:T(8,128)(2,1)S(1)} %constant_dynamic-update-slice_fusion), channel_id=1, source_target_pairs={{0,128},{8,136},{16,144},{24,152},{32,160},{40,168},{48,176},{56,1... | collective-permute-start | bytes 811016 | tf_op jit(solution)/shard_map/ppermute | solution.py:48
  11.7 1.3 %collective-permute-start.3 = (bf16[2,528,128]{2,1,0:T(8,128)(2,1)S(1)}, bf16[2,528,128]{2,1,0:T(8,128)(2,1)S(1)}, u32[]{:S(2)}, u32[]{:S(2)}) collective-permute-start(bf16[2,528,128]{2,1,0:T(8,128)(2,1)S(1)} %constant_dynamic-update-slice_fusion), channel_id=1, source_target_pairs={{0,64},{8,200},{16,80},{24,216},{32,96},{40,232},{48,112},{56,248}... | collective-permute-start | bytes 811016 | tf_op jit(solution)/shard_map/ppermute | solution.py:48
  13.0 1.5 %collective-permute-start.1 = (bf16[2,528,128]{2,1,0:T(8,128)(2,1)S(1)}, bf16[2,528,128]{2,1,0:T(8,128)(2,1)S(1)}, u32[]{:S(2)}, u32[]{:S(2)}) collective-permute-start(bf16[2,528,128]{2,1,0:T(8,128)(2,1)S(1)} %constant_dynamic-update-slice_fusion), channel_id=1, source_target_pairs={{0,16},{8,56},{16,32},{24,8},{32,48},{40,24},{48,0},{56,40},{64,80... | collective-permute-start | bytes 811016 | tf_op jit(solution)/shard_map/ppermute | solution.py:48
  14.5 2.3 %fusion = f32[256]{0:T(256)S(1)} fusion(bf16[256,5120]{1,0:T(8,128)(2,1)} %param.6), kind=kLoop, calls=%fused_computation.2 | loop fusion | flops 3931904 | bytes 2622464 | tf_op jit(solution)/shard_map/reduce_sum | solution.py:226
  16.9 5.6 %fusion.11 = bf16[512,256]{1,0:T(8,128)(2,1)S(1)} fusion(bf16[5120,512]{1,0:T(8,128)(2,1)} %param.10, bf16[256,5120]{1,0:T(8,128)(2,1)} %param.6, f32[256]{0:T(256)S(1)} %add_rsqrt_fusion), kind=kOutput, calls=%fused_computation.8 | convolution fusion | flops 1346371584 | bytes 8127488 | tf_op jit(solution)/shard_map/dot_general | solution.py:228
  22.5 1.9 %collective-permute-done.1.rest_1_ = bf16[2,528,128]{2,1,0:T(8,128)(2,1)S(1)} collective-permute-done((bf16[2,528,128]{2,1,0:T(8,128)(2,1)S(1)}, bf16[2,528,128]{2,1,0:T(8,128)(2,1)S(1)}, u32[]{:S(2)}, u32[]{:S(2)}) %collective-permute-start.1) | collective-permute-done | bytes 270368 | tf_op jit(solution)/shard_map/ppermute | solution.py:48
  27.5 3.4 %collective-permute-start.7 = (bf16[2,528,128]{2,1,0:T(8,128)(2,1)S(1)}, bf16[2,528,128]{2,1,0:T(8,128)(2,1)S(1)}, u32[]{:S(2)}, u32[]{:S(2)}) collective-permute-start(bf16[2,528,128]{2,1,0:T(8,128)(2,1)S(1)} %collective-permute-done.4.rest_4_), channel_id=1, source_target_pairs={{128,144},{136,184},{144,160},{152,136},{160,176},{168,152},{176,1... | collective-permute-start | bytes 811016 | tf_op jit(solution)/shard_map/ppermute | solution.py:48
  32.2 5.3 %attend_first.1 = (f32[528,256]{1,0:T(8,128)S(1)}, f32[528,256]{1,0:T(8,128)S(1)}) custom-call(s32[2]{0:T(128)S(1)} %pad_add_fusion.at_ref, bf16[1,528,128]{2,1,0:T(8,128)(2,1)S(1)} %maximum_bitcast_fusion.rest_0_, bf16[2,528,128]{2,1,0:T(8,128)(2,1)S(1)} %collective-permute-done.1.rest_1_, bf16[1,528,128]{2,1,0:T(8,128)(2,1)S(1)} %collective-permute-done.2.rest_2_, ...), custom_call_target="tpu_custom_call" | custom-call | flops 134217728 | bytes 135168 | tf_op jit(solution)/shard_map/attend_first/pallas_call | solution.py:245
  37.6 2.7 %collective-permute-done.8.rest_3_ = bf16[1,528,128]{2,1,0:T(8,128)(2,1)S(1)} collective-permute-done((bf16[1,528,128]{2,1,0:T(8,128)(2,1)S(1)}, bf16[1,528,128]{2,1,0:T(8,128)(2,1)S(1)}, u32[]{:S(2)}, u32[]{:S(2)}) %collective-permute-start.8) | collective-permute-done | bytes 135200 | tf_op jit(solution)/shard_map/ppermute | solution.py:48
  40.3 1.8 %collective-permute-done.6.rest_1_ = bf16[3,528,128]{2,1,0:T(8,128)(2,1)S(1)} collective-permute-done((bf16[3,528,128]{2,1,0:T(8,128)(2,1)S(1)}, bf16[3,528,128]{2,1,0:T(8,128)(2,1)S(1)}, u32[]{:S(2)}, u32[]{:S(2)}) %collective-permute-start.6) | collective-permute-done | bytes 405536 | tf_op jit(solution)/shard_map/ppermute | solution.py:48
  42.1 6.0 %attend_rest_other.1 = f32[528,256]{1,0:T(8,128)S(1)} custom-call(s32[2]{0:T(128)S(1)} %pad_add_fusion.at_ref, bf16[3,528,128]{2,1,0:T(8,128)(2,1)S(1)} %collective-permute-done.5.rest_0_, bf16[3,528,128]{2,1,0:T(8,128)(2,1)S(1)} %collective-permute-done.6.rest_1_, bf16[2,528,128]{2,1,0:T(8,128)(2,1)S(1)} %collective-permute-done.7.rest_2_, ...), custom_call_target="tpu_custom_call" | custom-call | flops 134217728 | bytes 135168 | tf_op jit(solution)/shard_map/attend_rest_other/pallas_call | solution.py:245
  48.4 6.0 %attend_rest_own.1.s_ref = f32[528,256]{1,0:T(8,128)S(1)} custom-call(s32[2]{0:T(128)S(1)} %pad_add_fusion.at_ref, bf16[3,528,128]{2,1,0:T(8,128)(2,1)S(1)} %collective-permute-done.5.rest_0_, bf16[3,528,128]{2,1,0:T(8,128)(2,1)S(1)} %collective-permute-done.6.rest_1_, bf16[2,528,128]{2,1,0:T(8,128)(2,1)S(1)} %collective-permute-done.7.rest_2_, ...), custom_call_target="tpu_custom_call" | custom-call | flops 134217728 | bytes 135168 | tf_op jit(solution)/shard_map/attend_rest_own/pallas_call | solution.py:245
  54.4 4.8 %project_attended.1 = (bf16[4,80,640]{2,1,0:T(8,128)(2,1)S(1)}, bf16[4,80,640]{2,1,0:T(8,128)(2,1)S(1)}, bf16[4,96,640]{2,1,0:T(8,128)(2,1)S(1)}, bf16[4,96,640]...) custom-call(s32[2]{0:T(128)S(1)} %pad_add_fusion.at_ref, ...), custom_call_target="tpu_custom_call" | custom-call | flops 1610612736 | bytes 1622016 | tf_op jit(solution)/shard_map/project_attended/pallas_call | solution.py:269
  59.2 1.6 %collective-permute-start.11 = (bf16[4,80,640]{2,1,0:T(8,128)(2,1)S(1)}, bf16[4,80,640]{2,1,0:T(8,128)(2,1)S(1)}, u32[]{:S(2)}, u32[]{:S(2)}) collective-permute-start(bf16[4,80,640]{2,1,0:T(8,128)(2,1)S(1)} %get-tuple-element.48), channel_id=1, source_target_pairs={{0,1},{1,0},{2,3},{3,2},{4,5},{5,4},{6,7},{7,6},{8,9},{9,8},{10,11... | collective-permute-start | bytes 1228808 | tf_op jit(solution)/shard_map/ppermute | solution.py:285
  61.8 2.1 %collective-permute-start.14 = (bf16[4,96,640]{2,1,0:T(8,128)(2,1)S(1)}, bf16[4,96,640]{2,1,0:T(8,128)(2,1)S(1)}, u32[]{:S(2)}, u32[]{:S(2)}) collective-permute-start(bf16[4,96,640]{2,1,0:T(8,128)(2,1)S(1)} %get-tuple-element.50), channel_id=1, source_target_pairs={{0,3},{1,2},{2,1},{3,0},{4,7},{5,6},{6,5},{7,4},{8,11},{9,10},{10,... | collective-permute-start | bytes 1474568 | tf_op jit(solution)/shard_map/ppermute | solution.py:285
  63.9 7.3 %collective-permute-done.11 = bf16[4,80,640]{2,1,0:T(8,128)(2,1)S(1)} collective-permute-done((bf16[4,80,640]{2,1,0:T(8,128)(2,1)S(1)}, bf16[4,80,640]{2,1,0:T(8,128)(2,1)S(1)}, u32[]{:S(2)}, u32[]{:S(2)}) %collective-permute-start.11) | collective-permute-done | bytes 409632 | tf_op jit(solution)/shard_map/ppermute | solution.py:285
  71.3 2.8 %collective-permute-start.12 = (bf16[2,80,640]{2,1,0:T(8,128)(2,1)S(1)}, bf16[2,80,640]{2,1,0:T(8,128)(2,1)S(1)}, u32[]{:S(2)}, u32[]{:S(2)}) collective-permute-start(bf16[2,80,640]{2,1,0:T(8,128)(2,1)S(1)} %slice.98), channel_id=1, source_target_pairs={{0,3},{1,2},{2,1},{3,0},{4,7},{5,6},{6,5},{7,4},{8,11},{9,10},{10,... | collective-permute-start | bytes 614408 | tf_op jit(solution)/shard_map/ppermute | solution.py:285
  74.5 2.5 %collective-permute-done.14 = bf16[4,96,640]{2,1,0:T(8,128)(2,1)S(1)} collective-permute-done((bf16[4,96,640]{2,1,0:T(8,128)(2,1)S(1)}, bf16[4,96,640]{2,1,0:T(8,128)(2,1)S(1)}, u32[]{:S(2)}, u32[]{:S(2)}) %collective-permute-start.14) | collective-permute-done | bytes 491552 | tf_op jit(solution)/shard_map/ppermute | solution.py:285
  78.3 2.1 %collective-permute-done.12 = bf16[2,80,640]{2,1,0:T(8,128)(2,1)S(1)} collective-permute-done((bf16[2,80,640]{2,1,0:T(8,128)(2,1)S(1)}, bf16[2,80,640]{2,1,0:T(8,128)(2,1)S(1)}, u32[]{:S(2)}, u32[]{:S(2)}) %collective-permute-start.12) | collective-permute-done | bytes 204832 | tf_op jit(solution)/shard_map/ppermute | solution.py:285
  81.7 2.2 %collective-permute-start.19 = (bf16[80,640]{1,0:T(8,128)(2,1)S(1)}, bf16[80,640]{1,0:T(8,128)(2,1)S(1)}, u32[]{:S(2)}, u32[]{:S(2)}) collective-permute-start(bf16[80,640]{1,0:T(8,128)(2,1)S(1)} %fusion.23), channel_id=1, source_target_pairs={{0,3},{1,2},{2,1},{3,0},{4,7},{5,6},{6,5},{7,4},{8,11},{9,10},{10,... | collective-permute-start | bytes 307208 | tf_op jit(solution)/shard_map/ppermute | solution.py:285
  83.8 1.8 %collective-permute-done.13 = bf16[80,640]{1,0:T(8,128)(2,1)S(1)} collective-permute-done((bf16[80,640]{1,0:T(8,128)(2,1)S(1)}, bf16[80,640]{1,0:T(8,128)(2,1)S(1)}, u32[]{:S(2)}, u32[]{:S(2)}) %collective-permute-start.13) | collective-permute-done | bytes 102432 | tf_op jit(solution)/shard_map/ppermute | solution.py:285
  86.0 1.6 %collective-permute-done.19 = bf16[80,640]{1,0:T(8,128)(2,1)S(1)} collective-permute-done((bf16[80,640]{1,0:T(8,128)(2,1)S(1)}, bf16[80,640]{1,0:T(8,128)(2,1)S(1)}, u32[]{:S(2)}, u32[]{:S(2)}) %collective-permute-start.19) | collective-permute-done | bytes 102432 | tf_op jit(solution)/shard_map/ppermute | solution.py:285
  87.7 3.1 %collective-permute-done.16 = bf16[96,640]{1,0:T(8,128)(2,1)S(1)} collective-permute-done((bf16[96,640]{1,0:T(8,128)(2,1)S(1)}, bf16[96,640]{1,0:T(8,128)(2,1)S(1)}, u32[]{:S(2)}, u32[]{:S(2)}) %collective-permute-start.16) | collective-permute-done | bytes 122912 | tf_op jit(solution)/shard_map/ppermute | solution.py:285
  (49 shorter events, 12.9 us)
Async XLA Ops:
  1.7 1.4 %collective-permute-start = (bf16[1,528,128]{2,1,0:T(8,128)(2,1)S(1)}, bf16[1,528,128]{2,1,0:T(8,128)(2,1)S(1)}, u32[]{:S(2)}, u32[]{:S(2)}) collective-permute-start(bf16[1,528,128]{2,1,0:T(8,128)(2,1)S(1)} %maximum_bitcast_fusion.rest_0_), channel_id=1, source_target_pairs={{0,8},{8,0},{16,24},{24,16},{32,40},{40,32},{48,56},{56,48},{64,72... | collective-permute-start | bytes 405512 | tf_op jit(solution)/shard_map/ppermute | solution.py:48
  3.1 19.3 %collective-permute-start.2 = (bf16[1,528,128]{2,1,0:T(8,128)(2,1)S(1)}, bf16[1,528,128]{2,1,0:T(8,128)(2,1)S(1)}, u32[]{:S(2)}, u32[]{:S(2)}) collective-permute-start(bf16[1,528,128]{2,1,0:T(8,128)(2,1)S(1)} %maximum_bitcast_fusion.rest_0_), channel_id=1, source_target_pairs={{0,32},{8,40},{16,48},{24,56},{32,0},{40,8},{48,16},{56,24},{64,96... | collective-permute-start | bytes 405512 | tf_op jit(solution)/shard_map/ppermute | solution.py:48
  10.4 12.1 %collective-permute-start.4 = (bf16[2,528,128]{2,1,0:T(8,128)(2,1)S(1)}, bf16[2,528,128]{2,1,0:T(8,128)(2,1)S(1)}, u32[]{:S(2)}, u32[]{:S(2)}) collective-permute-start(bf16[2,528,128]{2,1,0:T(8,128)(2,1)S(1)} %constant_dynamic-update-slice_fusion), channel_id=1, source_target_pairs={{0,128},{8,136},{16,144},{24,152},{32,160},{40,168},{48,176},{56,1... | collective-permute-start | bytes 811016 | tf_op jit(solution)/shard_map/ppermute | solution.py:48
  11.7 10.8 %collective-permute-start.3 = (bf16[2,528,128]{2,1,0:T(8,128)(2,1)S(1)}, bf16[2,528,128]{2,1,0:T(8,128)(2,1)S(1)}, u32[]{:S(2)}, u32[]{:S(2)}) collective-permute-start(bf16[2,528,128]{2,1,0:T(8,128)(2,1)S(1)} %constant_dynamic-update-slice_fusion), channel_id=1, source_target_pairs={{0,64},{8,200},{16,80},{24,216},{32,96},{40,232},{48,112},{56,248}... | collective-permute-start | bytes 811016 | tf_op jit(solution)/shard_map/ppermute | solution.py:48
  13.0 11.5 %collective-permute-start.1 = (bf16[2,528,128]{2,1,0:T(8,128)(2,1)S(1)}, bf16[2,528,128]{2,1,0:T(8,128)(2,1)S(1)}, u32[]{:S(2)}, u32[]{:S(2)}) collective-permute-start(bf16[2,528,128]{2,1,0:T(8,128)(2,1)S(1)} %constant_dynamic-update-slice_fusion), channel_id=1, source_target_pairs={{0,16},{8,56},{16,32},{24,8},{32,48},{40,24},{48,0},{56,40},{64,80... | collective-permute-start | bytes 811016 | tf_op jit(solution)/shard_map/ppermute | solution.py:48
  24.5 17.6 %collective-permute-start.6 = (bf16[3,528,128]{2,1,0:T(8,128)(2,1)S(1)}, bf16[3,528,128]{2,1,0:T(8,128)(2,1)S(1)}, u32[]{:S(2)}, u32[]{:S(2)}) collective-permute-start(bf16[3,528,128]{2,1,0:T(8,128)(2,1)S(1)} %constant_dynamic-update-slice_fusion.2), channel_id=1, source_target_pairs={{0,192},{8,200},{16,208},{24,216},{32,224},{40,232},{48,240},{56,2... | collective-permute-start | bytes 1216520 | tf_op jit(solution)/shard_map/ppermute | solution.py:48
  25.8 16.3 %collective-permute-start.5 = (bf16[3,528,128]{2,1,0:T(8,128)(2,1)S(1)}, bf16[3,528,128]{2,1,0:T(8,128)(2,1)S(1)}, u32[]{:S(2)}, u32[]{:S(2)}) collective-permute-start(bf16[3,528,128]{2,1,0:T(8,128)(2,1)S(1)} %constant_dynamic-update-slice_fusion.2), channel_id=1, source_target_pairs={{0,64},{8,72},{16,80},{24,88},{32,96},{40,104},{48,112},{56,120},{... | collective-permute-start | bytes 1216520 | tf_op jit(solution)/shard_map/ppermute | solution.py:48
  27.1 5.1 %collective-permute-start.9 = (bf16[640,256]{1,0:T(8,128)(2,1)S(1)}, bf16[640,256]{1,0:T(8,128)(2,1)S(1)}, u32[]{:S(2)}, u32[]{:S(2)}) collective-permute-start(bf16[640,256]{1,0:T(8,128)(2,1)S(1)} %pad_maximum_fusion.rest_5_.rest_4_), channel_id=1, source_target_pairs={{0,8},{8,0},{16,24},{24,16},{32,40},{40,32},{48,56},{56,48},{64,72... | collective-permute-start | bytes 983048 | tf_op jit(solution)/shard_map/ppermute | solution.py:48
  27.5 12.8 %collective-permute-start.7 = (bf16[2,528,128]{2,1,0:T(8,128)(2,1)S(1)}, bf16[2,528,128]{2,1,0:T(8,128)(2,1)S(1)}, u32[]{:S(2)}, u32[]{:S(2)}) collective-permute-start(bf16[2,528,128]{2,1,0:T(8,128)(2,1)S(1)} %collective-permute-done.4.rest_4_), channel_id=1, source_target_pairs={{128,144},{136,184},{144,160},{152,136},{160,176},{168,152},{176,1... | collective-permute-start | bytes 811016 | tf_op jit(solution)/shard_map/ppermute | solution.py:48
  30.9 9.4 %collective-permute-start.8 = (bf16[1,528,128]{2,1,0:T(8,128)(2,1)S(1)}, bf16[1,528,128]{2,1,0:T(8,128)(2,1)S(1)}, u32[]{:S(2)}, u32[]{:S(2)}) collective-permute-start(bf16[1,528,128]{2,1,0:T(8,128)(2,1)S(1)} %collective-permute-done.2.rest_2_), channel_id=1, source_target_pairs={{0,128},{8,136},{16,144},{24,152},{32,160},{40,168},{48,176},{56,1... | collective-permute-start | bytes 405512 | tf_op jit(solution)/shard_map/ppermute | solution.py:48
  48.1 6.3 %collective-permute-start.10 = (f32[528,256]{1,0:T(8,128)S(1)}, f32[528,256]{1,0:T(8,128)S(1)}, u32[]{:S(2)}, u32[]{:S(2)}) collective-permute-start(f32[528,256]{1,0:T(8,128)S(1)} %attend_rest_other.1), channel_id=1, source_target_pairs={{0,8},{8,0},{16,24},{24,16},{32,40},{40,32},{48,56},{56,48},{64,72... | collective-permute-start | bytes 1622024 | tf_op jit(solution)/shard_map/ppermute | solution.py:48
  59.2 12.0 %collective-permute-start.11 = (bf16[4,80,640]{2,1,0:T(8,128)(2,1)S(1)}, bf16[4,80,640]{2,1,0:T(8,128)(2,1)S(1)}, u32[]{:S(2)}, u32[]{:S(2)}) collective-permute-start(bf16[4,80,640]{2,1,0:T(8,128)(2,1)S(1)} %get-tuple-element.48), channel_id=1, source_target_pairs={{0,1},{1,0},{2,3},{3,2},{4,5},{5,4},{6,7},{7,6},{8,9},{9,8},{10,11... | collective-permute-start | bytes 1228808 | tf_op jit(solution)/shard_map/ppermute | solution.py:285
  60.8 13.3 %collective-permute-start.17 = (bf16[4,80,640]{2,1,0:T(8,128)(2,1)S(1)}, bf16[4,80,640]{2,1,0:T(8,128)(2,1)S(1)}, u32[]{:S(2)}, u32[]{:S(2)}) collective-permute-start(bf16[4,80,640]{2,1,0:T(8,128)(2,1)S(1)} %get-tuple-element.52), channel_id=1, source_target_pairs={{0,4},{1,5},{2,6},{3,7},{4,0},{5,1},{6,2},{7,3},{8,12},{9,13},{10,... | collective-permute-start | bytes 1228808 | tf_op jit(solution)/shard_map/ppermute | solution.py:285
  61.8 15.3 %collective-permute-start.14 = (bf16[4,96,640]{2,1,0:T(8,128)(2,1)S(1)}, bf16[4,96,640]{2,1,0:T(8,128)(2,1)S(1)}, u32[]{:S(2)}, u32[]{:S(2)}) collective-permute-start(bf16[4,96,640]{2,1,0:T(8,128)(2,1)S(1)} %get-tuple-element.50), channel_id=1, source_target_pairs={{0,3},{1,2},{2,1},{3,0},{4,7},{5,6},{6,5},{7,4},{8,11},{9,10},{10,... | collective-permute-start | bytes 1474568 | tf_op jit(solution)/shard_map/ppermute | solution.py:285
  71.3 9.2 %collective-permute-start.12 = (bf16[2,80,640]{2,1,0:T(8,128)(2,1)S(1)}, bf16[2,80,640]{2,1,0:T(8,128)(2,1)S(1)}, u32[]{:S(2)}, u32[]{:S(2)}) collective-permute-start(bf16[2,80,640]{2,1,0:T(8,128)(2,1)S(1)} %slice.98), channel_id=1, source_target_pairs={{0,3},{1,2},{2,1},{3,0},{4,7},{5,6},{6,5},{7,4},{8,11},{9,10},{10,... | collective-permute-start | bytes 614408 | tf_op jit(solution)/shard_map/ppermute | solution.py:285
  74.2 7.4 %collective-permute-start.18 = (bf16[2,80,640]{2,1,0:T(8,128)(2,1)S(1)}, bf16[2,80,640]{2,1,0:T(8,128)(2,1)S(1)}, u32[]{:S(2)}, u32[]{:S(2)}) collective-permute-start(bf16[2,80,640]{2,1,0:T(8,128)(2,1)S(1)} %slice.97), channel_id=1, source_target_pairs={{0,1},{1,0},{2,3},{3,2},{4,5},{5,4},{6,7},{7,6},{8,9},{9,8},{10,11... | collective-permute-start | bytes 614408 | tf_op jit(solution)/shard_map/ppermute | solution.py:285
  77.2 8.5 %collective-permute-start.15 = (bf16[2,96,640]{2,1,0:T(8,128)(2,1)S(1)}, bf16[2,96,640]{2,1,0:T(8,128)(2,1)S(1)}, u32[]{:S(2)}, u32[]{:S(2)}) collective-permute-start(bf16[2,96,640]{2,1,0:T(8,128)(2,1)S(1)} %slice.96), channel_id=1, source_target_pairs={{0,4},{1,5},{2,6},{3,7},{4,0},{5,1},{6,2},{7,3},{8,12},{9,13},{10,... | collective-permute-start | bytes 737288 | tf_op jit(solution)/shard_map/ppermute | solution.py:285
  80.5 5.2 %collective-permute-start.13 = (bf16[80,640]{1,0:T(8,128)(2,1)S(1)}, bf16[80,640]{1,0:T(8,128)(2,1)S(1)}, u32[]{:S(2)}, u32[]{:S(2)}) collective-permute-start(bf16[80,640]{1,0:T(8,128)(2,1)S(1)} %fusion.22), channel_id=1, source_target_pairs={{0,4},{1,5},{2,6},{3,7},{4,0},{5,1},{6,2},{7,3},{8,12},{9,13},{10,... | collective-permute-start | bytes 307208 | tf_op jit(solution)/shard_map/ppermute | solution.py:285
  81.7 6.0 %collective-permute-start.19 = (bf16[80,640]{1,0:T(8,128)(2,1)S(1)}, bf16[80,640]{1,0:T(8,128)(2,1)S(1)}, u32[]{:S(2)}, u32[]{:S(2)}) collective-permute-start(bf16[80,640]{1,0:T(8,128)(2,1)S(1)} %fusion.23), channel_id=1, source_target_pairs={{0,3},{1,2},{2,1},{3,0},{4,7},{5,6},{6,5},{7,4},{8,11},{9,10},{10,... | collective-permute-start | bytes 307208 | tf_op jit(solution)/shard_map/ppermute | solution.py:285
  85.8 5.0 %collective-permute-start.16 = (bf16[96,640]{1,0:T(8,128)(2,1)S(1)}, bf16[96,640]{1,0:T(8,128)(2,1)S(1)}, u32[]{:S(2)}, u32[]{:S(2)}) collective-permute-start(bf16[96,640]{1,0:T(8,128)(2,1)S(1)} %fusion.21), channel_id=1, source_target_pairs={{0,1},{1,0},{2,3},{3,2},{4,5},{5,4},{6,7},{7,6},{8,9},{9,8},{10,11... | collective-permute-start | bytes 368648 | tf_op jit(solution)/shard_map/ppermute | solution.py:285

commit v9 on v8

--- a/solution.py
+++ b/solution.py
@@ -93,7 +93,8 @@
     keys, values, visible = [], [], []
     for at in places:
         keys.append(kv_ref[at, 0:BLOCK, :])
-        values.append(jnp.transpose(kv_ref[at, BLOCK : 2 * BLOCK, :]))
+        ones = jnp.ones((16, BLOCK), BF16)
+        values.append(jnp.concatenate([jnp.transpose(kv_ref[at, BLOCK : 2 * BLOCK, :]), ones], axis=0))
         counts = kv_ref[at, 2 * BLOCK : PACK, :]
         first = jnp.dot(counts, q_ref[HOT, :], preferred_element_type=F32)[0:1, :].astype(jnp.int32)
         row = lax.broadcasted_iota(jnp.int32, (BLOCK, BLOCK), 0)
@@ -112,11 +113,8 @@
             m_new = jnp.maximum(m_new, jnp.max(s, axis=0, keepdims=True))
         weights = [jnp.exp(s - m_new) for s in masked]
         fade = jnp.exp(m_old - m_new)
-        total = fade * total
-        for p in weights:
-            total = total + jnp.sum(p, axis=0, keepdims=True)
         added = sum(jnp.dot(v, p.astype(BF16), preferred_element_type=F32) for v, p in zip(values, weights))
-        new.append((m_new, total, fade, added))
+        new.append((m_new, fade * total + added[HEAD_DIM : HEAD_DIM + 1], fade, added[:HEAD_DIM]))
     for h, rows in enumerate(heads):
         m_new, total, fade, added = new[h]
         state_ref[TOP + h : TOP + h + 1, :] = m_new
@@ -143,13 +141,15 @@
             order_ref[count] = n
             count += ((block < own) & (block >= own - REACH)).astype(jnp.int32)
 
-        @pl.loop(0, count // 2)
+        threes = count // 3
+
+        @pl.loop(0, threes)
         def _(g, q_ref=q_ref, state_ref=state_ref):
-            attend_blocks(all_ref, [order_ref[2 * g], order_ref[2 * g + 1]], False, q_ref, state_ref)
-
-        @pl.when(count % 2 == 1)
-        def _(count=count, q_ref=q_ref, state_ref=state_ref):
-            attend_blocks(all_ref, [order_ref[count - 1]], False, q_ref, state_ref)
+            attend_blocks(all_ref, [order_ref[3 * g + i] for i in range(3)], False, q_ref, state_ref)
+
+        @pl.loop(3 * threes, count)
+        def _(i, q_ref=q_ref, state_ref=state_ref):
+            attend_blocks(all_ref, [order_ref[i]], False, q_ref, state_ref)
 
 
 def start_kernel(slots, n, at_ref, *rest):
@@ -167,14 +167,17 @@
     attend_pieces(at_ref, slots, pieces, all_ref, order_ref, (q_ref, s_ref), (other,))
 
 
-def last_kernel(at_ref, s_ref, s_2_ref, w_hbm, *rest):
-    outs, (att_ref, w_ref, sems) = rest[:6], rest[6:]
+def more_and_fetch_kernel(slots, n, other, at_ref, *rest):
+    w_hbm, s_ref, w_ref, all_ref, order_ref, sem = rest[n + 2 :]
+    copy = pltpu.make_async_copy(w_hbm, w_ref, sem)
+    copy.start()
+    more_kernel(slots, n, other, at_ref, *rest[: n + 2], s_ref, all_ref, order_ref)
+    copy.wait()
+
+
+def last_kernel(at_ref, s_ref, s_2_ref, w_ref, *rest):
+    outs, att_ref = rest[:6], rest[6]
     section = at_ref[1]
-    fetched = []
-    for n, sides in enumerate(SIDES):
-        cols = pl.ds(pl.multiple_of((section ^ away(sides)) * COLS, 128), COLS)
-        fetched.append(pltpu.make_async_copy(w_hbm.at[:, cols], w_ref.at[n], sems.at[n]))
-        fetched[-1].start()
     for h in range(4):
         rows = slice(h * HEAD_DIM, (h + 1) * HEAD_DIM)
         tops = [r[TOP + h : TOP + h + 1, :] for r in (s_ref, s_2_ref)]
@@ -183,9 +186,9 @@
         total = sum(f * r[SUM + h : SUM + h + 1, :] for f, r in zip(fades, (s_ref, s_2_ref)))
         value = sum(f * r[rows, :] for f, r in zip(fades, (s_ref, s_2_ref)))
         att_ref[:, rows] = jnp.transpose(value / total).astype(BF16)
-    for n, sides in enumerate(SIDES):
-        fetched[n].wait()
-        part = jnp.dot(att_ref[...], w_ref[n], preferred_element_type=F32).astype(BF16)
+    for sides in SIDES:
+        cols = pl.ds(pl.multiple_of((section ^ away(sides)) * COLS, 128), COLS)
+        part = jnp.dot(att_ref[...], w_ref[:, cols], preferred_element_type=F32).astype(BF16)
         crossed = dict(zip(CHAINS[0][1], sides))
         for i, (rows, order) in enumerate(CHAINS):
             first, second, third = (crossed[step] for step in order)
@@ -195,7 +198,7 @@
 VMEM = pl.BlockSpec(memory_space=pltpu.VMEM)
 SMEM = pl.BlockSpec(memory_space=pltpu.SMEM)
 STATE = jax.ShapeDtypeStruct((4 * HEAD_DIM + 16, BLOCK), F32)
-LAST_LIMIT = 48
+LAST_LIMIT = 44
 LIMIT = pltpu.CompilerParams(vmem_limit_bytes=24 * 1024 * 1024)
 
 
@@ -257,10 +260,23 @@
     first = functools.partial(start_kernel, first_slots, len(pieces))
     state, state_2 = attend(first, 7, pieces, (q, q_2), (), "attend_first")
     pieces, state, state_2 = lax.optimization_barrier(((up, around, far_near, far_far), state, state_2))
-    rest = [functools.partial(more_kernel, rest_slots, len(pieces), other) for other in (0, 1)]
-    (state_2,) = attend(rest[1], 9, pieces, (q_2,), (state_2,), "attend_rest_other")
+    rest = functools.partial(more_kernel, rest_slots, len(pieces), 1)
+    (state_2,) = attend(rest, 9, pieces, (q_2,), (state_2,), "attend_rest_other")
     state_2, state = lax.optimization_barrier((state_2, state))
-    (state,) = attend(rest[0], 9, pieces, (q,), (state,), "attend_rest_own")
+    state, w_held = pl.pallas_call(
+        functools.partial(more_and_fetch_kernel, rest_slots, len(pieces), 0),
+        out_shape=(STATE, jax.ShapeDtypeStruct(w_out.shape, BF16)),
+        in_specs=[SMEM] + [VMEM] * (len(pieces) + 2) + [pl.BlockSpec(memory_space=pltpu.HBM)],
+        out_specs=(VMEM,) * 2,
+        scratch_shapes=[
+            pltpu.VMEM((9, PACK, HEAD_DIM), BF16),
+            pltpu.SMEM((16,), jnp.int32),
+            pltpu.SemaphoreType.DMA,
+        ],
+        compiler_params=pltpu.CompilerParams(vmem_limit_bytes=LAST_LIMIT * 1024 * 1024),
+        cost_estimate=cost(1),
+        name="attend_rest_own",
+    )(at, *pieces, q, state, w_out)
     state_2 = swap_cores(state_2)
 
     out_shape = []
@@ -269,17 +285,13 @@
     outs = pl.pallas_call(
         last_kernel,
         out_shape=tuple(out_shape),
-        in_specs=[SMEM, VMEM, VMEM, pl.BlockSpec(memory_space=pltpu.HBM)],
+        in_specs=[SMEM, VMEM, VMEM, VMEM],
         out_specs=(VMEM,) * 6,
-        scratch_shapes=[
-            pltpu.VMEM((BLOCK, 4 * HEAD_DIM), BF16),
-            pltpu.VMEM((8, w_out.shape[0], COLS), BF16),
-            pltpu.SemaphoreType.DMA((8,)),
-        ],
-        compiler_params=pltpu.CompilerParams(vmem_limit_bytes=LAST_LIMIT * 1024 * 1024),
+        scratch_shapes=[pltpu.VMEM((BLOCK, 4 * HEAD_DIM), BF16)],
+        compiler_params=LIMIT,
         cost_estimate=cost(12),
         name="project_attended",
-    )(at, state, state_2, w_out)
+    )(at, state, state_2, w_held)
 
     def exchange(x, step):
         return lax.ppermute(x, "section", [(i, i ^ step) for i in range(8)])

time: 91.9 us -> 87.3 us (0.950)
  Pallas kernels: 22.1 us -> 16.9 us
    pallas_call x3 -> x2, Pallas kernels: 17.3 us -> 9.6 us  [attend(): pl.pallas_call(kernel, out_shape=out_shape, in_specs=[SMEM] + [VMEM] * (l...]
    pallas_call x0 -> x1, Pallas kernels: none -> 4.83 us  [per_device(): pl.pallas_call(functools.partial(more_and_fetch_kernel, rest_slots, len(p...]
    pallas_call x1, Pallas kernels: 4.81 us -> 2.49 us  [per_device(): pl.pallas_call(last_kernel, out_shape=tuple(out_shape), in_specs=[SMEM, V...]
  transfers between devices with their start and end apart: 20 -> 20, of which waited for: 10 -> 10; matrix products, arithmetic and copies ran while one was open for 10% -> 11% of each run, Pallas kernels for 12% -> 11%
where the time goes in v9:
time: 87.3 us; the launch traced here: 86.9 us
  starting transfers between devices  31.5 us (36%)
  waiting for transfers between devices  26.4 us (30%)
  Pallas kernels  16.9 us (19%)
  other arithmetic  6.07 us (7%)
  matrix products  5.58 us (6%)
    ppermute x11, starting transfers between devices, move(): return lax.ppermute(x, 'ctx', ctx_pairs(step))  19.1 us
    ppermute x9, waiting for transfers between devices, exchange(): return lax.ppermute(x, 'section', [(i, i ^ step) for i in range(8)])  18.6 us
    ppermute x9, starting transfers between devices, exchange(): return lax.ppermute(x, 'section', [(i, i ^ step) for i in range(8)])  12.4 us
    pallas_call x2, Pallas kernels, attend(): pl.pallas_call(kernel, out_shape=out_shape, in_specs=[SMEM] + [VMEM] * (l...  9.6 us
    ppermute x11, waiting for transfers between devices, move(): return lax.ppermute(x, 'ctx', ctx_pairs(step))  7.82 us
    dot_general x1, matrix products, per_device(): lax.dot_general(w_query, normed, (((0,), (1,)), ((), ())), preferred_elem...  5.58 us
    pallas_call x1, Pallas kernels, per_device(): pl.pallas_call(functools.partial(more_and_fetch_kernel, rest_slots, len(p...  4.83 us
    pallas_call x1, Pallas kernels, per_device(): pl.pallas_call(last_kernel, out_shape=tuple(out_shape), in_specs=[SMEM, V...  2.49 us
  transfers between devices with their start and end apart: 20, of which 10 were waited for; matrix products, arithmetic and copies ran while one was open for 11% of the time, Pallas kernels for 11%

profile of v9, /device:TPU:24, one launch (start us, length us, event | category | flops | bytes accessed | tf_op | source)
XLA Modules:
  0.0 86.9 jit_solution(12094438143620617142)
XLA Ops:
  3.1 7.2 %collective-permute-start.2 = (bf16[1,528,128]{2,1,0:T(8,128)(2,1)S(1)}, bf16[1,528,128]{2,1,0:T(8,128)(2,1)S(1)}, u32[]{:S(2)}, u32[]{:S(2)}) collective-permute-start(bf16[1,528,128]{2,1,0:T(8,128)(2,1)S(1)} %maximum_bitcast_fusion.rest_0_), channel_id=1, source_target_pairs={{0,32},{8,40},{16,48},{24,56},{32,0},{40,8},{48,16},{56,24},{64,96... | collective-permute-start | bytes 405512 | tf_op jit(solution)/shard_map/ppermute | solution.py:48
  10.4 1.3 %collective-permute-start.4 = (bf16[2,528,128]{2,1,0:T(8,128)(2,1)S(1)}, bf16[2,528,128]{2,1,0:T(8,128)(2,1)S(1)}, u32[]{:S(2)}, u32[]{:S(2)}) collective-permute-start(bf16[2,528,128]{2,1,0:T(8,128)(2,1)S(1)} %constant_dynamic-update-slice_fusion), channel_id=1, source_target_pairs={{0,128},{8,136},{16,144},{24,152},{32,160},{40,168},{48,176},{56,1... | collective-permute-start | bytes 811016 | tf_op jit(solution)/shard_map/ppermute | solution.py:48
  11.7 1.3 %collective-permute-start.3 = (bf16[2,528,128]{2,1,0:T(8,128)(2,1)S(1)}, bf16[2,528,128]{2,1,0:T(8,128)(2,1)S(1)}, u32[]{:S(2)}, u32[]{:S(2)}) collective-permute-start(bf16[2,528,128]{2,1,0:T(8,128)(2,1)S(1)} %constant_dynamic-update-slice_fusion), channel_id=1, source_target_pairs={{0,64},{8,200},{16,80},{24,216},{32,96},{40,232},{48,112},{56,248}... | collective-permute-start | bytes 811016 | tf_op jit(solution)/shard_map/ppermute | solution.py:48
  13.0 1.5 %collective-permute-start.1 = (bf16[2,528,128]{2,1,0:T(8,128)(2,1)S(1)}, bf16[2,528,128]{2,1,0:T(8,128)(2,1)S(1)}, u32[]{:S(2)}, u32[]{:S(2)}) collective-permute-start(bf16[2,528,128]{2,1,0:T(8,128)(2,1)S(1)} %constant_dynamic-update-slice_fusion), channel_id=1, source_target_pairs={{0,16},{8,56},{16,32},{24,8},{32,48},{40,24},{48,0},{56,40},{64,80... | collective-permute-start | bytes 811016 | tf_op jit(solution)/shard_map/ppermute | solution.py:48
  14.5 2.3 %fusion = f32[256]{0:T(256)S(1)} fusion(bf16[256,5120]{1,0:T(8,128)(2,1)} %param.6), kind=kLoop, calls=%fused_computation.2 | loop fusion | flops 3931904 | bytes 2622464 | tf_op jit(solution)/shard_map/reduce_sum | solution.py:229
  16.9 5.6 %fusion.11 = bf16[512,256]{1,0:T(8,128)(2,1)S(1)} fusion(bf16[5120,512]{1,0:T(8,128)(2,1)} %param.10, bf16[256,5120]{1,0:T(8,128)(2,1)} %param.6, f32[256]{0:T(256)S(1)} %add_rsqrt_fusion), kind=kOutput, calls=%fused_computation.8 | convolution fusion | flops 1346371584 | bytes 8127488 | tf_op jit(solution)/shard_map/dot_general | solution.py:231
  22.5 1.9 %collective-permute-done.1.rest_1_ = bf16[2,528,128]{2,1,0:T(8,128)(2,1)S(1)} collective-permute-done((bf16[2,528,128]{2,1,0:T(8,128)(2,1)S(1)}, bf16[2,528,128]{2,1,0:T(8,128)(2,1)S(1)}, u32[]{:S(2)}, u32[]{:S(2)}) %collective-permute-start.1) | collective-permute-done | bytes 270368 | tf_op jit(solution)/shard_map/ppermute | solution.py:48
  27.5 3.4 %collective-permute-start.7 = (bf16[2,528,128]{2,1,0:T(8,128)(2,1)S(1)}, bf16[2,528,128]{2,1,0:T(8,128)(2,1)S(1)}, u32[]{:S(2)}, u32[]{:S(2)}) collective-permute-start(bf16[2,528,128]{2,1,0:T(8,128)(2,1)S(1)} %collective-permute-done.4.rest_4_), channel_id=1, source_target_pairs={{128,144},{136,184},{144,160},{152,136},{160,176},{168,152},{176,1... | collective-permute-start | bytes 811016 | tf_op jit(solution)/shard_map/ppermute | solution.py:48
  32.2 4.6 %attend_first.1 = (f32[528,256]{1,0:T(8,128)S(1)}, f32[528,256]{1,0:T(8,128)S(1)}) custom-call(s32[2]{0:T(128)S(1)} %pad_add_fusion.at_ref, bf16[1,528,128]{2,1,0:T(8,128)(2,1)S(1)} %maximum_bitcast_fusion.rest_0_, bf16[2,528,128]{2,1,0:T(8,128)(2,1)S(1)} %collective-permute-done.1.rest_1_, bf16[1,528,128]{2,1,0:T(8,128)(2,1)S(1)} %collective-permute-done.2.rest_2_, ...), custom_call_target="tpu_custom_call" | custom-call | flops 134217728 | bytes 135168 | tf_op jit(solution)/shard_map/attend_first/pallas_call | solution.py:248
  36.8 3.4 %collective-permute-done.8.rest_3_ = bf16[1,528,128]{2,1,0:T(8,128)(2,1)S(1)} collective-permute-done((bf16[1,528,128]{2,1,0:T(8,128)(2,1)S(1)}, bf16[1,528,128]{2,1,0:T(8,128)(2,1)S(1)}, u32[]{:S(2)}, u32[]{:S(2)}) %collective-permute-start.8) | collective-permute-done | bytes 135200 | tf_op jit(solution)/shard_map/ppermute | solution.py:48
  40.3 1.8 %collective-permute-done.6.rest_1_ = bf16[3,528,128]{2,1,0:T(8,128)(2,1)S(1)} collective-permute-done((bf16[3,528,128]{2,1,0:T(8,128)(2,1)S(1)}, bf16[3,528,128]{2,1,0:T(8,128)(2,1)S(1)}, u32[]{:S(2)}, u32[]{:S(2)}) %collective-permute-start.6) | collective-permute-done | bytes 405536 | tf_op jit(solution)/shard_map/ppermute | solution.py:48
  42.1 5.0 %attend_rest_other.1 = f32[528,256]{1,0:T(8,128)S(1)} custom-call(s32[2]{0:T(128)S(1)} %pad_add_fusion.at_ref, bf16[3,528,128]{2,1,0:T(8,128)(2,1)S(1)} %collective-permute-done.5.rest_0_, bf16[3,528,128]{2,1,0:T(8,128)(2,1)S(1)} %collective-permute-done.6.rest_1_, bf16[2,528,128]{2,1,0:T(8,128)(2,1)S(1)} %collective-permute-done.7.rest_2_, ...), custom_call_target="tpu_custom_call" | custom-call | flops 134217728 | bytes 135168 | tf_op jit(solution)/shard_map/attend_rest_other/pallas_call | solution.py:248
  47.2 4.8 %attend_rest_own.1 = (f32[528,256]{1,0:T(8,128)S(1)}, bf16[512,5120]{1,0:T(8,128)(2,1)S(1)}) custom-call(s32[2]{0:T(128)S(1)} %pad_add_fusion.at_ref, bf16[3,528,128]{2,1,0:T(8,128)(2,1)S(1)} %collective-permute-done.5.rest_0_, bf16[3,528,128]{2,1,0:T(8,128)(2,1)S(1)} %collective-permute-done.6.rest_1_, ...), custom_call_target="tpu_custom_call" | custom-call | flops 134217728 | bytes 135168 | tf_op jit(solution)/shard_map/attend_rest_own/pallas_call | solution.py:266
  52.0 2.5 %project_attended.1 = (bf16[4,80,640]{2,1,0:T(8,128)(2,1)S(1)}, bf16[4,80,640]{2,1,0:T(8,128)(2,1)S(1)}, bf16[4,96,640]{2,1,0:T(8,128)(2,1)S(1)}, bf16[4,96,640]...) custom-call(s32[2]{0:T(128)S(1)} %pad_add_fusion.at_ref, ...), custom_call_target="tpu_custom_call" | custom-call | flops 1610612736 | bytes 1622016 | tf_op jit(solution)/shard_map/project_attended/pallas_call | solution.py:285
  54.5 1.6 %collective-permute-start.11 = (bf16[4,80,640]{2,1,0:T(8,128)(2,1)S(1)}, bf16[4,80,640]{2,1,0:T(8,128)(2,1)S(1)}, u32[]{:S(2)}, u32[]{:S(2)}) collective-permute-start(bf16[4,80,640]{2,1,0:T(8,128)(2,1)S(1)} %get-tuple-element.52), channel_id=1, source_target_pairs={{0,1},{1,0},{2,3},{3,2},{4,5},{5,4},{6,7},{7,6},{8,9},{9,8},{10,11... | collective-permute-start | bytes 1228808 | tf_op jit(solution)/shard_map/ppermute | solution.py:297
  57.1 2.1 %collective-permute-start.14 = (bf16[4,96,640]{2,1,0:T(8,128)(2,1)S(1)}, bf16[4,96,640]{2,1,0:T(8,128)(2,1)S(1)}, u32[]{:S(2)}, u32[]{:S(2)}) collective-permute-start(bf16[4,96,640]{2,1,0:T(8,128)(2,1)S(1)} %get-tuple-element.54), channel_id=1, source_target_pairs={{0,3},{1,2},{2,1},{3,0},{4,7},{5,6},{6,5},{7,4},{8,11},{9,10},{10,... | collective-permute-start | bytes 1474568 | tf_op jit(solution)/shard_map/ppermute | solution.py:297
  59.2 7.3 %collective-permute-done.11 = bf16[4,80,640]{2,1,0:T(8,128)(2,1)S(1)} collective-permute-done((bf16[4,80,640]{2,1,0:T(8,128)(2,1)S(1)}, bf16[4,80,640]{2,1,0:T(8,128)(2,1)S(1)}, u32[]{:S(2)}, u32[]{:S(2)}) %collective-permute-start.11) | collective-permute-done | bytes 409632 | tf_op jit(solution)/shard_map/ppermute | solution.py:297
  66.6 2.8 %collective-permute-start.12 = (bf16[2,80,640]{2,1,0:T(8,128)(2,1)S(1)}, bf16[2,80,640]{2,1,0:T(8,128)(2,1)S(1)}, u32[]{:S(2)}, u32[]{:S(2)}) collective-permute-start(bf16[2,80,640]{2,1,0:T(8,128)(2,1)S(1)} %slice.98), channel_id=1, source_target_pairs={{0,3},{1,2},{2,1},{3,0},{4,7},{5,6},{6,5},{7,4},{8,11},{9,10},{10,... | collective-permute-start | bytes 614408 | tf_op jit(solution)/shard_map/ppermute | solution.py:297
  69.9 2.6 %collective-permute-done.14 = bf16[4,96,640]{2,1,0:T(8,128)(2,1)S(1)} collective-permute-done((bf16[4,96,640]{2,1,0:T(8,128)(2,1)S(1)}, bf16[4,96,640]{2,1,0:T(8,128)(2,1)S(1)}, u32[]{:S(2)}, u32[]{:S(2)}) %collective-permute-start.14) | collective-permute-done | bytes 491552 | tf_op jit(solution)/shard_map/ppermute | solution.py:297
  73.7 2.1 %collective-permute-done.12 = bf16[2,80,640]{2,1,0:T(8,128)(2,1)S(1)} collective-permute-done((bf16[2,80,640]{2,1,0:T(8,128)(2,1)S(1)}, bf16[2,80,640]{2,1,0:T(8,128)(2,1)S(1)}, u32[]{:S(2)}, u32[]{:S(2)}) %collective-permute-start.12) | collective-permute-done | bytes 204832 | tf_op jit(solution)/shard_map/ppermute | solution.py:297
  77.0 2.2 %collective-permute-start.19 = (bf16[80,640]{1,0:T(8,128)(2,1)S(1)}, bf16[80,640]{1,0:T(8,128)(2,1)S(1)}, u32[]{:S(2)}, u32[]{:S(2)}) collective-permute-start(bf16[80,640]{1,0:T(8,128)(2,1)S(1)} %fusion.23), channel_id=1, source_target_pairs={{0,3},{1,2},{2,1},{3,0},{4,7},{5,6},{6,5},{7,4},{8,11},{9,10},{10,... | collective-permute-start | bytes 307208 | tf_op jit(solution)/shard_map/ppermute | solution.py:297
  79.2 1.9 %collective-permute-done.13 = bf16[80,640]{1,0:T(8,128)(2,1)S(1)} collective-permute-done((bf16[80,640]{1,0:T(8,128)(2,1)S(1)}, bf16[80,640]{1,0:T(8,128)(2,1)S(1)}, u32[]{:S(2)}, u32[]{:S(2)}) %collective-permute-start.13) | collective-permute-done | bytes 102432 | tf_op jit(solution)/shard_map/ppermute | solution.py:297
  81.3 1.7 %collective-permute-done.19 = bf16[80,640]{1,0:T(8,128)(2,1)S(1)} collective-permute-done((bf16[80,640]{1,0:T(8,128)(2,1)S(1)}, bf16[80,640]{1,0:T(8,128)(2,1)S(1)}, u32[]{:S(2)}, u32[]{:S(2)}) %collective-permute-start.19) | collective-permute-done | bytes 102432 | tf_op jit(solution)/shard_map/ppermute | solution.py:297
  83.0 3.1 %collective-permute-done.16 = bf16[96,640]{1,0:T(8,128)(2,1)S(1)} collective-permute-done((bf16[96,640]{1,0:T(8,128)(2,1)S(1)}, bf16[96,640]{1,0:T(8,128)(2,1)S(1)}, u32[]{:S(2)}, u32[]{:S(2)}) %collective-permute-start.16) | collective-permute-done | bytes 122912 | tf_op jit(solution)/shard_map/ppermute | solution.py:297
  (49 shorter events, 12.7 us)
Async XLA Ops:
  1.7 1.4 %collective-permute-start = (bf16[1,528,128]{2,1,0:T(8,128)(2,1)S(1)}, bf16[1,528,128]{2,1,0:T(8,128)(2,1)S(1)}, u32[]{:S(2)}, u32[]{:S(2)}) collective-permute-start(bf16[1,528,128]{2,1,0:T(8,128)(2,1)S(1)} %maximum_bitcast_fusion.rest_0_), channel_id=1, source_target_pairs={{0,8},{8,0},{16,24},{24,16},{32,40},{40,32},{48,56},{56,48},{64,72... | collective-permute-start | bytes 405512 | tf_op jit(solution)/shard_map/ppermute | solution.py:48
  3.1 19.3 %collective-permute-start.2 = (bf16[1,528,128]{2,1,0:T(8,128)(2,1)S(1)}, bf16[1,528,128]{2,1,0:T(8,128)(2,1)S(1)}, u32[]{:S(2)}, u32[]{:S(2)}) collective-permute-start(bf16[1,528,128]{2,1,0:T(8,128)(2,1)S(1)} %maximum_bitcast_fusion.rest_0_), channel_id=1, source_target_pairs={{0,32},{8,40},{16,48},{24,56},{32,0},{40,8},{48,16},{56,24},{64,96... | collective-permute-start | bytes 405512 | tf_op jit(solution)/shard_map/ppermute | solution.py:48
  10.4 12.1 %collective-permute-start.4 = (bf16[2,528,128]{2,1,0:T(8,128)(2,1)S(1)}, bf16[2,528,128]{2,1,0:T(8,128)(2,1)S(1)}, u32[]{:S(2)}, u32[]{:S(2)}) collective-permute-start(bf16[2,528,128]{2,1,0:T(8,128)(2,1)S(1)} %constant_dynamic-update-slice_fusion), channel_id=1, source_target_pairs={{0,128},{8,136},{16,144},{24,152},{32,160},{40,168},{48,176},{56,1... | collective-permute-start | bytes 811016 | tf_op jit(solution)/shard_map/ppermute | solution.py:48
  11.7 10.8 %collective-permute-start.3 = (bf16[2,528,128]{2,1,0:T(8,128)(2,1)S(1)}, bf16[2,528,128]{2,1,0:T(8,128)(2,1)S(1)}, u32[]{:S(2)}, u32[]{:S(2)}) collective-permute-start(bf16[2,528,128]{2,1,0:T(8,128)(2,1)S(1)} %constant_dynamic-update-slice_fusion), channel_id=1, source_target_pairs={{0,64},{8,200},{16,80},{24,216},{32,96},{40,232},{48,112},{56,248}... | collective-permute-start | bytes 811016 | tf_op jit(solution)/shard_map/ppermute | solution.py:48
  13.0 11.5 %collective-permute-start.1 = (bf16[2,528,128]{2,1,0:T(8,128)(2,1)S(1)}, bf16[2,528,128]{2,1,0:T(8,128)(2,1)S(1)}, u32[]{:S(2)}, u32[]{:S(2)}) collective-permute-start(bf16[2,528,128]{2,1,0:T(8,128)(2,1)S(1)} %constant_dynamic-update-slice_fusion), channel_id=1, source_target_pairs={{0,16},{8,56},{16,32},{24,8},{32,48},{40,24},{48,0},{56,40},{64,80... | collective-permute-start | bytes 811016 | tf_op jit(solution)/shard_map/ppermute | solution.py:48
  24.5 17.6 %collective-permute-start.6 = (bf16[3,528,128]{2,1,0:T(8,128)(2,1)S(1)}, bf16[3,528,128]{2,1,0:T(8,128)(2,1)S(1)}, u32[]{:S(2)}, u32[]{:S(2)}) collective-permute-start(bf16[3,528,128]{2,1,0:T(8,128)(2,1)S(1)} %constant_dynamic-update-slice_fusion.2), channel_id=1, source_target_pairs={{0,192},{8,200},{16,208},{24,216},{32,224},{40,232},{48,240},{56,2... | collective-permute-start | bytes 1216520 | tf_op jit(solution)/shard_map/ppermute | solution.py:48
  25.8 16.3 %collective-permute-start.5 = (bf16[3,528,128]{2,1,0:T(8,128)(2,1)S(1)}, bf16[3,528,128]{2,1,0:T(8,128)(2,1)S(1)}, u32[]{:S(2)}, u32[]{:S(2)}) collective-permute-start(bf16[3,528,128]{2,1,0:T(8,128)(2,1)S(1)} %constant_dynamic-update-slice_fusion.2), channel_id=1, source_target_pairs={{0,64},{8,72},{16,80},{24,88},{32,96},{40,104},{48,112},{56,120},{... | collective-permute-start | bytes 1216520 | tf_op jit(solution)/shard_map/ppermute | solution.py:48
  27.1 5.1 %collective-permute-start.9 = (bf16[640,256]{1,0:T(8,128)(2,1)S(1)}, bf16[640,256]{1,0:T(8,128)(2,1)S(1)}, u32[]{:S(2)}, u32[]{:S(2)}) collective-permute-start(bf16[640,256]{1,0:T(8,128)(2,1)S(1)} %pad_maximum_fusion.rest_5_.rest_4_), channel_id=1, source_target_pairs={{0,8},{8,0},{16,24},{24,16},{32,40},{40,32},{48,56},{56,48},{64,72... | collective-permute-start | bytes 983048 | tf_op jit(solution)/shard_map/ppermute | solution.py:48
  27.5 12.8 %collective-permute-start.7 = (bf16[2,528,128]{2,1,0:T(8,128)(2,1)S(1)}, bf16[2,528,128]{2,1,0:T(8,128)(2,1)S(1)}, u32[]{:S(2)}, u32[]{:S(2)}) collective-permute-start(bf16[2,528,128]{2,1,0:T(8,128)(2,1)S(1)} %collective-permute-done.4.rest_4_), channel_id=1, source_target_pairs={{128,144},{136,184},{144,160},{152,136},{160,176},{168,152},{176,1... | collective-permute-start | bytes 811016 | tf_op jit(solution)/shard_map/ppermute | solution.py:48
  30.9 9.4 %collective-permute-start.8 = (bf16[1,528,128]{2,1,0:T(8,128)(2,1)S(1)}, bf16[1,528,128]{2,1,0:T(8,128)(2,1)S(1)}, u32[]{:S(2)}, u32[]{:S(2)}) collective-permute-start(bf16[1,528,128]{2,1,0:T(8,128)(2,1)S(1)} %collective-permute-done.2.rest_2_), channel_id=1, source_target_pairs={{0,128},{8,136},{16,144},{24,152},{32,160},{40,168},{48,176},{56,1... | collective-permute-start | bytes 405512 | tf_op jit(solution)/shard_map/ppermute | solution.py:48
  47.1 4.9 %collective-permute-start.10 = (f32[528,256]{1,0:T(8,128)S(1)}, f32[528,256]{1,0:T(8,128)S(1)}, u32[]{:S(2)}, u32[]{:S(2)}) collective-permute-start(f32[528,256]{1,0:T(8,128)S(1)} %attend_rest_other.1), channel_id=1, source_target_pairs={{0,8},{8,0},{16,24},{24,16},{32,40},{40,32},{48,56},{56,48},{64,72... | collective-permute-start | bytes 1622024 | tf_op jit(solution)/shard_map/ppermute | solution.py:48
  54.5 12.0 %collective-permute-start.11 = (bf16[4,80,640]{2,1,0:T(8,128)(2,1)S(1)}, bf16[4,80,640]{2,1,0:T(8,128)(2,1)S(1)}, u32[]{:S(2)}, u32[]{:S(2)}) collective-permute-start(bf16[4,80,640]{2,1,0:T(8,128)(2,1)S(1)} %get-tuple-element.52), channel_id=1, source_target_pairs={{0,1},{1,0},{2,3},{3,2},{4,5},{5,4},{6,7},{7,6},{8,9},{9,8},{10,11... | collective-permute-start | bytes 1228808 | tf_op jit(solution)/shard_map/ppermute | solution.py:297
  56.1 13.3 %collective-permute-start.17 = (bf16[4,80,640]{2,1,0:T(8,128)(2,1)S(1)}, bf16[4,80,640]{2,1,0:T(8,128)(2,1)S(1)}, u32[]{:S(2)}, u32[]{:S(2)}) collective-permute-start(bf16[4,80,640]{2,1,0:T(8,128)(2,1)S(1)} %get-tuple-element.56), channel_id=1, source_target_pairs={{0,4},{1,5},{2,6},{3,7},{4,0},{5,1},{6,2},{7,3},{8,12},{9,13},{10,... | collective-permute-start | bytes 1228808 | tf_op jit(solution)/shard_map/ppermute | solution.py:297
  57.1 15.3 %collective-permute-start.14 = (bf16[4,96,640]{2,1,0:T(8,128)(2,1)S(1)}, bf16[4,96,640]{2,1,0:T(8,128)(2,1)S(1)}, u32[]{:S(2)}, u32[]{:S(2)}) collective-permute-start(bf16[4,96,640]{2,1,0:T(8,128)(2,1)S(1)} %get-tuple-element.54), channel_id=1, source_target_pairs={{0,3},{1,2},{2,1},{3,0},{4,7},{5,6},{6,5},{7,4},{8,11},{9,10},{10,... | collective-permute-start | bytes 1474568 | tf_op jit(solution)/shard_map/ppermute | solution.py:297
  66.6 9.2 %collective-permute-start.12 = (bf16[2,80,640]{2,1,0:T(8,128)(2,1)S(1)}, bf16[2,80,640]{2,1,0:T(8,128)(2,1)S(1)}, u32[]{:S(2)}, u32[]{:S(2)}) collective-permute-start(bf16[2,80,640]{2,1,0:T(8,128)(2,1)S(1)} %slice.98), channel_id=1, source_target_pairs={{0,3},{1,2},{2,1},{3,0},{4,7},{5,6},{6,5},{7,4},{8,11},{9,10},{10,... | collective-permute-start | bytes 614408 | tf_op jit(solution)/shard_map/ppermute | solution.py:297
  69.6 7.4 %collective-permute-start.18 = (bf16[2,80,640]{2,1,0:T(8,128)(2,1)S(1)}, bf16[2,80,640]{2,1,0:T(8,128)(2,1)S(1)}, u32[]{:S(2)}, u32[]{:S(2)}) collective-permute-start(bf16[2,80,640]{2,1,0:T(8,128)(2,1)S(1)} %slice.97), channel_id=1, source_target_pairs={{0,1},{1,0},{2,3},{3,2},{4,5},{5,4},{6,7},{7,6},{8,9},{9,8},{10,11... | collective-permute-start | bytes 614408 | tf_op jit(solution)/shard_map/ppermute | solution.py:297
  72.6 8.5 %collective-permute-start.15 = (bf16[2,96,640]{2,1,0:T(8,128)(2,1)S(1)}, bf16[2,96,640]{2,1,0:T(8,128)(2,1)S(1)}, u32[]{:S(2)}, u32[]{:S(2)}) collective-permute-start(bf16[2,96,640]{2,1,0:T(8,128)(2,1)S(1)} %slice.96), channel_id=1, source_target_pairs={{0,4},{1,5},{2,6},{3,7},{4,0},{5,1},{6,2},{7,3},{8,12},{9,13},{10,... | collective-permute-start | bytes 737288 | tf_op jit(solution)/shard_map/ppermute | solution.py:297
  75.8 5.2 %collective-permute-start.13 = (bf16[80,640]{1,0:T(8,128)(2,1)S(1)}, bf16[80,640]{1,0:T(8,128)(2,1)S(1)}, u32[]{:S(2)}, u32[]{:S(2)}) collective-permute-start(bf16[80,640]{1,0:T(8,128)(2,1)S(1)} %fusion.22), channel_id=1, source_target_pairs={{0,4},{1,5},{2,6},{3,7},{4,0},{5,1},{6,2},{7,3},{8,12},{9,13},{10,... | collective-permute-start | bytes 307208 | tf_op jit(solution)/shard_map/ppermute | solution.py:297
  77.0 6.0 %collective-permute-start.19 = (bf16[80,640]{1,0:T(8,128)(2,1)S(1)}, bf16[80,640]{1,0:T(8,128)(2,1)S(1)}, u32[]{:S(2)}, u32[]{:S(2)}) collective-permute-start(bf16[80,640]{1,0:T(8,128)(2,1)S(1)} %fusion.23), channel_id=1, source_target_pairs={{0,3},{1,2},{2,1},{3,0},{4,7},{5,6},{6,5},{7,4},{8,11},{9,10},{10,... | collective-permute-start | bytes 307208 | tf_op jit(solution)/shard_map/ppermute | solution.py:297
  81.2 5.0 %collective-permute-start.16 = (bf16[96,640]{1,0:T(8,128)(2,1)S(1)}, bf16[96,640]{1,0:T(8,128)(2,1)S(1)}, u32[]{:S(2)}, u32[]{:S(2)}) collective-permute-start(bf16[96,640]{1,0:T(8,128)(2,1)S(1)} %fusion.21), channel_id=1, source_target_pairs={{0,1},{1,0},{2,3},{3,2},{4,5},{5,4},{6,7},{7,6},{8,9},{9,8},{10,11... | collective-permute-start | bytes 368648 | tf_op jit(solution)/shard_map/ppermute | solution.py:297

commit v10 on v9

--- a/solution.py
+++ b/solution.py
@@ -12,7 +12,8 @@
 HEAD_DIM = 128
 BLOCK = 256
 PACK = 2 * BLOCK + 16
-CHAINS = ((slice(0, 80), (1, 3, 4)), (slice(80, 176), (3, 4, 1)), (slice(176, 256), (4, 1, 3)))
+CHAINS = ((slice(0, 96), (1, 3, 4)), (slice(96, 176), (3, 4, 1)), (slice(176, 256), (4, 1, 3)))
+LINKS = (1, 3, 4)
 SIDES = tuple(itertools.product((0, 1), repeat=3))
 REACH = 24
 COLS = 640
@@ -26,7 +27,7 @@
 
 
 def away(sides):
-    return sum(step * side for step, side in zip((1, 3, 4), sides)) if sides[:2] != (1, 1) else 2 + 4 * sides[2]
+    return sum(step * side for step, side in zip(LINKS, sides)) if sides[:2] != (1, 1) else 2 + 4 * sides[2]
 
 
 def ctx_id(y, z, c):
@@ -84,8 +85,12 @@
 
 def rest_slots(y, z, c):
     d = 2 * c - 1
-    near = [[(y + e, z + d, c), (y + e, z + d, 1 - c), (y + e, z + 2, c)] for e in (-1, 1)]
-    return near + [[(y + 2, z + d, c), (y + 2, z + d, 1 - c)], [(y + 2, z + 2, c)]]
+    return [[(y + e, z + d, c), (y + e, z + d, 1 - c), (y + e, z + 2, c)] for e in (-1, 1)] + [[(y + 2, z + 2, c)]]
+
+
+def far_slots(y, z, c):
+    d = 2 * c - 1
+    return [[(y + 2, z + d, c), (y + 2, z + d, 1 - c)]]
 
 
 def attend_blocks(kv_ref, places, diagonal, q_ref, state_ref):
@@ -161,17 +166,21 @@
     attend_pieces(at_ref, slots, pieces, all_ref, order_ref, (q_ref, s_ref, q_2_ref, s_2_ref))
 
 
-def more_kernel(slots, n, other, at_ref, *rest):
-    pieces, (q_ref, s_in, s_ref, all_ref, order_ref) = rest[:n], rest[n:]
-    s_ref[...] = s_in[...]
-    attend_pieces(at_ref, slots, pieces, all_ref, order_ref, (q_ref, s_ref), (other,))
-
-
-def more_and_fetch_kernel(slots, n, other, at_ref, *rest):
+def more_kernel(slots, n, others, at_ref, *rest):
+    k = len(others)
+    pieces, queries, before, after = rest[:n], rest[n : n + k], rest[n + k : n + 2 * k], rest[n + 2 * k : n + 3 * k]
+    all_ref, order_ref = rest[n + 3 * k :]
+    for s_in, s_ref in zip(before, after):
+        s_ref[...] = s_in[...]
+    sets = [ref for pair in zip(queries, after) for ref in pair]
+    attend_pieces(at_ref, slots, pieces, all_ref, order_ref, sets, others)
+
+
+def more_and_fetch_kernel(slots, n, others, at_ref, *rest):
     w_hbm, s_ref, w_ref, all_ref, order_ref, sem = rest[n + 2 :]
     copy = pltpu.make_async_copy(w_hbm, w_ref, sem)
     copy.start()
-    more_kernel(slots, n, other, at_ref, *rest[: n + 2], s_ref, all_ref, order_ref)
+    more_kernel(slots, n, others, at_ref, *rest[: n + 2], s_ref, all_ref, order_ref)
     copy.wait()
 
 
@@ -189,7 +198,7 @@
     for sides in SIDES:
         cols = pl.ds(pl.multiple_of((section ^ away(sides)) * COLS, 128), COLS)
         part = jnp.dot(att_ref[...], w_ref[:, cols], preferred_element_type=F32).astype(BF16)
-        crossed = dict(zip(CHAINS[0][1], sides))
+        crossed = dict(zip(LINKS, sides))
         for i, (rows, order) in enumerate(CHAINS):
             first, second, third = (crossed[step] for step in order)
             outs[2 * i + 1 - first][2 * second + third] = part[rows]
@@ -219,11 +228,11 @@
     own = jnp.concatenate([k_cache, v_cache, jnp.broadcast_to(smaller[None, :], (16, HEAD_DIM))], axis=0)[None]
 
     own, other, hidden = lax.optimization_barrier((own, swap_cores(own), hidden))
-    pair = jnp.concatenate([own, other], axis=0)
+    pair = lax.optimization_barrier(jnp.concatenate([own, other], axis=0))
     z_near = along_z(pair)
     y_near = along_y(pair)
     y_far = move(pair, lambda y, z, c: (y + 2, z, c) if y < 2 else None)
-    z_far = move(own, lambda y, z, c: (y, z + 2, c))
+    z_far = move(pair[:1], lambda y, z, c: (y, z + 2, c))
 
     widened = hidden.astype(F32)
     normed = (widened * lax.rsqrt(jnp.mean(widened * widened, axis=-1, keepdims=True) + 1e-06)).astype(BF16)
@@ -259,17 +268,20 @@
     pieces = [own, z_near, z_far, y_near, y_far]
     first = functools.partial(start_kernel, first_slots, len(pieces))
     state, state_2 = attend(first, 7, pieces, (q, q_2), (), "attend_first")
-    pieces, state, state_2 = lax.optimization_barrier(((up, around, far_near, far_far), state, state_2))
-    rest = functools.partial(more_kernel, rest_slots, len(pieces), 1)
-    (state_2,) = attend(rest, 9, pieces, (q_2,), (state_2,), "attend_rest_other")
+    far_near, state, state_2 = lax.optimization_barrier((far_near, state, state_2))
+    far = functools.partial(more_kernel, far_slots, 1, (0, 1))
+    state, state_2 = attend(far, 2, [far_near], (q, q_2), (state, state_2), "attend_far")
+    pieces, state, state_2 = lax.optimization_barrier(((up, around, far_far), state, state_2))
+    rest = functools.partial(more_kernel, rest_slots, len(pieces), (1,))
+    (state_2,) = attend(rest, 7, pieces, (q_2,), (state_2,), "attend_rest_other")
     state_2, state = lax.optimization_barrier((state_2, state))
     state, w_held = pl.pallas_call(
-        functools.partial(more_and_fetch_kernel, rest_slots, len(pieces), 0),
+        functools.partial(more_and_fetch_kernel, rest_slots, len(pieces), (0,)),
         out_shape=(STATE, jax.ShapeDtypeStruct(w_out.shape, BF16)),
         in_specs=[SMEM] + [VMEM] * (len(pieces) + 2) + [pl.BlockSpec(memory_space=pltpu.HBM)],
         out_specs=(VMEM,) * 2,
         scratch_shapes=[
-            pltpu.VMEM((9, PACK, HEAD_DIM), BF16),
+            pltpu.VMEM((7, PACK, HEAD_DIM), BF16),
             pltpu.SMEM((16,), jnp.int32),
             pltpu.SemaphoreType.DMA,
         ],

time: 87.3 us -> 88.5 us (1.014)
  starting transfers between devices: 31.5 us -> 25.6 us
  waiting for transfers between devices: 26.4 us -> 31.9 us
  Pallas kernels: 16.9 us -> 18.5 us
    ppermute x9, starting transfers between devices: 12.4 us -> 8.1 us  [exchange(): return lax.ppermute(x, 'section', [(i, i ^ step) for i in range(8)])]
    ppermute x9, waiting for transfers between devices: 18.6 us -> 22.2 us  [exchange(): return lax.ppermute(x, 'section', [(i, i ^ step) for i in range(8)])]
    pallas_call x2 -> x3, Pallas kernels: 9.6 us -> 12 us  [attend(): pl.pallas_call(kernel, out_shape=out_shape, in_specs=[SMEM] + [VMEM] * (l...]
    ppermute x11, waiting for transfers between devices: 7.82 us -> 9.65 us  [move(): return lax.ppermute(x, 'ctx', ctx_pairs(step))]
    ppermute x11, starting transfers between devices: 19.1 us -> 17.5 us  [move(): return lax.ppermute(x, 'ctx', ctx_pairs(step))]
  transfers between devices with their start and end apart: 20 -> 20, of which waited for: 10 -> 11; matrix products, arithmetic and copies ran while one was open for 11% -> 11% of each run, Pallas kernels for 11% -> 14%
where the time goes in v10:
time: 88.5 us; the launch traced here: 88.1 us
  waiting for transfers between devices  31.9 us (36%)
  starting transfers between devices  25.6 us (29%)
  Pallas kernels  18.5 us (21%)
  other arithmetic  6.09 us (7%)
  matrix products  5.57 us (6%)
    ppermute x9, waiting for transfers between devices, exchange(): return lax.ppermute(x, 'section', [(i, i ^ step) for i in range(8)])  22.2 us
    ppermute x11, starting transfers between devices, move(): return lax.ppermute(x, 'ctx', ctx_pairs(step))  17.5 us
    pallas_call x3, Pallas kernels, attend(): pl.pallas_call(kernel, out_shape=out_shape, in_specs=[SMEM] + [VMEM] * (l...  12 us
    ppermute x11, waiting for transfers between devices, move(): return lax.ppermute(x, 'ctx', ctx_pairs(step))  9.65 us
    ppermute x9, starting transfers between devices, exchange(): return lax.ppermute(x, 'section', [(i, i ^ step) for i in range(8)])  8.1 us
    dot_general x1, matrix products, per_device(): lax.dot_general(w_query, normed, (((0,), (1,)), ((), ())), preferred_elem...  5.57 us
    pallas_call x1, Pallas kernels, per_device(): pl.pallas_call(functools.partial(more_and_fetch_kernel, rest_slots, len(p...  4.04 us
    pallas_call x1, Pallas kernels, per_device(): pl.pallas_call(last_kernel, out_shape=tuple(out_shape), in_specs=[SMEM, V...  2.5 us
  transfers between devices with their start and end apart: 20, of which 11 were waited for; matrix products, arithmetic and copies ran while one was open for 11% of the time, Pallas kernels for 14%

profile of v10, /device:TPU:24, one launch (start us, length us, event | category | flops | bytes accessed | tf_op | source)
XLA Modules:
  0.0 88.1 jit_solution(4211648323071133557)
XLA Ops:
  3.2 1.3 %collective-permute-start.4 = (bf16[2,528,128]{2,1,0:T(8,128)(2,1)S(1)}, bf16[2,528,128]{2,1,0:T(8,128)(2,1)S(1)}, u32[]{:S(2)}, u32[]{:S(2)}) collective-permute-start(bf16[2,528,128]{2,1,0:T(8,128)(2,1)S(1)} %pad_maximum_fusion.2), channel_id=1, source_target_pairs={{0,128},{8,136},{16,144},{24,152},{32,160},{40,168},{48,176},{56,1... | collective-permute-start | bytes 811016 | tf_op jit(solution)/shard_map/ppermute | solution.py:49
  4.5 1.3 %collective-permute-start.3 = (bf16[2,528,128]{2,1,0:T(8,128)(2,1)S(1)}, bf16[2,528,128]{2,1,0:T(8,128)(2,1)S(1)}, u32[]{:S(2)}, u32[]{:S(2)}) collective-permute-start(bf16[2,528,128]{2,1,0:T(8,128)(2,1)S(1)} %pad_maximum_fusion.2), channel_id=1, source_target_pairs={{0,64},{8,200},{16,80},{24,216},{32,96},{40,232},{48,112},{56,248}... | collective-permute-start | bytes 811016 | tf_op jit(solution)/shard_map/ppermute | solution.py:49
  5.8 3.3 %collective-permute-start.1 = (bf16[2,528,128]{2,1,0:T(8,128)(2,1)S(1)}, bf16[2,528,128]{2,1,0:T(8,128)(2,1)S(1)}, u32[]{:S(2)}, u32[]{:S(2)}) collective-permute-start(bf16[2,528,128]{2,1,0:T(8,128)(2,1)S(1)} %pad_maximum_fusion.2), channel_id=1, source_target_pairs={{0,16},{8,56},{16,32},{24,8},{32,48},{40,24},{48,0},{56,40},{64,80... | collective-permute-start | bytes 811016 | tf_op jit(solution)/shard_map/ppermute | solution.py:49
  9.1 2.3 %fusion = f32[256]{0:T(256)S(1)} fusion(bf16[256,5120]{1,0:T(8,128)(2,1)} %param.6), kind=kLoop, calls=%fused_computation.2 | loop fusion | flops 3931904 | bytes 2622464 | tf_op jit(solution)/shard_map/reduce_sum | solution.py:238
  11.5 5.5 %collective-permute-start.2 = (bf16[1,528,128]{2,1,0:T(8,128)(2,1)S(1)}, bf16[1,528,128]{2,1,0:T(8,128)(2,1)S(1)}, u32[]{:S(2)}, u32[]{:S(2)}) collective-permute-start(bf16[1,528,128]{2,1,0:T(8,128)(2,1)S(1)} %slice.58), channel_id=1, source_target_pairs={{0,32},{8,40},{16,48},{24,56},{32,0},{40,8},{48,16},{56,24},{64,96... | collective-permute-start | bytes 405512 | tf_op jit(solution)/shard_map/ppermute | solution.py:49
  17.0 5.6 %fusion.11 = bf16[512,256]{1,0:T(8,128)(2,1)S(1)} fusion(bf16[5120,512]{1,0:T(8,128)(2,1)} %param.10, bf16[256,5120]{1,0:T(8,128)(2,1)} %param.6, f32[256]{0:T(256)S(1)} %add_rsqrt_fusion), kind=kOutput, calls=%fused_computation.8 | convolution fusion | flops 1346371584 | bytes 8127488 | tf_op jit(solution)/shard_map/dot_general | solution.py:240
  22.6 3.7 %collective-permute-done.2.rest_2_ = bf16[1,528,128]{2,1,0:T(8,128)(2,1)S(1)} collective-permute-done((bf16[1,528,128]{2,1,0:T(8,128)(2,1)S(1)}, bf16[1,528,128]{2,1,0:T(8,128)(2,1)S(1)}, u32[]{:S(2)}, u32[]{:S(2)}) %collective-permute-start.2) | collective-permute-done | bytes 135200 | tf_op jit(solution)/shard_map/ppermute | solution.py:49
  26.3 1.3 %collective-permute-start.6 = (bf16[3,528,128]{2,1,0:T(8,128)(2,1)S(1)}, bf16[3,528,128]{2,1,0:T(8,128)(2,1)S(1)}, u32[]{:S(2)}, u32[]{:S(2)}) collective-permute-start(bf16[3,528,128]{2,1,0:T(8,128)(2,1)S(1)} %constant_dynamic-update-slice_fusion), channel_id=1, source_target_pairs={{0,192},{8,200},{16,208},{24,216},{32,224},{40,232},{48,240},{56,2... | collective-permute-start | bytes 1216520 | tf_op jit(solution)/shard_map/ppermute | solution.py:49
  27.6 1.3 %collective-permute-start.5 = (bf16[3,528,128]{2,1,0:T(8,128)(2,1)S(1)}, bf16[3,528,128]{2,1,0:T(8,128)(2,1)S(1)}, u32[]{:S(2)}, u32[]{:S(2)}) collective-permute-start(bf16[3,528,128]{2,1,0:T(8,128)(2,1)S(1)} %constant_dynamic-update-slice_fusion), channel_id=1, source_target_pairs={{0,64},{8,72},{16,80},{24,88},{32,96},{40,104},{48,112},{56,120},{... | collective-permute-start | bytes 1216520 | tf_op jit(solution)/shard_map/ppermute | solution.py:49
  29.0 1.9 %collective-permute-start.8 = (bf16[2,528,128]{2,1,0:T(8,128)(2,1)S(1)}, bf16[2,528,128]{2,1,0:T(8,128)(2,1)S(1)}, u32[]{:S(2)}, u32[]{:S(2)}) collective-permute-start(bf16[2,528,128]{2,1,0:T(8,128)(2,1)S(1)} %collective-permute-done.4.rest_4_), channel_id=1, source_target_pairs={{128,144},{136,184},{144,160},{152,136},{160,176},{168,152},{176,1... | collective-permute-start | bytes 811016 | tf_op jit(solution)/shard_map/ppermute | solution.py:49
  32.4 4.6 %attend_first.1 = (f32[528,256]{1,0:T(8,128)S(1)}, f32[528,256]{1,0:T(8,128)S(1)}) custom-call(s32[2]{0:T(128)S(1)} %pad_add_fusion.at_ref, bf16[1,528,128]{2,1,0:T(8,128)(2,1)S(1)} %maximum_bitcast_fusion.rest_0_, bf16[2,528,128]{2,1,0:T(8,128)(2,1)S(1)} %collective-permute-done.1.rest_1_, bf16[1,528,128]{2,1,0:T(8,128)(2,1)S(1)} %collective-permute-done.2.rest_2_, ...), custom_call_target="tpu_custom_call" | custom-call | flops 134217728 | bytes 135168 | tf_op jit(solution)/shard_map/attend_first/pallas_call | solution.py:257
  36.9 5.3 %collective-permute-done.8.rest_0_ = bf16[2,528,128]{2,1,0:T(8,128)(2,1)S(1)} collective-permute-done((bf16[2,528,128]{2,1,0:T(8,128)(2,1)S(1)}, bf16[2,528,128]{2,1,0:T(8,128)(2,1)S(1)}, u32[]{:S(2)}, u32[]{:S(2)}) %collective-permute-start.8) | collective-permute-done | bytes 270368 | tf_op jit(solution)/shard_map/ppermute | solution.py:49
  42.3 3.3 %attend_far.1 = (f32[528,256]{1,0:T(8,128)S(1)}, f32[528,256]{1,0:T(8,128)S(1)}) custom-call(s32[2]{0:T(128)S(1)} %pad_add_fusion.at_ref, bf16[2,528,128]{2,1,0:T(8,128)(2,1)S(1)} %collective-permute-done.8.rest_0_, bf16[640,256]{1,0:T(8,128)(2,1)S(1)} %pad_maximum_fusion.rest_5_.rest_1_.rest_3_, ...), custom_call_target="tpu_custom_call" | custom-call | flops 134217728 | bytes 135168 | tf_op jit(solution)/shard_map/attend_far/pallas_call | solution.py:257
  45.6 4.0 %attend_rest_other.1 = f32[528,256]{1,0:T(8,128)S(1)} custom-call(s32[2]{0:T(128)S(1)} %pad_add_fusion.at_ref, bf16[3,528,128]{2,1,0:T(8,128)(2,1)S(1)} %collective-permute-done.5.rest_0_, bf16[3,528,128]{2,1,0:T(8,128)(2,1)S(1)} %collective-permute-done.6.rest_1_, bf16[1,528,128]{2,1,0:T(8,128)(2,1)S(1)} %collective-permute-done.7.rest_2_, ...), custom_call_target="tpu_custom_call" | custom-call | flops 134217728 | bytes 135168 | tf_op jit(solution)/shard_map/attend_rest_other/pallas_call | solution.py:257
  49.8 4.0 %attend_rest_own.1 = (f32[528,256]{1,0:T(8,128)S(1)}, bf16[512,5120]{1,0:T(8,128)(2,1)S(1)}) custom-call(s32[2]{0:T(128)S(1)} %pad_add_fusion.at_ref, bf16[3,528,128]{2,1,0:T(8,128)(2,1)S(1)} %collective-permute-done.5.rest_0_, bf16[3,528,128]{2,1,0:T(8,128)(2,1)S(1)} %collective-permute-done.6.rest_1_, ...), custom_call_target="tpu_custom_call" | custom-call | flops 134217728 | bytes 135168 | tf_op jit(solution)/shard_map/attend_rest_own/pallas_call | solution.py:278
  53.8 2.5 %project_attended.1 = (bf16[4,96,640]{2,1,0:T(8,128)(2,1)S(1)}, bf16[4,96,640]{2,1,0:T(8,128)(2,1)S(1)}, bf16[4,80,640]{2,1,0:T(8,128)(2,1)S(1)}, bf16[4,80,640]...) custom-call(s32[2]{0:T(128)S(1)} %pad_add_fusion.at_ref, ...), custom_call_target="tpu_custom_call" | custom-call | flops 1610612736 | bytes 1622016 | tf_op jit(solution)/shard_map/project_attended/pallas_call | solution.py:297
  56.3 2.8 %collective-permute-start.14 = (bf16[4,80,640]{2,1,0:T(8,128)(2,1)S(1)}, bf16[4,80,640]{2,1,0:T(8,128)(2,1)S(1)}, u32[]{:S(2)}, u32[]{:S(2)}) collective-permute-start(bf16[4,80,640]{2,1,0:T(8,128)(2,1)S(1)} %get-tuple-element.62), channel_id=1, source_target_pairs={{0,3},{1,2},{2,1},{3,0},{4,7},{5,6},{6,5},{7,4},{8,11},{9,10},{10,... | collective-permute-start | bytes 1228808 | tf_op jit(solution)/shard_map/ppermute | solution.py:309
  59.4 10.1 %collective-permute-done.14 = bf16[4,80,640]{2,1,0:T(8,128)(2,1)S(1)} collective-permute-done((bf16[4,80,640]{2,1,0:T(8,128)(2,1)S(1)}, bf16[4,80,640]{2,1,0:T(8,128)(2,1)S(1)}, u32[]{:S(2)}, u32[]{:S(2)}) %collective-permute-start.14) | collective-permute-done | bytes 409632 | tf_op jit(solution)/shard_map/ppermute | solution.py:309
  71.2 1.3 %collective-permute-done.11 = bf16[4,96,640]{2,1,0:T(8,128)(2,1)S(1)} collective-permute-done((bf16[4,96,640]{2,1,0:T(8,128)(2,1)S(1)}, bf16[4,96,640]{2,1,0:T(8,128)(2,1)S(1)}, u32[]{:S(2)}, u32[]{:S(2)}) %collective-permute-start.11) | collective-permute-done | bytes 491552 | tf_op jit(solution)/shard_map/ppermute | solution.py:309
  73.2 3.2 %collective-permute-done.15 = bf16[2,80,640]{2,1,0:T(8,128)(2,1)S(1)} collective-permute-done((bf16[2,80,640]{2,1,0:T(8,128)(2,1)S(1)}, bf16[2,80,640]{2,1,0:T(8,128)(2,1)S(1)}, u32[]{:S(2)}, u32[]{:S(2)}) %collective-permute-start.15) | collective-permute-done | bytes 204832 | tf_op jit(solution)/shard_map/ppermute | solution.py:309
  77.4 2.1 %collective-permute-start.19 = (bf16[80,640]{1,0:T(8,128)(2,1)S(1)}, bf16[80,640]{1,0:T(8,128)(2,1)S(1)}, u32[]{:S(2)}, u32[]{:S(2)}) collective-permute-start(bf16[80,640]{1,0:T(8,128)(2,1)S(1)} %fusion.23), channel_id=1, source_target_pairs={{0,3},{1,2},{2,1},{3,0},{4,7},{5,6},{6,5},{7,4},{8,11},{9,10},{10,... | collective-permute-start | bytes 307208 | tf_op jit(solution)/shard_map/ppermute | solution.py:309
  79.6 1.7 %collective-permute-done.16 = bf16[80,640]{1,0:T(8,128)(2,1)S(1)} collective-permute-done((bf16[80,640]{1,0:T(8,128)(2,1)S(1)}, bf16[80,640]{1,0:T(8,128)(2,1)S(1)}, u32[]{:S(2)}, u32[]{:S(2)}) %collective-permute-start.16) | collective-permute-done | bytes 102432 | tf_op jit(solution)/shard_map/ppermute | solution.py:309
  82.4 1.5 %collective-permute-start.13 = (bf16[96,640]{1,0:T(8,128)(2,1)S(1)}, bf16[96,640]{1,0:T(8,128)(2,1)S(1)}, u32[]{:S(2)}, u32[]{:S(2)}) collective-permute-start(bf16[96,640]{1,0:T(8,128)(2,1)S(1)} %fusion.21), channel_id=1, source_target_pairs={{0,4},{1,5},{2,6},{3,7},{4,0},{5,1},{6,2},{7,3},{8,12},{9,13},{10,... | collective-permute-start | bytes 368648 | tf_op jit(solution)/shard_map/ppermute | solution.py:309
  83.9 3.4 %collective-permute-done.13 = bf16[96,640]{1,0:T(8,128)(2,1)S(1)} collective-permute-done((bf16[96,640]{1,0:T(8,128)(2,1)S(1)}, bf16[96,640]{1,0:T(8,128)(2,1)S(1)}, u32[]{:S(2)}, u32[]{:S(2)}) %collective-permute-start.13) | collective-permute-done | bytes 122912 | tf_op jit(solution)/shard_map/ppermute | solution.py:309
  (50 shorter events, 10.3 us)
Async XLA Ops:
  1.7 1.4 %collective-permute-start = (bf16[1,528,128]{2,1,0:T(8,128)(2,1)S(1)}, bf16[1,528,128]{2,1,0:T(8,128)(2,1)S(1)}, u32[]{:S(2)}, u32[]{:S(2)}) collective-permute-start(bf16[1,528,128]{2,1,0:T(8,128)(2,1)S(1)} %maximum_bitcast_fusion.rest_0_), channel_id=1, source_target_pairs={{0,8},{8,0},{16,24},{24,16},{32,40},{40,32},{48,56},{56,48},{64,72... | collective-permute-start | bytes 405512 | tf_op jit(solution)/shard_map/ppermute | solution.py:49
  3.2 23.1 %collective-permute-start.4 = (bf16[2,528,128]{2,1,0:T(8,128)(2,1)S(1)}, bf16[2,528,128]{2,1,0:T(8,128)(2,1)S(1)}, u32[]{:S(2)}, u32[]{:S(2)}) collective-permute-start(bf16[2,528,128]{2,1,0:T(8,128)(2,1)S(1)} %pad_maximum_fusion.2), channel_id=1, source_target_pairs={{0,128},{8,136},{16,144},{24,152},{32,160},{40,168},{48,176},{56,1... | collective-permute-start | bytes 811016 | tf_op jit(solution)/shard_map/ppermute | solution.py:49
  4.5 21.8 %collective-permute-start.3 = (bf16[2,528,128]{2,1,0:T(8,128)(2,1)S(1)}, bf16[2,528,128]{2,1,0:T(8,128)(2,1)S(1)}, u32[]{:S(2)}, u32[]{:S(2)}) collective-permute-start(bf16[2,528,128]{2,1,0:T(8,128)(2,1)S(1)} %pad_maximum_fusion.2), channel_id=1, source_target_pairs={{0,64},{8,200},{16,80},{24,216},{32,96},{40,232},{48,112},{56,248}... | collective-permute-start | bytes 811016 | tf_op jit(solution)/shard_map/ppermute | solution.py:49
  5.8 20.5 %collective-permute-start.1 = (bf16[2,528,128]{2,1,0:T(8,128)(2,1)S(1)}, bf16[2,528,128]{2,1,0:T(8,128)(2,1)S(1)}, u32[]{:S(2)}, u32[]{:S(2)}) collective-permute-start(bf16[2,528,128]{2,1,0:T(8,128)(2,1)S(1)} %pad_maximum_fusion.2), channel_id=1, source_target_pairs={{0,16},{8,56},{16,32},{24,8},{32,48},{40,24},{48,0},{56,40},{64,80... | collective-permute-start | bytes 811016 | tf_op jit(solution)/shard_map/ppermute | solution.py:49
  11.5 14.8 %collective-permute-start.2 = (bf16[1,528,128]{2,1,0:T(8,128)(2,1)S(1)}, bf16[1,528,128]{2,1,0:T(8,128)(2,1)S(1)}, u32[]{:S(2)}, u32[]{:S(2)}) collective-permute-start(bf16[1,528,128]{2,1,0:T(8,128)(2,1)S(1)} %slice.58), channel_id=1, source_target_pairs={{0,32},{8,40},{16,48},{24,56},{32,0},{40,8},{48,16},{56,24},{64,96... | collective-permute-start | bytes 405512 | tf_op jit(solution)/shard_map/ppermute | solution.py:49
  26.3 19.3 %collective-permute-start.6 = (bf16[3,528,128]{2,1,0:T(8,128)(2,1)S(1)}, bf16[3,528,128]{2,1,0:T(8,128)(2,1)S(1)}, u32[]{:S(2)}, u32[]{:S(2)}) collective-permute-start(bf16[3,528,128]{2,1,0:T(8,128)(2,1)S(1)} %constant_dynamic-update-slice_fusion), channel_id=1, source_target_pairs={{0,192},{8,200},{16,208},{24,216},{32,224},{40,232},{48,240},{56,2... | collective-permute-start | bytes 1216520 | tf_op jit(solution)/shard_map/ppermute | solution.py:49
  27.6 18.0 %collective-permute-start.5 = (bf16[3,528,128]{2,1,0:T(8,128)(2,1)S(1)}, bf16[3,528,128]{2,1,0:T(8,128)(2,1)S(1)}, u32[]{:S(2)}, u32[]{:S(2)}) collective-permute-start(bf16[3,528,128]{2,1,0:T(8,128)(2,1)S(1)} %constant_dynamic-update-slice_fusion), channel_id=1, source_target_pairs={{0,64},{8,72},{16,80},{24,88},{32,96},{40,104},{48,112},{56,120},{... | collective-permute-start | bytes 1216520 | tf_op jit(solution)/shard_map/ppermute | solution.py:49
  28.9 3.4 %collective-permute-start.9 = (bf16[640,256]{1,0:T(8,128)(2,1)S(1)}, bf16[640,256]{1,0:T(8,128)(2,1)S(1)}, u32[]{:S(2)}, u32[]{:S(2)}) collective-permute-start(bf16[640,256]{1,0:T(8,128)(2,1)S(1)} %pad_maximum_fusion.rest_5_.rest_1_.rest_3_), channel_id=1, source_target_pairs={{0,8},{8,0},{16,24},{24,16},{32,40},{40,32},{48,56},{56,48},{64,72... | collective-permute-start | bytes 983048 | tf_op jit(solution)/shard_map/ppermute | solution.py:49
  29.0 13.2 %collective-permute-start.8 = (bf16[2,528,128]{2,1,0:T(8,128)(2,1)S(1)}, bf16[2,528,128]{2,1,0:T(8,128)(2,1)S(1)}, u32[]{:S(2)}, u32[]{:S(2)}) collective-permute-start(bf16[2,528,128]{2,1,0:T(8,128)(2,1)S(1)} %collective-permute-done.4.rest_4_), channel_id=1, source_target_pairs={{128,144},{136,184},{144,160},{152,136},{160,176},{168,152},{176,1... | collective-permute-start | bytes 811016 | tf_op jit(solution)/shard_map/ppermute | solution.py:49
  31.0 14.6 %collective-permute-start.7 = (bf16[1,528,128]{2,1,0:T(8,128)(2,1)S(1)}, bf16[1,528,128]{2,1,0:T(8,128)(2,1)S(1)}, u32[]{:S(2)}, u32[]{:S(2)}) collective-permute-start(bf16[1,528,128]{2,1,0:T(8,128)(2,1)S(1)} %collective-permute-done.2.rest_2_), channel_id=1, source_target_pairs={{0,128},{8,136},{16,144},{24,152},{32,160},{40,168},{48,176},{56,1... | collective-permute-start | bytes 405512 | tf_op jit(solution)/shard_map/ppermute | solution.py:49
  49.7 4.2 %collective-permute-start.10 = (f32[528,256]{1,0:T(8,128)S(1)}, f32[528,256]{1,0:T(8,128)S(1)}, u32[]{:S(2)}, u32[]{:S(2)}) collective-permute-start(f32[528,256]{1,0:T(8,128)S(1)} %attend_rest_other.1), channel_id=1, source_target_pairs={{0,8},{8,0},{16,24},{24,16},{32,40},{40,32},{48,56},{56,48},{64,72... | collective-permute-start | bytes 1622024 | tf_op jit(solution)/shard_map/ppermute | solution.py:49
  56.3 13.2 %collective-permute-start.14 = (bf16[4,80,640]{2,1,0:T(8,128)(2,1)S(1)}, bf16[4,80,640]{2,1,0:T(8,128)(2,1)S(1)}, u32[]{:S(2)}, u32[]{:S(2)}) collective-permute-start(bf16[4,80,640]{2,1,0:T(8,128)(2,1)S(1)} %get-tuple-element.62), channel_id=1, source_target_pairs={{0,3},{1,2},{2,1},{3,0},{4,7},{5,6},{6,5},{7,4},{8,11},{9,10},{10,... | collective-permute-start | bytes 1228808 | tf_op jit(solution)/shard_map/ppermute | solution.py:309
  59.2 11.6 %collective-permute-start.17 = (bf16[4,80,640]{2,1,0:T(8,128)(2,1)S(1)}, bf16[4,80,640]{2,1,0:T(8,128)(2,1)S(1)}, u32[]{:S(2)}, u32[]{:S(2)}) collective-permute-start(bf16[4,80,640]{2,1,0:T(8,128)(2,1)S(1)} %get-tuple-element.64), channel_id=1, source_target_pairs={{0,4},{1,5},{2,6},{3,7},{4,0},{5,1},{6,2},{7,3},{8,12},{9,13},{10,... | collective-permute-start | bytes 1228808 | tf_op jit(solution)/shard_map/ppermute | solution.py:309
  59.2 13.3 %collective-permute-start.11 = (bf16[4,96,640]{2,1,0:T(8,128)(2,1)S(1)}, bf16[4,96,640]{2,1,0:T(8,128)(2,1)S(1)}, u32[]{:S(2)}, u32[]{:S(2)}) collective-permute-start(bf16[4,96,640]{2,1,0:T(8,128)(2,1)S(1)} %get-tuple-element.60), channel_id=1, source_target_pairs={{0,1},{1,0},{2,3},{3,2},{4,5},{5,4},{6,7},{7,6},{8,9},{9,8},{10,11... | collective-permute-start | bytes 1474568 | tf_op jit(solution)/shard_map/ppermute | solution.py:309
  69.6 6.8 %collective-permute-start.15 = (bf16[2,80,640]{2,1,0:T(8,128)(2,1)S(1)}, bf16[2,80,640]{2,1,0:T(8,128)(2,1)S(1)}, u32[]{:S(2)}, u32[]{:S(2)}) collective-permute-start(bf16[2,80,640]{2,1,0:T(8,128)(2,1)S(1)} %slice.103), channel_id=1, source_target_pairs={{0,4},{1,5},{2,6},{3,7},{4,0},{5,1},{6,2},{7,3},{8,12},{9,13},{10,... | collective-permute-start | bytes 614408 | tf_op jit(solution)/shard_map/ppermute | solution.py:309
  70.9 6.5 %collective-permute-start.18 = (bf16[2,80,640]{2,1,0:T(8,128)(2,1)S(1)}, bf16[2,80,640]{2,1,0:T(8,128)(2,1)S(1)}, u32[]{:S(2)}, u32[]{:S(2)}) collective-permute-start(bf16[2,80,640]{2,1,0:T(8,128)(2,1)S(1)} %slice.102), channel_id=1, source_target_pairs={{0,1},{1,0},{2,3},{3,2},{4,5},{5,4},{6,7},{7,6},{8,9},{9,8},{10,11... | collective-permute-start | bytes 614408 | tf_op jit(solution)/shard_map/ppermute | solution.py:309
  72.7 9.6 %collective-permute-start.12 = (bf16[2,96,640]{2,1,0:T(8,128)(2,1)S(1)}, bf16[2,96,640]{2,1,0:T(8,128)(2,1)S(1)}, u32[]{:S(2)}, u32[]{:S(2)}) collective-permute-start(bf16[2,96,640]{2,1,0:T(8,128)(2,1)S(1)} %slice.101), channel_id=1, source_target_pairs={{0,3},{1,2},{2,1},{3,0},{4,7},{5,6},{6,5},{7,4},{8,11},{9,10},{10,... | collective-permute-start | bytes 737288 | tf_op jit(solution)/shard_map/ppermute | solution.py:309
  76.5 4.7 %collective-permute-start.16 = (bf16[80,640]{1,0:T(8,128)(2,1)S(1)}, bf16[80,640]{1,0:T(8,128)(2,1)S(1)}, u32[]{:S(2)}, u32[]{:S(2)}) collective-permute-start(bf16[80,640]{1,0:T(8,128)(2,1)S(1)} %fusion.22), channel_id=1, source_target_pairs={{0,1},{1,0},{2,3},{3,2},{4,5},{5,4},{6,7},{7,6},{8,9},{9,8},{10,11... | collective-permute-start | bytes 307208 | tf_op jit(solution)/shard_map/ppermute | solution.py:309
  77.4 6.5 %collective-permute-start.19 = (bf16[80,640]{1,0:T(8,128)(2,1)S(1)}, bf16[80,640]{1,0:T(8,128)(2,1)S(1)}, u32[]{:S(2)}, u32[]{:S(2)}) collective-permute-start(bf16[80,640]{1,0:T(8,128)(2,1)S(1)} %fusion.23), channel_id=1, source_target_pairs={{0,3},{1,2},{2,1},{3,0},{4,7},{5,6},{6,5},{7,4},{8,11},{9,10},{10,... | collective-permute-start | bytes 307208 | tf_op jit(solution)/shard_map/ppermute | solution.py:309
  82.4 5.0 %collective-permute-start.13 = (bf16[96,640]{1,0:T(8,128)(2,1)S(1)}, bf16[96,640]{1,0:T(8,128)(2,1)S(1)}, u32[]{:S(2)}, u32[]{:S(2)}) collective-permute-start(bf16[96,640]{1,0:T(8,128)(2,1)S(1)} %fusion.21), channel_id=1, source_target_pairs={{0,4},{1,5},{2,6},{3,7},{4,0},{5,1},{6,2},{7,3},{8,12},{9,13},{10,... | collective-permute-start | bytes 368648 | tf_op jit(solution)/shard_map/ppermute | solution.py:309

commit v11 on v9

--- a/solution.py
+++ b/solution.py
@@ -12,7 +12,7 @@
 HEAD_DIM = 128
 BLOCK = 256
 PACK = 2 * BLOCK + 16
-CHAINS = ((slice(0, 80), (1, 3, 4)), (slice(80, 176), (3, 4, 1)), (slice(176, 256), (4, 1, 3)))
+CHAINS = ((slice(0, 96), (1, 3, 4)), (slice(96, 176), (3, 4, 1)), (slice(176, 256), (4, 1, 3)))
 SIDES = tuple(itertools.product((0, 1), repeat=3))
 REACH = 24
 COLS = 640
@@ -219,11 +219,11 @@
     own = jnp.concatenate([k_cache, v_cache, jnp.broadcast_to(smaller[None, :], (16, HEAD_DIM))], axis=0)[None]
 
     own, other, hidden = lax.optimization_barrier((own, swap_cores(own), hidden))
-    pair = jnp.concatenate([own, other], axis=0)
+    pair = lax.optimization_barrier(jnp.concatenate([own, other], axis=0))
     z_near = along_z(pair)
     y_near = along_y(pair)
     y_far = move(pair, lambda y, z, c: (y + 2, z, c) if y < 2 else None)
-    z_far = move(own, lambda y, z, c: (y, z + 2, c))
+    z_far = move(pair[:1], lambda y, z, c: (y, z + 2, c))
 
     widened = hidden.astype(F32)
     normed = (widened * lax.rsqrt(jnp.mean(widened * widened, axis=-1, keepdims=True) + 1e-06)).astype(BF16)
@@ -233,7 +233,7 @@
     hot = (jnp.arange(HEAD_DIM, dtype=jnp.int32)[:, None] == segment[None, :]).astype(BF16)
     q = jnp.concatenate([q_t, hot], axis=0)
 
-    (z_near, z_far, y_near, y_far), q = lax.optimization_barrier(((z_near, z_far, y_near, y_far), q))
+    (y_far, y_near, z_far, z_near), q = lax.optimization_barrier(((y_far, y_near, z_far, z_near), q))
     row = jnp.concatenate([z_near, z_far], axis=0)
     up = up_y(row)
     around = round_y(row)

time: 87.3 us -> 88.5 us (1.014)
  waiting for transfers between devices: 26.4 us -> 29.9 us
  starting transfers between devices: 31.5 us -> 29.2 us
    ppermute x9, starting transfers between devices: 12.4 us -> 8.04 us  [exchange(): return lax.ppermute(x, 'section', [(i, i ^ step) for i in range(8)])]
    ppermute x9, waiting for transfers between devices: 18.6 us -> 22.3 us  [exchange(): return lax.ppermute(x, 'section', [(i, i ^ step) for i in range(8)])]
    ppermute x11, starting transfers between devices: 19.1 us -> 21.2 us  [move(): return lax.ppermute(x, 'ctx', ctx_pairs(step))]
  transfers between devices with their start and end apart: 20 -> 20, of which waited for: 10 -> 11; matrix products, arithmetic and copies ran while one was open for 11% -> 11% of each run, Pallas kernels for 11% -> 11%
where the time goes in v11:
time: 88.5 us; the launch traced here: 88.1 us
  waiting for transfers between devices  29.9 us (34%)
  starting transfers between devices  29.2 us (33%)
  Pallas kernels  16.9 us (19%)
  other arithmetic  6.09 us (7%)
  matrix products  5.57 us (6%)
    ppermute x9, waiting for transfers between devices, exchange(): return lax.ppermute(x, 'section', [(i, i ^ step) for i in range(8)])  22.3 us
    ppermute x11, starting transfers between devices, move(): return lax.ppermute(x, 'ctx', ctx_pairs(step))  21.2 us
    pallas_call x2, Pallas kernels, attend(): pl.pallas_call(kernel, out_shape=out_shape, in_specs=[SMEM] + [VMEM] * (l...  9.6 us
    ppermute x9, starting transfers between devices, exchange(): return lax.ppermute(x, 'section', [(i, i ^ step) for i in range(8)])  8.04 us
    ppermute x11, waiting for transfers between devices, move(): return lax.ppermute(x, 'ctx', ctx_pairs(step))  7.56 us
    dot_general x1, matrix products, per_device(): lax.dot_general(w_query, normed, (((0,), (1,)), ((), ())), preferred_elem...  5.57 us
    pallas_call x1, Pallas kernels, per_device(): pl.pallas_call(functools.partial(more_and_fetch_kernel, rest_slots, len(p...  4.83 us
    pallas_call x1, Pallas kernels, per_device(): pl.pallas_call(last_kernel, out_shape=tuple(out_shape), in_specs=[SMEM, V...  2.49 us
  transfers between devices with their start and end apart: 20, of which 11 were waited for; matrix products, arithmetic and copies ran while one was open for 11% of the time, Pallas kernels for 11%

profile of v11, /device:TPU:24, one launch (start us, length us, event | category | flops | bytes accessed | tf_op | source)
XLA Modules:
  0.0 88.1 jit_solution(13295834381064461205)
XLA Ops:
  3.2 3.3 %collective-permute-start.4 = (bf16[2,528,128]{2,1,0:T(8,128)(2,1)S(1)}, bf16[2,528,128]{2,1,0:T(8,128)(2,1)S(1)}, u32[]{:S(2)}, u32[]{:S(2)}) collective-permute-start(bf16[2,528,128]{2,1,0:T(8,128)(2,1)S(1)} %pad_maximum_fusion.2), channel_id=1, source_target_pairs={{0,16},{8,56},{16,32},{24,8},{32,48},{40,24},{48,0},{56,40},{64,80... | collective-permute-start | bytes 811016 | tf_op jit(solution)/shard_map/ppermute | solution.py:48
  6.5 1.3 %collective-permute-start.2 = (bf16[2,528,128]{2,1,0:T(8,128)(2,1)S(1)}, bf16[2,528,128]{2,1,0:T(8,128)(2,1)S(1)}, u32[]{:S(2)}, u32[]{:S(2)}) collective-permute-start(bf16[2,528,128]{2,1,0:T(8,128)(2,1)S(1)} %pad_maximum_fusion.2), channel_id=1, source_target_pairs={{0,64},{8,200},{16,80},{24,216},{32,96},{40,232},{48,112},{56,248}... | collective-permute-start | bytes 811016 | tf_op jit(solution)/shard_map/ppermute | solution.py:48
  7.8 1.3 %collective-permute-start.1 = (bf16[2,528,128]{2,1,0:T(8,128)(2,1)S(1)}, bf16[2,528,128]{2,1,0:T(8,128)(2,1)S(1)}, u32[]{:S(2)}, u32[]{:S(2)}) collective-permute-start(bf16[2,528,128]{2,1,0:T(8,128)(2,1)S(1)} %pad_maximum_fusion.2), channel_id=1, source_target_pairs={{0,128},{8,136},{16,144},{24,152},{32,160},{40,168},{48,176},{56,1... | collective-permute-start | bytes 811016 | tf_op jit(solution)/shard_map/ppermute | solution.py:48
  9.1 2.3 %fusion = f32[256]{0:T(256)S(1)} fusion(bf16[256,5120]{1,0:T(8,128)(2,1)} %param.6), kind=kLoop, calls=%fused_computation.2 | loop fusion | flops 3931904 | bytes 2622464 | tf_op jit(solution)/shard_map/reduce_sum | solution.py:229
  11.5 5.5 %collective-permute-start.3 = (bf16[1,528,128]{2,1,0:T(8,128)(2,1)S(1)}, bf16[1,528,128]{2,1,0:T(8,128)(2,1)S(1)}, u32[]{:S(2)}, u32[]{:S(2)}) collective-permute-start(bf16[1,528,128]{2,1,0:T(8,128)(2,1)S(1)} %slice.58), channel_id=1, source_target_pairs={{0,32},{8,40},{16,48},{24,56},{32,0},{40,8},{48,16},{56,24},{64,96... | collective-permute-start | bytes 405512 | tf_op jit(solution)/shard_map/ppermute | solution.py:48
  16.9 5.6 %fusion.11 = bf16[512,256]{1,0:T(8,128)(2,1)S(1)} fusion(bf16[5120,512]{1,0:T(8,128)(2,1)} %param.10, bf16[256,5120]{1,0:T(8,128)(2,1)} %param.6, f32[256]{0:T(256)S(1)} %add_rsqrt_fusion), kind=kOutput, calls=%fused_computation.8 | convolution fusion | flops 1346371584 | bytes 8127488 | tf_op jit(solution)/shard_map/dot_general | solution.py:231
  22.6 1.3 %collective-permute-start.6 = (bf16[3,528,128]{2,1,0:T(8,128)(2,1)S(1)}, bf16[3,528,128]{2,1,0:T(8,128)(2,1)S(1)}, u32[]{:S(2)}, u32[]{:S(2)}) collective-permute-start(bf16[3,528,128]{2,1,0:T(8,128)(2,1)S(1)} %constant_dynamic-update-slice_fusion), channel_id=1, source_target_pairs={{0,192},{8,200},{16,208},{24,216},{32,224},{40,232},{48,240},{56,2... | collective-permute-start | bytes 1216520 | tf_op jit(solution)/shard_map/ppermute | solution.py:48
  23.9 1.3 %collective-permute-start.5 = (bf16[3,528,128]{2,1,0:T(8,128)(2,1)S(1)}, bf16[3,528,128]{2,1,0:T(8,128)(2,1)S(1)}, u32[]{:S(2)}, u32[]{:S(2)}) collective-permute-start(bf16[3,528,128]{2,1,0:T(8,128)(2,1)S(1)} %constant_dynamic-update-slice_fusion), channel_id=1, source_target_pairs={{0,64},{8,72},{16,80},{24,88},{32,96},{40,104},{48,112},{56,120},{... | collective-permute-start | bytes 1216520 | tf_op jit(solution)/shard_map/ppermute | solution.py:48
  26.0 4.9 %collective-permute-start.7 = (bf16[2,528,128]{2,1,0:T(8,128)(2,1)S(1)}, bf16[2,528,128]{2,1,0:T(8,128)(2,1)S(1)}, u32[]{:S(2)}, u32[]{:S(2)}) collective-permute-start(bf16[2,528,128]{2,1,0:T(8,128)(2,1)S(1)} %collective-permute-done.1.rest_4_), channel_id=1, source_target_pairs={{128,144},{136,184},{144,160},{152,136},{160,176},{168,152},{176,1... | collective-permute-start | bytes 811016 | tf_op jit(solution)/shard_map/ppermute | solution.py:48
  31.0 1.3 %collective-permute-start.8 = (bf16[1,528,128]{2,1,0:T(8,128)(2,1)S(1)}, bf16[1,528,128]{2,1,0:T(8,128)(2,1)S(1)}, u32[]{:S(2)}, u32[]{:S(2)}) collective-permute-start(bf16[1,528,128]{2,1,0:T(8,128)(2,1)S(1)} %collective-permute-done.3.rest_2_), channel_id=1, source_target_pairs={{0,128},{8,136},{16,144},{24,152},{32,160},{40,168},{48,176},{56,1... | collective-permute-start | bytes 405512 | tf_op jit(solution)/shard_map/ppermute | solution.py:48
  32.4 4.6 %attend_first.1 = (f32[528,256]{1,0:T(8,128)S(1)}, f32[528,256]{1,0:T(8,128)S(1)}) custom-call(s32[2]{0:T(128)S(1)} %pad_add_fusion.at_ref, bf16[1,528,128]{2,1,0:T(8,128)(2,1)S(1)} %maximum_bitcast_fusion.rest_0_, bf16[2,528,128]{2,1,0:T(8,128)(2,1)S(1)} %collective-permute-done.4.rest_1_, bf16[1,528,128]{2,1,0:T(8,128)(2,1)S(1)} %collective-permute-done.3.rest_2_, ...), custom_call_target="tpu_custom_call" | custom-call | flops 134217728 | bytes 135168 | tf_op jit(solution)/shard_map/attend_first/pallas_call | solution.py:248
  37.0 3.5 %collective-permute-done.8.rest_3_ = bf16[1,528,128]{2,1,0:T(8,128)(2,1)S(1)} collective-permute-done((bf16[1,528,128]{2,1,0:T(8,128)(2,1)S(1)}, bf16[1,528,128]{2,1,0:T(8,128)(2,1)S(1)}, u32[]{:S(2)}, u32[]{:S(2)}) %collective-permute-start.8) | collective-permute-done | bytes 135200 | tf_op jit(solution)/shard_map/ppermute | solution.py:48
  40.5 3.4 %collective-permute-done.6.rest_1_ = bf16[3,528,128]{2,1,0:T(8,128)(2,1)S(1)} collective-permute-done((bf16[3,528,128]{2,1,0:T(8,128)(2,1)S(1)}, bf16[3,528,128]{2,1,0:T(8,128)(2,1)S(1)}, u32[]{:S(2)}, u32[]{:S(2)}) %collective-permute-start.6) | collective-permute-done | bytes 405536 | tf_op jit(solution)/shard_map/ppermute | solution.py:48
  43.9 5.0 %attend_rest_other.1 = f32[528,256]{1,0:T(8,128)S(1)} custom-call(s32[2]{0:T(128)S(1)} %pad_add_fusion.at_ref, bf16[3,528,128]{2,1,0:T(8,128)(2,1)S(1)} %collective-permute-done.5.rest_0_, bf16[3,528,128]{2,1,0:T(8,128)(2,1)S(1)} %collective-permute-done.6.rest_1_, bf16[2,528,128]{2,1,0:T(8,128)(2,1)S(1)} %collective-permute-done.7.rest_2_, ...), custom_call_target="tpu_custom_call" | custom-call | flops 134217728 | bytes 135168 | tf_op jit(solution)/shard_map/attend_rest_other/pallas_call | solution.py:248
  49.0 4.8 %attend_rest_own.1 = (f32[528,256]{1,0:T(8,128)S(1)}, bf16[512,5120]{1,0:T(8,128)(2,1)S(1)}) custom-call(s32[2]{0:T(128)S(1)} %pad_add_fusion.at_ref, bf16[3,528,128]{2,1,0:T(8,128)(2,1)S(1)} %collective-permute-done.5.rest_0_, bf16[3,528,128]{2,1,0:T(8,128)(2,1)S(1)} %collective-permute-done.6.rest_1_, ...), custom_call_target="tpu_custom_call" | custom-call | flops 134217728 | bytes 135168 | tf_op jit(solution)/shard_map/attend_rest_own/pallas_call | solution.py:266
  53.8 2.5 %project_attended.1 = (bf16[4,96,640]{2,1,0:T(8,128)(2,1)S(1)}, bf16[4,96,640]{2,1,0:T(8,128)(2,1)S(1)}, bf16[4,80,640]{2,1,0:T(8,128)(2,1)S(1)}, bf16[4,80,640]...) custom-call(s32[2]{0:T(128)S(1)} %pad_add_fusion.at_ref, ...), custom_call_target="tpu_custom_call" | custom-call | flops 1610612736 | bytes 1622016 | tf_op jit(solution)/shard_map/project_attended/pallas_call | solution.py:285
  56.3 2.8 %collective-permute-start.14 = (bf16[4,80,640]{2,1,0:T(8,128)(2,1)S(1)}, bf16[4,80,640]{2,1,0:T(8,128)(2,1)S(1)}, u32[]{:S(2)}, u32[]{:S(2)}) collective-permute-start(bf16[4,80,640]{2,1,0:T(8,128)(2,1)S(1)} %get-tuple-element.54), channel_id=1, source_target_pairs={{0,3},{1,2},{2,1},{3,0},{4,7},{5,6},{6,5},{7,4},{8,11},{9,10},{10,... | collective-permute-start | bytes 1228808 | tf_op jit(solution)/shard_map/ppermute | solution.py:297
  59.4 10.1 %collective-permute-done.14 = bf16[4,80,640]{2,1,0:T(8,128)(2,1)S(1)} collective-permute-done((bf16[4,80,640]{2,1,0:T(8,128)(2,1)S(1)}, bf16[4,80,640]{2,1,0:T(8,128)(2,1)S(1)}, u32[]{:S(2)}, u32[]{:S(2)}) %collective-permute-start.14) | collective-permute-done | bytes 409632 | tf_op jit(solution)/shard_map/ppermute | solution.py:297
  71.2 1.3 %collective-permute-done.11 = bf16[4,96,640]{2,1,0:T(8,128)(2,1)S(1)} collective-permute-done((bf16[4,96,640]{2,1,0:T(8,128)(2,1)S(1)}, bf16[4,96,640]{2,1,0:T(8,128)(2,1)S(1)}, u32[]{:S(2)}, u32[]{:S(2)}) %collective-permute-start.11) | collective-permute-done | bytes 491552 | tf_op jit(solution)/shard_map/ppermute | solution.py:297
  73.2 3.2 %collective-permute-done.15 = bf16[2,80,640]{2,1,0:T(8,128)(2,1)S(1)} collective-permute-done((bf16[2,80,640]{2,1,0:T(8,128)(2,1)S(1)}, bf16[2,80,640]{2,1,0:T(8,128)(2,1)S(1)}, u32[]{:S(2)}, u32[]{:S(2)}) %collective-permute-start.15) | collective-permute-done | bytes 204832 | tf_op jit(solution)/shard_map/ppermute | solution.py:297
  77.4 2.1 %collective-permute-start.19 = (bf16[80,640]{1,0:T(8,128)(2,1)S(1)}, bf16[80,640]{1,0:T(8,128)(2,1)S(1)}, u32[]{:S(2)}, u32[]{:S(2)}) collective-permute-start(bf16[80,640]{1,0:T(8,128)(2,1)S(1)} %fusion.23), channel_id=1, source_target_pairs={{0,3},{1,2},{2,1},{3,0},{4,7},{5,6},{6,5},{7,4},{8,11},{9,10},{10,... | collective-permute-start | bytes 307208 | tf_op jit(solution)/shard_map/ppermute | solution.py:297
  79.5 1.7 %collective-permute-done.16 = bf16[80,640]{1,0:T(8,128)(2,1)S(1)} collective-permute-done((bf16[80,640]{1,0:T(8,128)(2,1)S(1)}, bf16[80,640]{1,0:T(8,128)(2,1)S(1)}, u32[]{:S(2)}, u32[]{:S(2)}) %collective-permute-start.16) | collective-permute-done | bytes 102432 | tf_op jit(solution)/shard_map/ppermute | solution.py:297
  82.4 1.5 %collective-permute-start.13 = (bf16[96,640]{1,0:T(8,128)(2,1)S(1)}, bf16[96,640]{1,0:T(8,128)(2,1)S(1)}, u32[]{:S(2)}, u32[]{:S(2)}) collective-permute-start(bf16[96,640]{1,0:T(8,128)(2,1)S(1)} %fusion.21), channel_id=1, source_target_pairs={{0,4},{1,5},{2,6},{3,7},{4,0},{5,1},{6,2},{7,3},{8,12},{9,13},{10,... | collective-permute-start | bytes 368648 | tf_op jit(solution)/shard_map/ppermute | solution.py:297
  83.9 3.4 %collective-permute-done.13 = bf16[96,640]{1,0:T(8,128)(2,1)S(1)} collective-permute-done((bf16[96,640]{1,0:T(8,128)(2,1)S(1)}, bf16[96,640]{1,0:T(8,128)(2,1)S(1)}, u32[]{:S(2)}, u32[]{:S(2)}) %collective-permute-start.13) | collective-permute-done | bytes 122912 | tf_op jit(solution)/shard_map/ppermute | solution.py:297
  (49 shorter events, 9.7 us)
Async XLA Ops:
  1.7 1.4 %collective-permute-start = (bf16[1,528,128]{2,1,0:T(8,128)(2,1)S(1)}, bf16[1,528,128]{2,1,0:T(8,128)(2,1)S(1)}, u32[]{:S(2)}, u32[]{:S(2)}) collective-permute-start(bf16[1,528,128]{2,1,0:T(8,128)(2,1)S(1)} %maximum_bitcast_fusion.rest_0_), channel_id=1, source_target_pairs={{0,8},{8,0},{16,24},{24,16},{32,40},{40,32},{48,56},{56,48},{64,72... | collective-permute-start | bytes 405512 | tf_op jit(solution)/shard_map/ppermute | solution.py:48
  3.2 19.4 %collective-permute-start.4 = (bf16[2,528,128]{2,1,0:T(8,128)(2,1)S(1)}, bf16[2,528,128]{2,1,0:T(8,128)(2,1)S(1)}, u32[]{:S(2)}, u32[]{:S(2)}) collective-permute-start(bf16[2,528,128]{2,1,0:T(8,128)(2,1)S(1)} %pad_maximum_fusion.2), channel_id=1, source_target_pairs={{0,16},{8,56},{16,32},{24,8},{32,48},{40,24},{48,0},{56,40},{64,80... | collective-permute-start | bytes 811016 | tf_op jit(solution)/shard_map/ppermute | solution.py:48
  6.5 16.0 %collective-permute-start.2 = (bf16[2,528,128]{2,1,0:T(8,128)(2,1)S(1)}, bf16[2,528,128]{2,1,0:T(8,128)(2,1)S(1)}, u32[]{:S(2)}, u32[]{:S(2)}) collective-permute-start(bf16[2,528,128]{2,1,0:T(8,128)(2,1)S(1)} %pad_maximum_fusion.2), channel_id=1, source_target_pairs={{0,64},{8,200},{16,80},{24,216},{32,96},{40,232},{48,112},{56,248}... | collective-permute-start | bytes 811016 | tf_op jit(solution)/shard_map/ppermute | solution.py:48
  7.8 14.8 %collective-permute-start.1 = (bf16[2,528,128]{2,1,0:T(8,128)(2,1)S(1)}, bf16[2,528,128]{2,1,0:T(8,128)(2,1)S(1)}, u32[]{:S(2)}, u32[]{:S(2)}) collective-permute-start(bf16[2,528,128]{2,1,0:T(8,128)(2,1)S(1)} %pad_maximum_fusion.2), channel_id=1, source_target_pairs={{0,128},{8,136},{16,144},{24,152},{32,160},{40,168},{48,176},{56,1... | collective-permute-start | bytes 811016 | tf_op jit(solution)/shard_map/ppermute | solution.py:48
  11.5 11.1 %collective-permute-start.3 = (bf16[1,528,128]{2,1,0:T(8,128)(2,1)S(1)}, bf16[1,528,128]{2,1,0:T(8,128)(2,1)S(1)}, u32[]{:S(2)}, u32[]{:S(2)}) collective-permute-start(bf16[1,528,128]{2,1,0:T(8,128)(2,1)S(1)} %slice.58), channel_id=1, source_target_pairs={{0,32},{8,40},{16,48},{24,56},{32,0},{40,8},{48,16},{56,24},{64,96... | collective-permute-start | bytes 405512 | tf_op jit(solution)/shard_map/ppermute | solution.py:48
  22.6 21.2 %collective-permute-start.6 = (bf16[3,528,128]{2,1,0:T(8,128)(2,1)S(1)}, bf16[3,528,128]{2,1,0:T(8,128)(2,1)S(1)}, u32[]{:S(2)}, u32[]{:S(2)}) collective-permute-start(bf16[3,528,128]{2,1,0:T(8,128)(2,1)S(1)} %constant_dynamic-update-slice_fusion), channel_id=1, source_target_pairs={{0,192},{8,200},{16,208},{24,216},{32,224},{40,232},{48,240},{56,2... | collective-permute-start | bytes 1216520 | tf_op jit(solution)/shard_map/ppermute | solution.py:48
  23.9 19.9 %collective-permute-start.5 = (bf16[3,528,128]{2,1,0:T(8,128)(2,1)S(1)}, bf16[3,528,128]{2,1,0:T(8,128)(2,1)S(1)}, u32[]{:S(2)}, u32[]{:S(2)}) collective-permute-start(bf16[3,528,128]{2,1,0:T(8,128)(2,1)S(1)} %constant_dynamic-update-slice_fusion), channel_id=1, source_target_pairs={{0,64},{8,72},{16,80},{24,88},{32,96},{40,104},{48,112},{56,120},{... | collective-permute-start | bytes 1216520 | tf_op jit(solution)/shard_map/ppermute | solution.py:48
  25.2 7.1 %collective-permute-start.9 = (bf16[640,256]{1,0:T(8,128)(2,1)S(1)}, bf16[640,256]{1,0:T(8,128)(2,1)S(1)}, u32[]{:S(2)}, u32[]{:S(2)}) collective-permute-start(bf16[640,256]{1,0:T(8,128)(2,1)S(1)} %pad_maximum_fusion.rest_5_.rest_4_), channel_id=1, source_target_pairs={{0,8},{8,0},{16,24},{24,16},{32,40},{40,32},{48,56},{56,48},{64,72... | collective-permute-start | bytes 983048 | tf_op jit(solution)/shard_map/ppermute | solution.py:48
  26.0 14.5 %collective-permute-start.7 = (bf16[2,528,128]{2,1,0:T(8,128)(2,1)S(1)}, bf16[2,528,128]{2,1,0:T(8,128)(2,1)S(1)}, u32[]{:S(2)}, u32[]{:S(2)}) collective-permute-start(bf16[2,528,128]{2,1,0:T(8,128)(2,1)S(1)} %collective-permute-done.1.rest_4_), channel_id=1, source_target_pairs={{128,144},{136,184},{144,160},{152,136},{160,176},{168,152},{176,1... | collective-permute-start | bytes 811016 | tf_op jit(solution)/shard_map/ppermute | solution.py:48
  31.0 9.5 %collective-permute-start.8 = (bf16[1,528,128]{2,1,0:T(8,128)(2,1)S(1)}, bf16[1,528,128]{2,1,0:T(8,128)(2,1)S(1)}, u32[]{:S(2)}, u32[]{:S(2)}) collective-permute-start(bf16[1,528,128]{2,1,0:T(8,128)(2,1)S(1)} %collective-permute-done.3.rest_2_), channel_id=1, source_target_pairs={{0,128},{8,136},{16,144},{24,152},{32,160},{40,168},{48,176},{56,1... | collective-permute-start | bytes 405512 | tf_op jit(solution)/shard_map/ppermute | solution.py:48
  48.9 4.9 %collective-permute-start.10 = (f32[528,256]{1,0:T(8,128)S(1)}, f32[528,256]{1,0:T(8,128)S(1)}, u32[]{:S(2)}, u32[]{:S(2)}) collective-permute-start(f32[528,256]{1,0:T(8,128)S(1)} %attend_rest_other.1), channel_id=1, source_target_pairs={{0,8},{8,0},{16,24},{24,16},{32,40},{40,32},{48,56},{56,48},{64,72... | collective-permute-start | bytes 1622024 | tf_op jit(solution)/shard_map/ppermute | solution.py:48
  56.3 13.2 %collective-permute-start.14 = (bf16[4,80,640]{2,1,0:T(8,128)(2,1)S(1)}, bf16[4,80,640]{2,1,0:T(8,128)(2,1)S(1)}, u32[]{:S(2)}, u32[]{:S(2)}) collective-permute-start(bf16[4,80,640]{2,1,0:T(8,128)(2,1)S(1)} %get-tuple-element.54), channel_id=1, source_target_pairs={{0,3},{1,2},{2,1},{3,0},{4,7},{5,6},{6,5},{7,4},{8,11},{9,10},{10,... | collective-permute-start | bytes 1228808 | tf_op jit(solution)/shard_map/ppermute | solution.py:297
  59.2 11.6 %collective-permute-start.17 = (bf16[4,80,640]{2,1,0:T(8,128)(2,1)S(1)}, bf16[4,80,640]{2,1,0:T(8,128)(2,1)S(1)}, u32[]{:S(2)}, u32[]{:S(2)}) collective-permute-start(bf16[4,80,640]{2,1,0:T(8,128)(2,1)S(1)} %get-tuple-element.56), channel_id=1, source_target_pairs={{0,4},{1,5},{2,6},{3,7},{4,0},{5,1},{6,2},{7,3},{8,12},{9,13},{10,... | collective-permute-start | bytes 1228808 | tf_op jit(solution)/shard_map/ppermute | solution.py:297
  59.2 13.3 %collective-permute-start.11 = (bf16[4,96,640]{2,1,0:T(8,128)(2,1)S(1)}, bf16[4,96,640]{2,1,0:T(8,128)(2,1)S(1)}, u32[]{:S(2)}, u32[]{:S(2)}) collective-permute-start(bf16[4,96,640]{2,1,0:T(8,128)(2,1)S(1)} %get-tuple-element.52), channel_id=1, source_target_pairs={{0,1},{1,0},{2,3},{3,2},{4,5},{5,4},{6,7},{7,6},{8,9},{9,8},{10,11... | collective-permute-start | bytes 1474568 | tf_op jit(solution)/shard_map/ppermute | solution.py:297
  69.6 6.8 %collective-permute-start.15 = (bf16[2,80,640]{2,1,0:T(8,128)(2,1)S(1)}, bf16[2,80,640]{2,1,0:T(8,128)(2,1)S(1)}, u32[]{:S(2)}, u32[]{:S(2)}) collective-permute-start(bf16[2,80,640]{2,1,0:T(8,128)(2,1)S(1)} %slice.103), channel_id=1, source_target_pairs={{0,4},{1,5},{2,6},{3,7},{4,0},{5,1},{6,2},{7,3},{8,12},{9,13},{10,... | collective-permute-start | bytes 614408 | tf_op jit(solution)/shard_map/ppermute | solution.py:297
  70.9 6.5 %collective-permute-start.18 = (bf16[2,80,640]{2,1,0:T(8,128)(2,1)S(1)}, bf16[2,80,640]{2,1,0:T(8,128)(2,1)S(1)}, u32[]{:S(2)}, u32[]{:S(2)}) collective-permute-start(bf16[2,80,640]{2,1,0:T(8,128)(2,1)S(1)} %slice.102), channel_id=1, source_target_pairs={{0,1},{1,0},{2,3},{3,2},{4,5},{5,4},{6,7},{7,6},{8,9},{9,8},{10,11... | collective-permute-start | bytes 614408 | tf_op jit(solution)/shard_map/ppermute | solution.py:297
  72.7 9.6 %collective-permute-start.12 = (bf16[2,96,640]{2,1,0:T(8,128)(2,1)S(1)}, bf16[2,96,640]{2,1,0:T(8,128)(2,1)S(1)}, u32[]{:S(2)}, u32[]{:S(2)}) collective-permute-start(bf16[2,96,640]{2,1,0:T(8,128)(2,1)S(1)} %slice.101), channel_id=1, source_target_pairs={{0,3},{1,2},{2,1},{3,0},{4,7},{5,6},{6,5},{7,4},{8,11},{9,10},{10,... | collective-permute-start | bytes 737288 | tf_op jit(solution)/shard_map/ppermute | solution.py:297
  76.5 4.7 %collective-permute-start.16 = (bf16[80,640]{1,0:T(8,128)(2,1)S(1)}, bf16[80,640]{1,0:T(8,128)(2,1)S(1)}, u32[]{:S(2)}, u32[]{:S(2)}) collective-permute-start(bf16[80,640]{1,0:T(8,128)(2,1)S(1)} %fusion.22), channel_id=1, source_target_pairs={{0,1},{1,0},{2,3},{3,2},{4,5},{5,4},{6,7},{7,6},{8,9},{9,8},{10,11... | collective-permute-start | bytes 307208 | tf_op jit(solution)/shard_map/ppermute | solution.py:297
  77.4 6.5 %collective-permute-start.19 = (bf16[80,640]{1,0:T(8,128)(2,1)S(1)}, bf16[80,640]{1,0:T(8,128)(2,1)S(1)}, u32[]{:S(2)}, u32[]{:S(2)}) collective-permute-start(bf16[80,640]{1,0:T(8,128)(2,1)S(1)} %fusion.23), channel_id=1, source_target_pairs={{0,3},{1,2},{2,1},{3,0},{4,7},{5,6},{6,5},{7,4},{8,11},{9,10},{10,... | collective-permute-start | bytes 307208 | tf_op jit(solution)/shard_map/ppermute | solution.py:297
  82.4 5.0 %collective-permute-start.13 = (bf16[96,640]{1,0:T(8,128)(2,1)S(1)}, bf16[96,640]{1,0:T(8,128)(2,1)S(1)}, u32[]{:S(2)}, u32[]{:S(2)}) collective-permute-start(bf16[96,640]{1,0:T(8,128)(2,1)S(1)} %fusion.21), channel_id=1, source_target_pairs={{0,4},{1,5},{2,6},{3,7},{4,0},{5,1},{6,2},{7,3},{8,12},{9,13},{10,... | collective-permute-start | bytes 368648 | tf_op jit(solution)/shard_map/ppermute | solution.py:297

commit v12 on v10

--- a/solution.py
+++ b/solution.py
@@ -13,7 +13,6 @@
 BLOCK = 256
 PACK = 2 * BLOCK + 16
 CHAINS = ((slice(0, 96), (1, 3, 4)), (slice(96, 176), (3, 4, 1)), (slice(176, 256), (4, 1, 3)))
-LINKS = (1, 3, 4)
 SIDES = tuple(itertools.product((0, 1), repeat=3))
 REACH = 24
 COLS = 640
@@ -27,7 +26,7 @@
 
 
 def away(sides):
-    return sum(step * side for step, side in zip(LINKS, sides)) if sides[:2] != (1, 1) else 2 + 4 * sides[2]
+    return sum(step * side for step, side in zip((1, 3, 4), sides)) if sides[:2] != (1, 1) else 2 + 4 * sides[2]
 
 
 def ctx_id(y, z, c):
@@ -83,14 +82,15 @@
     return row + [[(y + d, z, c), (y + d, z, 1 - c)], [(y + 2, z, c)]]
 
 
+def up_slots(y, z, c):
+    d = 2 * c - 1
+    return [[(y - 1, z + d, c), (y - 1, z + d, 1 - c), (y - 1, z + 2, c)]]
+
+
 def rest_slots(y, z, c):
     d = 2 * c - 1
-    return [[(y + e, z + d, c), (y + e, z + d, 1 - c), (y + e, z + 2, c)] for e in (-1, 1)] + [[(y + 2, z + 2, c)]]
-
-
-def far_slots(y, z, c):
-    d = 2 * c - 1
-    return [[(y + 2, z + d, c), (y + 2, z + d, 1 - c)]]
+    around = [(y + 1, z + d, c), (y + 1, z + d, 1 - c), (y + 1, z + 2, c)]
+    return [around, [(y + 2, z + d, c), (y + 2, z + d, 1 - c)], [(y + 2, z + 2, c)]]
 
 
 def attend_blocks(kv_ref, places, diagonal, q_ref, state_ref):
@@ -198,7 +198,7 @@
     for sides in SIDES:
         cols = pl.ds(pl.multiple_of((section ^ away(sides)) * COLS, 128), COLS)
         part = jnp.dot(att_ref[...], w_ref[:, cols], preferred_element_type=F32).astype(BF16)
-        crossed = dict(zip(LINKS, sides))
+        crossed = dict(zip(CHAINS[0][1], sides))
         for i, (rows, order) in enumerate(CHAINS):
             first, second, third = (crossed[step] for step in order)
             outs[2 * i + 1 - first][2 * second + third] = part[rows]
@@ -228,11 +228,11 @@
     own = jnp.concatenate([k_cache, v_cache, jnp.broadcast_to(smaller[None, :], (16, HEAD_DIM))], axis=0)[None]
 
     own, other, hidden = lax.optimization_barrier((own, swap_cores(own), hidden))
-    pair = lax.optimization_barrier(jnp.concatenate([own, other], axis=0))
+    pair = jnp.concatenate([own, other], axis=0)
     z_near = along_z(pair)
     y_near = along_y(pair)
     y_far = move(pair, lambda y, z, c: (y + 2, z, c) if y < 2 else None)
-    z_far = move(pair[:1], lambda y, z, c: (y, z + 2, c))
+    z_far = move(own, lambda y, z, c: (y, z + 2, c))
 
     widened = hidden.astype(F32)
     normed = (widened * lax.rsqrt(jnp.mean(widened * widened, axis=-1, keepdims=True) + 1e-06)).astype(BF16)
@@ -268,12 +268,12 @@
     pieces = [own, z_near, z_far, y_near, y_far]
     first = functools.partial(start_kernel, first_slots, len(pieces))
     state, state_2 = attend(first, 7, pieces, (q, q_2), (), "attend_first")
-    far_near, state, state_2 = lax.optimization_barrier((far_near, state, state_2))
-    far = functools.partial(more_kernel, far_slots, 1, (0, 1))
-    state, state_2 = attend(far, 2, [far_near], (q, q_2), (state, state_2), "attend_far")
-    pieces, state, state_2 = lax.optimization_barrier(((up, around, far_far), state, state_2))
+    up, state, state_2 = lax.optimization_barrier((up, state, state_2))
+    near = functools.partial(more_kernel, up_slots, 1, (0, 1))
+    state, state_2 = attend(near, 3, [up], (q, q_2), (state, state_2), "attend_up")
+    pieces, state, state_2 = lax.optimization_barrier(((around, far_near, far_far), state, state_2))
     rest = functools.partial(more_kernel, rest_slots, len(pieces), (1,))
-    (state_2,) = attend(rest, 7, pieces, (q_2,), (state_2,), "attend_rest_other")
+    (state_2,) = attend(rest, 6, pieces, (q_2,), (state_2,), "attend_rest_other")
     state_2, state = lax.optimization_barrier((state_2, state))
     state, w_held = pl.pallas_call(
         functools.partial(more_and_fetch_kernel, rest_slots, len(pieces), (0,)),
@@ -281,7 +281,7 @@
         in_specs=[SMEM] + [VMEM] * (len(pieces) + 2) + [pl.BlockSpec(memory_space=pltpu.HBM)],
         out_specs=(VMEM,) * 2,
         scratch_shapes=[
-            pltpu.VMEM((7, PACK, HEAD_DIM), BF16),
+            pltpu.VMEM((6, PACK, HEAD_DIM), BF16),
             pltpu.SMEM((16,), jnp.int32),
             pltpu.SemaphoreType.DMA,
         ],

time: 88.5 us -> 85.4 us (0.965)
  waiting for transfers between devices: 31.9 us -> 26.4 us
  starting transfers between devices: 25.6 us -> 29 us
  Pallas kernels: 18.5 us -> 17.5 us
    ppermute x11, waiting for transfers between devices: 9.65 us -> 5.52 us  [move(): return lax.ppermute(x, 'ctx', ctx_pairs(step))]
    ppermute x9, starting transfers between devices: 8.1 us -> 9.86 us  [exchange(): return lax.ppermute(x, 'section', [(i, i ^ step) for i in range(8)])]
    ppermute x11, starting transfers between devices: 17.5 us -> 19.1 us  [move(): return lax.ppermute(x, 'ctx', ctx_pairs(step))]
    ppermute x9, waiting for transfers between devices: 22.2 us -> 20.9 us  [exchange(): return lax.ppermute(x, 'section', [(i, i ^ step) for i in range(8)])]
where the time goes in v12:
time: 85.4 us; the launch traced here: 85 us
  starting transfers between devices  29 us (34%)
  waiting for transfers between devices  26.4 us (31%)
  Pallas kernels  17.5 us (20%)
  other arithmetic  6.06 us (7%)
  matrix products  5.58 us (7%)
    ppermute x9, waiting for transfers between devices, exchange(): return lax.ppermute(x, 'section', [(i, i ^ step) for i in range(8)])  20.9 us
    ppermute x11, starting transfers between devices, move(): return lax.ppermute(x, 'ctx', ctx_pairs(step))  19.1 us
    pallas_call x3, Pallas kernels, attend(): pl.pallas_call(kernel, out_shape=out_shape, in_specs=[SMEM] + [VMEM] * (l...  11.6 us
    ppermute x9, starting transfers between devices, exchange(): return lax.ppermute(x, 'section', [(i, i ^ step) for i in range(8)])  9.86 us
    dot_general x1, matrix products, per_device(): lax.dot_general(w_query, normed, (((0,), (1,)), ((), ())), preferred_elem...  5.58 us
    ppermute x11, waiting for transfers between devices, move(): return lax.ppermute(x, 'ctx', ctx_pairs(step))  5.52 us
    pallas_call x1, Pallas kernels, per_device(): pl.pallas_call(functools.partial(more_and_fetch_kernel, rest_slots, len(p...  3.41 us
    pallas_call x1, Pallas kernels, per_device(): pl.pallas_call(last_kernel, out_shape=tuple(out_shape), in_specs=[SMEM, V...  2.51 us
  transfers between devices with their start and end apart: 20, of which 11 were waited for; matrix products, arithmetic and copies ran while one was open for 11% of the time, Pallas kernels for 14%

profile of v12, /device:TPU:24, one launch (start us, length us, event | category | flops | bytes accessed | tf_op | source)
XLA Modules:
  0.0 85.0 jit_solution(5444681059419216951)
XLA Ops:
  3.1 7.2 %collective-permute-start.2 = (bf16[1,528,128]{2,1,0:T(8,128)(2,1)S(1)}, bf16[1,528,128]{2,1,0:T(8,128)(2,1)S(1)}, u32[]{:S(2)}, u32[]{:S(2)}) collective-permute-start(bf16[1,528,128]{2,1,0:T(8,128)(2,1)S(1)} %maximum_bitcast_fusion.rest_0_), channel_id=1, source_target_pairs={{0,32},{8,40},{16,48},{24,56},{32,0},{40,8},{48,16},{56,24},{64,96... | collective-permute-start | bytes 405512 | tf_op jit(solution)/shard_map/ppermute | solution.py:48
  10.4 1.3 %collective-permute-start.4 = (bf16[2,528,128]{2,1,0:T(8,128)(2,1)S(1)}, bf16[2,528,128]{2,1,0:T(8,128)(2,1)S(1)}, u32[]{:S(2)}, u32[]{:S(2)}) collective-permute-start(bf16[2,528,128]{2,1,0:T(8,128)(2,1)S(1)} %constant_dynamic-update-slice_fusion), channel_id=1, source_target_pairs={{0,128},{8,136},{16,144},{24,152},{32,160},{40,168},{48,176},{56,1... | collective-permute-start | bytes 811016 | tf_op jit(solution)/shard_map/ppermute | solution.py:48
  11.7 1.3 %collective-permute-start.3 = (bf16[2,528,128]{2,1,0:T(8,128)(2,1)S(1)}, bf16[2,528,128]{2,1,0:T(8,128)(2,1)S(1)}, u32[]{:S(2)}, u32[]{:S(2)}) collective-permute-start(bf16[2,528,128]{2,1,0:T(8,128)(2,1)S(1)} %constant_dynamic-update-slice_fusion), channel_id=1, source_target_pairs={{0,64},{8,200},{16,80},{24,216},{32,96},{40,232},{48,112},{56,248}... | collective-permute-start | bytes 811016 | tf_op jit(solution)/shard_map/ppermute | solution.py:48
  13.0 1.5 %collective-permute-start.1 = (bf16[2,528,128]{2,1,0:T(8,128)(2,1)S(1)}, bf16[2,528,128]{2,1,0:T(8,128)(2,1)S(1)}, u32[]{:S(2)}, u32[]{:S(2)}) collective-permute-start(bf16[2,528,128]{2,1,0:T(8,128)(2,1)S(1)} %constant_dynamic-update-slice_fusion), channel_id=1, source_target_pairs={{0,16},{8,56},{16,32},{24,8},{32,48},{40,24},{48,0},{56,40},{64,80... | collective-permute-start | bytes 811016 | tf_op jit(solution)/shard_map/ppermute | solution.py:48
  14.5 2.3 %fusion = f32[256]{0:T(256)S(1)} fusion(bf16[256,5120]{1,0:T(8,128)(2,1)} %param.6), kind=kLoop, calls=%fused_computation.2 | loop fusion | flops 3931904 | bytes 2622464 | tf_op jit(solution)/shard_map/reduce_sum | solution.py:238
  16.9 5.6 %fusion.11 = bf16[512,256]{1,0:T(8,128)(2,1)S(1)} fusion(bf16[5120,512]{1,0:T(8,128)(2,1)} %param.10, bf16[256,5120]{1,0:T(8,128)(2,1)} %param.6, f32[256]{0:T(256)S(1)} %add_rsqrt_fusion), kind=kOutput, calls=%fused_computation.8 | convolution fusion | flops 1346371584 | bytes 8127488 | tf_op jit(solution)/shard_map/dot_general | solution.py:240
  22.5 1.9 %collective-permute-done.1.rest_1_ = bf16[2,528,128]{2,1,0:T(8,128)(2,1)S(1)} collective-permute-done((bf16[2,528,128]{2,1,0:T(8,128)(2,1)S(1)}, bf16[2,528,128]{2,1,0:T(8,128)(2,1)S(1)}, u32[]{:S(2)}, u32[]{:S(2)}) %collective-permute-start.1) | collective-permute-done | bytes 270368 | tf_op jit(solution)/shard_map/ppermute | solution.py:48
  24.5 1.3 %collective-permute-start.8 = (bf16[3,528,128]{2,1,0:T(8,128)(2,1)S(1)}, bf16[3,528,128]{2,1,0:T(8,128)(2,1)S(1)}, u32[]{:S(2)}, u32[]{:S(2)}) collective-permute-start(bf16[3,528,128]{2,1,0:T(8,128)(2,1)S(1)} %constant_dynamic-update-slice_fusion.2), channel_id=1, source_target_pairs={{0,64},{8,72},{16,80},{24,88},{32,96},{40,104},{48,112},{56,120},{... | collective-permute-start | bytes 1216520 | tf_op jit(solution)/shard_map/ppermute | solution.py:48
  25.8 1.3 %collective-permute-start.5 = (bf16[3,528,128]{2,1,0:T(8,128)(2,1)S(1)}, bf16[3,528,128]{2,1,0:T(8,128)(2,1)S(1)}, u32[]{:S(2)}, u32[]{:S(2)}) collective-permute-start(bf16[3,528,128]{2,1,0:T(8,128)(2,1)S(1)} %constant_dynamic-update-slice_fusion.2), channel_id=1, source_target_pairs={{0,192},{8,200},{16,208},{24,216},{32,224},{40,232},{48,240},{56,2... | collective-permute-start | bytes 1216520 | tf_op jit(solution)/shard_map/ppermute | solution.py:48
  27.5 3.4 %collective-permute-start.6 = (bf16[2,528,128]{2,1,0:T(8,128)(2,1)S(1)}, bf16[2,528,128]{2,1,0:T(8,128)(2,1)S(1)}, u32[]{:S(2)}, u32[]{:S(2)}) collective-permute-start(bf16[2,528,128]{2,1,0:T(8,128)(2,1)S(1)} %collective-permute-done.4.rest_4_), channel_id=1, source_target_pairs={{128,144},{136,184},{144,160},{152,136},{160,176},{168,152},{176,1... | collective-permute-start | bytes 811016 | tf_op jit(solution)/shard_map/ppermute | solution.py:48
  30.9 1.3 %collective-permute-start.7 = (bf16[1,528,128]{2,1,0:T(8,128)(2,1)S(1)}, bf16[1,528,128]{2,1,0:T(8,128)(2,1)S(1)}, u32[]{:S(2)}, u32[]{:S(2)}) collective-permute-start(bf16[1,528,128]{2,1,0:T(8,128)(2,1)S(1)} %collective-permute-done.2.rest_2_), channel_id=1, source_target_pairs={{0,128},{8,136},{16,144},{24,152},{32,160},{40,168},{48,176},{56,1... | collective-permute-start | bytes 405512 | tf_op jit(solution)/shard_map/ppermute | solution.py:48
  32.2 4.6 %attend_first.1 = (f32[528,256]{1,0:T(8,128)S(1)}, f32[528,256]{1,0:T(8,128)S(1)}) custom-call(s32[2]{0:T(128)S(1)} %pad_add_fusion.at_ref, bf16[1,528,128]{2,1,0:T(8,128)(2,1)S(1)} %maximum_bitcast_fusion.rest_0_, bf16[2,528,128]{2,1,0:T(8,128)(2,1)S(1)} %collective-permute-done.1.rest_1_, bf16[1,528,128]{2,1,0:T(8,128)(2,1)S(1)} %collective-permute-done.2.rest_2_, ...), custom_call_target="tpu_custom_call" | custom-call | flops 134217728 | bytes 135168 | tf_op jit(solution)/shard_map/attend_first/pallas_call | solution.py:257
  38.0 3.6 %attend_up.1 = (f32[528,256]{1,0:T(8,128)S(1)}, f32[528,256]{1,0:T(8,128)S(1)}) custom-call(s32[2]{0:T(128)S(1)} %pad_add_fusion.at_ref, bf16[3,528,128]{2,1,0:T(8,128)(2,1)S(1)} %collective-permute-done.8.rest_0_, bf16[640,256]{1,0:T(8,128)(2,1)S(1)} %pad_maximum_fusion.rest_5_.rest_1_.rest_3_, ...), custom_call_target="tpu_custom_call" | custom-call | flops 134217728 | bytes 135168 | tf_op jit(solution)/shard_map/attend_up/pallas_call | solution.py:257
  41.6 1.8 %collective-permute-done.5.rest_0_ = bf16[3,528,128]{2,1,0:T(8,128)(2,1)S(1)} collective-permute-done((bf16[3,528,128]{2,1,0:T(8,128)(2,1)S(1)}, bf16[3,528,128]{2,1,0:T(8,128)(2,1)S(1)}, u32[]{:S(2)}, u32[]{:S(2)}) %collective-permute-start.5) | collective-permute-done | bytes 405536 | tf_op jit(solution)/shard_map/ppermute | solution.py:48
  43.4 3.4 %attend_rest_other.1 = f32[528,256]{1,0:T(8,128)S(1)} custom-call(s32[2]{0:T(128)S(1)} %pad_add_fusion.at_ref, bf16[3,528,128]{2,1,0:T(8,128)(2,1)S(1)} %collective-permute-done.5.rest_0_, bf16[2,528,128]{2,1,0:T(8,128)(2,1)S(1)} %collective-permute-done.6.rest_1_, bf16[1,528,128]{2,1,0:T(8,128)(2,1)S(1)} %collective-permute-done.7.rest_2_, ...), custom_call_target="tpu_custom_call" | custom-call | flops 134217728 | bytes 135168 | tf_op jit(solution)/shard_map/attend_rest_other/pallas_call | solution.py:257
  46.9 3.4 %attend_rest_own.1 = (f32[528,256]{1,0:T(8,128)S(1)}, bf16[512,5120]{1,0:T(8,128)(2,1)S(1)}) custom-call(s32[2]{0:T(128)S(1)} %pad_add_fusion.at_ref, bf16[3,528,128]{2,1,0:T(8,128)(2,1)S(1)} %collective-permute-done.5.rest_0_, bf16[2,528,128]{2,1,0:T(8,128)(2,1)S(1)} %collective-permute-done.6.rest_1_, ...), custom_call_target="tpu_custom_call" | custom-call | flops 134217728 | bytes 135168 | tf_op jit(solution)/shard_map/attend_rest_own/pallas_call | solution.py:278
  50.3 2.5 %project_attended.1 = (bf16[4,96,640]{2,1,0:T(8,128)(2,1)S(1)}, bf16[4,96,640]{2,1,0:T(8,128)(2,1)S(1)}, bf16[4,80,640]{2,1,0:T(8,128)(2,1)S(1)}, bf16[4,80,640]...) custom-call(s32[2]{0:T(128)S(1)} %pad_add_fusion.at_ref, ...), custom_call_target="tpu_custom_call" | custom-call | flops 1610612736 | bytes 1622016 | tf_op jit(solution)/shard_map/project_attended/pallas_call | solution.py:297
  52.8 2.8 %collective-permute-start.14 = (bf16[4,80,640]{2,1,0:T(8,128)(2,1)S(1)}, bf16[4,80,640]{2,1,0:T(8,128)(2,1)S(1)}, u32[]{:S(2)}, u32[]{:S(2)}) collective-permute-start(bf16[4,80,640]{2,1,0:T(8,128)(2,1)S(1)} %get-tuple-element.62), channel_id=1, source_target_pairs={{0,3},{1,2},{2,1},{3,0},{4,7},{5,6},{6,5},{7,4},{8,11},{9,10},{10,... | collective-permute-start | bytes 1228808 | tf_op jit(solution)/shard_map/ppermute | solution.py:309
  56.9 9.1 %collective-permute-done.14 = bf16[4,80,640]{2,1,0:T(8,128)(2,1)S(1)} collective-permute-done((bf16[4,80,640]{2,1,0:T(8,128)(2,1)S(1)}, bf16[4,80,640]{2,1,0:T(8,128)(2,1)S(1)}, u32[]{:S(2)}, u32[]{:S(2)}) %collective-permute-start.14) | collective-permute-done | bytes 409632 | tf_op jit(solution)/shard_map/ppermute | solution.py:309
  67.7 2.3 %collective-permute-done.11 = bf16[4,96,640]{2,1,0:T(8,128)(2,1)S(1)} collective-permute-done((bf16[4,96,640]{2,1,0:T(8,128)(2,1)S(1)}, bf16[4,96,640]{2,1,0:T(8,128)(2,1)S(1)}, u32[]{:S(2)}, u32[]{:S(2)}) %collective-permute-start.11) | collective-permute-done | bytes 491552 | tf_op jit(solution)/shard_map/ppermute | solution.py:309
  70.4 2.4 %collective-permute-done.15 = bf16[2,80,640]{2,1,0:T(8,128)(2,1)S(1)} collective-permute-done((bf16[2,80,640]{2,1,0:T(8,128)(2,1)S(1)}, bf16[2,80,640]{2,1,0:T(8,128)(2,1)S(1)}, u32[]{:S(2)}, u32[]{:S(2)}) %collective-permute-start.15) | collective-permute-done | bytes 204832 | tf_op jit(solution)/shard_map/ppermute | solution.py:309
  74.2 2.5 %collective-permute-start.19 = (bf16[80,640]{1,0:T(8,128)(2,1)S(1)}, bf16[80,640]{1,0:T(8,128)(2,1)S(1)}, u32[]{:S(2)}, u32[]{:S(2)}) collective-permute-start(bf16[80,640]{1,0:T(8,128)(2,1)S(1)} %fusion.23), channel_id=1, source_target_pairs={{0,3},{1,2},{2,1},{3,0},{4,7},{5,6},{6,5},{7,4},{8,11},{9,10},{10,... | collective-permute-start | bytes 307208 | tf_op jit(solution)/shard_map/ppermute | solution.py:309
  77.7 1.5 %collective-permute-done.12 = bf16[2,96,640]{2,1,0:T(8,128)(2,1)S(1)} collective-permute-done((bf16[2,96,640]{2,1,0:T(8,128)(2,1)S(1)}, bf16[2,96,640]{2,1,0:T(8,128)(2,1)S(1)}, u32[]{:S(2)}, u32[]{:S(2)}) %collective-permute-start.12) | collective-permute-done | bytes 245792 | tf_op jit(solution)/shard_map/ppermute | solution.py:309
  80.4 3.8 %collective-permute-done.13 = bf16[96,640]{1,0:T(8,128)(2,1)S(1)} collective-permute-done((bf16[96,640]{1,0:T(8,128)(2,1)S(1)}, bf16[96,640]{1,0:T(8,128)(2,1)S(1)}, u32[]{:S(2)}, u32[]{:S(2)}) %collective-permute-start.13) | collective-permute-done | bytes 122912 | tf_op jit(solution)/shard_map/ppermute | solution.py:309
  (50 shorter events, 12.6 us)
Async XLA Ops:
  1.7 1.4 %collective-permute-start = (bf16[1,528,128]{2,1,0:T(8,128)(2,1)S(1)}, bf16[1,528,128]{2,1,0:T(8,128)(2,1)S(1)}, u32[]{:S(2)}, u32[]{:S(2)}) collective-permute-start(bf16[1,528,128]{2,1,0:T(8,128)(2,1)S(1)} %maximum_bitcast_fusion.rest_0_), channel_id=1, source_target_pairs={{0,8},{8,0},{16,24},{24,16},{32,40},{40,32},{48,56},{56,48},{64,72... | collective-permute-start | bytes 405512 | tf_op jit(solution)/shard_map/ppermute | solution.py:48
  3.1 19.3 %collective-permute-start.2 = (bf16[1,528,128]{2,1,0:T(8,128)(2,1)S(1)}, bf16[1,528,128]{2,1,0:T(8,128)(2,1)S(1)}, u32[]{:S(2)}, u32[]{:S(2)}) collective-permute-start(bf16[1,528,128]{2,1,0:T(8,128)(2,1)S(1)} %maximum_bitcast_fusion.rest_0_), channel_id=1, source_target_pairs={{0,32},{8,40},{16,48},{24,56},{32,0},{40,8},{48,16},{56,24},{64,96... | collective-permute-start | bytes 405512 | tf_op jit(solution)/shard_map/ppermute | solution.py:48
  10.4 12.1 %collective-permute-start.4 = (bf16[2,528,128]{2,1,0:T(8,128)(2,1)S(1)}, bf16[2,528,128]{2,1,0:T(8,128)(2,1)S(1)}, u32[]{:S(2)}, u32[]{:S(2)}) collective-permute-start(bf16[2,528,128]{2,1,0:T(8,128)(2,1)S(1)} %constant_dynamic-update-slice_fusion), channel_id=1, source_target_pairs={{0,128},{8,136},{16,144},{24,152},{32,160},{40,168},{48,176},{56,1... | collective-permute-start | bytes 811016 | tf_op jit(solution)/shard_map/ppermute | solution.py:48
  11.7 10.8 %collective-permute-start.3 = (bf16[2,528,128]{2,1,0:T(8,128)(2,1)S(1)}, bf16[2,528,128]{2,1,0:T(8,128)(2,1)S(1)}, u32[]{:S(2)}, u32[]{:S(2)}) collective-permute-start(bf16[2,528,128]{2,1,0:T(8,128)(2,1)S(1)} %constant_dynamic-update-slice_fusion), channel_id=1, source_target_pairs={{0,64},{8,200},{16,80},{24,216},{32,96},{40,232},{48,112},{56,248}... | collective-permute-start | bytes 811016 | tf_op jit(solution)/shard_map/ppermute | solution.py:48
  13.0 11.5 %collective-permute-start.1 = (bf16[2,528,128]{2,1,0:T(8,128)(2,1)S(1)}, bf16[2,528,128]{2,1,0:T(8,128)(2,1)S(1)}, u32[]{:S(2)}, u32[]{:S(2)}) collective-permute-start(bf16[2,528,128]{2,1,0:T(8,128)(2,1)S(1)} %constant_dynamic-update-slice_fusion), channel_id=1, source_target_pairs={{0,16},{8,56},{16,32},{24,8},{32,48},{40,24},{48,0},{56,40},{64,80... | collective-permute-start | bytes 811016 | tf_op jit(solution)/shard_map/ppermute | solution.py:48
  24.5 13.5 %collective-permute-start.8 = (bf16[3,528,128]{2,1,0:T(8,128)(2,1)S(1)}, bf16[3,528,128]{2,1,0:T(8,128)(2,1)S(1)}, u32[]{:S(2)}, u32[]{:S(2)}) collective-permute-start(bf16[3,528,128]{2,1,0:T(8,128)(2,1)S(1)} %constant_dynamic-update-slice_fusion.2), channel_id=1, source_target_pairs={{0,64},{8,72},{16,80},{24,88},{32,96},{40,104},{48,112},{56,120},{... | collective-permute-start | bytes 1216520 | tf_op jit(solution)/shard_map/ppermute | solution.py:48
  25.8 17.6 %collective-permute-start.5 = (bf16[3,528,128]{2,1,0:T(8,128)(2,1)S(1)}, bf16[3,528,128]{2,1,0:T(8,128)(2,1)S(1)}, u32[]{:S(2)}, u32[]{:S(2)}) collective-permute-start(bf16[3,528,128]{2,1,0:T(8,128)(2,1)S(1)} %constant_dynamic-update-slice_fusion.2), channel_id=1, source_target_pairs={{0,192},{8,200},{16,208},{24,216},{32,224},{40,232},{48,240},{56,2... | collective-permute-start | bytes 1216520 | tf_op jit(solution)/shard_map/ppermute | solution.py:48
  27.1 5.1 %collective-permute-start.9 = (bf16[640,256]{1,0:T(8,128)(2,1)S(1)}, bf16[640,256]{1,0:T(8,128)(2,1)S(1)}, u32[]{:S(2)}, u32[]{:S(2)}) collective-permute-start(bf16[640,256]{1,0:T(8,128)(2,1)S(1)} %pad_maximum_fusion.rest_5_.rest_1_.rest_3_), channel_id=1, source_target_pairs={{0,8},{8,0},{16,24},{24,16},{32,40},{40,32},{48,56},{56,48},{64,72... | collective-permute-start | bytes 983048 | tf_op jit(solution)/shard_map/ppermute | solution.py:48
  27.5 14.1 %collective-permute-start.6 = (bf16[2,528,128]{2,1,0:T(8,128)(2,1)S(1)}, bf16[2,528,128]{2,1,0:T(8,128)(2,1)S(1)}, u32[]{:S(2)}, u32[]{:S(2)}) collective-permute-start(bf16[2,528,128]{2,1,0:T(8,128)(2,1)S(1)} %collective-permute-done.4.rest_4_), channel_id=1, source_target_pairs={{128,144},{136,184},{144,160},{152,136},{160,176},{168,152},{176,1... | collective-permute-start | bytes 811016 | tf_op jit(solution)/shard_map/ppermute | solution.py:48
  30.9 10.7 %collective-permute-start.7 = (bf16[1,528,128]{2,1,0:T(8,128)(2,1)S(1)}, bf16[1,528,128]{2,1,0:T(8,128)(2,1)S(1)}, u32[]{:S(2)}, u32[]{:S(2)}) collective-permute-start(bf16[1,528,128]{2,1,0:T(8,128)(2,1)S(1)} %collective-permute-done.2.rest_2_), channel_id=1, source_target_pairs={{0,128},{8,136},{16,144},{24,152},{32,160},{40,168},{48,176},{56,1... | collective-permute-start | bytes 405512 | tf_op jit(solution)/shard_map/ppermute | solution.py:48
  46.8 3.5 %collective-permute-start.10 = (f32[528,256]{1,0:T(8,128)S(1)}, f32[528,256]{1,0:T(8,128)S(1)}, u32[]{:S(2)}, u32[]{:S(2)}) collective-permute-start(f32[528,256]{1,0:T(8,128)S(1)} %attend_rest_other.1), channel_id=1, source_target_pairs={{0,8},{8,0},{16,24},{24,16},{32,40},{40,32},{48,56},{56,48},{64,72... | collective-permute-start | bytes 1622024 | tf_op jit(solution)/shard_map/ppermute | solution.py:48
  52.8 13.2 %collective-permute-start.14 = (bf16[4,80,640]{2,1,0:T(8,128)(2,1)S(1)}, bf16[4,80,640]{2,1,0:T(8,128)(2,1)S(1)}, u32[]{:S(2)}, u32[]{:S(2)}) collective-permute-start(bf16[4,80,640]{2,1,0:T(8,128)(2,1)S(1)} %get-tuple-element.62), channel_id=1, source_target_pairs={{0,3},{1,2},{2,1},{3,0},{4,7},{5,6},{6,5},{7,4},{8,11},{9,10},{10,... | collective-permute-start | bytes 1228808 | tf_op jit(solution)/shard_map/ppermute | solution.py:309
  55.7 11.6 %collective-permute-start.17 = (bf16[4,80,640]{2,1,0:T(8,128)(2,1)S(1)}, bf16[4,80,640]{2,1,0:T(8,128)(2,1)S(1)}, u32[]{:S(2)}, u32[]{:S(2)}) collective-permute-start(bf16[4,80,640]{2,1,0:T(8,128)(2,1)S(1)} %get-tuple-element.64), channel_id=1, source_target_pairs={{0,4},{1,5},{2,6},{3,7},{4,0},{5,1},{6,2},{7,3},{8,12},{9,13},{10,... | collective-permute-start | bytes 1228808 | tf_op jit(solution)/shard_map/ppermute | solution.py:309
  56.7 13.3 %collective-permute-start.11 = (bf16[4,96,640]{2,1,0:T(8,128)(2,1)S(1)}, bf16[4,96,640]{2,1,0:T(8,128)(2,1)S(1)}, u32[]{:S(2)}, u32[]{:S(2)}) collective-permute-start(bf16[4,96,640]{2,1,0:T(8,128)(2,1)S(1)} %get-tuple-element.60), channel_id=1, source_target_pairs={{0,1},{1,0},{2,3},{3,2},{4,5},{5,4},{6,7},{7,6},{8,9},{9,8},{10,11... | collective-permute-start | bytes 1474568 | tf_op jit(solution)/shard_map/ppermute | solution.py:309
  66.1 6.8 %collective-permute-start.15 = (bf16[2,80,640]{2,1,0:T(8,128)(2,1)S(1)}, bf16[2,80,640]{2,1,0:T(8,128)(2,1)S(1)}, u32[]{:S(2)}, u32[]{:S(2)}) collective-permute-start(bf16[2,80,640]{2,1,0:T(8,128)(2,1)S(1)} %slice.98), channel_id=1, source_target_pairs={{0,4},{1,5},{2,6},{3,7},{4,0},{5,1},{6,2},{7,3},{8,12},{9,13},{10,... | collective-permute-start | bytes 614408 | tf_op jit(solution)/shard_map/ppermute | solution.py:309
  67.4 6.8 %collective-permute-start.18 = (bf16[2,80,640]{2,1,0:T(8,128)(2,1)S(1)}, bf16[2,80,640]{2,1,0:T(8,128)(2,1)S(1)}, u32[]{:S(2)}, u32[]{:S(2)}) collective-permute-start(bf16[2,80,640]{2,1,0:T(8,128)(2,1)S(1)} %slice.97), channel_id=1, source_target_pairs={{0,1},{1,0},{2,3},{3,2},{4,5},{5,4},{6,7},{7,6},{8,9},{9,8},{10,11... | collective-permute-start | bytes 614408 | tf_op jit(solution)/shard_map/ppermute | solution.py:309
  70.1 9.1 %collective-permute-start.12 = (bf16[2,96,640]{2,1,0:T(8,128)(2,1)S(1)}, bf16[2,96,640]{2,1,0:T(8,128)(2,1)S(1)}, u32[]{:S(2)}, u32[]{:S(2)}) collective-permute-start(bf16[2,96,640]{2,1,0:T(8,128)(2,1)S(1)} %slice.96), channel_id=1, source_target_pairs={{0,3},{1,2},{2,1},{3,0},{4,7},{5,6},{6,5},{7,4},{8,11},{9,10},{10,... | collective-permute-start | bytes 737288 | tf_op jit(solution)/shard_map/ppermute | solution.py:309
  73.0 4.7 %collective-permute-start.16 = (bf16[80,640]{1,0:T(8,128)(2,1)S(1)}, bf16[80,640]{1,0:T(8,128)(2,1)S(1)}, u32[]{:S(2)}, u32[]{:S(2)}) collective-permute-start(bf16[80,640]{1,0:T(8,128)(2,1)S(1)} %fusion.22), channel_id=1, source_target_pairs={{0,1},{1,0},{2,3},{3,2},{4,5},{5,4},{6,7},{7,6},{8,9},{9,8},{10,11... | collective-permute-start | bytes 307208 | tf_op jit(solution)/shard_map/ppermute | solution.py:309
  74.2 6.2 %collective-permute-start.19 = (bf16[80,640]{1,0:T(8,128)(2,1)S(1)}, bf16[80,640]{1,0:T(8,128)(2,1)S(1)}, u32[]{:S(2)}, u32[]{:S(2)}) collective-permute-start(bf16[80,640]{1,0:T(8,128)(2,1)S(1)} %fusion.23), channel_id=1, source_target_pairs={{0,3},{1,2},{2,1},{3,0},{4,7},{5,6},{6,5},{7,4},{8,11},{9,10},{10,... | collective-permute-start | bytes 307208 | tf_op jit(solution)/shard_map/ppermute | solution.py:309
  79.3 5.0 %collective-permute-start.13 = (bf16[96,640]{1,0:T(8,128)(2,1)S(1)}, bf16[96,640]{1,0:T(8,128)(2,1)S(1)}, u32[]{:S(2)}, u32[]{:S(2)}) collective-permute-start(bf16[96,640]{1,0:T(8,128)(2,1)S(1)} %fusion.21), channel_id=1, source_target_pairs={{0,4},{1,5},{2,6},{3,7},{4,0},{5,1},{6,2},{7,3},{8,12},{9,13},{10,... | collective-permute-start | bytes 368648 | tf_op jit(solution)/shard_map/ppermute | solution.py:309

commit v13 on v12

--- a/solution.py
+++ b/solution.py
@@ -89,8 +89,12 @@
 
 def rest_slots(y, z, c):
     d = 2 * c - 1
-    around = [(y + 1, z + d, c), (y + 1, z + d, 1 - c), (y + 1, z + 2, c)]
-    return [around, [(y + 2, z + d, c), (y + 2, z + d, 1 - c)], [(y + 2, z + 2, c)]]
+    return [[(y + 1, z + d, c), (y + 1, z + d, 1 - c), (y + 1, z + 2, c)]]
+
+
+def far_slots(y, z, c):
+    d = 2 * c - 1
+    return [[(y + 2, z + d, c), (y + 2, z + d, 1 - c)], [(y + 2, z + 2, c)]]
 
 
 def attend_blocks(kv_ref, places, diagonal, q_ref, state_ref):
@@ -271,9 +275,12 @@
     up, state, state_2 = lax.optimization_barrier((up, state, state_2))
     near = functools.partial(more_kernel, up_slots, 1, (0, 1))
     state, state_2 = attend(near, 3, [up], (q, q_2), (state, state_2), "attend_up")
-    pieces, state, state_2 = lax.optimization_barrier(((around, far_near, far_far), state, state_2))
+    fars, state, state_2 = lax.optimization_barrier(((far_near, far_far), state, state_2))
+    far = functools.partial(more_kernel, far_slots, 2, (0, 1))
+    state, state_2 = attend(far, 3, fars, (q, q_2), (state, state_2), "attend_far")
+    pieces, state, state_2 = lax.optimization_barrier(((around,), state, state_2))
     rest = functools.partial(more_kernel, rest_slots, len(pieces), (1,))
-    (state_2,) = attend(rest, 6, pieces, (q_2,), (state_2,), "attend_rest_other")
+    (state_2,) = attend(rest, 3, pieces, (q_2,), (state_2,), "attend_rest_other")
     state_2, state = lax.optimization_barrier((state_2, state))
     state, w_held = pl.pallas_call(
         functools.partial(more_and_fetch_kernel, rest_slots, len(pieces), (0,)),
@@ -281,7 +288,7 @@
         in_specs=[SMEM] + [VMEM] * (len(pieces) + 2) + [pl.BlockSpec(memory_space=pltpu.HBM)],
         out_specs=(VMEM,) * 2,
         scratch_shapes=[
-            pltpu.VMEM((6, PACK, HEAD_DIM), BF16),
+            pltpu.VMEM((3, PACK, HEAD_DIM), BF16),
             pltpu.SMEM((16,), jnp.int32),
             pltpu.SemaphoreType.DMA,
         ],

time: 85.4 us -> 85.6 us (level)
  waiting for transfers between devices: 26.4 us -> 24.6 us
  Pallas kernels: 17.5 us -> 19.2 us
    pallas_call x3 -> x4, Pallas kernels: 11.6 us -> 13.6 us  [attend(): pl.pallas_call(kernel, out_shape=out_shape, in_specs=[SMEM] + [VMEM] * (l...]
    ppermute x11, waiting for transfers between devices: 5.52 us -> 3.73 us  [move(): return lax.ppermute(x, 'ctx', ctx_pairs(step))]
  transfers between devices with their start and end apart: 20 -> 20, of which waited for: 11 -> 11; matrix products, arithmetic and copies ran while one was open for 11% -> 11% of each run, Pallas kernels for 14% -> 17%
where the time goes in v13:
time: 85.6 us; the launch traced here: 85.1 us
  starting transfers between devices  29.2 us (34%)
  waiting for transfers between devices  24.6 us (29%)
  Pallas kernels  19.2 us (22%)
  other arithmetic  6.06 us (7%)
  matrix products  5.58 us (7%)
    ppermute x9, waiting for transfers between devices, exchange(): return lax.ppermute(x, 'section', [(i, i ^ step) for i in range(8)])  20.9 us
    ppermute x11, starting transfers between devices, move(): return lax.ppermute(x, 'ctx', ctx_pairs(step))  19.1 us
    pallas_call x4, Pallas kernels, attend(): pl.pallas_call(kernel, out_shape=out_shape, in_specs=[SMEM] + [VMEM] * (l...  13.6 us
    ppermute x9, starting transfers between devices, exchange(): return lax.ppermute(x, 'section', [(i, i ^ step) for i in range(8)])  10.1 us
    dot_general x1, matrix products, per_device(): lax.dot_general(w_query, normed, (((0,), (1,)), ((), ())), preferred_elem...  5.58 us
    ppermute x11, waiting for transfers between devices, move(): return lax.ppermute(x, 'ctx', ctx_pairs(step))  3.73 us
    pallas_call x1, Pallas kernels, per_device(): pl.pallas_call(functools.partial(more_and_fetch_kernel, rest_slots, len(p...  3.04 us
    pallas_call x1, Pallas kernels, per_device(): pl.pallas_call(last_kernel, out_shape=tuple(out_shape), in_specs=[SMEM, V...  2.5 us
  transfers between devices with their start and end apart: 20, of which 11 were waited for; matrix products, arithmetic and copies ran while one was open for 11% of the time, Pallas kernels for 17%

profile of v13, /device:TPU:24, one launch (start us, length us, event | category | flops | bytes accessed | tf_op | source)
XLA Modules:
  0.0 85.1 jit_solution(10710014611539242722)
XLA Ops:
  3.1 7.2 %collective-permute-start.2 = (bf16[1,528,128]{2,1,0:T(8,128)(2,1)S(1)}, bf16[1,528,128]{2,1,0:T(8,128)(2,1)S(1)}, u32[]{:S(2)}, u32[]{:S(2)}) collective-permute-start(bf16[1,528,128]{2,1,0:T(8,128)(2,1)S(1)} %maximum_bitcast_fusion.rest_0_), channel_id=1, source_target_pairs={{0,32},{8,40},{16,48},{24,56},{32,0},{40,8},{48,16},{56,24},{64,96... | collective-permute-start | bytes 405512 | tf_op jit(solution)/shard_map/ppermute | solution.py:48
  10.4 1.3 %collective-permute-start.4 = (bf16[2,528,128]{2,1,0:T(8,128)(2,1)S(1)}, bf16[2,528,128]{2,1,0:T(8,128)(2,1)S(1)}, u32[]{:S(2)}, u32[]{:S(2)}) collective-permute-start(bf16[2,528,128]{2,1,0:T(8,128)(2,1)S(1)} %constant_dynamic-update-slice_fusion), channel_id=1, source_target_pairs={{0,128},{8,136},{16,144},{24,152},{32,160},{40,168},{48,176},{56,1... | collective-permute-start | bytes 811016 | tf_op jit(solution)/shard_map/ppermute | solution.py:48
  11.7 1.3 %collective-permute-start.3 = (bf16[2,528,128]{2,1,0:T(8,128)(2,1)S(1)}, bf16[2,528,128]{2,1,0:T(8,128)(2,1)S(1)}, u32[]{:S(2)}, u32[]{:S(2)}) collective-permute-start(bf16[2,528,128]{2,1,0:T(8,128)(2,1)S(1)} %constant_dynamic-update-slice_fusion), channel_id=1, source_target_pairs={{0,64},{8,200},{16,80},{24,216},{32,96},{40,232},{48,112},{56,248}... | collective-permute-start | bytes 811016 | tf_op jit(solution)/shard_map/ppermute | solution.py:48
  13.0 1.5 %collective-permute-start.1 = (bf16[2,528,128]{2,1,0:T(8,128)(2,1)S(1)}, bf16[2,528,128]{2,1,0:T(8,128)(2,1)S(1)}, u32[]{:S(2)}, u32[]{:S(2)}) collective-permute-start(bf16[2,528,128]{2,1,0:T(8,128)(2,1)S(1)} %constant_dynamic-update-slice_fusion), channel_id=1, source_target_pairs={{0,16},{8,56},{16,32},{24,8},{32,48},{40,24},{48,0},{56,40},{64,80... | collective-permute-start | bytes 811016 | tf_op jit(solution)/shard_map/ppermute | solution.py:48
  14.5 2.3 %fusion = f32[256]{0:T(256)S(1)} fusion(bf16[256,5120]{1,0:T(8,128)(2,1)} %param.6), kind=kLoop, calls=%fused_computation.2 | loop fusion | flops 3931904 | bytes 2622464 | tf_op jit(solution)/shard_map/reduce_sum | solution.py:242
  16.9 5.6 %fusion.11 = bf16[512,256]{1,0:T(8,128)(2,1)S(1)} fusion(bf16[5120,512]{1,0:T(8,128)(2,1)} %param.10, bf16[256,5120]{1,0:T(8,128)(2,1)} %param.6, f32[256]{0:T(256)S(1)} %add_rsqrt_fusion), kind=kOutput, calls=%fused_computation.8 | convolution fusion | flops 1346371584 | bytes 8127488 | tf_op jit(solution)/shard_map/dot_general | solution.py:244
  22.5 1.9 %collective-permute-done.1.rest_1_ = bf16[2,528,128]{2,1,0:T(8,128)(2,1)S(1)} collective-permute-done((bf16[2,528,128]{2,1,0:T(8,128)(2,1)S(1)}, bf16[2,528,128]{2,1,0:T(8,128)(2,1)S(1)}, u32[]{:S(2)}, u32[]{:S(2)}) %collective-permute-start.1) | collective-permute-done | bytes 270368 | tf_op jit(solution)/shard_map/ppermute | solution.py:48
  24.5 1.3 %collective-permute-start.8 = (bf16[3,528,128]{2,1,0:T(8,128)(2,1)S(1)}, bf16[3,528,128]{2,1,0:T(8,128)(2,1)S(1)}, u32[]{:S(2)}, u32[]{:S(2)}) collective-permute-start(bf16[3,528,128]{2,1,0:T(8,128)(2,1)S(1)} %constant_dynamic-update-slice_fusion.2), channel_id=1, source_target_pairs={{0,64},{8,72},{16,80},{24,88},{32,96},{40,104},{48,112},{56,120},{... | collective-permute-start | bytes 1216520 | tf_op jit(solution)/shard_map/ppermute | solution.py:48
  25.8 1.3 %collective-permute-start.5 = (bf16[3,528,128]{2,1,0:T(8,128)(2,1)S(1)}, bf16[3,528,128]{2,1,0:T(8,128)(2,1)S(1)}, u32[]{:S(2)}, u32[]{:S(2)}) collective-permute-start(bf16[3,528,128]{2,1,0:T(8,128)(2,1)S(1)} %constant_dynamic-update-slice_fusion.2), channel_id=1, source_target_pairs={{0,192},{8,200},{16,208},{24,216},{32,224},{40,232},{48,240},{56,2... | collective-permute-start | bytes 1216520 | tf_op jit(solution)/shard_map/ppermute | solution.py:48
  27.5 3.4 %collective-permute-start.6 = (bf16[2,528,128]{2,1,0:T(8,128)(2,1)S(1)}, bf16[2,528,128]{2,1,0:T(8,128)(2,1)S(1)}, u32[]{:S(2)}, u32[]{:S(2)}) collective-permute-start(bf16[2,528,128]{2,1,0:T(8,128)(2,1)S(1)} %collective-permute-done.4.rest_4_), channel_id=1, source_target_pairs={{128,144},{136,184},{144,160},{152,136},{160,176},{168,152},{176,1... | collective-permute-start | bytes 811016 | tf_op jit(solution)/shard_map/ppermute | solution.py:48
  30.9 1.3 %collective-permute-start.7 = (bf16[1,528,128]{2,1,0:T(8,128)(2,1)S(1)}, bf16[1,528,128]{2,1,0:T(8,128)(2,1)S(1)}, u32[]{:S(2)}, u32[]{:S(2)}) collective-permute-start(bf16[1,528,128]{2,1,0:T(8,128)(2,1)S(1)} %collective-permute-done.2.rest_2_), channel_id=1, source_target_pairs={{0,128},{8,136},{16,144},{24,152},{32,160},{40,168},{48,176},{56,1... | collective-permute-start | bytes 405512 | tf_op jit(solution)/shard_map/ppermute | solution.py:48
  32.2 4.6 %attend_first.1 = (f32[528,256]{1,0:T(8,128)S(1)}, f32[528,256]{1,0:T(8,128)S(1)}) custom-call(s32[2]{0:T(128)S(1)} %pad_add_fusion.at_ref, bf16[1,528,128]{2,1,0:T(8,128)(2,1)S(1)} %maximum_bitcast_fusion.rest_0_, bf16[2,528,128]{2,1,0:T(8,128)(2,1)S(1)} %collective-permute-done.1.rest_1_, bf16[1,528,128]{2,1,0:T(8,128)(2,1)S(1)} %collective-permute-done.2.rest_2_, ...), custom_call_target="tpu_custom_call" | custom-call | flops 134217728 | bytes 135168 | tf_op jit(solution)/shard_map/attend_first/pallas_call | solution.py:261
  38.0 3.6 %attend_up.1 = (f32[528,256]{1,0:T(8,128)S(1)}, f32[528,256]{1,0:T(8,128)S(1)}) custom-call(s32[2]{0:T(128)S(1)} %pad_add_fusion.at_ref, bf16[3,528,128]{2,1,0:T(8,128)(2,1)S(1)} %collective-permute-done.8.rest_0_, bf16[640,256]{1,0:T(8,128)(2,1)S(1)} %pad_maximum_fusion.rest_5_.rest_1_.rest_2_, ...), custom_call_target="tpu_custom_call" | custom-call | flops 134217728 | bytes 135168 | tf_op jit(solution)/shard_map/attend_up/pallas_call | solution.py:261
  41.6 3.4 %attend_far.1 = (f32[528,256]{1,0:T(8,128)S(1)}, f32[528,256]{1,0:T(8,128)S(1)}) custom-call(s32[2]{0:T(128)S(1)} %pad_add_fusion.at_ref, bf16[2,528,128]{2,1,0:T(8,128)(2,1)S(1)} %collective-permute-done.6.rest_0_, bf16[1,528,128]{2,1,0:T(8,128)(2,1)S(1)} %collective-permute-done.7.rest_1_, bf16[640,256]{1,0:T(8,128)(2,1)S(1)} %pad_maximum_fusion.rest_5_.rest_1_.rest_2_, ...), custom_call_target="tpu_custom_call" | custom-call | flops 134217728 | bytes 135168 | tf_op jit(solution)/shard_map/attend_far/pallas_call | solution.py:261
  45.0 2.0 %attend_rest_other.1 = f32[528,256]{1,0:T(8,128)S(1)} custom-call(s32[2]{0:T(128)S(1)} %pad_add_fusion.at_ref, bf16[3,528,128]{2,1,0:T(8,128)(2,1)S(1)} %collective-permute-done.5.rest_0_, bf16[640,256]{1,0:T(8,128)(2,1)S(1)} %collective-permute-done.9.rest_6_.rest_2_.rest_3_.rest_1_, f32[528,256]{1,0:T(8,128)S(1)} %get-tuple-element.61.rest_2_), custom_call_target="tpu_custom_call" | custom-call | flops 134217728 | bytes 135168 | tf_op jit(solution)/shard_map/attend_rest_other/pallas_call | solution.py:261
  47.1 3.0 %attend_rest_own.1 = (f32[528,256]{1,0:T(8,128)S(1)}, bf16[512,5120]{1,0:T(8,128)(2,1)S(1)}) custom-call(s32[2]{0:T(128)S(1)} %pad_add_fusion.at_ref, bf16[3,528,128]{2,1,0:T(8,128)(2,1)S(1)} %collective-permute-done.5.rest_0_, bf16[640,256]{1,0:T(8,128)(2,1)S(1)} %pad_maximum_fusion.rest_5_.rest_1_.rest_2_, f32[528,256]{1,0:T(8,128)S(1)} %get-tuple-element.63.rest_2_, ...), custom_call_target="tpu_custom_call" | custom-call | flops 134217728 | bytes 135168 | tf_op jit(solution)/shard_map/attend_rest_own/pallas_call | solution.py:285
  50.2 2.5 %project_attended.1 = (bf16[4,96,640]{2,1,0:T(8,128)(2,1)S(1)}, bf16[4,96,640]{2,1,0:T(8,128)(2,1)S(1)}, bf16[4,80,640]{2,1,0:T(8,128)(2,1)S(1)}, bf16[4,80,640]...) custom-call(s32[2]{0:T(128)S(1)} %pad_add_fusion.at_ref, ...), custom_call_target="tpu_custom_call" | custom-call | flops 1610612736 | bytes 1622016 | tf_op jit(solution)/shard_map/project_attended/pallas_call | solution.py:304
  52.7 3.1 %collective-permute-start.14 = (bf16[4,80,640]{2,1,0:T(8,128)(2,1)S(1)}, bf16[4,80,640]{2,1,0:T(8,128)(2,1)S(1)}, u32[]{:S(2)}, u32[]{:S(2)}) collective-permute-start(bf16[4,80,640]{2,1,0:T(8,128)(2,1)S(1)} %get-tuple-element.70), channel_id=1, source_target_pairs={{0,3},{1,2},{2,1},{3,0},{4,7},{5,6},{6,5},{7,4},{8,11},{9,10},{10,... | collective-permute-start | bytes 1228808 | tf_op jit(solution)/shard_map/ppermute | solution.py:316
  57.0 9.1 %collective-permute-done.14 = bf16[4,80,640]{2,1,0:T(8,128)(2,1)S(1)} collective-permute-done((bf16[4,80,640]{2,1,0:T(8,128)(2,1)S(1)}, bf16[4,80,640]{2,1,0:T(8,128)(2,1)S(1)}, u32[]{:S(2)}, u32[]{:S(2)}) %collective-permute-start.14) | collective-permute-done | bytes 409632 | tf_op jit(solution)/shard_map/ppermute | solution.py:316
  67.8 2.3 %collective-permute-done.11 = bf16[4,96,640]{2,1,0:T(8,128)(2,1)S(1)} collective-permute-done((bf16[4,96,640]{2,1,0:T(8,128)(2,1)S(1)}, bf16[4,96,640]{2,1,0:T(8,128)(2,1)S(1)}, u32[]{:S(2)}, u32[]{:S(2)}) %collective-permute-start.11) | collective-permute-done | bytes 491552 | tf_op jit(solution)/shard_map/ppermute | solution.py:316
  70.6 2.4 %collective-permute-done.15 = bf16[2,80,640]{2,1,0:T(8,128)(2,1)S(1)} collective-permute-done((bf16[2,80,640]{2,1,0:T(8,128)(2,1)S(1)}, bf16[2,80,640]{2,1,0:T(8,128)(2,1)S(1)}, u32[]{:S(2)}, u32[]{:S(2)}) %collective-permute-start.15) | collective-permute-done | bytes 204832 | tf_op jit(solution)/shard_map/ppermute | solution.py:316
  74.3 2.5 %collective-permute-start.19 = (bf16[80,640]{1,0:T(8,128)(2,1)S(1)}, bf16[80,640]{1,0:T(8,128)(2,1)S(1)}, u32[]{:S(2)}, u32[]{:S(2)}) collective-permute-start(bf16[80,640]{1,0:T(8,128)(2,1)S(1)} %fusion.23), channel_id=1, source_target_pairs={{0,3},{1,2},{2,1},{3,0},{4,7},{5,6},{6,5},{7,4},{8,11},{9,10},{10,... | collective-permute-start | bytes 307208 | tf_op jit(solution)/shard_map/ppermute | solution.py:316
  77.8 1.5 %collective-permute-done.12 = bf16[2,96,640]{2,1,0:T(8,128)(2,1)S(1)} collective-permute-done((bf16[2,96,640]{2,1,0:T(8,128)(2,1)S(1)}, bf16[2,96,640]{2,1,0:T(8,128)(2,1)S(1)}, u32[]{:S(2)}, u32[]{:S(2)}) %collective-permute-start.12) | collective-permute-done | bytes 245792 | tf_op jit(solution)/shard_map/ppermute | solution.py:316
  80.5 3.8 %collective-permute-done.13 = bf16[96,640]{1,0:T(8,128)(2,1)S(1)} collective-permute-done((bf16[96,640]{1,0:T(8,128)(2,1)S(1)}, bf16[96,640]{1,0:T(8,128)(2,1)S(1)}, u32[]{:S(2)}, u32[]{:S(2)}) %collective-permute-start.13) | collective-permute-done | bytes 122912 | tf_op jit(solution)/shard_map/ppermute | solution.py:316
  (51 shorter events, 12.6 us)
Async XLA Ops:
  1.7 1.4 %collective-permute-start = (bf16[1,528,128]{2,1,0:T(8,128)(2,1)S(1)}, bf16[1,528,128]{2,1,0:T(8,128)(2,1)S(1)}, u32[]{:S(2)}, u32[]{:S(2)}) collective-permute-start(bf16[1,528,128]{2,1,0:T(8,128)(2,1)S(1)} %maximum_bitcast_fusion.rest_0_), channel_id=1, source_target_pairs={{0,8},{8,0},{16,24},{24,16},{32,40},{40,32},{48,56},{56,48},{64,72... | collective-permute-start | bytes 405512 | tf_op jit(solution)/shard_map/ppermute | solution.py:48
  3.1 19.3 %collective-permute-start.2 = (bf16[1,528,128]{2,1,0:T(8,128)(2,1)S(1)}, bf16[1,528,128]{2,1,0:T(8,128)(2,1)S(1)}, u32[]{:S(2)}, u32[]{:S(2)}) collective-permute-start(bf16[1,528,128]{2,1,0:T(8,128)(2,1)S(1)} %maximum_bitcast_fusion.rest_0_), channel_id=1, source_target_pairs={{0,32},{8,40},{16,48},{24,56},{32,0},{40,8},{48,16},{56,24},{64,96... | collective-permute-start | bytes 405512 | tf_op jit(solution)/shard_map/ppermute | solution.py:48
  10.4 12.1 %collective-permute-start.4 = (bf16[2,528,128]{2,1,0:T(8,128)(2,1)S(1)}, bf16[2,528,128]{2,1,0:T(8,128)(2,1)S(1)}, u32[]{:S(2)}, u32[]{:S(2)}) collective-permute-start(bf16[2,528,128]{2,1,0:T(8,128)(2,1)S(1)} %constant_dynamic-update-slice_fusion), channel_id=1, source_target_pairs={{0,128},{8,136},{16,144},{24,152},{32,160},{40,168},{48,176},{56,1... | collective-permute-start | bytes 811016 | tf_op jit(solution)/shard_map/ppermute | solution.py:48
  11.7 10.8 %collective-permute-start.3 = (bf16[2,528,128]{2,1,0:T(8,128)(2,1)S(1)}, bf16[2,528,128]{2,1,0:T(8,128)(2,1)S(1)}, u32[]{:S(2)}, u32[]{:S(2)}) collective-permute-start(bf16[2,528,128]{2,1,0:T(8,128)(2,1)S(1)} %constant_dynamic-update-slice_fusion), channel_id=1, source_target_pairs={{0,64},{8,200},{16,80},{24,216},{32,96},{40,232},{48,112},{56,248}... | collective-permute-start | bytes 811016 | tf_op jit(solution)/shard_map/ppermute | solution.py:48
  13.0 11.5 %collective-permute-start.1 = (bf16[2,528,128]{2,1,0:T(8,128)(2,1)S(1)}, bf16[2,528,128]{2,1,0:T(8,128)(2,1)S(1)}, u32[]{:S(2)}, u32[]{:S(2)}) collective-permute-start(bf16[2,528,128]{2,1,0:T(8,128)(2,1)S(1)} %constant_dynamic-update-slice_fusion), channel_id=1, source_target_pairs={{0,16},{8,56},{16,32},{24,8},{32,48},{40,24},{48,0},{56,40},{64,80... | collective-permute-start | bytes 811016 | tf_op jit(solution)/shard_map/ppermute | solution.py:48
  24.5 13.5 %collective-permute-start.8 = (bf16[3,528,128]{2,1,0:T(8,128)(2,1)S(1)}, bf16[3,528,128]{2,1,0:T(8,128)(2,1)S(1)}, u32[]{:S(2)}, u32[]{:S(2)}) collective-permute-start(bf16[3,528,128]{2,1,0:T(8,128)(2,1)S(1)} %constant_dynamic-update-slice_fusion.2), channel_id=1, source_target_pairs={{0,64},{8,72},{16,80},{24,88},{32,96},{40,104},{48,112},{56,120},{... | collective-permute-start | bytes 1216520 | tf_op jit(solution)/shard_map/ppermute | solution.py:48
  25.8 19.2 %collective-permute-start.5 = (bf16[3,528,128]{2,1,0:T(8,128)(2,1)S(1)}, bf16[3,528,128]{2,1,0:T(8,128)(2,1)S(1)}, u32[]{:S(2)}, u32[]{:S(2)}) collective-permute-start(bf16[3,528,128]{2,1,0:T(8,128)(2,1)S(1)} %constant_dynamic-update-slice_fusion.2), channel_id=1, source_target_pairs={{0,192},{8,200},{16,208},{24,216},{32,224},{40,232},{48,240},{56,2... | collective-permute-start | bytes 1216520 | tf_op jit(solution)/shard_map/ppermute | solution.py:48
  27.1 5.1 %collective-permute-start.9 = (bf16[640,256]{1,0:T(8,128)(2,1)S(1)}, bf16[640,256]{1,0:T(8,128)(2,1)S(1)}, u32[]{:S(2)}, u32[]{:S(2)}) collective-permute-start(bf16[640,256]{1,0:T(8,128)(2,1)S(1)} %pad_maximum_fusion.rest_5_.rest_1_.rest_2_), channel_id=1, source_target_pairs={{0,8},{8,0},{16,24},{24,16},{32,40},{40,32},{48,56},{56,48},{64,72... | collective-permute-start | bytes 983048 | tf_op jit(solution)/shard_map/ppermute | solution.py:48
  27.5 14.1 %collective-permute-start.6 = (bf16[2,528,128]{2,1,0:T(8,128)(2,1)S(1)}, bf16[2,528,128]{2,1,0:T(8,128)(2,1)S(1)}, u32[]{:S(2)}, u32[]{:S(2)}) collective-permute-start(bf16[2,528,128]{2,1,0:T(8,128)(2,1)S(1)} %collective-permute-done.4.rest_4_), channel_id=1, source_target_pairs={{128,144},{136,184},{144,160},{152,136},{160,176},{168,152},{176,1... | collective-permute-start | bytes 811016 | tf_op jit(solution)/shard_map/ppermute | solution.py:48
  30.9 10.7 %collective-permute-start.7 = (bf16[1,528,128]{2,1,0:T(8,128)(2,1)S(1)}, bf16[1,528,128]{2,1,0:T(8,128)(2,1)S(1)}, u32[]{:S(2)}, u32[]{:S(2)}) collective-permute-start(bf16[1,528,128]{2,1,0:T(8,128)(2,1)S(1)} %collective-permute-done.2.rest_2_), channel_id=1, source_target_pairs={{0,128},{8,136},{16,144},{24,152},{32,160},{40,168},{48,176},{56,1... | collective-permute-start | bytes 405512 | tf_op jit(solution)/shard_map/ppermute | solution.py:48
  47.0 3.1 %collective-permute-start.10 = (f32[528,256]{1,0:T(8,128)S(1)}, f32[528,256]{1,0:T(8,128)S(1)}, u32[]{:S(2)}, u32[]{:S(2)}) collective-permute-start(f32[528,256]{1,0:T(8,128)S(1)} %attend_rest_other.1), channel_id=1, source_target_pairs={{0,8},{8,0},{16,24},{24,16},{32,40},{40,32},{48,56},{56,48},{64,72... | collective-permute-start | bytes 1622024 | tf_op jit(solution)/shard_map/ppermute | solution.py:48
  52.7 13.4 %collective-permute-start.14 = (bf16[4,80,640]{2,1,0:T(8,128)(2,1)S(1)}, bf16[4,80,640]{2,1,0:T(8,128)(2,1)S(1)}, u32[]{:S(2)}, u32[]{:S(2)}) collective-permute-start(bf16[4,80,640]{2,1,0:T(8,128)(2,1)S(1)} %get-tuple-element.70), channel_id=1, source_target_pairs={{0,3},{1,2},{2,1},{3,0},{4,7},{5,6},{6,5},{7,4},{8,11},{9,10},{10,... | collective-permute-start | bytes 1228808 | tf_op jit(solution)/shard_map/ppermute | solution.py:316
  55.8 11.6 %collective-permute-start.17 = (bf16[4,80,640]{2,1,0:T(8,128)(2,1)S(1)}, bf16[4,80,640]{2,1,0:T(8,128)(2,1)S(1)}, u32[]{:S(2)}, u32[]{:S(2)}) collective-permute-start(bf16[4,80,640]{2,1,0:T(8,128)(2,1)S(1)} %get-tuple-element.72), channel_id=1, source_target_pairs={{0,4},{1,5},{2,6},{3,7},{4,0},{5,1},{6,2},{7,3},{8,12},{9,13},{10,... | collective-permute-start | bytes 1228808 | tf_op jit(solution)/shard_map/ppermute | solution.py:316
  56.8 13.3 %collective-permute-start.11 = (bf16[4,96,640]{2,1,0:T(8,128)(2,1)S(1)}, bf16[4,96,640]{2,1,0:T(8,128)(2,1)S(1)}, u32[]{:S(2)}, u32[]{:S(2)}) collective-permute-start(bf16[4,96,640]{2,1,0:T(8,128)(2,1)S(1)} %get-tuple-element.68), channel_id=1, source_target_pairs={{0,1},{1,0},{2,3},{3,2},{4,5},{5,4},{6,7},{7,6},{8,9},{9,8},{10,11... | collective-permute-start | bytes 1474568 | tf_op jit(solution)/shard_map/ppermute | solution.py:316
  66.2 6.8 %collective-permute-start.15 = (bf16[2,80,640]{2,1,0:T(8,128)(2,1)S(1)}, bf16[2,80,640]{2,1,0:T(8,128)(2,1)S(1)}, u32[]{:S(2)}, u32[]{:S(2)}) collective-permute-start(bf16[2,80,640]{2,1,0:T(8,128)(2,1)S(1)} %slice.98), channel_id=1, source_target_pairs={{0,4},{1,5},{2,6},{3,7},{4,0},{5,1},{6,2},{7,3},{8,12},{9,13},{10,... | collective-permute-start | bytes 614408 | tf_op jit(solution)/shard_map/ppermute | solution.py:316
  67.5 6.7 %collective-permute-start.18 = (bf16[2,80,640]{2,1,0:T(8,128)(2,1)S(1)}, bf16[2,80,640]{2,1,0:T(8,128)(2,1)S(1)}, u32[]{:S(2)}, u32[]{:S(2)}) collective-permute-start(bf16[2,80,640]{2,1,0:T(8,128)(2,1)S(1)} %slice.97), channel_id=1, source_target_pairs={{0,1},{1,0},{2,3},{3,2},{4,5},{5,4},{6,7},{7,6},{8,9},{9,8},{10,11... | collective-permute-start | bytes 614408 | tf_op jit(solution)/shard_map/ppermute | solution.py:316
  70.2 9.1 %collective-permute-start.12 = (bf16[2,96,640]{2,1,0:T(8,128)(2,1)S(1)}, bf16[2,96,640]{2,1,0:T(8,128)(2,1)S(1)}, u32[]{:S(2)}, u32[]{:S(2)}) collective-permute-start(bf16[2,96,640]{2,1,0:T(8,128)(2,1)S(1)} %slice.96), channel_id=1, source_target_pairs={{0,3},{1,2},{2,1},{3,0},{4,7},{5,6},{6,5},{7,4},{8,11},{9,10},{10,... | collective-permute-start | bytes 737288 | tf_op jit(solution)/shard_map/ppermute | solution.py:316
  73.1 4.7 %collective-permute-start.16 = (bf16[80,640]{1,0:T(8,128)(2,1)S(1)}, bf16[80,640]{1,0:T(8,128)(2,1)S(1)}, u32[]{:S(2)}, u32[]{:S(2)}) collective-permute-start(bf16[80,640]{1,0:T(8,128)(2,1)S(1)} %fusion.22), channel_id=1, source_target_pairs={{0,1},{1,0},{2,3},{3,2},{4,5},{5,4},{6,7},{7,6},{8,9},{9,8},{10,11... | collective-permute-start | bytes 307208 | tf_op jit(solution)/shard_map/ppermute | solution.py:316
  74.3 6.2 %collective-permute-start.19 = (bf16[80,640]{1,0:T(8,128)(2,1)S(1)}, bf16[80,640]{1,0:T(8,128)(2,1)S(1)}, u32[]{:S(2)}, u32[]{:S(2)}) collective-permute-start(bf16[80,640]{1,0:T(8,128)(2,1)S(1)} %fusion.23), channel_id=1, source_target_pairs={{0,3},{1,2},{2,1},{3,0},{4,7},{5,6},{6,5},{7,4},{8,11},{9,10},{10,... | collective-permute-start | bytes 307208 | tf_op jit(solution)/shard_map/ppermute | solution.py:316
  79.4 5.0 %collective-permute-start.13 = (bf16[96,640]{1,0:T(8,128)(2,1)S(1)}, bf16[96,640]{1,0:T(8,128)(2,1)S(1)}, u32[]{:S(2)}, u32[]{:S(2)}) collective-permute-start(bf16[96,640]{1,0:T(8,128)(2,1)S(1)} %fusion.21), channel_id=1, source_target_pairs={{0,4},{1,5},{2,6},{3,7},{4,0},{5,1},{6,2},{7,3},{8,12},{9,13},{10,... | collective-permute-start | bytes 368648 | tf_op jit(solution)/shard_map/ppermute | solution.py:316

commit v14 on v13

--- a/solution.py
+++ b/solution.py
@@ -181,10 +181,11 @@
 
 
 def more_and_fetch_kernel(slots, n, others, at_ref, *rest):
-    w_hbm, s_ref, w_ref, all_ref, order_ref, sem = rest[n + 2 :]
+    given = n + 2 * len(others)
+    w_hbm, (w_ref, all_ref, order_ref, sem) = rest[given], rest[-4:]
     copy = pltpu.make_async_copy(w_hbm, w_ref, sem)
     copy.start()
-    more_kernel(slots, n, others, at_ref, *rest[: n + 2], s_ref, all_ref, order_ref)
+    more_kernel(slots, n, others, at_ref, *rest[:given], *rest[given + 1 : -4], all_ref, order_ref)
     copy.wait()
 
 
@@ -276,17 +277,11 @@
     near = functools.partial(more_kernel, up_slots, 1, (0, 1))
     state, state_2 = attend(near, 3, [up], (q, q_2), (state, state_2), "attend_up")
     fars, state, state_2 = lax.optimization_barrier(((far_near, far_far), state, state_2))
-    far = functools.partial(more_kernel, far_slots, 2, (0, 1))
-    state, state_2 = attend(far, 3, fars, (q, q_2), (state, state_2), "attend_far")
-    pieces, state, state_2 = lax.optimization_barrier(((around,), state, state_2))
-    rest = functools.partial(more_kernel, rest_slots, len(pieces), (1,))
-    (state_2,) = attend(rest, 3, pieces, (q_2,), (state_2,), "attend_rest_other")
-    state_2, state = lax.optimization_barrier((state_2, state))
-    state, w_held = pl.pallas_call(
-        functools.partial(more_and_fetch_kernel, rest_slots, len(pieces), (0,)),
-        out_shape=(STATE, jax.ShapeDtypeStruct(w_out.shape, BF16)),
-        in_specs=[SMEM] + [VMEM] * (len(pieces) + 2) + [pl.BlockSpec(memory_space=pltpu.HBM)],
-        out_specs=(VMEM,) * 2,
+    state, state_2, w_held = pl.pallas_call(
+        functools.partial(more_and_fetch_kernel, far_slots, 2, (0, 1)),
+        out_shape=(STATE, STATE, jax.ShapeDtypeStruct(w_out.shape, BF16)),
+        in_specs=[SMEM] + [VMEM] * 6 + [pl.BlockSpec(memory_space=pltpu.HBM)],
+        out_specs=(VMEM,) * 3,
         scratch_shapes=[
             pltpu.VMEM((3, PACK, HEAD_DIM), BF16),
             pltpu.SMEM((16,), jnp.int32),
@@ -294,8 +289,14 @@
         ],
         compiler_params=pltpu.CompilerParams(vmem_limit_bytes=LAST_LIMIT * 1024 * 1024),
         cost_estimate=cost(1),
-        name="attend_rest_own",
-    )(at, *pieces, q, state, w_out)
+        name="attend_far",
+    )(at, *fars, q, q_2, state, state_2, w_out)
+    pieces, state, state_2 = lax.optimization_barrier(((around,), state, state_2))
+    rest = functools.partial(more_kernel, rest_slots, len(pieces), (1,))
+    (state_2,) = attend(rest, 3, pieces, (q_2,), (state_2,), "attend_rest_other")
+    state_2, state = lax.optimization_barrier((state_2, state))
+    rest = functools.partial(more_kernel, rest_slots, len(pieces), (0,))
+    (state,) = attend(rest, 3, pieces, (q,), (state,), "attend_rest_own")
     state_2 = swap_cores(state_2)
 
     out_shape = []

time: 85.6 us -> 84.4 us (0.986)
  Pallas kernels: 19.2 us -> 18.1 us
    pallas_call x4, Pallas kernels: 13.6 us -> 12.2 us  [attend(): pl.pallas_call(kernel, out_shape=out_shape, in_specs=[SMEM] + [VMEM] * (l...]
  transfers between devices with their start and end apart: 20 -> 20, of which waited for: 11 -> 10; matrix products, arithmetic and copies ran while one was open for 11% -> 11% of each run, Pallas kernels for 17% -> 16%
where the time goes in v14:
time: 84.4 us; the launch traced here: 84.1 us
  starting transfers between devices  29.2 us (35%)
  waiting for transfers between devices  24.7 us (29%)
  Pallas kernels  18.1 us (21%)
  other arithmetic  6.06 us (7%)
  matrix products  5.58 us (7%)
    ppermute x9, waiting for transfers between devices, exchange(): return lax.ppermute(x, 'section', [(i, i ^ step) for i in range(8)])  20.9 us
    ppermute x11, starting transfers between devices, move(): return lax.ppermute(x, 'ctx', ctx_pairs(step))  19.1 us
    pallas_call x4, Pallas kernels, attend(): pl.pallas_call(kernel, out_shape=out_shape, in_specs=[SMEM] + [VMEM] * (l...  12.2 us
    ppermute x9, starting transfers between devices, exchange(): return lax.ppermute(x, 'section', [(i, i ^ step) for i in range(8)])  10.1 us
    dot_general x1, matrix products, per_device(): lax.dot_general(w_query, normed, (((0,), (1,)), ((), ())), preferred_elem...  5.58 us
    ppermute x11, waiting for transfers between devices, move(): return lax.ppermute(x, 'ctx', ctx_pairs(step))  3.74 us
    pallas_call x1, Pallas kernels, per_device(): pl.pallas_call(functools.partial(more_and_fetch_kernel, far_slots, 2, (0,...  3.43 us
    pallas_call x1, Pallas kernels, per_device(): pl.pallas_call(last_kernel, out_shape=tuple(out_shape), in_specs=[SMEM, V...  2.49 us
  transfers between devices with their start and end apart: 20, of which 10 were waited for; matrix products, arithmetic and copies ran while one was open for 11% of the time, Pallas kernels for 16%

profile of v14, /device:TPU:24, one launch (start us, length us, event | category | flops | bytes accessed | tf_op | source)
XLA Modules:
  0.0 84.1 jit_solution(8279563254363675850)
XLA Ops:
  3.1 7.2 %collective-permute-start.2 = (bf16[1,528,128]{2,1,0:T(8,128)(2,1)S(1)}, bf16[1,528,128]{2,1,0:T(8,128)(2,1)S(1)}, u32[]{:S(2)}, u32[]{:S(2)}) collective-permute-start(bf16[1,528,128]{2,1,0:T(8,128)(2,1)S(1)} %maximum_bitcast_fusion.rest_0_), channel_id=1, source_target_pairs={{0,32},{8,40},{16,48},{24,56},{32,0},{40,8},{48,16},{56,24},{64,96... | collective-permute-start | bytes 405512 | tf_op jit(solution)/shard_map/ppermute | solution.py:48
  10.4 1.3 %collective-permute-start.4 = (bf16[2,528,128]{2,1,0:T(8,128)(2,1)S(1)}, bf16[2,528,128]{2,1,0:T(8,128)(2,1)S(1)}, u32[]{:S(2)}, u32[]{:S(2)}) collective-permute-start(bf16[2,528,128]{2,1,0:T(8,128)(2,1)S(1)} %constant_dynamic-update-slice_fusion), channel_id=1, source_target_pairs={{0,128},{8,136},{16,144},{24,152},{32,160},{40,168},{48,176},{56,1... | collective-permute-start | bytes 811016 | tf_op jit(solution)/shard_map/ppermute | solution.py:48
  11.7 1.3 %collective-permute-start.3 = (bf16[2,528,128]{2,1,0:T(8,128)(2,1)S(1)}, bf16[2,528,128]{2,1,0:T(8,128)(2,1)S(1)}, u32[]{:S(2)}, u32[]{:S(2)}) collective-permute-start(bf16[2,528,128]{2,1,0:T(8,128)(2,1)S(1)} %constant_dynamic-update-slice_fusion), channel_id=1, source_target_pairs={{0,64},{8,200},{16,80},{24,216},{32,96},{40,232},{48,112},{56,248}... | collective-permute-start | bytes 811016 | tf_op jit(solution)/shard_map/ppermute | solution.py:48
  13.0 1.5 %collective-permute-start.1 = (bf16[2,528,128]{2,1,0:T(8,128)(2,1)S(1)}, bf16[2,528,128]{2,1,0:T(8,128)(2,1)S(1)}, u32[]{:S(2)}, u32[]{:S(2)}) collective-permute-start(bf16[2,528,128]{2,1,0:T(8,128)(2,1)S(1)} %constant_dynamic-update-slice_fusion), channel_id=1, source_target_pairs={{0,16},{8,56},{16,32},{24,8},{32,48},{40,24},{48,0},{56,40},{64,80... | collective-permute-start | bytes 811016 | tf_op jit(solution)/shard_map/ppermute | solution.py:48
  14.5 2.3 %fusion = f32[256]{0:T(256)S(1)} fusion(bf16[256,5120]{1,0:T(8,128)(2,1)} %param.6), kind=kLoop, calls=%fused_computation.2 | loop fusion | flops 3931904 | bytes 2622464 | tf_op jit(solution)/shard_map/reduce_sum | solution.py:243
  16.9 5.6 %fusion.11 = bf16[512,256]{1,0:T(8,128)(2,1)S(1)} fusion(bf16[5120,512]{1,0:T(8,128)(2,1)} %param.10, bf16[256,5120]{1,0:T(8,128)(2,1)} %param.6, f32[256]{0:T(256)S(1)} %add_rsqrt_fusion), kind=kOutput, calls=%fused_computation.8 | convolution fusion | flops 1346371584 | bytes 8127488 | tf_op jit(solution)/shard_map/dot_general | solution.py:245
  22.5 1.9 %collective-permute-done.1.rest_1_ = bf16[2,528,128]{2,1,0:T(8,128)(2,1)S(1)} collective-permute-done((bf16[2,528,128]{2,1,0:T(8,128)(2,1)S(1)}, bf16[2,528,128]{2,1,0:T(8,128)(2,1)S(1)}, u32[]{:S(2)}, u32[]{:S(2)}) %collective-permute-start.1) | collective-permute-done | bytes 270368 | tf_op jit(solution)/shard_map/ppermute | solution.py:48
  24.5 1.3 %collective-permute-start.8 = (bf16[3,528,128]{2,1,0:T(8,128)(2,1)S(1)}, bf16[3,528,128]{2,1,0:T(8,128)(2,1)S(1)}, u32[]{:S(2)}, u32[]{:S(2)}) collective-permute-start(bf16[3,528,128]{2,1,0:T(8,128)(2,1)S(1)} %constant_dynamic-update-slice_fusion.2), channel_id=1, source_target_pairs={{0,64},{8,72},{16,80},{24,88},{32,96},{40,104},{48,112},{56,120},{... | collective-permute-start | bytes 1216520 | tf_op jit(solution)/shard_map/ppermute | solution.py:48
  25.8 1.3 %collective-permute-start.5 = (bf16[3,528,128]{2,1,0:T(8,128)(2,1)S(1)}, bf16[3,528,128]{2,1,0:T(8,128)(2,1)S(1)}, u32[]{:S(2)}, u32[]{:S(2)}) collective-permute-start(bf16[3,528,128]{2,1,0:T(8,128)(2,1)S(1)} %constant_dynamic-update-slice_fusion.2), channel_id=1, source_target_pairs={{0,192},{8,200},{16,208},{24,216},{32,224},{40,232},{48,240},{56,2... | collective-permute-start | bytes 1216520 | tf_op jit(solution)/shard_map/ppermute | solution.py:48
  27.5 3.4 %collective-permute-start.6 = (bf16[2,528,128]{2,1,0:T(8,128)(2,1)S(1)}, bf16[2,528,128]{2,1,0:T(8,128)(2,1)S(1)}, u32[]{:S(2)}, u32[]{:S(2)}) collective-permute-start(bf16[2,528,128]{2,1,0:T(8,128)(2,1)S(1)} %collective-permute-done.4.rest_4_), channel_id=1, source_target_pairs={{128,144},{136,184},{144,160},{152,136},{160,176},{168,152},{176,1... | collective-permute-start | bytes 811016 | tf_op jit(solution)/shard_map/ppermute | solution.py:48
  30.9 1.3 %collective-permute-start.7 = (bf16[1,528,128]{2,1,0:T(8,128)(2,1)S(1)}, bf16[1,528,128]{2,1,0:T(8,128)(2,1)S(1)}, u32[]{:S(2)}, u32[]{:S(2)}) collective-permute-start(bf16[1,528,128]{2,1,0:T(8,128)(2,1)S(1)} %collective-permute-done.2.rest_2_), channel_id=1, source_target_pairs={{0,128},{8,136},{16,144},{24,152},{32,160},{40,168},{48,176},{56,1... | collective-permute-start | bytes 405512 | tf_op jit(solution)/shard_map/ppermute | solution.py:48
  32.2 4.6 %attend_first.1 = (f32[528,256]{1,0:T(8,128)S(1)}, f32[528,256]{1,0:T(8,128)S(1)}) custom-call(s32[2]{0:T(128)S(1)} %pad_add_fusion.at_ref, bf16[1,528,128]{2,1,0:T(8,128)(2,1)S(1)} %maximum_bitcast_fusion.rest_0_, bf16[2,528,128]{2,1,0:T(8,128)(2,1)S(1)} %collective-permute-done.1.rest_1_, bf16[1,528,128]{2,1,0:T(8,128)(2,1)S(1)} %collective-permute-done.2.rest_2_, ...), custom_call_target="tpu_custom_call" | custom-call | flops 134217728 | bytes 135168 | tf_op jit(solution)/shard_map/attend_first/pallas_call | solution.py:262
  38.0 3.6 %attend_up.1 = (f32[528,256]{1,0:T(8,128)S(1)}, f32[528,256]{1,0:T(8,128)S(1)}) custom-call(s32[2]{0:T(128)S(1)} %pad_add_fusion.at_ref, bf16[3,528,128]{2,1,0:T(8,128)(2,1)S(1)} %collective-permute-done.8.rest_0_, bf16[640,256]{1,0:T(8,128)(2,1)S(1)} %pad_maximum_fusion.rest_5_.rest_1_.rest_2_, ...), custom_call_target="tpu_custom_call" | custom-call | flops 134217728 | bytes 135168 | tf_op jit(solution)/shard_map/attend_up/pallas_call | solution.py:262
  41.6 3.4 %attend_far.1 = (f32[528,256]{1,0:T(8,128)S(1)}, f32[528,256]{1,0:T(8,128)S(1)}, bf16[512,5120]{1,0:T(8,128)(2,1)S(1)}) custom-call(s32[2]{0:T(128)S(1)} %pad_add_fusion.at_ref, bf16[2,528,128]{2,1,0:T(8,128)(2,1)S(1)} %collective-permute-done.6.rest_0_, bf16[1,528,128]{2,1,0:T(8,128)(2,1)S(1)} %collective-permute-done.7.rest_1_, ...), custom_call_target="tpu_custom_call" | custom-call | flops 134217728 | bytes 135168 | tf_op jit(solution)/shard_map/attend_far/pallas_call | solution.py:280
  45.0 2.0 %attend_rest_other.1 = f32[528,256]{1,0:T(8,128)S(1)} custom-call(s32[2]{0:T(128)S(1)} %pad_add_fusion.at_ref, bf16[3,528,128]{2,1,0:T(8,128)(2,1)S(1)} %collective-permute-done.5.rest_0_, bf16[640,256]{1,0:T(8,128)(2,1)S(1)} %collective-permute-done.9.rest_6_.rest_2_.rest_3_.rest_1_, f32[528,256]{1,0:T(8,128)S(1)} %get-tuple-element.60.rest_2_), custom_call_target="tpu_custom_call" | custom-call | flops 134217728 | bytes 135168 | tf_op jit(solution)/shard_map/attend_rest_other/pallas_call | solution.py:262
  47.1 2.0 %attend_rest_own.1.s_ref = f32[528,256]{1,0:T(8,128)S(1)} custom-call(s32[2]{0:T(128)S(1)} %pad_add_fusion.at_ref, bf16[3,528,128]{2,1,0:T(8,128)(2,1)S(1)} %collective-permute-done.5.rest_0_, bf16[640,256]{1,0:T(8,128)(2,1)S(1)} %pad_maximum_fusion.rest_5_.rest_1_.rest_2_, f32[528,256]{1,0:T(8,128)S(1)} %get-tuple-element.62.rest_2_), custom_call_target="tpu_custom_call" | custom-call | flops 134217728 | bytes 135168 | tf_op jit(solution)/shard_map/attend_rest_own/pallas_call | solution.py:262
  49.2 2.5 %project_attended.1 = (bf16[4,96,640]{2,1,0:T(8,128)(2,1)S(1)}, bf16[4,96,640]{2,1,0:T(8,128)(2,1)S(1)}, bf16[4,80,640]{2,1,0:T(8,128)(2,1)S(1)}, bf16[4,80,640]...) custom-call(s32[2]{0:T(128)S(1)} %pad_add_fusion.at_ref, ...), custom_call_target="tpu_custom_call" | custom-call | flops 1610612736 | bytes 1622016 | tf_op jit(solution)/shard_map/project_attended/pallas_call | solution.py:305
  51.7 3.1 %collective-permute-start.14 = (bf16[4,80,640]{2,1,0:T(8,128)(2,1)S(1)}, bf16[4,80,640]{2,1,0:T(8,128)(2,1)S(1)}, u32[]{:S(2)}, u32[]{:S(2)}) collective-permute-start(bf16[4,80,640]{2,1,0:T(8,128)(2,1)S(1)} %get-tuple-element.68), channel_id=1, source_target_pairs={{0,3},{1,2},{2,1},{3,0},{4,7},{5,6},{6,5},{7,4},{8,11},{9,10},{10,... | collective-permute-start | bytes 1228808 | tf_op jit(solution)/shard_map/ppermute | solution.py:317
  56.0 9.1 %collective-permute-done.14 = bf16[4,80,640]{2,1,0:T(8,128)(2,1)S(1)} collective-permute-done((bf16[4,80,640]{2,1,0:T(8,128)(2,1)S(1)}, bf16[4,80,640]{2,1,0:T(8,128)(2,1)S(1)}, u32[]{:S(2)}, u32[]{:S(2)}) %collective-permute-start.14) | collective-permute-done | bytes 409632 | tf_op jit(solution)/shard_map/ppermute | solution.py:317
  66.8 2.3 %collective-permute-done.11 = bf16[4,96,640]{2,1,0:T(8,128)(2,1)S(1)} collective-permute-done((bf16[4,96,640]{2,1,0:T(8,128)(2,1)S(1)}, bf16[4,96,640]{2,1,0:T(8,128)(2,1)S(1)}, u32[]{:S(2)}, u32[]{:S(2)}) %collective-permute-start.11) | collective-permute-done | bytes 491552 | tf_op jit(solution)/shard_map/ppermute | solution.py:317
  69.5 2.4 %collective-permute-done.15 = bf16[2,80,640]{2,1,0:T(8,128)(2,1)S(1)} collective-permute-done((bf16[2,80,640]{2,1,0:T(8,128)(2,1)S(1)}, bf16[2,80,640]{2,1,0:T(8,128)(2,1)S(1)}, u32[]{:S(2)}, u32[]{:S(2)}) %collective-permute-start.15) | collective-permute-done | bytes 204832 | tf_op jit(solution)/shard_map/ppermute | solution.py:317
  73.3 2.5 %collective-permute-start.19 = (bf16[80,640]{1,0:T(8,128)(2,1)S(1)}, bf16[80,640]{1,0:T(8,128)(2,1)S(1)}, u32[]{:S(2)}, u32[]{:S(2)}) collective-permute-start(bf16[80,640]{1,0:T(8,128)(2,1)S(1)} %fusion.23), channel_id=1, source_target_pairs={{0,3},{1,2},{2,1},{3,0},{4,7},{5,6},{6,5},{7,4},{8,11},{9,10},{10,... | collective-permute-start | bytes 307208 | tf_op jit(solution)/shard_map/ppermute | solution.py:317
  76.8 1.5 %collective-permute-done.12 = bf16[2,96,640]{2,1,0:T(8,128)(2,1)S(1)} collective-permute-done((bf16[2,96,640]{2,1,0:T(8,128)(2,1)S(1)}, bf16[2,96,640]{2,1,0:T(8,128)(2,1)S(1)}, u32[]{:S(2)}, u32[]{:S(2)}) %collective-permute-start.12) | collective-permute-done | bytes 245792 | tf_op jit(solution)/shard_map/ppermute | solution.py:317
  79.5 3.8 %collective-permute-done.13 = bf16[96,640]{1,0:T(8,128)(2,1)S(1)} collective-permute-done((bf16[96,640]{1,0:T(8,128)(2,1)S(1)}, bf16[96,640]{1,0:T(8,128)(2,1)S(1)}, u32[]{:S(2)}, u32[]{:S(2)}) %collective-permute-start.13) | collective-permute-done | bytes 122912 | tf_op jit(solution)/shard_map/ppermute | solution.py:317
  (51 shorter events, 12.6 us)
Async XLA Ops:
  1.7 1.4 %collective-permute-start = (bf16[1,528,128]{2,1,0:T(8,128)(2,1)S(1)}, bf16[1,528,128]{2,1,0:T(8,128)(2,1)S(1)}, u32[]{:S(2)}, u32[]{:S(2)}) collective-permute-start(bf16[1,528,128]{2,1,0:T(8,128)(2,1)S(1)} %maximum_bitcast_fusion.rest_0_), channel_id=1, source_target_pairs={{0,8},{8,0},{16,24},{24,16},{32,40},{40,32},{48,56},{56,48},{64,72... | collective-permute-start | bytes 405512 | tf_op jit(solution)/shard_map/ppermute | solution.py:48
  3.1 19.3 %collective-permute-start.2 = (bf16[1,528,128]{2,1,0:T(8,128)(2,1)S(1)}, bf16[1,528,128]{2,1,0:T(8,128)(2,1)S(1)}, u32[]{:S(2)}, u32[]{:S(2)}) collective-permute-start(bf16[1,528,128]{2,1,0:T(8,128)(2,1)S(1)} %maximum_bitcast_fusion.rest_0_), channel_id=1, source_target_pairs={{0,32},{8,40},{16,48},{24,56},{32,0},{40,8},{48,16},{56,24},{64,96... | collective-permute-start | bytes 405512 | tf_op jit(solution)/shard_map/ppermute | solution.py:48
  10.4 12.1 %collective-permute-start.4 = (bf16[2,528,128]{2,1,0:T(8,128)(2,1)S(1)}, bf16[2,528,128]{2,1,0:T(8,128)(2,1)S(1)}, u32[]{:S(2)}, u32[]{:S(2)}) collective-permute-start(bf16[2,528,128]{2,1,0:T(8,128)(2,1)S(1)} %constant_dynamic-update-slice_fusion), channel_id=1, source_target_pairs={{0,128},{8,136},{16,144},{24,152},{32,160},{40,168},{48,176},{56,1... | collective-permute-start | bytes 811016 | tf_op jit(solution)/shard_map/ppermute | solution.py:48
  11.7 10.8 %collective-permute-start.3 = (bf16[2,528,128]{2,1,0:T(8,128)(2,1)S(1)}, bf16[2,528,128]{2,1,0:T(8,128)(2,1)S(1)}, u32[]{:S(2)}, u32[]{:S(2)}) collective-permute-start(bf16[2,528,128]{2,1,0:T(8,128)(2,1)S(1)} %constant_dynamic-update-slice_fusion), channel_id=1, source_target_pairs={{0,64},{8,200},{16,80},{24,216},{32,96},{40,232},{48,112},{56,248}... | collective-permute-start | bytes 811016 | tf_op jit(solution)/shard_map/ppermute | solution.py:48
  13.0 11.5 %collective-permute-start.1 = (bf16[2,528,128]{2,1,0:T(8,128)(2,1)S(1)}, bf16[2,528,128]{2,1,0:T(8,128)(2,1)S(1)}, u32[]{:S(2)}, u32[]{:S(2)}) collective-permute-start(bf16[2,528,128]{2,1,0:T(8,128)(2,1)S(1)} %constant_dynamic-update-slice_fusion), channel_id=1, source_target_pairs={{0,16},{8,56},{16,32},{24,8},{32,48},{40,24},{48,0},{56,40},{64,80... | collective-permute-start | bytes 811016 | tf_op jit(solution)/shard_map/ppermute | solution.py:48
  24.5 13.5 %collective-permute-start.8 = (bf16[3,528,128]{2,1,0:T(8,128)(2,1)S(1)}, bf16[3,528,128]{2,1,0:T(8,128)(2,1)S(1)}, u32[]{:S(2)}, u32[]{:S(2)}) collective-permute-start(bf16[3,528,128]{2,1,0:T(8,128)(2,1)S(1)} %constant_dynamic-update-slice_fusion.2), channel_id=1, source_target_pairs={{0,64},{8,72},{16,80},{24,88},{32,96},{40,104},{48,112},{56,120},{... | collective-permute-start | bytes 1216520 | tf_op jit(solution)/shard_map/ppermute | solution.py:48
  25.8 19.2 %collective-permute-start.5 = (bf16[3,528,128]{2,1,0:T(8,128)(2,1)S(1)}, bf16[3,528,128]{2,1,0:T(8,128)(2,1)S(1)}, u32[]{:S(2)}, u32[]{:S(2)}) collective-permute-start(bf16[3,528,128]{2,1,0:T(8,128)(2,1)S(1)} %constant_dynamic-update-slice_fusion.2), channel_id=1, source_target_pairs={{0,192},{8,200},{16,208},{24,216},{32,224},{40,232},{48,240},{56,2... | collective-permute-start | bytes 1216520 | tf_op jit(solution)/shard_map/ppermute | solution.py:48
  27.1 5.1 %collective-permute-start.9 = (bf16[640,256]{1,0:T(8,128)(2,1)S(1)}, bf16[640,256]{1,0:T(8,128)(2,1)S(1)}, u32[]{:S(2)}, u32[]{:S(2)}) collective-permute-start(bf16[640,256]{1,0:T(8,128)(2,1)S(1)} %pad_maximum_fusion.rest_5_.rest_1_.rest_2_), channel_id=1, source_target_pairs={{0,8},{8,0},{16,24},{24,16},{32,40},{40,32},{48,56},{56,48},{64,72... | collective-permute-start | bytes 983048 | tf_op jit(solution)/shard_map/ppermute | solution.py:48
  27.5 14.1 %collective-permute-start.6 = (bf16[2,528,128]{2,1,0:T(8,128)(2,1)S(1)}, bf16[2,528,128]{2,1,0:T(8,128)(2,1)S(1)}, u32[]{:S(2)}, u32[]{:S(2)}) collective-permute-start(bf16[2,528,128]{2,1,0:T(8,128)(2,1)S(1)} %collective-permute-done.4.rest_4_), channel_id=1, source_target_pairs={{128,144},{136,184},{144,160},{152,136},{160,176},{168,152},{176,1... | collective-permute-start | bytes 811016 | tf_op jit(solution)/shard_map/ppermute | solution.py:48
  30.9 10.7 %collective-permute-start.7 = (bf16[1,528,128]{2,1,0:T(8,128)(2,1)S(1)}, bf16[1,528,128]{2,1,0:T(8,128)(2,1)S(1)}, u32[]{:S(2)}, u32[]{:S(2)}) collective-permute-start(bf16[1,528,128]{2,1,0:T(8,128)(2,1)S(1)} %collective-permute-done.2.rest_2_), channel_id=1, source_target_pairs={{0,128},{8,136},{16,144},{24,152},{32,160},{40,168},{48,176},{56,1... | collective-permute-start | bytes 405512 | tf_op jit(solution)/shard_map/ppermute | solution.py:48
  47.0 2.1 %collective-permute-start.10 = (f32[528,256]{1,0:T(8,128)S(1)}, f32[528,256]{1,0:T(8,128)S(1)}, u32[]{:S(2)}, u32[]{:S(2)}) collective-permute-start(f32[528,256]{1,0:T(8,128)S(1)} %attend_rest_other.1), channel_id=1, source_target_pairs={{0,8},{8,0},{16,24},{24,16},{32,40},{40,32},{48,56},{56,48},{64,72... | collective-permute-start | bytes 1622024 | tf_op jit(solution)/shard_map/ppermute | solution.py:48
  51.7 13.4 %collective-permute-start.14 = (bf16[4,80,640]{2,1,0:T(8,128)(2,1)S(1)}, bf16[4,80,640]{2,1,0:T(8,128)(2,1)S(1)}, u32[]{:S(2)}, u32[]{:S(2)}) collective-permute-start(bf16[4,80,640]{2,1,0:T(8,128)(2,1)S(1)} %get-tuple-element.68), channel_id=1, source_target_pairs={{0,3},{1,2},{2,1},{3,0},{4,7},{5,6},{6,5},{7,4},{8,11},{9,10},{10,... | collective-permute-start | bytes 1228808 | tf_op jit(solution)/shard_map/ppermute | solution.py:317
  54.7 11.6 %collective-permute-start.17 = (bf16[4,80,640]{2,1,0:T(8,128)(2,1)S(1)}, bf16[4,80,640]{2,1,0:T(8,128)(2,1)S(1)}, u32[]{:S(2)}, u32[]{:S(2)}) collective-permute-start(bf16[4,80,640]{2,1,0:T(8,128)(2,1)S(1)} %get-tuple-element.70), channel_id=1, source_target_pairs={{0,4},{1,5},{2,6},{3,7},{4,0},{5,1},{6,2},{7,3},{8,12},{9,13},{10,... | collective-permute-start | bytes 1228808 | tf_op jit(solution)/shard_map/ppermute | solution.py:317
  55.8 13.3 %collective-permute-start.11 = (bf16[4,96,640]{2,1,0:T(8,128)(2,1)S(1)}, bf16[4,96,640]{2,1,0:T(8,128)(2,1)S(1)}, u32[]{:S(2)}, u32[]{:S(2)}) collective-permute-start(bf16[4,96,640]{2,1,0:T(8,128)(2,1)S(1)} %get-tuple-element.66), channel_id=1, source_target_pairs={{0,1},{1,0},{2,3},{3,2},{4,5},{5,4},{6,7},{7,6},{8,9},{9,8},{10,11... | collective-permute-start | bytes 1474568 | tf_op jit(solution)/shard_map/ppermute | solution.py:317
  65.2 6.8 %collective-permute-start.15 = (bf16[2,80,640]{2,1,0:T(8,128)(2,1)S(1)}, bf16[2,80,640]{2,1,0:T(8,128)(2,1)S(1)}, u32[]{:S(2)}, u32[]{:S(2)}) collective-permute-start(bf16[2,80,640]{2,1,0:T(8,128)(2,1)S(1)} %slice.98), channel_id=1, source_target_pairs={{0,4},{1,5},{2,6},{3,7},{4,0},{5,1},{6,2},{7,3},{8,12},{9,13},{10,... | collective-permute-start | bytes 614408 | tf_op jit(solution)/shard_map/ppermute | solution.py:317
  66.4 6.8 %collective-permute-start.18 = (bf16[2,80,640]{2,1,0:T(8,128)(2,1)S(1)}, bf16[2,80,640]{2,1,0:T(8,128)(2,1)S(1)}, u32[]{:S(2)}, u32[]{:S(2)}) collective-permute-start(bf16[2,80,640]{2,1,0:T(8,128)(2,1)S(1)} %slice.97), channel_id=1, source_target_pairs={{0,1},{1,0},{2,3},{3,2},{4,5},{5,4},{6,7},{7,6},{8,9},{9,8},{10,11... | collective-permute-start | bytes 614408 | tf_op jit(solution)/shard_map/ppermute | solution.py:317
  69.2 9.1 %collective-permute-start.12 = (bf16[2,96,640]{2,1,0:T(8,128)(2,1)S(1)}, bf16[2,96,640]{2,1,0:T(8,128)(2,1)S(1)}, u32[]{:S(2)}, u32[]{:S(2)}) collective-permute-start(bf16[2,96,640]{2,1,0:T(8,128)(2,1)S(1)} %slice.96), channel_id=1, source_target_pairs={{0,3},{1,2},{2,1},{3,0},{4,7},{5,6},{6,5},{7,4},{8,11},{9,10},{10,... | collective-permute-start | bytes 737288 | tf_op jit(solution)/shard_map/ppermute | solution.py:317
  72.0 4.7 %collective-permute-start.16 = (bf16[80,640]{1,0:T(8,128)(2,1)S(1)}, bf16[80,640]{1,0:T(8,128)(2,1)S(1)}, u32[]{:S(2)}, u32[]{:S(2)}) collective-permute-start(bf16[80,640]{1,0:T(8,128)(2,1)S(1)} %fusion.22), channel_id=1, source_target_pairs={{0,1},{1,0},{2,3},{3,2},{4,5},{5,4},{6,7},{7,6},{8,9},{9,8},{10,11... | collective-permute-start | bytes 307208 | tf_op jit(solution)/shard_map/ppermute | solution.py:317
  73.3 6.2 %collective-permute-start.19 = (bf16[80,640]{1,0:T(8,128)(2,1)S(1)}, bf16[80,640]{1,0:T(8,128)(2,1)S(1)}, u32[]{:S(2)}, u32[]{:S(2)}) collective-permute-start(bf16[80,640]{1,0:T(8,128)(2,1)S(1)} %fusion.23), channel_id=1, source_target_pairs={{0,3},{1,2},{2,1},{3,0},{4,7},{5,6},{6,5},{7,4},{8,11},{9,10},{10,... | collective-permute-start | bytes 307208 | tf_op jit(solution)/shard_map/ppermute | solution.py:317
  78.4 5.0 %collective-permute-start.13 = (bf16[96,640]{1,0:T(8,128)(2,1)S(1)}, bf16[96,640]{1,0:T(8,128)(2,1)S(1)}, u32[]{:S(2)}, u32[]{:S(2)}) collective-permute-start(bf16[96,640]{1,0:T(8,128)(2,1)S(1)} %fusion.21), channel_id=1, source_target_pairs={{0,4},{1,5},{2,6},{3,7},{4,0},{5,1},{6,2},{7,3},{8,12},{9,13},{10,... | collective-permute-start | bytes 368648 | tf_op jit(solution)/shard_map/ppermute | solution.py:317
